TPU v7x, 32 devices: a whole 2x2x4 slice. The times are simulated.
32 devices in a mesh: ep: 16 (over z, y, x), tp: 2 (over core).
Axes of the slice: x: 2, y: 2, z: 4, core: 2. Of those that a mesh axis runs over, the one named last changes fastest.
Arguments:
- tokens: bfloat16 [2048, 4096], P('ep', 'tp'), may hold values from -6 to 6
- routes: int32 [2048, 8], P('ep'), may hold values from 0 to 31, as said below
- gates: float32 [2048, 8], P('ep'), may hold values from 0.02 to 0.5
- up_weight: bfloat16 [32, 4096, 1024], P('ep', 'tp'), may hold values from -0.09375 to 0.09375
- replica_on: int32 [32], replicated, may hold values from 0 to 1, as said below
- grad_out: bfloat16 [2048, 1024], P('ep', 'tp'), may hold values from -6 to 6
Outputs:
- mixed: bfloat16 [2048, 1024], P('ep', 'tp')
- grad_tokens: bfloat16 [2048, 4096], P('ep', 'tp')
- grad_gates: float32 [2048, 8], P('ep')
- grad_up: bfloat16 [32, 4096, 1024], P('ep', 'tp')
Inputs may be any that keep to these rules, and one draw needn't show every extreme that they name: `routes`: each row names 8 different experts; every expert is named by some row. `replica_on`: of the experts j * 2 to (j + 1) * 2 - 1, exactly one has value 1, for every j.
All inputs are finite; a program needn't handle non-finite values.
Results may differ from a plain program's by a relative error of at most 0.0095.
Values may be sent and summed in bfloat16 or wider, within the bound.
No kernel may reach another device: no remote copies, remote signals or barrier semaphores. Data moves between devices by JAX's collectives and lax.ppermute only.
A program may use at most 192 MiB of HBM per device.

v0:
```python
import jax
import jax.numpy as jnp
from jax import lax
from jax.sharding import PartitionSpec as P


def from_behind(value, axis, steps):
    count = lax.axis_size(axis)
    pairs = [(source, (source + steps) % count) for source in range(count)]
    return lax.ppermute(value, axis, pairs)


def derivative(hidden):
    sig = jax.nn.sigmoid(hidden)
    return sig * (1.0 + hidden * (1.0 - sig))


def on_device(tokens, routes, gates, up_weight, replica_on, grad_out):
    count, feat = tokens.shape
    topk = routes.shape[1]
    experts = replica_on.shape[0]
    local = up_weight.shape[0]
    share = grad_out.shape[1]
    n_ep = lax.axis_size("ep")
    half_dev = n_ep // 2
    half_exp = experts // 2
    capacity = 3 * count * topk // (4 * experts)
    pairs = count * topk
    width = 2 * capacity
    total = experts * width
    flat = routes.reshape(pairs)
    onehot = (flat[:, None] == jnp.arange(experts, dtype=jnp.int32)[None, :]).astype(jnp.int32)
    before = jnp.cumsum(onehot, 0) - onehot
    rank = jnp.sum(before * onehot, 1)
    copies = 1 + jnp.sum(onehot * replica_on[None, :], 1)
    copy_index = rank % copies
    slot = rank // copies
    kept = slot < capacity
    target = jnp.where(copy_index == 0, flat, (flat + half_exp) % experts)
    position = jnp.where(kept, target * width + copy_index * capacity + slot, total)
    match = position[None, :] == jnp.arange(total, dtype=jnp.int32)[:, None]
    table = jnp.sum(jnp.where(match, jnp.arange(pairs, dtype=jnp.int32)[None, :], 0), 1)
    table = table + jnp.where(jnp.any(match, 1), 0, pairs).astype(jnp.int32)
    padded_x = jnp.concatenate([tokens, jnp.zeros((1, feat), tokens.dtype)], 0)
    sent_rows = padded_x[table // topk].reshape(experts, width, feat)
    received = lax.all_to_all(sent_rows, "ep", split_axis=0, concat_axis=0, tiled=True).reshape(
        n_ep, local, 2, capacity, feat
    )
    up_copy = from_behind(up_weight, "ep", half_dev)
    up_both = jnp.stack([up_weight, up_copy])
    partial_value = jnp.einsum(
        "nescd,sedf->nescf", received, up_both, preferred_element_type=jnp.float32
    )
    hidden_full = lax.psum(partial_value, "tp")
    start = lax.axis_index("tp") * share
    hidden = lax.dynamic_slice_in_dim(hidden_full, start, share, 4)
    act_share = jax.nn.silu(hidden).astype(jnp.bfloat16).reshape(n_ep * local, width, share)
    returned = lax.all_to_all(act_share, "ep", split_axis=0, concat_axis=0, tiled=True).reshape(
        total, share
    )
    returned = jnp.concatenate([returned, jnp.zeros((1, share), jnp.bfloat16)], 0)
    act_pairs = returned[position].reshape(count, topk, share).astype(jnp.float32)
    mixed = jnp.einsum("tk,tkf->tf", gates, act_pairs).astype(jnp.bfloat16)
    gate_part = jnp.einsum("tkf,tf->tk", act_pairs, grad_out.astype(jnp.float32))
    grad_gates = lax.psum(gate_part, "tp")
    row_grad = (gates[:, :, None] * grad_out[:, None, :].astype(jnp.float32)).astype(jnp.bfloat16)
    padded_g = jnp.concatenate(
        [row_grad.reshape(pairs, share), jnp.zeros((1, share), jnp.bfloat16)], 0
    )
    sent_grads = padded_g[table].reshape(experts, width, share)
    grads_in = lax.all_to_all(sent_grads, "ep", split_axis=0, concat_axis=0, tiled=True).reshape(
        n_ep, local, 2, capacity, share
    )
    grad_part = (grads_in.astype(jnp.float32) * derivative(hidden)).astype(jnp.bfloat16)
    hidden_grad = lax.all_gather(grad_part, "tp", axis=4, tiled=True)
    up_grads = jnp.einsum(
        "nescd,nescf->sedf", received, hidden_grad, preferred_element_type=jnp.float32
    )
    input_rows = jnp.einsum(
        "nescf,sedf->nescd", hidden_grad, up_both, preferred_element_type=jnp.float32
    ).astype(jnp.bfloat16)
    input_rows = input_rows.reshape(n_ep * local, width, feat)
    back_rows = lax.all_to_all(input_rows, "ep", split_axis=0, concat_axis=0, tiled=True).reshape(
        total, feat
    )
    back_rows = jnp.concatenate([back_rows, jnp.zeros((1, feat), jnp.bfloat16)], 0)
    input_pairs = back_rows[position].reshape(count, topk, feat)
    grad_tokens = jnp.sum(input_pairs.astype(jnp.float32), 1).astype(jnp.bfloat16)
    up_back = from_behind(up_grads[1], "ep", half_dev)
    grad_up = (up_grads[0] + up_back).astype(jnp.bfloat16)
    return (mixed, grad_tokens, grad_gates, grad_up)


def solution(mesh):
    return jax.shard_map(
        on_device,
        mesh=mesh,
        in_specs=(
            P("ep", "tp"),
            P("ep", None),
            P("ep", None),
            P("ep", "tp", None),
            P(),
            P("ep", "tp"),
        ),
        out_specs=(P("ep", "tp"), P("ep", "tp"), P("ep", None), P("ep", "tp", None)),
        check_vma=False,
    )
```

profile of v0, /device:TPU:0, one launch (start us, length us, event | category | flops | bytes accessed | tf_op | source)
XLA Modules:
  0.0 1582.1 jit_solution(10375285423189300138)
XLA Ops:
  8.6 9.0 reduce-window.6
  22.1 7.0 gather_fusion
  29.1 8.4 all-to-all-start
  40.4 494.8 %collective-permute-done = bf16[2,2048,1024]{2,1,0:T(8,128)(2,1)} collective-permute-done((bf16[2,2048,1024]{2,1,0:T(8,128)(2,1)}, bf16[2,2048,1024]{2,1,0:T(8,128)(2,1)}, u32[]{:S(2)}, u32[]{:S(2)}) %collective-permute-start) | collective-permute-done | bytes 8388640 | tf_op jit(solution)/shard_map/ppermute | solution.py:10
  535.1 13.8 fusion.10
  550.2 5.4 gather_fusion.2
  555.6 8.7 all-to-all-start.2
  564.5 33.0 %all-to-all-done.2 = bf16[32,48,512]{2,1,0:T(8,128)(2,1)S(1)} async-done(((bf16[32,48,512]{2,1,0:T(8,128)(2,1)}), bf16[32,48,512]{2,1,0:T(8,128)(2,1)S(1)}, u32[]{:S(2)}, u32[]{:S(2)}) %all-to-all-start.2) | async-done | bytes 1572896 | tf_op jit(solution)/shard_map/all_to_all | solution.py:71
  597.5 4.4 fusion.9
  601.9 14.0 all-gather.2.cloned.1.call-done
  615.9 18.1 %fusion.4 = f32[2,2,2048,1024,1]{3,2,1,0,4:T(8,128)} fusion(bf16[16,2,2,24,2048]{4,3,2,1,0:T(8,128)(2,1)} %bitcast.7, bf16[16,2,2,24,1024]{4,3,0,2,1:T(8,128)(2,1)} %all-gather.2.cloned.1.call-done), kind=kOutput, calls=%fused_computation.12 | convolution fusion | flops 6442450944 | bytes 42991616 | tf_op jit(solution)/shard_map/nescd,nescf->sedf/dot_general | solution.py:76
  634.0 12.1 copy.63
  646.1 6.0 slice_bitcast_fusion
  656.3 4.7 all-to-all-start.1
  660.9 13.0 convert_bitcast_fusion
  673.9 6.6 copy.33
  680.5 724.8 %all-to-all-done.1 = bf16[32,48,512]{2,1,0:T(8,128)(2,1)S(1)} async-done(((bf16[32,48,512]{2,1,0:T(8,128)(2,1)}), bf16[32,48,512]{2,1,0:T(8,128)(2,1)S(1)}, u32[]{:S(2)}, u32[]{:S(2)}) %all-to-all-start.1) | async-done | bytes 1572896 | tf_op jit(solution)/shard_map/all_to_all | solution.py:58
  1405.3 10.6 all-to-all-start.3
  1417.0 4.0 gather_fusion.1
  1425.7 109.5 %all-to-all-done.3 = bf16[32,48,2048]{2,1,0:T(8,128)(2,1)} async-done(((bf16[32,48,2048]{2,1,0:T(8,128)(2,1)}), bf16[32,48,2048]{2,1,0:T(8,128)(2,1)}, u32[]{:S(2)}, u32[]{:S(2)}) %all-to-all-start.3) | async-done | bytes 6291488 | tf_op jit(solution)/shard_map/all_to_all | solution.py:83
  1535.3 6.6 concatenate.15
  1541.9 12.4 gather_fusion.3
  1554.3 5.9 bitcast_reduce_fusion
  1560.2 15.1 fusion.1
  (57 shorter events, 20.1 us)
Async XLA Ops:
  8.0 0.6 copy-start
  18.8 0.6 copy-start.3
  29.1 506.0 %all-to-all-start = ((bf16[32,48,2048]{2,1,0:T(8,128)(2,1)}), bf16[32,48,2048]{2,1,0:T(8,128)(2,1)}, u32[]{:S(2)}, u32[]{:S(2)}) async-start(bf16[32,48,2048]{2,1,0:T(8,128)(2,1)} %bitcast.80), calls=%async_computation | async-start | bytes 12582912 | tf_op jit(solution)/shard_map/all_to_all | solution.py:46
  37.5 560.0 %all-reduce.6.cloned.1.call-start = ((), (), s32[]{:S(2)}) async-start(), calls=%async_computation.4 | async-start | bytes 12582912 | tf_op jit(solution)/shard_map/psum | solution.py:54
  37.5 497.6 %collective-permute-start = (bf16[2,2048,1024]{2,1,0:T(8,128)(2,1)}, bf16[2,2048,1024]{2,1,0:T(8,128)(2,1)}, u32[]{:S(2)}, u32[]{:S(2)}) collective-permute-start(bf16[2,2048,1024]{2,1,0:T(8,128)(2,1)} %param.9), channel_id=1, source_target_pairs={{0,16},{2,18},{4,20},{6,22},{8,24},{10,26},{12,28},{14,30},{16,0},... | collective-permute-start | bytes 25165832 | tf_op jit(solution)/shard_map/ppermute | solution.py:10
  548.9 0.7 copy-start.5
  548.9 0.9 copy-start.2
  555.6 41.9 %all-to-all-start.2 = ((bf16[32,48,512]{2,1,0:T(8,128)(2,1)}), bf16[32,48,512]{2,1,0:T(8,128)(2,1)S(1)}, u32[]{:S(2)}, u32[]{:S(2)}) async-start(bf16[32,48,512]{2,1,0:T(8,128)(2,1)} %bitcast.19), calls=%async_computation.2 | async-start | bytes 3145728 | tf_op jit(solution)/shard_map/all_to_all | solution.py:71
  564.3 51.6 %all-gather.2.cloned.1.call-start = ((), (), s32[]{:S(2)}) async-start(), calls=%async_computation.5 | async-start | bytes 4718592 | tf_op jit(solution)/shard_map/all_gather | solution.py:75
  652.2 908.0 %collective-permute-start.1 = (f32[2,2048,1024]{2,1,0:T(8,128)}, f32[2,2048,1024]{2,1,0:T(8,128)}, u32[]{:S(2)}, u32[]{:S(2)}) collective-permute-start(f32[2,2048,1024]{2,1,0:T(8,128)} %slice_bitcast_fusion), channel_id=1, source_target_pairs={{0,16},{2,18},{4,20},{6,22},{8,24},{10,26},{12,28},{14,30},{16,0},... | collective-permute-start | bytes 50331656 | tf_op jit(solution)/shard_map/ppermute | solution.py:10
  656.3 749.1 %all-to-all-start.1 = ((bf16[32,48,512]{2,1,0:T(8,128)(2,1)}), bf16[32,48,512]{2,1,0:T(8,128)(2,1)S(1)}, u32[]{:S(2)}, u32[]{:S(2)}) async-start(bf16[32,48,512]{2,1,0:T(8,128)(2,1)} %bitcast.9), calls=%async_computation.1 | async-start | bytes 3145728 | tf_op jit(solution)/shard_map/all_to_all | solution.py:58
  1405.3 10.6 copy-start.1
  1405.3 10.8 copy-start.4
  1405.3 10.8 copy-start.6
  1405.3 130.0 %all-to-all-start.3 = ((bf16[32,48,2048]{2,1,0:T(8,128)(2,1)}), bf16[32,48,2048]{2,1,0:T(8,128)(2,1)}, u32[]{:S(2)}, u32[]{:S(2)}) async-start(bf16[32,48,2048]{2,1,0:T(8,128)(2,1)} %bitcast.79), calls=%async_computation.3 | async-start | bytes 12582912 | tf_op jit(solution)/shard_map/all_to_all | solution.py:83
Sparse Core Ops, SparseCore 0:
  549.1 35.0 all-reduce.5
  602.0 13.8 all-gather.1
where the time goes:
time: 1600 us; the launch traced here: 1580 us
  waiting for transfers between devices  1380 us (86%)
  local copies, waits for them, and re-layouts  66.4 us (4%)
  matrix products  45.9 us (3%)
  other arithmetic  38.4 us (2%)
  starting transfers between devices  38 us (2%)
    all_to_all x1, waiting for transfers between devices, on_device(): lax.all_to_all(act_share, 'ep', split_axis=0, concat_axis=0, tiled=True)  725 us
    ppermute x2, waiting for transfers between devices, from_behind(): return lax.ppermute(value, axis, pairs)  495 us
    all_to_all x1, waiting for transfers between devices, on_device(): lax.all_to_all(input_rows, 'ep', split_axis=0, concat_axis=0, tiled=True)  110 us
    all_to_all x1, waiting for transfers between devices, on_device(): lax.all_to_all(sent_grads, 'ep', split_axis=0, concat_axis=0, tiled=True)  33 us
  transfers between devices with their start and end apart: 8, of which 5 were waited for; matrix products, arithmetic and copies ran while one was open for 4% of the time, Pallas kernels for 0%

commit v1 on v0

v1 whole, which is shorter than its diff:
```python
import functools

import jax
import jax.numpy as jnp
from jax import lax
from jax.experimental import pallas as pl
from jax.experimental.pallas import tpu as pltpu
from jax.sharding import PartitionSpec as P

INNER = 4
CHUNKS = 4
TAIL = 128
LIMIT = 44 * 1024 * 1024
F32, BF16, I32 = jnp.float32, jnp.bfloat16, jnp.int32


def params(**extra):
    return pltpu.CompilerParams(vmem_limit_bytes=LIMIT, **extra)


def cost(flops, moved):
    return pl.CostEstimate(flops=int(flops), bytes_accessed=int(moved), transcendentals=0)


def whole_specs(n):
    return [pl.BlockSpec(memory_space=pltpu.VMEM)] * n


def hot_of(info, device):
    return info[2 + 2 * device + 1]


def rows_joined(pieces):
    if all(piece.shape[0] % 16 == 0 for piece in pieces):
        return jnp.concatenate(pieces, 0)
    return jnp.concatenate([piece.astype(F32) for piece in pieces], 0).astype(BF16)


def payload_kernel(tokens, routes, gates, grad_out, out):
    count, feat = tokens.shape
    share = grad_out.shape[1]
    topk = routes.shape[0]
    out[:, :feat] = tokens[...]
    out[:, feat : feat + share] = grad_out[...]
    ids = routes[...].astype(F32)
    gate = gates[...]
    high = gate.astype(BF16).astype(F32)
    middle = (gate - high).astype(BF16).astype(F32)
    low = (gate - high - middle).astype(BF16).astype(F32)
    rest = jnp.zeros((TAIL - 5 * topk, count), F32)
    tail = jnp.concatenate([ids, ids, high, middle, low, rest], 0)
    out[:, feat + share :] = tail.T.astype(BF16)


def select_kernel(m, hot_rows, cold_rows, topk, n_next, info, *refs):
    payloads, passed, refs = refs[:m], refs[m : m + n_next], refs[m + n_next + 1 :]
    outs, picks, passed_on = refs[:INNER], refs[INNER : INNER + m], refs[INNER + m :]
    for source, target in zip(passed, passed_on):
        target[...] = source[...]
    count, width = payloads[0].shape
    rows = m * (hot_rows + cold_rows)
    cols = INNER * rows
    me = info[0]
    outer, inner = me // INNER, me % INNER
    spot = lax.broadcasted_iota(I32, (8, cols), 1)
    which = jnp.zeros((8, cols), I32)
    for d in range(1, INNER):
        which += (spot >= d * rows).astype(I32)
    within = spot - which * rows
    is_hot = within < m * hot_rows
    group = jnp.zeros((8, cols), I32)
    for s in range(1, m):
        edge = jnp.where(is_hot, s * hot_rows, m * hot_rows + s * cold_rows)
        group += (within >= edge).astype(I32)
    slot = jnp.where(is_hot, within - group * hot_rows, within - m * hot_rows - group * cold_rows)
    expert = jnp.zeros((8, cols), I32)
    for d in range(INNER):
        device = outer * INNER + (inner ^ d)
        hot = hot_of(info, device)
        ids = jnp.where(is_hot, 2 * device + hot, 2 * device + 1 - hot)
        expert = jnp.where(which == d, ids, expert)
    expert = expert.astype(F32)[0:1]
    slot = slot.astype(F32)[0:1]
    group = group[0:1]
    before = lax.broadcasted_iota(I32, (count, count), 1) < lax.broadcasted_iota(I32, (count, count), 0)
    before = jnp.where(before, 1.0, 0.0).astype(BF16)
    found = []
    for s in range(m):
        ids = payloads[s][:, width - TAIL :].astype(F32)
        match = ids[:, 0:1] == expert
        for k in range(1, topk):
            match = match | (ids[:, k : k + 1] == expert)
        ones = jnp.where(match, 1.0, 0.0)
        rank = jnp.dot(before, ones.astype(BF16), preferred_element_type=F32)
        pick = jnp.where((rank == slot) & (group == s), ones, 0.0).astype(BF16)
        picks[s][...] = pick
        found.append(pick)
    step = 384 if width % 384 == 0 else 128
    for at in range(0, width, step):
        total = None
        for s in range(m):
            part = lax.dot_general(
                found[s],
                payloads[s][:, at : at + step],
                (((0,), (0,)), ((), ())),
                preferred_element_type=F32,
            )
            total = part if total is None else total + part
        for d in range(INNER):
            outs[d][:, at : at + step] = total[d * rows : (d + 1) * rows].astype(BF16)


def hidden_kernel(m, hot_rows, cold_rows, feat, info, *refs):
    blocks = refs[:INNER]
    weight, _, part, x_hot, x_cold = refs[INNER:]
    hots = INNER * m * hot_rows
    ff_tile = weight.shape[2]
    ff = part.shape[1] - (blocks[0].shape[1] - feat - TAIL)
    share = part.shape[1] - ff
    j = pl.program_id(0)
    hot = hot_of(info, info[0])

    @pl.when(j == 0)
    def _():
        split = m * hot_rows
        x_hot[...] = rows_joined([b[:split, :feat] for b in blocks])
        x_cold[...] = rows_joined([b[split:, :feat] for b in blocks])
        part[:hots, ff:] = rows_joined([b[:split, feat : feat + share] for b in blocks])
        part[hots:, ff:] = rows_joined([b[split:, feat : feat + share] for b in blocks])

    at = pl.ds(pl.multiple_of(j * ff_tile, ff_tile), ff_tile)
    part[:hots, at] = jnp.dot(x_hot[...], weight[hot], preferred_element_type=F32).astype(BF16)
    part[hots:, at] = jnp.dot(x_cold[...], weight[1 - hot], preferred_element_type=F32).astype(BF16)


def back_kernel(m, hot_rows, cold_rows, n_parts, n_grads, topk, share, info, *refs):
    sums, grads = refs[:n_parts], refs[n_parts : n_parts + n_grads]
    refs = refs[n_parts + n_grads :]
    tails, weight, outs = refs[:INNER], refs[INNER], refs[INNER + 2 : 2 * INNER + 2]
    g_hot, g_cold = refs[2 * INNER + 2 :]
    hots, colds = INNER * m * hot_rows, INNER * m * cold_rows
    ff = weight.shape[2]
    tile = weight.shape[1]
    width = outs[0].shape[1]
    me, tp = info[0], info[1]
    hot = hot_of(info, me)
    split = m * hot_rows
    j = pl.program_id(0)
    own = width - TAIL

    @pl.when(j == 0)
    def _():
        for first, size, piece, target, expert in (
            (0, hots, m * hot_rows, g_hot, 2 * me + hot),
            (hots, colds, m * cold_rows, g_cold, 2 * me + 1 - hot),
        ):
            begin = 0 if first == 0 else split
            tail_rows = [t[begin : begin + piece].astype(F32) for t in tails]
            per = 1 if piece % 16 == 0 else INNER
            for d in range(0, INNER, per):
                count = piece * per
                rows = slice(first + d * piece, first + d * piece + count)
                tail = jnp.concatenate(tail_rows[d : d + per], 0)
                hidden = sums[0][rows, :ff].astype(F32)
                for more in sums[1:]:
                    hidden = hidden + more[rows, :ff].astype(F32)
                if n_grads == 1:
                    grad = grads[0][rows].astype(F32)
                else:
                    mine, other = grads[0][rows].astype(F32), grads[1][rows].astype(F32)
                    even = tp == 0
                    grad = jnp.concatenate(
                        [jnp.where(even, mine, other), jnp.where(even, other, mine)], 1
                    )
                e = expert.astype(F32)
                ids = tail[:, :topk]
                gate = (tail[:, 2 * topk : 3 * topk] + tail[:, 3 * topk : 4 * topk]) + tail[:, 4 * topk : 5 * topk]
                gate = jnp.sum(jnp.where(ids == e, gate, 0.0), 1, keepdims=True)
                sig = 1.0 / (1.0 + jnp.exp(-hidden))
                act = (hidden * sig).astype(BF16).astype(F32)
                row_grad = (gate * grad).astype(BF16).astype(F32)
                hidden_grad = row_grad * (sig * (1.0 + hidden * (1.0 - sig)))
                target[d * piece : d * piece + count] = hidden_grad.astype(BF16)
                gate_grad = jnp.sum(act * grad, 1, keepdims=True)
                high = gate_grad.astype(BF16).astype(F32)
                low = gate_grad - high
                lane = lax.broadcasted_iota(I32, tail.shape, 1)
                values = jnp.where(lane < topk, high, low)
                end = jnp.where((tail == e) & (lane < 2 * topk), values, 0.0)
                gated = None
                for n in range(ff // share):
                    piece_act = jnp.where(tp == n, act[:, n * share : (n + 1) * share], 0.0)
                    gated = piece_act if gated is None else gated + piece_act
                gated = gate * gated
                for n in range(per):
                    at = slice(n * piece, (n + 1) * piece)
                    outs[d + n][begin : begin + piece, own - share : own] = gated[at].astype(BF16)
                    outs[d + n][begin : begin + piece, own:] = end[at].astype(BF16)

    at = pl.ds(pl.multiple_of(j * tile, tile), tile)
    for target, weight_now, begin, piece in (
        (g_hot, weight[hot], 0, m * hot_rows),
        (g_cold, weight[1 - hot], split, m * cold_rows),
    ):
        rows = lax.dot_general(
            target[...], weight_now, (((1,), (1,)), ((), ())), preferred_element_type=F32
        )
        for d in range(INNER):
            outs[d][begin : begin + piece, at] = rows[d * piece : (d + 1) * piece].astype(BF16)


def expand_kernel(m, *refs):
    blocks, picks, outs = refs[:INNER], refs[INNER : INNER + m], refs[INNER + m + 1 :]
    width = blocks[0].shape[1]
    step = 384 if width % 384 == 0 else 128
    for at in range(0, width, step):
        rows = rows_joined([b[:, at : at + step] for b in blocks])
        for s in range(m):
            outs[s][:, at : at + step] = jnp.dot(
                picks[s][...], rows, preferred_element_type=F32
            ).astype(BF16)


def final_kernel(n, topk, *refs):
    parts = refs[:n]
    mixed, grad_tokens, grad_gates = refs[n:]
    feat, share = grad_tokens.shape[1], mixed.shape[1]

    def total(columns):
        out = parts[0][:, columns].astype(F32)
        for part in parts[1:]:
            out = out + part[:, columns].astype(F32)
        return out

    grad_tokens[...] = total(slice(0, feat)).astype(BF16)
    mixed[...] = total(slice(feat, feat + share)).astype(BF16)
    tail = total(slice(feat + share, feat + share + TAIL))
    tail = tail.T
    grad_gates[...] = tail[:topk] + tail[topk : 2 * topk]


def up_kernel(n, info, *refs):
    x_hot, x_cold = refs[:n], refs[n : 2 * n]
    g_hot, g_cold = refs[2 * n : 3 * n], refs[3 * n : 4 * n]
    out = refs[4 * n + 1]

    def total(xs, gs):
        acc = None
        for x, g in zip(xs, gs):
            part = lax.dot_general(
                x[...], g[...], (((0,), (0,)), ((), ())), preferred_element_type=F32
            )
            acc = part if acc is None else acc + part
        out[0] = acc.astype(BF16)

    @pl.when(pl.program_id(0) == 0)
    def _():
        total(x_hot, g_hot)

    @pl.when(pl.program_id(0) == 1)
    def _():
        total(x_cold, g_cold)


def on_device(tokens, routes, gates, up_weight, replica_on, grad_out):
    count, feat = tokens.shape
    topk = routes.shape[1]
    experts = replica_on.shape[0]
    share = grad_out.shape[1]
    ff = up_weight.shape[2]
    n_ep, n_tp = lax.axis_size("ep"), lax.axis_size("tp")
    outer = n_ep // INNER
    capacity = 3 * count * topk // (4 * experts)
    hot_rows, cold_rows = 2 * capacity, capacity
    width = feat + share + TAIL
    me, tp = lax.axis_index("ep"), lax.axis_index("tp")
    info = jnp.concatenate([jnp.stack([me, tp]).astype(I32), replica_on])
    smem = pl.BlockSpec(memory_space=pltpu.SMEM)

    def along(value, shift):
        pairs = [
            (o * INNER + i, ((o + shift) % outer) * INNER + i)
            for o in range(outer)
            for i in range(INNER)
        ]
        return lax.ppermute(value, "ep", pairs)

    def across(value, d):
        pairs = [(o * INNER + i, o * INNER + (i ^ d)) for o in range(outer) for i in range(INNER)]
        return lax.ppermute(value, "ep", pairs)

    payload = pl.pallas_call(
        payload_kernel,
        out_shape=jax.ShapeDtypeStruct((count, width), BF16),
        in_specs=whole_specs(4),
        out_specs=whole_specs(1)[0],
        compiler_params=params(),
        cost_estimate=cost(0, 4 * count * width),
        name="payload",
    )(tokens, routes.T, gates.T, grad_out)

    last = [payload]
    rest_spec = pl.BlockSpec(memory_space=pl.ANY)
    m = max(1, outer // CHUNKS)
    chunks = [list(range(first, first + m)) for first in range(0, outer, m)]
    n = len(chunks)
    rows = m * (hot_rows + cold_rows)
    hots, colds = INNER * m * hot_rows, INNER * m * cold_rows
    ff_tile = 256 if ff % 256 == 0 else ff
    d_tile = 512 if feat % 512 == 0 else feat
    small = cost(10**6, 10**5)

    def block(shape, dtype=BF16):
        return jax.ShapeDtypeStruct(shape, dtype)

    carried = {0: payload, 1: payload}
    picks, blocks, sums, grads, sent, partials = {}, {}, {}, {}, {}, {}
    x_hots, x_colds, g_hots, g_colds = {}, {}, {}, {}

    def select(c):
        passed = [payload] if 0 < c < n - 1 else []
        made = pl.pallas_call(
            functools.partial(select_kernel, m, hot_rows, cold_rows, topk, len(passed)),
            out_shape=[block((rows, width))] * INNER
            + [block((count, INNER * rows))] * m
            + [block((count, width))] * len(passed),
            in_specs=[smem] + whole_specs(m + len(passed)) + [rest_spec],
            out_specs=whole_specs(INNER + m + len(passed)),
            compiler_params=params(),
            cost_estimate=small,
            name="select",
        )(info, *[along(carried[c], s) if s else payload for s in chunks[c]], *passed, last[0])
        picks[c] = made[INNER : INNER + m]
        if passed:
            carried[c + 1] = made[INNER + m]
        blocks[c] = [made[0]] + [across(made[d], d) for d in range(1, INNER)]
        last[0] = picks[c][0]

    def hidden(c):
        part, x_hots[c], x_colds[c] = pl.pallas_call(
            functools.partial(hidden_kernel, m, hot_rows, cold_rows, feat),
            out_shape=[block((INNER * rows, ff + share)), block((hots, feat)), block((colds, feat))],
            grid=(ff // ff_tile,),
            in_specs=[smem]
            + [pl.BlockSpec((rows, width), lambda j: (0, 0))] * INNER
            + [pl.BlockSpec((2, feat, ff_tile), lambda j: (0, 0, j)), rest_spec],
            out_specs=[
                pl.BlockSpec((INNER * rows, ff + share), lambda j: (0, 0)),
                pl.BlockSpec((hots, feat), lambda j: (0, 0)),
                pl.BlockSpec((colds, feat), lambda j: (0, 0)),
            ],
            compiler_params=params(),
            cost_estimate=small,
            name="hidden",
        )(info, *blocks[c], up_weight, last[0])
        last[0] = x_colds[c]
        if n_tp == 2:
            sums[c] = [part, lax.ppermute(part, "tp", [(0, 1), (1, 0)])]
            grads[c] = sums[c]
        else:
            sums[c] = [lax.psum(part[:, :ff].astype(F32), "tp")]
            grads[c] = [lax.all_gather(part[:, ff:], "tp", axis=1, tiled=True)]

    def back(c):
        if n_tp == 2:
            grad_specs = [pl.BlockSpec((INNER * rows, share), lambda j: (0, ff // share))] * 2
        else:
            grad_specs = [pl.BlockSpec((INNER * rows, ff), lambda j: (0, 0))]
        made = pl.pallas_call(
            functools.partial(
                back_kernel, m, hot_rows, cold_rows, len(sums[c]), len(grads[c]), topk, share
            ),
            out_shape=[block((rows, width))] * INNER + [block((hots, ff)), block((colds, ff))],
            grid=(feat // d_tile,),
            in_specs=[smem]
            + [pl.BlockSpec((INNER * rows, ff), lambda j: (0, 0))] * len(sums[c])
            + grad_specs
            + [pl.BlockSpec((rows, TAIL), lambda j: (0, width // TAIL - 1))] * INNER
            + [pl.BlockSpec((2, d_tile, ff), lambda j: (0, j, 0)), rest_spec],
            out_specs=[pl.BlockSpec((rows, width), lambda j: (0, 0))] * INNER
            + [pl.BlockSpec((hots, ff), lambda j: (0, 0)), pl.BlockSpec((colds, ff), lambda j: (0, 0))],
            compiler_params=params(),
            cost_estimate=small,
            name="back",
        )(info, *sums[c], *grads[c], *blocks[c], up_weight, last[0])
        g_hots[c], g_colds[c] = made[INNER:]
        sent[c] = [made[0]] + [across(made[d], d) for d in range(1, INNER)]
        last[0] = g_colds[c]

    def expand(c):
        made = pl.pallas_call(
            functools.partial(expand_kernel, m),
            out_shape=[block((count, width))] * m,
            in_specs=whole_specs(INNER + m) + [rest_spec],
            out_specs=whole_specs(m),
            compiler_params=params(),
            cost_estimate=small,
            name="expand",
        )(*sent[c], *picks[c], last[0])
        for s, value in zip(chunks[c], made):
            partials[s] = along(value, outer - s) if s else value
        last[0] = made[0]

    def weight_grad():
        grad_up = pl.pallas_call(
            functools.partial(up_kernel, n),
            out_shape=block(up_weight.shape),
            grid_spec=pltpu.PrefetchScalarGridSpec(
                num_scalar_prefetch=1,
                grid=(2, feat // 256),
                in_specs=[pl.BlockSpec((hots, 256), lambda e, j, info: (0, j))] * n
                + [pl.BlockSpec((colds, 256), lambda e, j, info: (0, j))] * n
                + [pl.BlockSpec((hots, ff), lambda e, j, info: (0, 0))] * n
                + [pl.BlockSpec((colds, ff), lambda e, j, info: (0, 0))] * n
                + [rest_spec],
                out_specs=pl.BlockSpec(
                    (1, 256, ff),
                    lambda e, j, info: (e + hot_of(info, info[0]) * (1 - 2 * e), j, 0),
                ),
            ),
            compiler_params=params(),
            cost_estimate=small,
            name="grad_up",
        )(
            info,
            *[x_hots[c] for c in range(n)],
            *[x_colds[c] for c in range(n)],
            *[g_hots[c] for c in range(n)],
            *[g_colds[c] for c in range(n)],
            last[0],
        )
        last[0] = grad_up
        return grad_up

    select(0)
    select(1)
    hidden(0)
    hidden(1)
    select(2)
    back(1)
    select(3)
    hidden(2)
    expand(1)
    back(2)
    hidden(3)
    back(3)
    expand(2)
    back(0)
    expand(3)
    grad_up = weight_grad()
    expand(0)

    mixed, grad_tokens, grad_gates = pl.pallas_call(
        functools.partial(final_kernel, outer, topk),
        out_shape=[block((count, share)), block((count, feat)), block((topk, count), F32)],
        in_specs=whole_specs(outer),
        out_specs=whole_specs(3),
        compiler_params=params(),
        cost_estimate=small,
        name="final",
    )(*[partials[s] for s in range(outer)])
    return mixed, grad_tokens, grad_gates.T, grad_up


def solution(mesh):
    return jax.shard_map(
        on_device,
        mesh=mesh,
        in_specs=(
            P("ep", "tp"),
            P("ep", None),
            P("ep", None),
            P("ep", "tp", None),
            P(),
            P("ep", "tp"),
        ),
        out_specs=(P("ep", "tp"), P("ep", "tp"), P("ep", None), P("ep", "tp", None)),
        check_vma=False,
    )
```

time: 1600 us -> 223 us (0.14); the launches traced: 1580 us -> 222 us
  waiting for transfers between devices: 1380 us -> 96.2 us
  Pallas kernels: 0 us -> 76.7 us
  local copies, waits for them, and re-layouts: 66.4 us -> 3.31 us
  matrix products: 45.9 us -> 0 us
  other arithmetic: 38.4 us -> 0.73 us
    all_to_all x4 -> x0, waiting for transfers between devices: 867 us -> none  [the longest x1 725 us: on_device(): lax.all_to_all(act_share, 'ep', split_axis=0, concat_axis=0, tiled=True)]
    ppermute x2 -> x34, waiting for transfers between devices: 495 us -> 96.2 us  [the longest x24 50.9 us: across(): return lax.ppermute(value, 'ep', pairs)]
    pallas_call x0 -> x19, Pallas kernels: none -> 76.7 us  [the longest x4 30.1 us: back(): pl.pallas_call(functools.partial(back_kernel, m, hot_rows, cold_rows, len...]
    dot_general x5 -> x0, matrix products: 45.9 us -> none  [the longest x1 18.1 us: on_device(): jnp.einsum('nescd,nescf->sedf', received, hidden_grad, preferred_element_...]
    ppermute x2 -> x34, starting transfers between devices: 5.51 us -> 44.7 us  [the longest x24 35.4 us: across(): return lax.ppermute(value, 'ep', pairs)]
    all_to_all x4 -> x0, starting transfers between devices: 32.3 us -> none  [the longest x1 10.6 us: on_device(): lax.all_to_all(input_rows, 'ep', split_axis=0, concat_axis=0, tiled=True)]
    gather x4 -> x0, local copies, waits for them, and re-layouts: 28.8 us -> none  [the longest x1 12.4 us: on_device(): input_pairs = back_rows[position].reshape(count, topk, feat)]
    convert_element_type x5 -> x0, other arithmetic: 19.7 us -> none  [the longest x1 15.1 us: on_device(): grad_up = (up_grads[0] + up_back).astype(jnp.bfloat16)]
  transfers between devices with their start and end apart: 8 -> 34, of which waited for: 5 -> 14; matrix products, arithmetic and copies ran while one was open for 4% -> 0% of each run, Pallas kernels for 0% -> 29%
where the time goes in v1:
time: 223 us; the launch traced here: 222 us
  waiting for transfers between devices  96.2 us (43%)
  Pallas kernels  76.7 us (34%)
  starting transfers between devices  44.7 us (20%)
  local copies, waits for them, and re-layouts  3.31 us (1%)
    ppermute x24, waiting for transfers between devices, across(): return lax.ppermute(value, 'ep', pairs)  50.9 us
    ppermute x6, waiting for transfers between devices, along(): return lax.ppermute(value, 'ep', pairs)  45.2 us
    ppermute x24, starting transfers between devices, across(): return lax.ppermute(value, 'ep', pairs)  35.4 us
    pallas_call x4, Pallas kernels, back(): pl.pallas_call(functools.partial(back_kernel, m, hot_rows, cold_rows, len...  30.1 us
    pallas_call x4, Pallas kernels, hidden(): pl.pallas_call(functools.partial(hidden_kernel, m, hot_rows, cold_rows, f...  20.7 us
    pallas_call x1, Pallas kernels, weight_grad(): pl.pallas_call(functools.partial(up_kernel, n), out_shape=block(up_weight...  15.7 us
    ppermute x6, starting transfers between devices, along(): return lax.ppermute(value, 'ep', pairs)  8.55 us
    pallas_call x4, Pallas kernels, select(): pl.pallas_call(functools.partial(select_kernel, m, hot_rows, cold_rows, t...  6.17 us
  transfers between devices with their start and end apart: 34, of which 14 were waited for; matrix products, arithmetic and copies ran while one was open for 0% of the time, Pallas kernels for 29%

profile of v1, /device:TPU:0, one launch (start us, length us, event | category | flops | bytes accessed | tf_op | source)
XLA Modules:
  0.0 222.4 jit_solution(5827125757266818128)
XLA Ops:
  4.1 3.1 %collective-permute-start.3 = (bf16[128,2688]{1,0:T(8,128)(2,1)S(1)}, bf16[128,2688]{1,0:T(8,128)(2,1)S(1)}, u32[]{:S(2)}, u32[]{:S(2)}) collective-permute-start(bf16[128,2688]{1,0:T(8,128)(2,1)S(1)} %payload.1.refs_0_.refs_1_), channel_id=1, source_target_pairs={{0,8},{2,10},{4,12},{6,14},{8,16},{10,18},{12,20},{14,22},{16,24},... | collective-permute-start | bytes 2064392 | tf_op jit(solution)/shard_map/ppermute | solution.py:286
  12.5 12.1 %collective-permute-done.3.refs_0_ = bf16[128,2688]{1,0:T(8,128)(2,1)S(1)} collective-permute-done((bf16[128,2688]{1,0:T(8,128)(2,1)S(1)}, bf16[128,2688]{1,0:T(8,128)(2,1)S(1)}, u32[]{:S(2)}, u32[]{:S(2)}) %collective-permute-start.3) | collective-permute-done | bytes 688160 | tf_op jit(solution)/shard_map/ppermute | solution.py:286
  26.9 2.4 %collective-permute-start.2 = (bf16[72,2688]{1,0:T(8,128)(2,1)S(1)}, bf16[72,2688]{1,0:T(8,128)(2,1)S(1)}, u32[]{:S(2)}, u32[]{:S(2)}) collective-permute-start(bf16[72,2688]{1,0:T(8,128)(2,1)S(1)} %get-tuple-element.68), channel_id=1, source_target_pairs={{0,6},{2,4},{4,2},{6,0},{8,14},{10,12},{12,10},{14,8},{16,22},{18,... | collective-permute-start | bytes 1161224 | tf_op jit(solution)/shard_map/ppermute | solution.py:290
  32.9 6.9 %collective-permute-done.2.refs_3_.refs_7_ = bf16[72,2688]{1,0:T(8,128)(2,1)S(1)} collective-permute-done((bf16[72,2688]{1,0:T(8,128)(2,1)S(1)}, bf16[72,2688]{1,0:T(8,128)(2,1)S(1)}, u32[]{:S(2)}, u32[]{:S(2)}) %collective-permute-start.2) | collective-permute-done | bytes 387104 | tf_op jit(solution)/shard_map/ppermute | solution.py:290
  39.8 5.2 %hidden.4 = (bf16[288,1536]{1,0:T(8,128)(2,1)S(1)}, bf16[192,2048]{1,0:T(8,128)(2,1)S(1)}, bf16[96,2048]{1,0:T(8,128)(2,1)S(1)}) custom-call(s32[34]{0:T(128)S(1)} %pad_add_fusion.info, bf16[72,2688]{1,0:T(8,128)(2,1)S(1)} %get-tuple-element.65.refs_0_.refs_4_, bf16[72,2688]{1,0:T(8,128)(2,1)S(1)} %collective-permute-done.refs_1_.refs_5_, ...), custom_call_target="tpu_custom_call" | custom-call | flops 1000000 | bytes 100000 | tf_op jit(solution)/shard_map/hidden/pallas_call | solution.py:340
  45.0 3.1 %collective-permute-done.6.refs_1_.refs_5_ = bf16[72,2688]{1,0:T(8,128)(2,1)S(1)} collective-permute-done((bf16[72,2688]{1,0:T(8,128)(2,1)S(1)}, bf16[72,2688]{1,0:T(8,128)(2,1)S(1)}, u32[]{:S(2)}, u32[]{:S(2)}) %collective-permute-start.6) | collective-permute-done | bytes 387104 | tf_op jit(solution)/shard_map/ppermute | solution.py:290
  48.1 5.9 %collective-permute-done.8.refs_3_.refs_7_ = bf16[72,2688]{1,0:T(8,128)(2,1)S(1)} collective-permute-done((bf16[72,2688]{1,0:T(8,128)(2,1)S(1)}, bf16[72,2688]{1,0:T(8,128)(2,1)S(1)}, u32[]{:S(2)}, u32[]{:S(2)}) %collective-permute-start.8) | collective-permute-done | bytes 387104 | tf_op jit(solution)/shard_map/ppermute | solution.py:290
  54.0 5.2 %hidden.5 = (bf16[288,1536]{1,0:T(8,128)(2,1)S(1)}, bf16[192,2048]{1,0:T(8,128)(2,1)S(1)}, bf16[96,2048]{1,0:T(8,128)(2,1)S(1)}) custom-call(s32[34]{0:T(128)S(1)} %pad_add_fusion.info, bf16[72,2688]{1,0:T(8,128)(2,1)S(1)} %get-tuple-element.73.refs_0_.refs_4_, bf16[72,2688]{1,0:T(8,128)(2,1)S(1)} %collective-permute-done.6.refs_1_.refs_5_, ...), custom_call_target="tpu_custom_call" | custom-call | flops 1000000 | bytes 100000 | tf_op jit(solution)/shard_map/hidden/pallas_call | solution.py:340
  65.9 7.1 %back.4 = (bf16[72,2688]{1,0:T(8,128)(2,1)S(1)}, bf16[72,2688]{1,0:T(8,128)(2,1)S(1)}, bf16[72,2688]{1,0:T(8,128)(2,1)S(1)}, bf16[72,2688]{1,0:T(8,128)(2,1)S(1)...) custom-call(s32[34]{0:T(128)S(1)} %pad_add_fusion.info, ...), custom_call_target="tpu_custom_call" | custom-call | flops 1000000 | bytes 100000 | tf_op jit(solution)/shard_map/back/pallas_call | solution.py:369
  73.0 5.9 %collective-permute-done.12.refs_0_ = bf16[128,2688]{1,0:T(8,128)(2,1)S(1)} collective-permute-done((bf16[128,2688]{1,0:T(8,128)(2,1)S(1)}, bf16[128,2688]{1,0:T(8,128)(2,1)S(1)}, u32[]{:S(2)}, u32[]{:S(2)}) %collective-permute-start.12) | collective-permute-done | bytes 688160 | tf_op jit(solution)/shard_map/ppermute | solution.py:286
  80.5 2.6 %collective-permute-done.10.refs_2_.refs_6_ = bf16[72,2688]{1,0:T(8,128)(2,1)S(1)} collective-permute-done((bf16[72,2688]{1,0:T(8,128)(2,1)S(1)}, bf16[72,2688]{1,0:T(8,128)(2,1)S(1)}, u32[]{:S(2)}, u32[]{:S(2)}) %collective-permute-start.10) | collective-permute-done | bytes 387104 | tf_op jit(solution)/shard_map/ppermute | solution.py:290
  83.1 5.2 %hidden.6 = (bf16[288,1536]{1,0:T(8,128)(2,1)S(1)}, bf16[192,2048]{1,0:T(8,128)(2,1)S(1)}, bf16[96,2048]{1,0:T(8,128)(2,1)S(1)}) custom-call(s32[34]{0:T(128)S(1)} %pad_add_fusion.info, bf16[72,2688]{1,0:T(8,128)(2,1)S(1)} %get-tuple-element.79.refs_0_.refs_4_, bf16[72,2688]{1,0:T(8,128)(2,1)S(1)} %collective-permute-done.9.refs_1_.refs_5_, ...), custom_call_target="tpu_custom_call" | custom-call | flops 1000000 | bytes 100000 | tf_op jit(solution)/shard_map/hidden/pallas_call | solution.py:340
  93.1 7.1 %collective-permute-done.15.refs_1_ = bf16[72,2688]{1,0:T(8,128)(2,1)S(1)} collective-permute-done((bf16[72,2688]{1,0:T(8,128)(2,1)S(1)}, bf16[72,2688]{1,0:T(8,128)(2,1)S(1)}, u32[]{:S(2)}, u32[]{:S(2)}) %collective-permute-start.15) | collective-permute-done | bytes 387104 | tf_op jit(solution)/shard_map/ppermute | solution.py:290
  101.7 5.3 %collective-permute-done.16.refs_2_ = bf16[72,2688]{1,0:T(8,128)(2,1)S(1)} collective-permute-done((bf16[72,2688]{1,0:T(8,128)(2,1)S(1)}, bf16[72,2688]{1,0:T(8,128)(2,1)S(1)}, u32[]{:S(2)}, u32[]{:S(2)}) %collective-permute-start.16) | collective-permute-done | bytes 387104 | tf_op jit(solution)/shard_map/ppermute | solution.py:290
  107.0 4.1 %collective-permute-start.23 = (bf16[72,2688]{1,0:T(8,128)(2,1)S(1)}, bf16[72,2688]{1,0:T(8,128)(2,1)S(1)}, u32[]{:S(2)}, u32[]{:S(2)}) collective-permute-start(bf16[72,2688]{1,0:T(8,128)(2,1)S(1)} %get-tuple-element.101), channel_id=1, source_target_pairs={{0,6},{2,4},{4,2},{6,0},{8,14},{10,12},{12,10},{14,8},{16,22},{18,... | collective-permute-start | bytes 1161224 | tf_op jit(solution)/shard_map/ppermute | solution.py:290
  111.8 8.0 %back.5 = (bf16[72,2688]{1,0:T(8,128)(2,1)S(1)}, bf16[72,2688]{1,0:T(8,128)(2,1)}, bf16[72,2688]{1,0:T(8,128)(2,1)}, bf16[72,2688]{1,0:T(8,128)(2,1)S(1)}, bf16[...) custom-call(s32[34]{0:T(128)S(1)} %pad_add_fusion.info, bf16[288,1536]{1,0:T(8,128)(2,1)S(1)} %get-tuple-element.88.refs_0_.refs_2_, ...), custom_call_target="tpu_custom_call" | custom-call | flops 1000000 | bytes 100000 | tf_op jit(solution)/shard_map/back/pallas_call | solution.py:369
  119.7 5.9 %collective-permute-done.23.refs_3_.refs_7_ = bf16[72,2688]{1,0:T(8,128)(2,1)S(1)} collective-permute-done((bf16[72,2688]{1,0:T(8,128)(2,1)S(1)}, bf16[72,2688]{1,0:T(8,128)(2,1)S(1)}, u32[]{:S(2)}, u32[]{:S(2)}) %collective-permute-start.23) | collective-permute-done | bytes 387104 | tf_op jit(solution)/shard_map/ppermute | solution.py:290
  125.6 5.2 %hidden.7 = (bf16[288,1536]{1,0:T(8,128)(2,1)S(1)}, bf16[192,2048]{1,0:T(8,128)(2,1)S(1)}, bf16[96,2048]{1,0:T(8,128)(2,1)S(1)}) custom-call(s32[34]{0:T(128)S(1)} %pad_add_fusion.info, bf16[72,2688]{1,0:T(8,128)(2,1)S(1)} %get-tuple-element.98.refs_0_.refs_4_, bf16[72,2688]{1,0:T(8,128)(2,1)S(1)} %collective-permute-done.21.refs_1_.refs_5_, ...), custom_call_target="tpu_custom_call" | custom-call | flops 1000000 | bytes 100000 | tf_op jit(solution)/shard_map/hidden/pallas_call | solution.py:340
  134.8 8.0 %back.6 = (bf16[72,2688]{1,0:T(8,128)(2,1)S(1)}, bf16[72,2688]{1,0:T(8,128)(2,1)}, bf16[72,2688]{1,0:T(8,128)(2,1)}, bf16[72,2688]{1,0:T(8,128)(2,1)S(1)}, bf16[...) custom-call(s32[34]{0:T(128)S(1)} %pad_add_fusion.info, bf16[288,1536]{1,0:T(8,128)(2,1)S(1)} %get-tuple-element.103.refs_0_.refs_2_, ...), custom_call_target="tpu_custom_call" | custom-call | flops 1000000 | bytes 100000 | tf_op jit(solution)/shard_map/back/pallas_call | solution.py:369
  145.1 5.7 %collective-permute-done.19.refs_2_ = bf16[72,2688]{1,0:T(8,128)(2,1)S(1)} collective-permute-done((bf16[72,2688]{1,0:T(8,128)(2,1)}, bf16[72,2688]{1,0:T(8,128)(2,1)S(1)}, u32[]{:S(2)}, u32[]{:S(2)}) %collective-permute-start.19) | collective-permute-done | bytes 387104 | tf_op jit(solution)/shard_map/ppermute | solution.py:290
  153.1 7.1 %back.7 = (bf16[72,2688]{1,0:T(8,128)(2,1)S(1)}, bf16[72,2688]{1,0:T(8,128)(2,1)S(1)}, bf16[72,2688]{1,0:T(8,128)(2,1)S(1)}, bf16[72,2688]{1,0:T(8,128)(2,1)S(1)...) custom-call(s32[34]{0:T(128)S(1)} %pad_add_fusion.info, ...), custom_call_target="tpu_custom_call" | custom-call | flops 1000000 | bytes 100000 | tf_op jit(solution)/shard_map/back/pallas_call | solution.py:369
  171.2 4.6 %collective-permute-done.25.refs_1_ = bf16[72,2688]{1,0:T(8,128)(2,1)S(1)} collective-permute-done((bf16[72,2688]{1,0:T(8,128)(2,1)S(1)}, bf16[72,2688]{1,0:T(8,128)(2,1)S(1)}, u32[]{:S(2)}, u32[]{:S(2)}) %collective-permute-start.25) | collective-permute-done | bytes 387104 | tf_op jit(solution)/shard_map/ppermute | solution.py:290
  177.5 15.7 %grad_up.1.refs_5_ = bf16[2,2048,1024]{2,1,0:T(8,128)(2,1)} custom-call(s32[34]{0:T(128)S(1)} %pad_add_fusion.info, bf16[192,2048]{1,0:T(8,128)(2,1)S(1)} %get-tuple-element.110.refs_0_, bf16[192,2048]{1,0:T(8,128)(2,1)S(1)} %get-tuple-element.111.refs_1_, bf16[192,2048]{1,0:T(8,128)(2,1)S(1)} %get-tuple-element.112.refs_2_, ...), custom_call_target="tpu_custom_call" | custom-call | flops 1000000 | bytes 100000 | tf_op jit(solution)/shard_map/grad_up/pallas_call | solution.py:405
  193.8 27.2 %collective-permute-done.32.refs_2_ = bf16[128,2688]{1,0:T(8,128)(2,1)S(1)} collective-permute-done((bf16[128,2688]{1,0:T(8,128)(2,1)S(1)}, bf16[128,2688]{1,0:T(8,128)(2,1)S(1)}, u32[]{:S(2)}, u32[]{:S(2)}) %collective-permute-start.32) | collective-permute-done | bytes 688160 | tf_op jit(solution)/shard_map/ppermute | solution.py:286
  (72 shorter events, 53.0 us)
Async XLA Ops:
  4.1 20.5 %collective-permute-start.3 = (bf16[128,2688]{1,0:T(8,128)(2,1)S(1)}, bf16[128,2688]{1,0:T(8,128)(2,1)S(1)}, u32[]{:S(2)}, u32[]{:S(2)}) collective-permute-start(bf16[128,2688]{1,0:T(8,128)(2,1)S(1)} %payload.1.refs_0_.refs_1_), channel_id=1, source_target_pairs={{0,8},{2,10},{4,12},{6,14},{8,16},{10,18},{12,20},{14,22},{16,24},... | collective-permute-start | bytes 2064392 | tf_op jit(solution)/shard_map/ppermute | solution.py:286
  9.4 20.5 %collective-permute-start = (bf16[72,2688]{1,0:T(8,128)(2,1)S(1)}, bf16[72,2688]{1,0:T(8,128)(2,1)S(1)}, u32[]{:S(2)}, u32[]{:S(2)}) collective-permute-start(bf16[72,2688]{1,0:T(8,128)(2,1)S(1)} %get-tuple-element.66), channel_id=1, source_target_pairs={{0,2},{2,0},{4,6},{6,4},{8,10},{10,8},{12,14},{14,12},{16,18},{18,... | collective-permute-start | bytes 1161224 | tf_op jit(solution)/shard_map/ppermute | solution.py:290
  11.0 19.5 %collective-permute-start.1 = (bf16[72,2688]{1,0:T(8,128)(2,1)S(1)}, bf16[72,2688]{1,0:T(8,128)(2,1)S(1)}, u32[]{:S(2)}, u32[]{:S(2)}) collective-permute-start(bf16[72,2688]{1,0:T(8,128)(2,1)S(1)} %get-tuple-element.67), channel_id=1, source_target_pairs={{0,4},{2,6},{4,0},{6,2},{8,12},{10,14},{12,8},{14,10},{16,20},{18,... | collective-permute-start | bytes 1161224 | tf_op jit(solution)/shard_map/ppermute | solution.py:290
  26.1 33.1 %collective-permute-start.5 = (bf16[128,2688]{1,0:T(8,128)(2,1)S(1)}, bf16[128,2688]{1,0:T(8,128)(2,1)S(1)}, u32[]{:S(2)}, u32[]{:S(2)}) collective-permute-start(bf16[128,2688]{1,0:T(8,128)(2,1)S(1)} %get-tuple-element.72), channel_id=1, source_target_pairs={{0,16},{2,18},{4,20},{6,22},{8,24},{10,26},{12,28},{14,30},{16,0},... | collective-permute-start | bytes 2064392 | tf_op jit(solution)/shard_map/ppermute | solution.py:286
  29.4 18.7 %collective-permute-start.6 = (bf16[72,2688]{1,0:T(8,128)(2,1)S(1)}, bf16[72,2688]{1,0:T(8,128)(2,1)S(1)}, u32[]{:S(2)}, u32[]{:S(2)}) collective-permute-start(bf16[72,2688]{1,0:T(8,128)(2,1)S(1)} %get-tuple-element.74), channel_id=1, source_target_pairs={{0,2},{2,0},{4,6},{6,4},{8,10},{10,8},{12,14},{14,12},{16,18},{18,... | collective-permute-start | bytes 1161224 | tf_op jit(solution)/shard_map/ppermute | solution.py:290
  29.9 18.2 %collective-permute-start.7 = (bf16[72,2688]{1,0:T(8,128)(2,1)S(1)}, bf16[72,2688]{1,0:T(8,128)(2,1)S(1)}, u32[]{:S(2)}, u32[]{:S(2)}) collective-permute-start(bf16[72,2688]{1,0:T(8,128)(2,1)S(1)} %get-tuple-element.75), channel_id=1, source_target_pairs={{0,4},{2,6},{4,0},{6,2},{8,12},{10,14},{12,8},{14,10},{16,20},{18,... | collective-permute-start | bytes 1161224 | tf_op jit(solution)/shard_map/ppermute | solution.py:290
  30.4 23.6 %collective-permute-start.8 = (bf16[72,2688]{1,0:T(8,128)(2,1)S(1)}, bf16[72,2688]{1,0:T(8,128)(2,1)S(1)}, u32[]{:S(2)}, u32[]{:S(2)}) collective-permute-start(bf16[72,2688]{1,0:T(8,128)(2,1)S(1)} %get-tuple-element.76), channel_id=1, source_target_pairs={{0,6},{2,4},{4,2},{6,0},{8,14},{10,12},{12,10},{14,8},{16,22},{18,... | collective-permute-start | bytes 1161224 | tf_op jit(solution)/shard_map/ppermute | solution.py:290
  60.9 18.1 %collective-permute-start.12 = (bf16[128,2688]{1,0:T(8,128)(2,1)S(1)}, bf16[128,2688]{1,0:T(8,128)(2,1)S(1)}, u32[]{:S(2)}, u32[]{:S(2)}) collective-permute-start(bf16[128,2688]{1,0:T(8,128)(2,1)S(1)} %get-tuple-element.83), channel_id=1, source_target_pairs={{0,24},{2,26},{4,28},{6,30},{8,0},{10,2},{12,4},{14,6},{16,8},{18,... | collective-permute-start | bytes 2064392 | tf_op jit(solution)/shard_map/ppermute | solution.py:286
  62.5 18.0 %collective-permute-start.9 = (bf16[72,2688]{1,0:T(8,128)(2,1)S(1)}, bf16[72,2688]{1,0:T(8,128)(2,1)S(1)}, u32[]{:S(2)}, u32[]{:S(2)}) collective-permute-start(bf16[72,2688]{1,0:T(8,128)(2,1)S(1)} %get-tuple-element.80), channel_id=1, source_target_pairs={{0,2},{2,0},{4,6},{6,4},{8,10},{10,8},{12,14},{14,12},{16,18},{18,... | collective-permute-start | bytes 1161224 | tf_op jit(solution)/shard_map/ppermute | solution.py:290
  63.9 19.1 %collective-permute-start.10 = (bf16[72,2688]{1,0:T(8,128)(2,1)S(1)}, bf16[72,2688]{1,0:T(8,128)(2,1)S(1)}, u32[]{:S(2)}, u32[]{:S(2)}) collective-permute-start(bf16[72,2688]{1,0:T(8,128)(2,1)S(1)} %get-tuple-element.81), channel_id=1, source_target_pairs={{0,4},{2,6},{4,0},{6,2},{8,12},{10,14},{12,8},{14,10},{16,20},{18,... | collective-permute-start | bytes 1161224 | tf_op jit(solution)/shard_map/ppermute | solution.py:290
  88.2 23.5 %collective-permute-start.14 = (bf16[288,1536]{1,0:T(8,128)(2,1)S(1)}, bf16[288,1536]{1,0:T(8,128)(2,1)S(1)}, u32[]{:S(2)}, u32[]{:S(2)}) collective-permute-start(bf16[288,1536]{1,0:T(8,128)(2,1)S(1)} %get-tuple-element.88.refs_0_.refs_2_), channel_id=1, source_target_pairs={{0,1},{1,0},{2,3},{3,2},{4,5},{5,4},{6,7},{7,6},{8,9},{9,8},{10,11... | collective-permute-start | bytes 2654216 | tf_op jit(solution)/shard_map/ppermute | solution.py:358
  90.4 20.7 %collective-permute-start.17 = (bf16[72,2688]{1,0:T(8,128)(2,1)S(1)}, bf16[72,2688]{1,0:T(8,128)(2,1)S(1)}, u32[]{:S(2)}, u32[]{:S(2)}) collective-permute-start(bf16[72,2688]{1,0:T(8,128)(2,1)S(1)} %get-tuple-element.92), channel_id=1, source_target_pairs={{0,6},{2,4},{4,2},{6,0},{8,14},{10,12},{12,10},{14,8},{16,22},{18,... | collective-permute-start | bytes 1161224 | tf_op jit(solution)/shard_map/ppermute | solution.py:290
  91.9 27.8 %collective-permute-start.21 = (bf16[72,2688]{1,0:T(8,128)(2,1)S(1)}, bf16[72,2688]{1,0:T(8,128)(2,1)S(1)}, u32[]{:S(2)}, u32[]{:S(2)}) collective-permute-start(bf16[72,2688]{1,0:T(8,128)(2,1)S(1)} %get-tuple-element.99), channel_id=1, source_target_pairs={{0,2},{2,0},{4,6},{6,4},{8,10},{10,8},{12,14},{14,12},{16,18},{18,... | collective-permute-start | bytes 1161224 | tf_op jit(solution)/shard_map/ppermute | solution.py:290
  100.2 19.6 %collective-permute-start.22 = (bf16[72,2688]{1,0:T(8,128)(2,1)S(1)}, bf16[72,2688]{1,0:T(8,128)(2,1)S(1)}, u32[]{:S(2)}, u32[]{:S(2)}) collective-permute-start(bf16[72,2688]{1,0:T(8,128)(2,1)S(1)} %get-tuple-element.100), channel_id=1, source_target_pairs={{0,4},{2,6},{4,0},{6,2},{8,12},{10,14},{12,8},{14,10},{16,20},{18,... | collective-permute-start | bytes 1161224 | tf_op jit(solution)/shard_map/ppermute | solution.py:290
  107.0 18.6 %collective-permute-start.23 = (bf16[72,2688]{1,0:T(8,128)(2,1)S(1)}, bf16[72,2688]{1,0:T(8,128)(2,1)S(1)}, u32[]{:S(2)}, u32[]{:S(2)}) collective-permute-start(bf16[72,2688]{1,0:T(8,128)(2,1)S(1)} %get-tuple-element.101), channel_id=1, source_target_pairs={{0,6},{2,4},{4,2},{6,0},{8,14},{10,12},{12,10},{14,8},{16,22},{18,... | collective-permute-start | bytes 1161224 | tf_op jit(solution)/shard_map/ppermute | solution.py:290
  130.9 22.3 %collective-permute-start.4 = (bf16[288,1536]{1,0:T(8,128)(2,1)S(1)}, bf16[288,1536]{1,0:T(8,128)(2,1)S(1)}, u32[]{:S(2)}, u32[]{:S(2)}) collective-permute-start(bf16[288,1536]{1,0:T(8,128)(2,1)S(1)} %get-tuple-element.71.refs_0_.refs_2_), channel_id=1, source_target_pairs={{0,1},{1,0},{2,3},{3,2},{4,5},{5,4},{6,7},{7,6},{8,9},{9,8},{10,11... | collective-permute-start | bytes 2654216 | tf_op jit(solution)/shard_map/ppermute | solution.py:358
  132.1 18.7 %collective-permute-start.19 = (bf16[72,2688]{1,0:T(8,128)(2,1)}, bf16[72,2688]{1,0:T(8,128)(2,1)S(1)}, u32[]{:S(2)}, u32[]{:S(2)}) collective-permute-start(bf16[72,2688]{1,0:T(8,128)(2,1)} %get-tuple-element.96), channel_id=1, source_target_pairs={{0,4},{2,6},{4,0},{6,2},{8,12},{10,14},{12,8},{14,10},{16,20},{18,... | collective-permute-start | bytes 1161224 | tf_op jit(solution)/shard_map/ppermute | solution.py:290
  133.6 18.9 %collective-permute-start.20 = (bf16[72,2688]{1,0:T(8,128)(2,1)S(1)}, bf16[72,2688]{1,0:T(8,128)(2,1)S(1)}, u32[]{:S(2)}, u32[]{:S(2)}) collective-permute-start(bf16[72,2688]{1,0:T(8,128)(2,1)S(1)} %get-tuple-element.97), channel_id=1, source_target_pairs={{0,6},{2,4},{4,2},{6,0},{8,14},{10,12},{12,10},{14,8},{16,22},{18,... | collective-permute-start | bytes 1161224 | tf_op jit(solution)/shard_map/ppermute | solution.py:290
  142.8 22.0 %collective-permute-start.28 = (bf16[72,2688]{1,0:T(8,128)(2,1)}, bf16[72,2688]{1,0:T(8,128)(2,1)S(1)}, u32[]{:S(2)}, u32[]{:S(2)}) collective-permute-start(bf16[72,2688]{1,0:T(8,128)(2,1)} %get-tuple-element.120), channel_id=1, source_target_pairs={{0,2},{2,0},{4,6},{6,4},{8,10},{10,8},{12,14},{14,12},{16,18},{18,... | collective-permute-start | bytes 1161224 | tf_op jit(solution)/shard_map/ppermute | solution.py:290
  143.6 23.6 %collective-permute-start.29 = (bf16[72,2688]{1,0:T(8,128)(2,1)}, bf16[72,2688]{1,0:T(8,128)(2,1)S(1)}, u32[]{:S(2)}, u32[]{:S(2)}) collective-permute-start(bf16[72,2688]{1,0:T(8,128)(2,1)} %get-tuple-element.121), channel_id=1, source_target_pairs={{0,4},{2,6},{4,0},{6,2},{8,12},{10,14},{12,8},{14,10},{16,20},{18,... | collective-permute-start | bytes 1161224 | tf_op jit(solution)/shard_map/ppermute | solution.py:290
  162.4 31.4 %collective-permute-start.31 = (bf16[128,2688]{1,0:T(8,128)(2,1)S(1)}, bf16[128,2688]{1,0:T(8,128)(2,1)S(1)}, u32[]{:S(2)}, u32[]{:S(2)}) collective-permute-start(bf16[128,2688]{1,0:T(8,128)(2,1)S(1)} %expand.4.refs_9_), channel_id=1, source_target_pairs={{0,24},{2,26},{4,28},{6,30},{8,0},{10,2},{12,4},{14,6},{16,8},{18,... | collective-permute-start | bytes 2064392 | tf_op jit(solution)/shard_map/ppermute | solution.py:286
  164.8 56.2 %collective-permute-start.32 = (bf16[128,2688]{1,0:T(8,128)(2,1)S(1)}, bf16[128,2688]{1,0:T(8,128)(2,1)S(1)}, u32[]{:S(2)}, u32[]{:S(2)}) collective-permute-start(bf16[128,2688]{1,0:T(8,128)(2,1)S(1)} %expand.5.refs_9_), channel_id=1, source_target_pairs={{0,16},{2,18},{4,20},{6,22},{8,24},{10,26},{12,28},{14,30},{16,0},... | collective-permute-start | bytes 2064392 | tf_op jit(solution)/shard_map/ppermute | solution.py:286
  169.2 51.8 %collective-permute-start.33 = (bf16[128,2688]{1,0:T(8,128)(2,1)S(1)}, bf16[128,2688]{1,0:T(8,128)(2,1)S(1)}, u32[]{:S(2)}, u32[]{:S(2)}) collective-permute-start(bf16[128,2688]{1,0:T(8,128)(2,1)S(1)} %expand.6.refs_16_), channel_id=1, source_target_pairs={{0,8},{2,10},{4,12},{6,14},{8,16},{10,18},{12,20},{14,22},{16,24},... | collective-permute-start | bytes 2064392 | tf_op jit(solution)/shard_map/ppermute | solution.py:286
  169.9 23.2 %collective-permute-start.26 = (bf16[72,2688]{1,0:T(8,128)(2,1)S(1)}, bf16[72,2688]{1,0:T(8,128)(2,1)S(1)}, u32[]{:S(2)}, u32[]{:S(2)}) collective-permute-start(bf16[72,2688]{1,0:T(8,128)(2,1)S(1)} %get-tuple-element.108), channel_id=1, source_target_pairs={{0,4},{2,6},{4,0},{6,2},{8,12},{10,14},{12,8},{14,10},{16,20},{18,... | collective-permute-start | bytes 1161224 | tf_op jit(solution)/shard_map/ppermute | solution.py:290
  (14 other events, 136.7 us)

commit v2 on v1

v2 whole, which is shorter than its diff:
```python
import functools

import jax
import jax.numpy as jnp
from jax import lax
from jax.experimental import pallas as pl
from jax.experimental.pallas import tpu as pltpu
from jax.sharding import PartitionSpec as P

INNER = 4
CHUNKS = 4
PLAN = ((0, None), (1, None), (2, None), (3, 0), (None, 1), (None, 2), (None, 3))
ORDER = ("x1", "h0", "x2", "h1", "x3", "h2", "x4", "h3", "x5", "e0", "e1", "x6", "e2", "u", "e3")
PASSED = (3,)
COSTS = {"x": 1, "b": 1, "h": 1, "e": 1, "u": 1}
TAIL = 128
LIMIT = 44 * 1024 * 1024
F32, BF16, I32 = jnp.float32, jnp.bfloat16, jnp.int32


def params(**extra):
    return pltpu.CompilerParams(vmem_limit_bytes=LIMIT, **extra)


def cost(flops, moved):
    return pl.CostEstimate(flops=int(flops), bytes_accessed=int(moved), transcendentals=0)


def whole_specs(n):
    return [pl.BlockSpec(memory_space=pltpu.VMEM)] * n


def hot_of(info, device):
    return info[2 + 2 * device + 1]


def rows_joined(pieces):
    if all(piece.shape[0] % 16 == 0 for piece in pieces):
        return jnp.concatenate(pieces, 0)
    return jnp.concatenate([piece.astype(F32) for piece in pieces], 0).astype(BF16)


def pick_rows(m, hot_rows, cold_rows, topk, info, tails):
    count = tails[0].shape[0]
    rows = m * (hot_rows + cold_rows)
    cols = INNER * rows
    me = info[0]
    outer, inner = me // INNER, me % INNER
    spot = lax.broadcasted_iota(I32, (8, cols), 1)
    which = jnp.zeros((8, cols), I32)
    for d in range(1, INNER):
        which += (spot >= d * rows).astype(I32)
    within = spot - which * rows
    is_hot = within < m * hot_rows
    group = jnp.zeros((8, cols), I32)
    for s in range(1, m):
        edge = jnp.where(is_hot, s * hot_rows, m * hot_rows + s * cold_rows)
        group += (within >= edge).astype(I32)
    slot = jnp.where(is_hot, within - group * hot_rows, within - m * hot_rows - group * cold_rows)
    expert = jnp.zeros((8, cols), I32)
    for d in range(INNER):
        device = outer * INNER + (inner ^ d)
        hot = hot_of(info, device)
        ids = jnp.where(is_hot, 2 * device + hot, 2 * device + 1 - hot)
        expert = jnp.where(which == d, ids, expert)
    expert = expert.astype(F32)[0:1]
    slot = slot.astype(F32)[0:1]
    group = group[0:1]
    before = lax.broadcasted_iota(I32, (count, count), 1) < lax.broadcasted_iota(I32, (count, count), 0)
    before = jnp.where(before, 1.0, 0.0).astype(BF16)
    found = []
    for s, ids in enumerate(tails):
        match = ids[:, 0:1] == expert
        for k in range(1, topk):
            match = match | (ids[:, k : k + 1] == expert)
        ones = jnp.where(match, 1.0, 0.0)
        rank = jnp.dot(before, ones.astype(BF16), preferred_element_type=F32)
        found.append(jnp.where((rank == slot) & (group == s), ones, 0.0).astype(BF16))
    return found


def picked(picks, payloads, columns):
    total = None
    for pick, payload in zip(picks, payloads):
        part = lax.dot_general(
            pick[...], payload[:, columns], (((0,), (0,)), ((), ())), preferred_element_type=F32
        )
        total = part if total is None else total + part
    return total


def select_all(picks, payloads, outs):
    rows, width = outs[0].shape
    step = 384 if width % 384 == 0 else 128
    for at in range(0, width, step):
        columns = slice(at, at + step)
        total = picked(picks, payloads, columns)
        for d in range(INNER):
            outs[d][:, columns] = total[d * rows : (d + 1) * rows].astype(BF16)


def start_kernel(m, hot_rows, cold_rows, info, tokens, routes, gates, grad_out, *refs):
    out, refs = refs[0], refs[1:]
    outs, picks = refs[:INNER], refs[INNER:]
    count, feat = tokens.shape
    share = grad_out.shape[1]
    topk = routes.shape[0]
    out[:, :feat] = tokens[...]
    out[:, feat : feat + share] = grad_out[...]
    ids = routes[...].astype(F32)
    gate = gates[...]
    high = gate.astype(BF16).astype(F32)
    middle = (gate - high).astype(BF16).astype(F32)
    low = (gate - high - middle).astype(BF16).astype(F32)
    rest = jnp.zeros((TAIL - 5 * topk, count), F32)
    tail = jnp.concatenate([ids, ids, high, middle, low, rest], 0).T
    out[:, feat + share :] = tail.astype(BF16)
    if picks:
        picks[0][...] = pick_rows(m, hot_rows, cold_rows, topk, info, [tail])[0]
        select_all(picks, [out], outs)


def select_kernel(m, hot_rows, cold_rows, topk, info, *refs):
    payloads, refs = refs[:m], refs[m + 1 :]
    outs, picks, passed = refs[:INNER], refs[INNER : INNER + m], refs[INNER + m :]
    width = payloads[0].shape[1]
    for source, target in zip(payloads, passed):
        target[...] = source[...]
    tails = [payload[:, width - TAIL :].astype(F32) for payload in payloads]
    for pick, found in zip(picks, pick_rows(m, hot_rows, cold_rows, topk, info, tails)):
        pick[...] = found
    select_all(picks, payloads, outs)


def forward_rows(block, both, hots, columns):
    if not both:
        return block[:hots, columns], block[hots:, columns]
    colds = block.shape[0] // 2 - hots
    return block[:hots, columns], block[2 * hots : 2 * hots + colds, columns]


def returned_rows(block, both, hots, columns):
    if not both:
        return block[:, columns]
    colds = block.shape[0] // 2 - hots
    cold = block[2 * hots :, columns].astype(F32)[colds:]
    return jnp.concatenate([block[hots : 2 * hots, columns].astype(F32), cold], 0)


def hidden_kernel(m, hot_rows, cold_rows, feat, both, info, *refs):
    blocks = refs[:INNER]
    weight, _, part, x_hot, x_cold = refs[INNER:]
    hots = INNER * m * hot_rows
    ff_tile = weight.shape[2]
    share = blocks[0].shape[1] - feat - TAIL
    ff = part.shape[1] - share
    j = pl.program_id(0)
    hot = hot_of(info, info[0])

    @pl.when(j == 0)
    def _():
        split = m * hot_rows
        rows = [forward_rows(b, both, split, slice(0, feat)) for b in blocks]
        x_hot[...] = rows_joined([hot_part for hot_part, _ in rows])
        x_cold[...] = rows_joined([cold_part for _, cold_part in rows])
        rows = [forward_rows(b, both, split, slice(feat, feat + share)) for b in blocks]
        part[:hots, ff:] = rows_joined([hot_part for hot_part, _ in rows])
        part[hots:, ff:] = rows_joined([cold_part for _, cold_part in rows])

    at = pl.ds(pl.multiple_of(j * ff_tile, ff_tile), ff_tile)
    part[:hots, at] = jnp.dot(x_hot[...], weight[hot], preferred_element_type=F32).astype(BF16)
    part[hots:, at] = jnp.dot(x_cold[...], weight[1 - hot], preferred_element_type=F32).astype(BF16)


def back_kernel(m, hot_rows, cold_rows, n_parts, n_grads, topk, share, both, n_pay, info, *refs):
    sums, grads = refs[:n_parts], refs[n_parts : n_parts + n_grads]
    refs = refs[n_parts + n_grads :]
    tails, weight, payloads = refs[:INNER], refs[INNER], refs[INNER + 1 : INNER + 1 + n_pay]
    refs = refs[INNER + 2 + n_pay :]
    outs, g_hot, g_cold, picks = refs[:INNER], refs[INNER], refs[INNER + 1], refs[INNER + 2 :]
    hots, colds = m * hot_rows, m * cold_rows
    rows = hots + colds
    ff = weight.shape[2]
    tile = weight.shape[1]
    width = outs[0].shape[1]
    feat = width - share - TAIL
    me, tp = info[0], info[1]
    hot = hot_of(info, me)
    j = pl.program_id(0)

    def put(columns, back_hot, back_cold):
        there = picked(picks, payloads, columns) if n_pay else None
        for d in range(INNER):
            hot_now = back_hot[d * hots : (d + 1) * hots]
            cold_now = back_cold[d * colds : (d + 1) * colds]
            if n_pay:
                mine = there[d * rows : (d + 1) * rows]
                outs[d][:hots, columns] = mine[:hots].astype(BF16)
                outs[d][hots : 2 * hots, columns] = hot_now.astype(BF16)
                outs[d][2 * hots :, columns] = jnp.concatenate([mine[hots:], cold_now], 0).astype(BF16)
            else:
                outs[d][:hots, columns] = hot_now.astype(BF16)
                outs[d][hots:, columns] = cold_now.astype(BF16)

    @pl.when(j == 0)
    def _():
        if n_pay:
            ids = [payload[:, width - TAIL :].astype(F32) for payload in payloads]
            for pick, found in zip(picks, pick_rows(m, hot_rows, cold_rows, topk, info, ids)):
                pick[...] = found
        tail_rows = [forward_rows(t, both, hots, slice(None)) for t in tails]
        ends = []
        for kind, first, piece, target, expert in (
            (0, 0, hots, g_hot, 2 * me + hot),
            (1, INNER * hots, colds, g_cold, 2 * me + 1 - hot),
        ):
            made = []
            per = 1 if piece % 16 == 0 else INNER
            for d in range(0, INNER, per):
                count = piece * per
                now = slice(first + d * piece, first + d * piece + count)
                tail = jnp.concatenate([t[kind].astype(F32) for t in tail_rows[d : d + per]], 0)
                hidden = sums[0][now, :ff].astype(F32)
                for more in sums[1:]:
                    hidden = hidden + more[now, :ff].astype(F32)
                if n_grads == 1:
                    grad = grads[0][now].astype(F32)
                else:
                    mine, other = grads[0][now].astype(F32), grads[1][now].astype(F32)
                    even = tp == 0
                    grad = jnp.concatenate(
                        [jnp.where(even, mine, other), jnp.where(even, other, mine)], 1
                    )
                e = expert.astype(F32)
                ids = tail[:, :topk]
                gate = (tail[:, 2 * topk : 3 * topk] + tail[:, 3 * topk : 4 * topk]) + tail[:, 4 * topk : 5 * topk]
                gate = jnp.sum(jnp.where(ids == e, gate, 0.0), 1, keepdims=True)
                sig = 1.0 / (1.0 + jnp.exp(-hidden))
                act = (hidden * sig).astype(BF16).astype(F32)
                row_grad = (gate * grad).astype(BF16).astype(F32)
                hidden_grad = row_grad * (sig * (1.0 + hidden * (1.0 - sig)))
                target[d * piece : d * piece + count] = hidden_grad.astype(BF16)
                gate_grad = jnp.sum(act * grad, 1, keepdims=True)
                high = gate_grad.astype(BF16).astype(F32)
                low = gate_grad - high
                lane = lax.broadcasted_iota(I32, tail.shape, 1)
                values = jnp.where(lane < topk, high, low)
                end = jnp.where((tail == e) & (lane < 2 * topk), values, 0.0)
                gated = None
                for n in range(ff // share):
                    piece_act = jnp.where(tp == n, act[:, n * share : (n + 1) * share], 0.0)
                    gated = piece_act if gated is None else gated + piece_act
                made.append(jnp.concatenate([gate * gated, end], 1))
            ends.append(jnp.concatenate(made, 0))
        put(slice(feat, width), *ends)

    at = pl.ds(pl.multiple_of(j * tile, tile), tile)
    across_rows = (((1,), (1,)), ((), ()))
    put(
        at,
        lax.dot_general(g_hot[...], weight[hot], across_rows, preferred_element_type=F32),
        lax.dot_general(g_cold[...], weight[1 - hot], across_rows, preferred_element_type=F32),
    )


def expand_kernel(m, hots, both, n_more, *refs):
    blocks, picks, refs = refs[:INNER], refs[INNER : INNER + m], refs[INNER + m :]
    more, outs = refs[:n_more], refs[n_more + 1 :]
    width = blocks[0].shape[1]
    step = 384 if width % 384 == 0 else 128
    for at in range(0, width, step):
        columns = slice(at, at + step)
        rows = rows_joined([returned_rows(b, both, hots, columns) for b in blocks]).astype(BF16)
        for s in range(m):
            total = jnp.dot(picks[s][...], rows, preferred_element_type=F32)
            if more:
                total = total + more[s][:, columns].astype(F32)
            outs[s][:, columns] = total.astype(BF16)


def final_kernel(n, topk, *refs):
    parts = refs[:n]
    mixed, grad_tokens, grad_gates = refs[n:]
    feat, share = grad_tokens.shape[1], mixed.shape[1]

    def total(columns):
        out = parts[0][:, columns].astype(F32)
        for part in parts[1:]:
            out = out + part[:, columns].astype(F32)
        return out

    grad_tokens[...] = total(slice(0, feat)).astype(BF16)
    mixed[...] = total(slice(feat, feat + share)).astype(BF16)
    tail = total(slice(feat + share, feat + share + TAIL))
    tail = tail.T
    grad_gates[...] = tail[:topk] + tail[topk : 2 * topk]


def up_kernel(n, info, *refs):
    x_hot, x_cold = refs[:n], refs[n : 2 * n]
    g_hot, g_cold = refs[2 * n : 3 * n], refs[3 * n : 4 * n]
    out = refs[4 * n + 1]

    def total(xs, gs):
        acc = None
        for x, g in zip(xs, gs):
            part = lax.dot_general(
                x[...], g[...], (((0,), (0,)), ((), ())), preferred_element_type=F32
            )
            acc = part if acc is None else acc + part
        out[0] = acc.astype(BF16)

    @pl.when(pl.program_id(0) == 0)
    def _():
        total(x_hot, g_hot)

    @pl.when(pl.program_id(0) == 1)
    def _():
        total(x_cold, g_cold)


def on_device(tokens, routes, gates, up_weight, replica_on, grad_out):
    count, feat = tokens.shape
    topk = routes.shape[1]
    experts = replica_on.shape[0]
    share = grad_out.shape[1]
    ff = up_weight.shape[2]
    n_ep, n_tp = lax.axis_size("ep"), lax.axis_size("tp")
    outer = n_ep // INNER
    capacity = 3 * count * topk // (4 * experts)
    hot_rows, cold_rows = 2 * capacity, capacity
    width = feat + share + TAIL
    me, tp = lax.axis_index("ep"), lax.axis_index("tp")
    info = jnp.concatenate([jnp.stack([me, tp]).astype(I32), replica_on])
    smem = pl.BlockSpec(memory_space=pltpu.SMEM)

    def along(value, shift):
        pairs = [
            (o * INNER + i, ((o + shift) % outer) * INNER + i)
            for o in range(outer)
            for i in range(INNER)
        ]
        return lax.ppermute(value, "ep", pairs)

    def across(value, d):
        pairs = [(o * INNER + i, o * INNER + (i ^ d)) for o in range(outer) for i in range(INNER)]
        return lax.ppermute(value, "ep", pairs)

    rest_spec = pl.BlockSpec(memory_space=pl.ANY)
    m = max(1, outer // CHUNKS)
    chunks = [list(range(first, first + m)) for first in range(0, outer, m)]
    n = len(chunks)
    rows = m * (hot_rows + cold_rows)
    hots, colds = INNER * m * hot_rows, INNER * m * cold_rows
    ff_tile = 256 if ff % 256 == 0 else ff
    d_tile = 512 if feat % 512 == 0 else feat
    sizes = (m, hot_rows, cold_rows)

    def block(shape, dtype=BF16):
        return jax.ShapeDtypeStruct(shape, dtype)

    def fixed(shape):
        return pl.BlockSpec(shape, lambda j: (0,) * len(shape))

    going = {f: k for k, (f, _) in enumerate(PLAN) if f is not None}
    coming = {r: k for k, (_, r) in enumerate(PLAN) if r is not None}

    def doubled(k):
        return None not in PLAN[k]

    def weigh(kind):
        return cost(COSTS[kind] * 10**6, COSTS[kind] * 10**4)

    arrived, picks, blocks, sums, grads, partials = {}, {}, {}, {}, {}, {}
    x_hots, x_colds, g_hots, g_colds = {}, {}, {}, {}

    def exchange(k, made):
        blocks[k] = [made[0]] + [across(made[d], d) for d in range(1, INNER)]

    own_rows = m == 1
    made = pl.pallas_call(
        functools.partial(start_kernel, *sizes),
        out_shape=[block((count, width))]
        + ([block((rows, width))] * INNER + [block((count, INNER * rows))] if own_rows else []),
        grid=(1,),
        in_specs=[
            smem,
            fixed((count, feat)),
            fixed((topk, count)),
            fixed((topk, count)),
            fixed((count, share)),
        ],
        out_specs=[fixed((count, width))]
        + ([fixed((rows, width))] * INNER + [fixed((count, INNER * rows))] if own_rows else []),
        compiler_params=params(),
        cost_estimate=weigh("x"),
        name="start",
    )(info, tokens, routes.T, gates.T, grad_out)
    payload = made[0]
    last = [payload]
    for c in range(n):
        for s in chunks[c] if c not in PASSED else ():
            if s == 0:
                arrived[s] = payload
            else:
                arrived[s] = along(arrived[s - m], m) if c else along(payload, s)

    def select(k):
        c = PLAN[k][0]
        more = m if c + 1 in PASSED else 0
        made = pl.pallas_call(
            functools.partial(select_kernel, *sizes, topk),
            out_shape=[block((rows, width))] * INNER
            + [block((count, INNER * rows))] * m
            + [block((count, width))] * more,
            in_specs=[smem] + whole_specs(m) + [rest_spec],
            out_specs=whole_specs(INNER + m + more),
            compiler_params=params(),
            cost_estimate=weigh("x"),
            name="select",
        )(info, *[arrived[s] for s in chunks[c]], last[0])
        picks[c] = made[INNER : INNER + m]
        exchange(k, made)
        if more:
            for s, value in zip(chunks[c + 1], made[INNER + m :]):
                arrived[s] = along(value, m)
        last[0] = picks[c][0]

    def hidden(c):
        k = going[c]
        held = (2 if doubled(k) else 1) * rows
        part, x_hots[c], x_colds[c] = pl.pallas_call(
            functools.partial(hidden_kernel, *sizes, feat, doubled(k)),
            out_shape=[block((INNER * rows, ff + share)), block((hots, feat)), block((colds, feat))],
            grid=(ff // ff_tile,),
            in_specs=[smem]
            + [fixed((held, width))] * INNER
            + [pl.BlockSpec((2, feat, ff_tile), lambda j: (0, 0, j)), rest_spec],
            out_specs=[fixed((INNER * rows, ff + share)), fixed((hots, feat)), fixed((colds, feat))],
            compiler_params=params(),
            cost_estimate=weigh("h"),
            name="hidden",
        )(info, *blocks[k], up_weight, last[0])
        last[0] = x_colds[c]
        if n_tp == 2:
            sums[c] = [part, lax.ppermute(part, "tp", [(0, 1), (1, 0)])]
            grads[c] = sums[c]
        else:
            sums[c] = [lax.psum(part[:, :ff].astype(F32), "tp")]
            grads[c] = [lax.all_gather(part[:, ff:], "tp", axis=1, tiled=True)]

    def step(k):
        f, c = PLAN[k]
        if c is None:
            return select(k)
        if n_tp == 2:
            grad_specs = [pl.BlockSpec((INNER * rows, share), lambda j: (0, ff // share))] * 2
        else:
            grad_specs = [fixed((INNER * rows, ff))]
        came = (2 if doubled(going[c]) else 1) * rows
        sent = (2 if doubled(k) else 1) * rows
        there = [arrived[s] for s in chunks[f]] if f is not None else []
        made = pl.pallas_call(
            functools.partial(
                back_kernel,
                *sizes,
                len(sums[c]),
                len(grads[c]),
                topk,
                share,
                doubled(going[c]),
                len(there),
            ),
            out_shape=[block((sent, width))] * INNER
            + [block((hots, ff)), block((colds, ff))]
            + [block((count, INNER * rows))] * len(there),
            grid=(feat // d_tile,),
            in_specs=[smem]
            + [fixed((INNER * rows, ff))] * len(sums[c])
            + grad_specs
            + [pl.BlockSpec((came, TAIL), lambda j: (0, width // TAIL - 1))] * INNER
            + [pl.BlockSpec((2, d_tile, ff), lambda j: (0, j, 0))]
            + [fixed((count, width))] * len(there)
            + [rest_spec],
            out_specs=[fixed((sent, width))] * INNER
            + [fixed((hots, ff)), fixed((colds, ff))]
            + [fixed((count, INNER * rows))] * len(there),
            compiler_params=params(),
            cost_estimate=weigh("b"),
            name="back",
        )(info, *sums[c], *grads[c], *blocks[going[c]], up_weight, *there, last[0])
        g_hots[c], g_colds[c] = made[INNER : INNER + 2]
        if f is not None:
            picks[f] = made[INNER + 2 :]
        exchange(k, made)
        last[0] = g_colds[c]

    def expand(c):
        more = [along(partials[s - m], m) for s in chunks[c]] if c > 1 else []
        k = coming[c]
        made = pl.pallas_call(
            functools.partial(expand_kernel, m, m * hot_rows, doubled(k), len(more)),
            out_shape=[block((count, width))] * m,
            in_specs=whole_specs(INNER + m + len(more)) + [rest_spec],
            out_specs=whole_specs(m),
            compiler_params=params(),
            cost_estimate=weigh("e"),
            name="expand",
        )(*blocks[k], *picks[c], *more, last[0])
        for s, value in zip(chunks[c], made):
            partials[s] = value
        last[0] = made[0]

    def weight_grad():
        grad_up = pl.pallas_call(
            functools.partial(up_kernel, n),
            out_shape=block(up_weight.shape),
            grid_spec=pltpu.PrefetchScalarGridSpec(
                num_scalar_prefetch=1,
                grid=(2, feat // 256),
                in_specs=[pl.BlockSpec((hots, 256), lambda e, j, info: (0, j))] * n
                + [pl.BlockSpec((colds, 256), lambda e, j, info: (0, j))] * n
                + [pl.BlockSpec((hots, ff), lambda e, j, info: (0, 0))] * n
                + [pl.BlockSpec((colds, ff), lambda e, j, info: (0, 0))] * n
                + [rest_spec],
                out_specs=pl.BlockSpec(
                    (1, 256, ff),
                    lambda e, j, info: (e + hot_of(info, info[0]) * (1 - 2 * e), j, 0),
                ),
            ),
            compiler_params=params(),
            cost_estimate=weigh("u"),
            name="grad_up",
        )(
            info,
            *[x_hots[c] for c in range(n)],
            *[x_colds[c] for c in range(n)],
            *[g_hots[c] for c in range(n)],
            *[g_colds[c] for c in range(n)],
            last[0],
        )
        last[0] = grad_up
        return grad_up

    if own_rows:
        picks[0] = made[INNER + 1 :]
        exchange(0, made[1 : INNER + 1])
    else:
        select(0)
    grad_up = None
    for word in ORDER:
        number = int(word[1:] or 0)
        if word[0] == "u":
            grad_up = weight_grad()
        else:
            {"x": step, "h": hidden, "e": expand}[word[0]](number)

    sums_back = [along(partials[s], m) for s in chunks[n - 1]]
    parts = [sums_back[0], partials[0]]
    for s in chunks[0][1:]:
        parts.append(along(sums_back[s] + partials[s], outer - s))
    mixed, grad_tokens, grad_gates = pl.pallas_call(
        functools.partial(final_kernel, len(parts), topk),
        out_shape=[block((count, share)), block((count, feat)), block((topk, count), F32)],
        in_specs=whole_specs(len(parts)),
        out_specs=whole_specs(3),
        compiler_params=params(),
        cost_estimate=weigh("e"),
        name="final",
    )(*parts)
    return mixed, grad_tokens, grad_gates.T, grad_up


def solution(mesh):
    return jax.shard_map(
        on_device,
        mesh=mesh,
        in_specs=(
            P("ep", "tp"),
            P("ep", None),
            P("ep", None),
            P("ep", "tp", None),
            P(),
            P("ep", "tp"),
        ),
        out_specs=(P("ep", "tp"), P("ep", "tp"), P("ep", None), P("ep", "tp", None)),
        check_vma=False,
    )
```

time: 223 us -> 198 us (0.89)
  waiting for transfers between devices: 96.2 us -> 77.4 us
  starting transfers between devices: 44.7 us -> 36.3 us
    ppermute x24 -> x21, waiting for transfers between devices: 50.9 us -> 40.8 us  [across(): return lax.ppermute(value, 'ep', pairs)]
    ppermute x6, waiting for transfers between devices: 45.2 us -> 36.5 us  [along(): return lax.ppermute(value, 'ep', pairs)]
    ppermute x24 -> x21, starting transfers between devices: 35.4 us -> 28.1 us  [across(): return lax.ppermute(value, 'ep', pairs)]
    unnamed x8 -> x16, local copies, waits for them, and re-layouts: 3.31 us -> 5.06 us
    pallas_call x18 -> x16, Pallas kernels: 60.9 us -> 60.9 us  [the longest x4 31.8 us: step(): pl.pallas_call(functools.partial(back_kernel, *sizes, len(sums[c]), len(g...]
  transfers between devices with their start and end apart: 34 -> 31, of which waited for: 14 -> 10; matrix products, arithmetic and copies ran while one was open for 0% -> 0% of each run, Pallas kernels for 29% -> 37%
where the time goes in v2:
time: 198 us; the launch traced here: 197 us
  waiting for transfers between devices  77.4 us (39%)
  Pallas kernels  76.6 us (39%)
  starting transfers between devices  36.3 us (18%)
  local copies, waits for them, and re-layouts  5.06 us (3%)
    ppermute x21, waiting for transfers between devices, across(): return lax.ppermute(value, 'ep', pairs)  40.8 us
    ppermute x6, waiting for transfers between devices, along(): return lax.ppermute(value, 'ep', pairs)  36.5 us
    pallas_call x4, Pallas kernels, step(): pl.pallas_call(functools.partial(back_kernel, *sizes, len(sums[c]), len(g...  31.8 us
    ppermute x21, starting transfers between devices, across(): return lax.ppermute(value, 'ep', pairs)  28.1 us
    pallas_call x4, Pallas kernels, hidden(): pl.pallas_call(functools.partial(hidden_kernel, *sizes, feat, doubled(k))...  20.7 us
    pallas_call x1, Pallas kernels, weight_grad(): pl.pallas_call(functools.partial(up_kernel, n), out_shape=block(up_weight...  15.7 us
    ppermute x6, starting transfers between devices, along(): return lax.ppermute(value, 'ep', pairs)  7.92 us
    unnamed x16, local copies, waits for them, and re-layouts  5.06 us
  transfers between devices with their start and end apart: 31, of which 10 were waited for; matrix products, arithmetic and copies ran while one was open for 0% of the time, Pallas kernels for 37%

profile of v2, /device:TPU:0, one launch (start us, length us, event | category | flops | bytes accessed | tf_op | source)
XLA Modules:
  0.0 196.9 jit_solution(5395653881056431116)
XLA Ops:
  4.7 1.7 start.1
  6.4 3.1 %collective-permute-start.3 = (bf16[128,2688]{1,0:T(8,128)(2,1)S(1)}, bf16[128,2688]{1,0:T(8,128)(2,1)S(1)}, u32[]{:S(2)}, u32[]{:S(2)}) collective-permute-start(bf16[128,2688]{1,0:T(8,128)(2,1)S(1)} %get-tuple-element.65.refs_1_), channel_id=1, source_target_pairs={{0,8},{2,10},{4,12},{6,14},{8,16},{10,18},{12,20},{14,22},{16,24},... | collective-permute-start | bytes 2064392 | tf_op jit(solution)/shard_map/ppermute | solution.py:343
  10.9 1.5 collective-permute-start.1
  12.9 14.0 %collective-permute-done.3.refs_0_ = bf16[128,2688]{1,0:T(8,128)(2,1)S(1)} collective-permute-done((bf16[128,2688]{1,0:T(8,128)(2,1)S(1)}, bf16[128,2688]{1,0:T(8,128)(2,1)S(1)}, u32[]{:S(2)}, u32[]{:S(2)}) %collective-permute-start.3) | collective-permute-done | bytes 688160 | tf_op jit(solution)/shard_map/ppermute | solution.py:343
  26.9 1.6 select.2
  29.4 5.2 %hidden.4 = (bf16[288,1536]{1,0:T(8,128)(2,1)S(1)}, bf16[192,2048]{1,0:T(8,128)(2,1)S(1)}, bf16[96,2048]{1,0:T(8,128)(2,1)S(1)}) custom-call(s32[34]{0:T(128)S(1)} %pad_add_fusion.info, bf16[72,2688]{1,0:T(8,128)(2,1)S(1)} %get-tuple-element.61.refs_0_.refs_4_, bf16[72,2688]{1,0:T(8,128)(2,1)S(1)} %collective-permute-done.refs_1_.refs_5_, ...), custom_call_target="tpu_custom_call" | custom-call | flops 1000000 | bytes 10000 | tf_op jit(solution)/shard_map/hidden/pallas_call | solution.py:432
  36.0 9.4 %collective-permute-done.5.refs_0_ = bf16[128,2688]{1,0:T(8,128)(2,1)S(1)} collective-permute-done((bf16[128,2688]{1,0:T(8,128)(2,1)S(1)}, bf16[128,2688]{1,0:T(8,128)(2,1)S(1)}, u32[]{:S(2)}, u32[]{:S(2)}) %collective-permute-start.5) | collective-permute-done | bytes 688160 | tf_op jit(solution)/shard_map/ppermute | solution.py:343
  45.3 1.6 select.3
  50.7 14.0 %collective-permute-done.8.refs_2_.refs_6_ = bf16[72,2688]{1,0:T(8,128)(2,1)S(1)} collective-permute-done((bf16[72,2688]{1,0:T(8,128)(2,1)S(1)}, bf16[72,2688]{1,0:T(8,128)(2,1)S(1)}, u32[]{:S(2)}, u32[]{:S(2)}) %collective-permute-start.8) | collective-permute-done | bytes 387104 | tf_op jit(solution)/shard_map/ppermute | solution.py:347
  67.2 5.2 %hidden.5 = (bf16[288,1536]{1,0:T(8,128)(2,1)S(1)}, bf16[192,2048]{1,0:T(8,128)(2,1)S(1)}, bf16[96,2048]{1,0:T(8,128)(2,1)S(1)}) custom-call(s32[34]{0:T(128)S(1)} %pad_add_fusion.info, bf16[72,2688]{1,0:T(8,128)(2,1)S(1)} %get-tuple-element.70.refs_0_.refs_4_, bf16[72,2688]{1,0:T(8,128)(2,1)S(1)} %collective-permute-done.7.refs_1_.refs_5_, ...), custom_call_target="tpu_custom_call" | custom-call | flops 1000000 | bytes 10000 | tf_op jit(solution)/shard_map/hidden/pallas_call | solution.py:432
  72.5 8.9 %back.4 = (bf16[144,2688]{1,0:T(8,128)(2,1)S(1)}, bf16[144,2688]{1,0:T(8,128)(2,1)}, bf16[144,2688]{1,0:T(8,128)(2,1)}, bf16[144,2688]{1,0:T(8,128)(2,1)S(1)}, b...) custom-call(s32[34]{0:T(128)S(1)} %pad_add_fusion.info, ...), custom_call_target="tpu_custom_call" | custom-call | flops 1000000 | bytes 10000 | tf_op jit(solution)/shard_map/back/pallas_call | solution.py:463
  84.9 5.2 %hidden.6 = (bf16[288,1536]{1,0:T(8,128)(2,1)S(1)}, bf16[192,2048]{1,0:T(8,128)(2,1)S(1)}, bf16[96,2048]{1,0:T(8,128)(2,1)S(1)}) custom-call(s32[34]{0:T(128)S(1)} %pad_add_fusion.info, bf16[72,2688]{1,0:T(8,128)(2,1)S(1)} %get-tuple-element.81.refs_0_.refs_4_, bf16[72,2688]{1,0:T(8,128)(2,1)S(1)} %collective-permute-done.14.refs_1_.refs_5_, ...), custom_call_target="tpu_custom_call" | custom-call | flops 1000000 | bytes 10000 | tf_op jit(solution)/shard_map/hidden/pallas_call | solution.py:432
  90.1 8.0 %back.5 = (bf16[72,2688]{1,0:T(8,128)(2,1)S(1)}, bf16[72,2688]{1,0:T(8,128)(2,1)}, bf16[72,2688]{1,0:T(8,128)(2,1)}, bf16[72,2688]{1,0:T(8,128)(2,1)S(1)}, bf16[...) custom-call(s32[34]{0:T(128)S(1)} %pad_add_fusion.info, bf16[288,1536]{1,0:T(8,128)(2,1)S(1)} %get-tuple-element.80.refs_0_.refs_2_, ...), custom_call_target="tpu_custom_call" | custom-call | flops 1000000 | bytes 10000 | tf_op jit(solution)/shard_map/back/pallas_call | solution.py:463
  99.2 2.5 %collective-permute-done.10.refs_1_.refs_5_ = bf16[144,2688]{1,0:T(8,128)(2,1)S(1)} collective-permute-done((bf16[144,2688]{1,0:T(8,128)(2,1)}, bf16[144,2688]{1,0:T(8,128)(2,1)S(1)}, u32[]{:S(2)}, u32[]{:S(2)}) %collective-permute-start.10) | collective-permute-done | bytes 774176 | tf_op jit(solution)/shard_map/ppermute | solution.py:347
  101.7 1.5 collective-permute-start.19
  103.2 13.8 %collective-permute-done.11.refs_2_.refs_6_ = bf16[144,2688]{1,0:T(8,128)(2,1)S(1)} collective-permute-done((bf16[144,2688]{1,0:T(8,128)(2,1)}, bf16[144,2688]{1,0:T(8,128)(2,1)S(1)}, u32[]{:S(2)}, u32[]{:S(2)}) %collective-permute-start.11) | collective-permute-done | bytes 774176 | tf_op jit(solution)/shard_map/ppermute | solution.py:347
  117.0 4.2 %collective-permute-start.20 = (bf16[72,2688]{1,0:T(8,128)(2,1)S(1)}, bf16[72,2688]{1,0:T(8,128)(2,1)S(1)}, u32[]{:S(2)}, u32[]{:S(2)}) collective-permute-start(bf16[72,2688]{1,0:T(8,128)(2,1)S(1)} %get-tuple-element.92), channel_id=1, source_target_pairs={{0,6},{2,4},{4,2},{6,0},{8,14},{10,12},{12,10},{14,8},{16,22},{18,... | collective-permute-start | bytes 1161224 | tf_op jit(solution)/shard_map/ppermute | solution.py:347
  121.2 5.2 %hidden.7 = (bf16[288,1536]{1,0:T(8,128)(2,1)S(1)}, bf16[192,2048]{1,0:T(8,128)(2,1)S(1)}, bf16[96,2048]{1,0:T(8,128)(2,1)S(1)}) custom-call(s32[34]{0:T(128)S(1)} %pad_add_fusion.info, bf16[144,2688]{1,0:T(8,128)(2,1)S(1)} %get-tuple-element.76.refs_0_.refs_4_, bf16[144,2688]{1,0:T(8,128)(2,1)S(1)} %collective-permute-done.10.refs_1_.refs_5_, ...), custom_call_target="tpu_custom_call" | custom-call | flops 1000000 | bytes 10000 | tf_op jit(solution)/shard_map/hidden/pallas_call | solution.py:432
  126.4 7.8 %back.6 = (bf16[72,2688]{1,0:T(8,128)(2,1)S(1)}, bf16[72,2688]{1,0:T(8,128)(2,1)}, bf16[72,2688]{1,0:T(8,128)(2,1)S(1)}, bf16[72,2688]{1,0:T(8,128)(2,1)S(1)}, b...) custom-call(s32[34]{0:T(128)S(1)} %pad_add_fusion.info, ...), custom_call_target="tpu_custom_call" | custom-call | flops 1000000 | bytes 10000 | tf_op jit(solution)/shard_map/back/pallas_call | solution.py:463
  141.6 7.1 %back.7 = (bf16[72,2688]{1,0:T(8,128)(2,1)S(1)}, bf16[72,2688]{1,0:T(8,128)(2,1)S(1)}, bf16[72,2688]{1,0:T(8,128)(2,1)S(1)}, bf16[72,2688]{1,0:T(8,128)(2,1)S(1)...) custom-call(s32[34]{0:T(128)S(1)} %pad_add_fusion.info, ...), custom_call_target="tpu_custom_call" | custom-call | flops 1000000 | bytes 10000 | tf_op jit(solution)/shard_map/back/pallas_call | solution.py:463
  150.2 7.6 %collective-permute-done.26.refs_2_ = bf16[72,2688]{1,0:T(8,128)(2,1)S(1)} collective-permute-done((bf16[72,2688]{1,0:T(8,128)(2,1)S(1)}, bf16[72,2688]{1,0:T(8,128)(2,1)S(1)}, u32[]{:S(2)}, u32[]{:S(2)}) %collective-permute-start.26) | collective-permute-done | bytes 387104 | tf_op jit(solution)/shard_map/ppermute | solution.py:347
  162.2 15.7 %grad_up.1.refs_6_ = bf16[2,2048,1024]{2,1,0:T(8,128)(2,1)} custom-call(s32[34]{0:T(128)S(1)} %pad_add_fusion.info, bf16[192,2048]{1,0:T(8,128)(2,1)S(1)} %get-tuple-element.107.refs_0_, bf16[192,2048]{1,0:T(8,128)(2,1)S(1)} %get-tuple-element.108.refs_1_, bf16[192,2048]{1,0:T(8,128)(2,1)S(1)} %get-tuple-element.109.refs_2_, ...), custom_call_target="tpu_custom_call" | custom-call | flops 1000000 | bytes 10000 | tf_op jit(solution)/shard_map/grad_up/pallas_call | solution.py:515
  178.6 4.1 %collective-permute-start.30 = (bf16[128,2688]{1,0:T(8,128)(2,1)S(1)}, bf16[128,2688]{1,0:T(8,128)(2,1)S(1)}, u32[]{:S(2)}, u32[]{:S(2)}) collective-permute-start(bf16[128,2688]{1,0:T(8,128)(2,1)S(1)} %expand.7), channel_id=1, source_target_pairs={{0,8},{2,10},{4,12},{6,14},{8,16},{10,18},{12,20},{14,22},{16,24},... | collective-permute-start | bytes 2064392 | tf_op jit(solution)/shard_map/ppermute | solution.py:343
  182.7 13.2 %collective-permute-done.30.refs_0_ = bf16[128,2688]{1,0:T(8,128)(2,1)S(1)} collective-permute-done((bf16[128,2688]{1,0:T(8,128)(2,1)S(1)}, bf16[128,2688]{1,0:T(8,128)(2,1)S(1)}, u32[]{:S(2)}, u32[]{:S(2)}) %collective-permute-start.30) | collective-permute-done | bytes 688160 | tf_op jit(solution)/shard_map/ppermute | solution.py:343
  (72 shorter events, 34.2 us)
Async XLA Ops:
  6.4 20.5 %collective-permute-start.3 = (bf16[128,2688]{1,0:T(8,128)(2,1)S(1)}, bf16[128,2688]{1,0:T(8,128)(2,1)S(1)}, u32[]{:S(2)}, u32[]{:S(2)}) collective-permute-start(bf16[128,2688]{1,0:T(8,128)(2,1)S(1)} %get-tuple-element.65.refs_1_), channel_id=1, source_target_pairs={{0,8},{2,10},{4,12},{6,14},{8,16},{10,18},{12,20},{14,22},{16,24},... | collective-permute-start | bytes 2064392 | tf_op jit(solution)/shard_map/ppermute | solution.py:343
  9.5 19.0 %collective-permute-start = (bf16[72,2688]{1,0:T(8,128)(2,1)S(1)}, bf16[72,2688]{1,0:T(8,128)(2,1)S(1)}, u32[]{:S(2)}, u32[]{:S(2)}) collective-permute-start(bf16[72,2688]{1,0:T(8,128)(2,1)S(1)} %get-tuple-element.62), channel_id=1, source_target_pairs={{0,2},{2,0},{4,6},{6,4},{8,10},{10,8},{12,14},{14,12},{16,18},{18,... | collective-permute-start | bytes 1161224 | tf_op jit(solution)/shard_map/ppermute | solution.py:347
  10.9 18.5 %collective-permute-start.1 = (bf16[72,2688]{1,0:T(8,128)(2,1)S(1)}, bf16[72,2688]{1,0:T(8,128)(2,1)S(1)}, u32[]{:S(2)}, u32[]{:S(2)}) collective-permute-start(bf16[72,2688]{1,0:T(8,128)(2,1)S(1)} %get-tuple-element.63), channel_id=1, source_target_pairs={{0,4},{2,6},{4,0},{6,2},{8,12},{10,14},{12,8},{14,10},{16,20},{18,... | collective-permute-start | bytes 1161224 | tf_op jit(solution)/shard_map/ppermute | solution.py:347
  26.9 18.4 %collective-permute-start.5 = (bf16[128,2688]{1,0:T(8,128)(2,1)S(1)}, bf16[128,2688]{1,0:T(8,128)(2,1)S(1)}, u32[]{:S(2)}, u32[]{:S(2)}) collective-permute-start(bf16[128,2688]{1,0:T(8,128)(2,1)S(1)} %collective-permute-done.3.refs_0_), channel_id=1, source_target_pairs={{0,8},{2,10},{4,12},{6,14},{8,16},{10,18},{12,20},{14,22},{16,24},... | collective-permute-start | bytes 2064392 | tf_op jit(solution)/shard_map/ppermute | solution.py:343
  34.6 37.8 %collective-permute-start.4 = (bf16[288,1536]{1,0:T(8,128)(2,1)S(1)}, bf16[288,1536]{1,0:T(8,128)(2,1)S(1)}, u32[]{:S(2)}, u32[]{:S(2)}) collective-permute-start(bf16[288,1536]{1,0:T(8,128)(2,1)S(1)} %get-tuple-element.67.refs_0_.refs_2_), channel_id=1, source_target_pairs={{0,1},{1,0},{2,3},{3,2},{4,5},{5,4},{6,7},{7,6},{8,9},{9,8},{10,11... | collective-permute-start | bytes 2654216 | tf_op jit(solution)/shard_map/ppermute | solution.py:446
  46.9 25.6 %collective-permute-start.6 = (bf16[128,2688]{1,0:T(8,128)(2,1)S(1)}, bf16[128,2688]{1,0:T(8,128)(2,1)S(1)}, u32[]{:S(2)}, u32[]{:S(2)}) collective-permute-start(bf16[128,2688]{1,0:T(8,128)(2,1)S(1)} %get-tuple-element.69), channel_id=1, source_target_pairs={{0,8},{2,10},{4,12},{6,14},{8,16},{10,18},{12,20},{14,22},{16,24},... | collective-permute-start | bytes 2064392 | tf_op jit(solution)/shard_map/ppermute | solution.py:343
  47.2 17.6 %collective-permute-start.8 = (bf16[72,2688]{1,0:T(8,128)(2,1)S(1)}, bf16[72,2688]{1,0:T(8,128)(2,1)S(1)}, u32[]{:S(2)}, u32[]{:S(2)}) collective-permute-start(bf16[72,2688]{1,0:T(8,128)(2,1)S(1)} %get-tuple-element.72), channel_id=1, source_target_pairs={{0,4},{2,6},{4,0},{6,2},{8,12},{10,14},{12,8},{14,10},{16,20},{18,... | collective-permute-start | bytes 1161224 | tf_op jit(solution)/shard_map/ppermute | solution.py:347
  49.9 32.5 %collective-permute-start.14 = (bf16[72,2688]{1,0:T(8,128)(2,1)S(1)}, bf16[72,2688]{1,0:T(8,128)(2,1)S(1)}, u32[]{:S(2)}, u32[]{:S(2)}) collective-permute-start(bf16[72,2688]{1,0:T(8,128)(2,1)S(1)} %get-tuple-element.82), channel_id=1, source_target_pairs={{0,2},{2,0},{4,6},{6,4},{8,10},{10,8},{12,14},{14,12},{16,18},{18,... | collective-permute-start | bytes 1161224 | tf_op jit(solution)/shard_map/ppermute | solution.py:347
  64.8 18.7 %collective-permute-start.15 = (bf16[72,2688]{1,0:T(8,128)(2,1)S(1)}, bf16[72,2688]{1,0:T(8,128)(2,1)S(1)}, u32[]{:S(2)}, u32[]{:S(2)}) collective-permute-start(bf16[72,2688]{1,0:T(8,128)(2,1)S(1)} %get-tuple-element.83), channel_id=1, source_target_pairs={{0,4},{2,6},{4,0},{6,2},{8,12},{10,14},{12,8},{14,10},{16,20},{18,... | collective-permute-start | bytes 1161224 | tf_op jit(solution)/shard_map/ppermute | solution.py:347
  65.8 19.1 %collective-permute-start.16 = (bf16[72,2688]{1,0:T(8,128)(2,1)S(1)}, bf16[72,2688]{1,0:T(8,128)(2,1)S(1)}, u32[]{:S(2)}, u32[]{:S(2)}) collective-permute-start(bf16[72,2688]{1,0:T(8,128)(2,1)S(1)} %get-tuple-element.84), channel_id=1, source_target_pairs={{0,6},{2,4},{4,2},{6,0},{8,14},{10,12},{12,10},{14,8},{16,22},{18,... | collective-permute-start | bytes 1161224 | tf_op jit(solution)/shard_map/ppermute | solution.py:347
  72.4 17.7 %collective-permute-start.13 = (bf16[288,1536]{1,0:T(8,128)(2,1)S(1)}, bf16[288,1536]{1,0:T(8,128)(2,1)S(1)}, u32[]{:S(2)}, u32[]{:S(2)}) collective-permute-start(bf16[288,1536]{1,0:T(8,128)(2,1)S(1)} %get-tuple-element.80.refs_0_.refs_2_), channel_id=1, source_target_pairs={{0,1},{1,0},{2,3},{3,2},{4,5},{5,4},{6,7},{7,6},{8,9},{9,8},{10,11... | collective-permute-start | bytes 2654216 | tf_op jit(solution)/shard_map/ppermute | solution.py:446
  81.4 20.3 %collective-permute-start.10 = (bf16[144,2688]{1,0:T(8,128)(2,1)}, bf16[144,2688]{1,0:T(8,128)(2,1)S(1)}, u32[]{:S(2)}, u32[]{:S(2)}) collective-permute-start(bf16[144,2688]{1,0:T(8,128)(2,1)} %get-tuple-element.77), channel_id=1, source_target_pairs={{0,2},{2,0},{4,6},{6,4},{8,10},{10,8},{12,14},{14,12},{16,18},{18,... | collective-permute-start | bytes 2322440 | tf_op jit(solution)/shard_map/ppermute | solution.py:347
  82.4 34.5 %collective-permute-start.11 = (bf16[144,2688]{1,0:T(8,128)(2,1)}, bf16[144,2688]{1,0:T(8,128)(2,1)S(1)}, u32[]{:S(2)}, u32[]{:S(2)}) collective-permute-start(bf16[144,2688]{1,0:T(8,128)(2,1)} %get-tuple-element.78), channel_id=1, source_target_pairs={{0,4},{2,6},{4,0},{6,2},{8,12},{10,14},{12,8},{14,10},{16,20},{18,... | collective-permute-start | bytes 2322440 | tf_op jit(solution)/shard_map/ppermute | solution.py:347
  83.5 37.7 %collective-permute-start.12 = (bf16[144,2688]{1,0:T(8,128)(2,1)S(1)}, bf16[144,2688]{1,0:T(8,128)(2,1)S(1)}, u32[]{:S(2)}, u32[]{:S(2)}) collective-permute-start(bf16[144,2688]{1,0:T(8,128)(2,1)S(1)} %get-tuple-element.79), channel_id=1, source_target_pairs={{0,6},{2,4},{4,2},{6,0},{8,14},{10,12},{12,10},{14,8},{16,22},{18,... | collective-permute-start | bytes 2322440 | tf_op jit(solution)/shard_map/ppermute | solution.py:347
  90.1 36.4 %collective-permute-start.21 = (bf16[288,1536]{1,0:T(8,128)(2,1)S(1)}, bf16[288,1536]{1,0:T(8,128)(2,1)S(1)}, u32[]{:S(2)}, u32[]{:S(2)}) collective-permute-start(bf16[288,1536]{1,0:T(8,128)(2,1)S(1)} %get-tuple-element.94.refs_0_.refs_2_), channel_id=1, source_target_pairs={{0,1},{1,0},{2,3},{3,2},{4,5},{5,4},{6,7},{7,6},{8,9},{9,8},{10,11... | collective-permute-start | bytes 2654216 | tf_op jit(solution)/shard_map/ppermute | solution.py:446
  98.1 36.8 %collective-permute-start.18 = (bf16[72,2688]{1,0:T(8,128)(2,1)}, bf16[72,2688]{1,0:T(8,128)(2,1)S(1)}, u32[]{:S(2)}, u32[]{:S(2)}) collective-permute-start(bf16[72,2688]{1,0:T(8,128)(2,1)} %get-tuple-element.90), channel_id=1, source_target_pairs={{0,2},{2,0},{4,6},{6,4},{8,10},{10,8},{12,14},{14,12},{16,18},{18,... | collective-permute-start | bytes 1161224 | tf_op jit(solution)/shard_map/ppermute | solution.py:347
  101.7 33.2 %collective-permute-start.19 = (bf16[72,2688]{1,0:T(8,128)(2,1)}, bf16[72,2688]{1,0:T(8,128)(2,1)S(1)}, u32[]{:S(2)}, u32[]{:S(2)}) collective-permute-start(bf16[72,2688]{1,0:T(8,128)(2,1)} %get-tuple-element.91), channel_id=1, source_target_pairs={{0,4},{2,6},{4,0},{6,2},{8,12},{10,14},{12,8},{14,10},{16,20},{18,... | collective-permute-start | bytes 1161224 | tf_op jit(solution)/shard_map/ppermute | solution.py:347
  117.0 18.5 %collective-permute-start.20 = (bf16[72,2688]{1,0:T(8,128)(2,1)S(1)}, bf16[72,2688]{1,0:T(8,128)(2,1)S(1)}, u32[]{:S(2)}, u32[]{:S(2)}) collective-permute-start(bf16[72,2688]{1,0:T(8,128)(2,1)S(1)} %get-tuple-element.92), channel_id=1, source_target_pairs={{0,6},{2,4},{4,2},{6,0},{8,14},{10,12},{12,10},{14,8},{16,22},{18,... | collective-permute-start | bytes 1161224 | tf_op jit(solution)/shard_map/ppermute | solution.py:347
  137.8 20.1 %collective-permute-start.28 = (bf16[128,2688]{1,0:T(8,128)(2,1)S(1)}, bf16[128,2688]{1,0:T(8,128)(2,1)S(1)}, u32[]{:S(2)}, u32[]{:S(2)}) collective-permute-start(bf16[128,2688]{1,0:T(8,128)(2,1)S(1)} %expand.5.refs_9_), channel_id=1, source_target_pairs={{0,8},{2,10},{4,12},{6,14},{8,16},{10,18},{12,20},{14,22},{16,24},... | collective-permute-start | bytes 2064392 | tf_op jit(solution)/shard_map/ppermute | solution.py:343
  138.9 18.9 %collective-permute-start.26 = (bf16[72,2688]{1,0:T(8,128)(2,1)S(1)}, bf16[72,2688]{1,0:T(8,128)(2,1)S(1)}, u32[]{:S(2)}, u32[]{:S(2)}) collective-permute-start(bf16[72,2688]{1,0:T(8,128)(2,1)S(1)} %get-tuple-element.104), channel_id=1, source_target_pairs={{0,4},{2,6},{4,0},{6,2},{8,12},{10,14},{12,8},{14,10},{16,20},{18,... | collective-permute-start | bytes 1161224 | tf_op jit(solution)/shard_map/ppermute | solution.py:347
  140.4 17.4 %collective-permute-start.27 = (bf16[72,2688]{1,0:T(8,128)(2,1)S(1)}, bf16[72,2688]{1,0:T(8,128)(2,1)S(1)}, u32[]{:S(2)}, u32[]{:S(2)}) collective-permute-start(bf16[72,2688]{1,0:T(8,128)(2,1)S(1)} %get-tuple-element.105), channel_id=1, source_target_pairs={{0,6},{2,4},{4,2},{6,0},{8,14},{10,12},{12,10},{14,8},{16,22},{18,... | collective-permute-start | bytes 1161224 | tf_op jit(solution)/shard_map/ppermute | solution.py:347
  158.5 19.5 %collective-permute-start.29 = (bf16[128,2688]{1,0:T(8,128)(2,1)S(1)}, bf16[128,2688]{1,0:T(8,128)(2,1)S(1)}, u32[]{:S(2)}, u32[]{:S(2)}) collective-permute-start(bf16[128,2688]{1,0:T(8,128)(2,1)S(1)} %expand.6.refs_16_), channel_id=1, source_target_pairs={{0,8},{2,10},{4,12},{6,14},{8,16},{10,18},{12,20},{14,22},{16,24},... | collective-permute-start | bytes 2064392 | tf_op jit(solution)/shard_map/ppermute | solution.py:343
  158.7 19.2 %collective-permute-start.22 = (bf16[72,2688]{1,0:T(8,128)(2,1)S(1)}, bf16[72,2688]{1,0:T(8,128)(2,1)S(1)}, u32[]{:S(2)}, u32[]{:S(2)}) collective-permute-start(bf16[72,2688]{1,0:T(8,128)(2,1)S(1)} %get-tuple-element.98), channel_id=1, source_target_pairs={{0,2},{2,0},{4,6},{6,4},{8,10},{10,8},{12,14},{14,12},{16,18},{18,... | collective-permute-start | bytes 1161224 | tf_op jit(solution)/shard_map/ppermute | solution.py:347
  160.1 17.8 %collective-permute-start.23 = (bf16[72,2688]{1,0:T(8,128)(2,1)S(1)}, bf16[72,2688]{1,0:T(8,128)(2,1)S(1)}, u32[]{:S(2)}, u32[]{:S(2)}) collective-permute-start(bf16[72,2688]{1,0:T(8,128)(2,1)S(1)} %get-tuple-element.99), channel_id=1, source_target_pairs={{0,4},{2,6},{4,0},{6,2},{8,12},{10,14},{12,8},{14,10},{16,20},{18,... | collective-permute-start | bytes 1161224 | tf_op jit(solution)/shard_map/ppermute | solution.py:347
  (15 other events, 174.4 us)

commit v3 on v2

v3 whole, which is shorter than its diff:
```python
import functools

import jax
import jax.numpy as jnp
from jax import lax
from jax.experimental import pallas as pl
from jax.experimental.pallas import tpu as pltpu
from jax.sharding import PartitionSpec as P

INNER = 4
CHUNKS = 4
PLAN = ((0, None), (1, None), (2, None), (3, None), (None, 1), (None, 2), (None, 3), (None, 0))
ORDER = ('x1', 'h0', 'x2', 'h1', 'x3', 'h2', 'x4', 'h3', 'e1', 'x5', 'x6', 'e2', 'x7', 'e3', 'u', 'e0')
PASSED = ()
FIRST = 0
COSTS = {'x': 5000, 'b': 100, 'h': 5000, 'e': 20000, 'u': 20000}
TAIL = 128
LIMIT = 20 * 1024 * 1024
WIDE = 56 * 1024 * 1024
F32, BF16, I32 = jnp.float32, jnp.bfloat16, jnp.int32


def params(limit=LIMIT):
    return pltpu.CompilerParams(vmem_limit_bytes=limit)


def cost(flops, moved):
    return pl.CostEstimate(flops=int(flops), bytes_accessed=int(moved), transcendentals=0)


def whole_specs(n):
    return [pl.BlockSpec(memory_space=pltpu.VMEM)] * n


def hot_of(plan, device):
    return plan[2 * device + 1]


def rows_joined(pieces):
    if all(piece.shape[0] % 16 == 0 for piece in pieces):
        return jnp.concatenate(pieces, 0)
    return jnp.concatenate([piece.astype(F32) for piece in pieces], 0).astype(BF16)


def pick_rows(m, hot_rows, cold_rows, topk, plan, tails):
    count = tails[0].shape[0]
    rows = m * (hot_rows + cold_rows)
    cols = INNER * rows
    me = lax.axis_index("ep")
    outer, inner = me // INNER, me % INNER
    spot = lax.broadcasted_iota(I32, (8, cols), 1)
    which = jnp.zeros((8, cols), I32)
    for d in range(1, INNER):
        which += (spot >= d * rows).astype(I32)
    within = spot - which * rows
    is_hot = within < m * hot_rows
    group = jnp.zeros((8, cols), I32)
    for s in range(1, m):
        edge = jnp.where(is_hot, s * hot_rows, m * hot_rows + s * cold_rows)
        group += (within >= edge).astype(I32)
    slot = jnp.where(is_hot, within - group * hot_rows, within - m * hot_rows - group * cold_rows)
    expert = jnp.zeros((8, cols), I32)
    for d in range(INNER):
        device = outer * INNER + (inner ^ d)
        hot = hot_of(plan, device)
        ids = jnp.where(is_hot, 2 * device + hot, 2 * device + 1 - hot)
        expert = jnp.where(which == d, ids, expert)
    expert = expert.astype(F32)[0:1]
    slot = slot.astype(F32)[0:1]
    group = group[0:1]
    before = lax.broadcasted_iota(I32, (count, count), 1) < lax.broadcasted_iota(I32, (count, count), 0)
    before = jnp.where(before, 1.0, 0.0).astype(BF16)
    found = []
    for s, ids in enumerate(tails):
        match = ids[:, 0:1] == expert
        for k in range(1, topk):
            match = match | (ids[:, k : k + 1] == expert)
        ones = jnp.where(match, 1.0, 0.0)
        rank = jnp.dot(before, ones.astype(BF16), preferred_element_type=F32)
        found.append(jnp.where((rank == slot) & (group == s), ones, 0.0).astype(BF16))
    return found


def picked(picks, payloads, columns):
    total = None
    for pick, payload in zip(picks, payloads):
        part = lax.dot_general(
            pick[...], payload[:, columns], (((0,), (0,)), ((), ())), preferred_element_type=F32
        )
        total = part if total is None else total + part
    return total


def select_all(picks, payloads, outs):
    rows, width = outs[0].shape
    step = 384 if width % 384 == 0 else 128
    for at in range(0, width, step):
        columns = slice(at, at + step)
        total = picked(picks, payloads, columns)
        for d in range(INNER):
            outs[d][:, columns] = total[d * rows : (d + 1) * rows].astype(BF16)


def start_kernel(m, hot_rows, cold_rows, plan, tokens, routes, gates, grad_out, *refs):
    out, refs = refs[0], refs[1:]
    here_routes, here_gates, sems = refs[-3:]
    outs, picks = refs[:INNER], refs[INNER:-3]
    count, feat = tokens.shape
    share = grad_out.shape[1]
    topk = routes.shape[0]
    copies = [
        pltpu.make_async_copy(source, target, sems.at[n])
        for n, (source, target) in enumerate(
            (
                (routes, here_routes),
                (gates, here_gates),
                (tokens, out.at[:, :feat]),
                (grad_out, out.at[:, feat : feat + share]),
            )
        )
    ]
    for copy in copies:
        copy.start()
    for copy in copies[:2]:
        copy.wait()
    ids = here_routes[...].astype(F32)
    gate = here_gates[...]
    high = gate.astype(BF16).astype(F32)
    middle = (gate - high).astype(BF16).astype(F32)
    low = (gate - high - middle).astype(BF16).astype(F32)
    rest = jnp.zeros((TAIL - 5 * topk, count), F32)
    tail = jnp.concatenate([ids, ids, high, middle, low, rest], 0).T
    out[:, feat + share :] = tail.astype(BF16)
    if picks:
        picks[0][...] = pick_rows(m, hot_rows, cold_rows, topk, plan, [tail])[0]
    for copy in copies[2:]:
        copy.wait()
    if picks:
        select_all(picks, [out], outs)


def select_kernel(m, hot_rows, cold_rows, topk, waits, plan, *refs):
    payloads, refs = refs[:m], refs[m + waits :]
    outs, picks, passed = refs[:INNER], refs[INNER : INNER + m], refs[INNER + m :]
    width = payloads[0].shape[1]
    for source, target in zip(payloads, passed):
        target[...] = source[...]
    tails = [payload[:, width - TAIL :].astype(F32) for payload in payloads]
    for pick, found in zip(picks, pick_rows(m, hot_rows, cold_rows, topk, plan, tails)):
        pick[...] = found
    select_all(picks, payloads, outs)


def forward_rows(block, both, hots, columns):
    if not both:
        return block[:hots, columns], block[hots:, columns]
    colds = block.shape[0] // 2 - hots
    return block[:hots, columns], block[2 * hots : 2 * hots + colds, columns]


def returned_rows(block, both, hots, columns):
    if not both:
        return block[:, columns]
    colds = block.shape[0] // 2 - hots
    cold = block[2 * hots :, columns].astype(F32)[colds:]
    return jnp.concatenate([block[hots : 2 * hots, columns].astype(F32), cold], 0)


def hidden_kernel(m, hot_rows, cold_rows, feat, both, streamed, plan, *refs):
    blocks = refs[:INNER]
    weight, _, part, x_hot, x_cold = refs[INNER:]
    hots = INNER * m * hot_rows
    share = blocks[0].shape[1] - feat - TAIL
    ff = part.shape[1] - share
    tile = 256 if ff % 256 == 0 else ff
    hot = hot_of(plan, lax.axis_index("ep"))
    split = m * hot_rows

    def gather():
        rows = [forward_rows(b, both, split, slice(0, feat)) for b in blocks]
        x_hot[...] = rows_joined([hot_part for hot_part, _ in rows])
        x_cold[...] = rows_joined([cold_part for _, cold_part in rows])
        rows = [forward_rows(b, both, split, slice(feat, feat + share)) for b in blocks]
        part[:hots, ff:] = rows_joined([hot_part for hot_part, _ in rows])
        part[hots:, ff:] = rows_joined([cold_part for _, cold_part in rows])

    def columns(j, source):
        at = pl.ds(pl.multiple_of(j * tile, tile), tile)
        part[:hots, at] = jnp.dot(
            x_hot[...], weight[hot, :, source], preferred_element_type=F32
        ).astype(BF16)
        part[hots:, at] = jnp.dot(
            x_cold[...], weight[1 - hot, :, source], preferred_element_type=F32
        ).astype(BF16)

    if streamed:
        pl.when(pl.program_id(0) == 0)(gather)
        columns(pl.program_id(0), slice(None))
    else:
        gather()

        @pl.loop(0, ff // tile)
        def _(j):
            columns(j, pl.ds(pl.multiple_of(j * tile, tile), tile))


def back_kernel(m, hot_rows, cold_rows, n_parts, n_grads, topk, share, both, n_pay, plan, *refs):
    sums, grads = refs[:n_parts], refs[n_parts : n_parts + n_grads]
    refs = refs[n_parts + n_grads :]
    tails, weight, payloads = refs[:INNER], refs[INNER], refs[INNER + 1 : INNER + 1 + n_pay]
    refs = refs[INNER + 2 + n_pay :]
    outs, g_hot, g_cold, picks = refs[:INNER], refs[INNER], refs[INNER + 1], refs[INNER + 2 :]
    hots, colds = m * hot_rows, m * cold_rows
    rows = hots + colds
    ff = weight.shape[2]
    width = outs[0].shape[1]
    feat = width - share - TAIL
    tile = 512 if feat % 512 == 0 else feat
    me, tp = lax.axis_index("ep"), lax.axis_index("tp")
    hot = hot_of(plan, me)

    def put(columns, back_hot, back_cold):
        there = picked(picks, payloads, columns) if n_pay else None
        for d in range(INNER):
            hot_now = back_hot[d * hots : (d + 1) * hots]
            cold_now = back_cold[d * colds : (d + 1) * colds]
            if n_pay:
                mine = there[d * rows : (d + 1) * rows]
                outs[d][:hots, columns] = mine[:hots].astype(BF16)
                outs[d][hots : 2 * hots, columns] = hot_now.astype(BF16)
                outs[d][2 * hots :, columns] = jnp.concatenate([mine[hots:], cold_now], 0).astype(BF16)
            else:
                outs[d][:hots, columns] = hot_now.astype(BF16)
                outs[d][hots:, columns] = cold_now.astype(BF16)

    if n_pay:
        ids = [payload[:, width - TAIL :].astype(F32) for payload in payloads]
        for pick, found in zip(picks, pick_rows(m, hot_rows, cold_rows, topk, plan, ids)):
            pick[...] = found
    tail_rows = [forward_rows(t, both, hots, slice(width - TAIL, width)) for t in tails]
    ends = []
    for kind, first, piece, target, expert in (
        (0, 0, hots, g_hot, 2 * me + hot),
        (1, INNER * hots, colds, g_cold, 2 * me + 1 - hot),
    ):
        made = []
        per = 1 if piece % 16 == 0 else INNER
        for d in range(0, INNER, per):
            count = piece * per
            now = slice(first + d * piece, first + d * piece + count)
            tail = jnp.concatenate([t[kind].astype(F32) for t in tail_rows[d : d + per]], 0)
            hidden = sums[0][now, :ff].astype(F32)
            for more in sums[1:]:
                hidden = hidden + more[now, :ff].astype(F32)
            if n_grads == 1:
                grad = grads[0][now].astype(F32)
            else:
                mine, other = (g[now, ff:].astype(F32) for g in grads)
                even = tp == 0
                grad = jnp.concatenate(
                    [jnp.where(even, mine, other), jnp.where(even, other, mine)], 1
                )
            e = expert.astype(F32)
            ids = tail[:, :topk]
            gate = (tail[:, 2 * topk : 3 * topk] + tail[:, 3 * topk : 4 * topk]) + tail[:, 4 * topk : 5 * topk]
            gate = jnp.sum(jnp.where(ids == e, gate, 0.0), 1, keepdims=True)
            sig = 1.0 / (1.0 + jnp.exp(-hidden))
            act = (hidden * sig).astype(BF16).astype(F32)
            row_grad = (gate * grad).astype(BF16).astype(F32)
            hidden_grad = row_grad * (sig * (1.0 + hidden * (1.0 - sig)))
            target[d * piece : d * piece + count] = hidden_grad.astype(BF16)
            gate_grad = jnp.sum(act * grad, 1, keepdims=True)
            high = gate_grad.astype(BF16).astype(F32)
            low = gate_grad - high
            lane = lax.broadcasted_iota(I32, tail.shape, 1)
            values = jnp.where(lane < topk, high, low)
            end = jnp.where((tail == e) & (lane < 2 * topk), values, 0.0)
            gated = None
            for n in range(ff // share):
                piece_act = jnp.where(tp == n, act[:, n * share : (n + 1) * share], 0.0)
                gated = piece_act if gated is None else gated + piece_act
            made.append(jnp.concatenate([gate * gated, end], 1))
        ends.append(jnp.concatenate(made, 0))
    put(slice(feat, width), *ends)

    across_rows = (((1,), (1,)), ((), ()))

    def features(j, carry):
        at = pl.ds(pl.multiple_of(j * tile, tile), tile)
        put(
            at,
            lax.dot_general(
                g_hot[...], weight[hot, at, :], across_rows, preferred_element_type=F32
            ),
            lax.dot_general(
                g_cold[...], weight[1 - hot, at, :], across_rows, preferred_element_type=F32
            ),
        )
        return carry

    lax.fori_loop(0, feat // tile, features, 0)


def expand_kernel(m, hots, both, n_more, *refs):
    blocks, picks, refs = refs[:INNER], refs[INNER : INNER + m], refs[INNER + m :]
    more, outs = refs[:n_more], refs[n_more + 1 :]
    width = blocks[0].shape[1]
    step = 384 if width % 384 == 0 else 128
    for at in range(0, width, step):
        columns = slice(at, at + step)
        rows = rows_joined([returned_rows(b, both, hots, columns) for b in blocks]).astype(BF16)
        for s in range(m):
            total = jnp.dot(picks[s][...], rows, preferred_element_type=F32)
            if more:
                total = total + more[s][:, columns].astype(F32)
            outs[s][:, columns] = total.astype(BF16)


def final_kernel(n, topk, *refs):
    parts = refs[:n]
    mixed, grad_tokens, grad_gates = refs[n:]
    feat, share = grad_tokens.shape[1], mixed.shape[1]

    def total(columns):
        out = parts[0][:, columns].astype(F32)
        for part in parts[1:]:
            out = out + part[:, columns].astype(F32)
        return out

    grad_tokens[...] = total(slice(0, feat)).astype(BF16)
    mixed[...] = total(slice(feat, feat + share)).astype(BF16)
    tail = total(slice(feat + share, feat + share + TAIL))
    tail = tail.T
    grad_gates[...] = tail[:topk] + tail[topk : 2 * topk]


def up_kernel(n, plan, *refs):
    x_hot, x_cold = refs[:n], refs[n : 2 * n]
    g_hot, g_cold = refs[2 * n : 3 * n], refs[3 * n : 4 * n]
    out, token, all_hot, all_cold = refs[4 * n + 1 :]
    tile = out.shape[1]
    e, j = pl.program_id(0), pl.program_id(1)
    hot = hot_of(plan, lax.axis_index("ep"))
    at = pl.ds(pl.multiple_of(j * tile, tile), tile)

    @pl.when((e == 0) & (j == 0))
    def _():
        token[...] = jnp.zeros_like(token)
        all_hot[...] = jnp.concatenate([g[...] for g in g_hot], 0)
        all_cold[...] = jnp.concatenate([g[...] for g in g_cold], 0)

    def total(xs, grads):
        rows = jnp.concatenate([x[:, at] for x in xs], 0)
        out[0] = lax.dot_general(
            rows, grads[...], (((0,), (0,)), ((), ())), preferred_element_type=F32
        ).astype(BF16)

    pl.when(e == hot)(lambda: total(x_hot, all_hot))
    pl.when(e != hot)(lambda: total(x_cold, all_cold))


def on_device(tokens, routes, gates, up_weight, replica_on, grad_out):
    count, feat = tokens.shape
    topk = routes.shape[1]
    experts = replica_on.shape[0]
    share = grad_out.shape[1]
    ff = up_weight.shape[2]
    n_ep, n_tp = lax.axis_size("ep"), lax.axis_size("tp")
    outer = n_ep // INNER
    capacity = 3 * count * topk // (4 * experts)
    hot_rows, cold_rows = 2 * capacity, capacity
    width = feat + share + TAIL
    smem = pl.BlockSpec(memory_space=pltpu.SMEM)

    def along(value, shift):
        pairs = [
            (o * INNER + i, ((o + shift) % outer) * INNER + i)
            for o in range(outer)
            for i in range(INNER)
        ]
        return lax.ppermute(value, "ep", pairs)

    def across(value, d):
        pairs = [(o * INNER + i, o * INNER + (i ^ d)) for o in range(outer) for i in range(INNER)]
        return lax.ppermute(value, "ep", pairs)

    rest_spec = pl.BlockSpec(memory_space=pl.ANY)
    m = max(1, outer // CHUNKS)
    chunks = [list(range(first, first + m)) for first in range(0, outer, m)]
    n = len(chunks)
    rows = m * (hot_rows + cold_rows)
    hots, colds = INNER * m * hot_rows, INNER * m * cold_rows
    sizes = (m, hot_rows, cold_rows)

    def block(shape, dtype=BF16):
        return jax.ShapeDtypeStruct(shape, dtype)

    def fixed(shape):
        return pl.BlockSpec(shape, lambda j: (0,) * len(shape))

    going = {f: k for k, (f, _) in enumerate(PLAN) if f is not None}
    coming = {r: k for k, (_, r) in enumerate(PLAN) if r is not None}

    def doubled(k):
        return None not in PLAN[k]

    def weigh(kind):
        return cost(COSTS[kind] * 10**6, COSTS[kind] * 10**4)

    arrived, picks, blocks, sums, grads, partials = {}, {}, {}, {}, {}, {}
    x_hots, x_colds, g_hots, g_colds = {}, {}, {}, {}

    def exchange(k, made):
        blocks[k] = [made[0]] + [across(made[d], d) for d in range(1, INNER)]

    own_rows = m == 1
    made = pl.pallas_call(
        functools.partial(start_kernel, *sizes),
        out_shape=[block((count, width))]
        + ([block((rows, width))] * INNER + [block((count, INNER * rows))] if own_rows else []),
        in_specs=[smem] + [rest_spec] * 4,
        out_specs=whole_specs(1 + (INNER + 1 if own_rows else 0)),
        scratch_shapes=[
            pltpu.VMEM((topk, count), I32),
            pltpu.VMEM((topk, count), F32),
            pltpu.SemaphoreType.DMA((4,)),
        ],
        compiler_params=params(WIDE),
        cost_estimate=weigh("x"),
        name="start",
    )(replica_on, tokens, routes.T, gates.T, grad_out)
    payload = made[0]
    last = []
    for c in range(n):
        for s in chunks[c] if c not in PASSED else ():
            if s == 0:
                arrived[s] = payload
            else:
                arrived[s] = along(arrived[s - m], m) if c else along(payload, s)

    def select(k):
        c = PLAN[k][0]
        more = m if c + 1 in PASSED else 0
        made = pl.pallas_call(
            functools.partial(select_kernel, *sizes, topk, len(last)),
            out_shape=[block((rows, width))] * INNER
            + [block((count, INNER * rows))] * m
            + [block((count, width))] * more,
            in_specs=[smem] + whole_specs(m) + [rest_spec] * len(last),
            out_specs=whole_specs(INNER + m + more),
            compiler_params=params(),
            cost_estimate=weigh("x"),
            name="select",
        )(replica_on, *[arrived[s] for s in chunks[c]], *last)
        picks[c] = made[INNER : INNER + m]
        exchange(k, made)
        if more:
            for s, value in zip(chunks[c + 1], made[INNER + m :]):
                arrived[s] = along(value, m)
        last[:] = [picks[c][0]]

    def hidden(c):
        k = going[c]
        tile = 256 if ff % 256 == 0 else ff
        shapes = [(INNER * rows, ff + share), (hots, feat), (colds, feat)]
        streamed = c == 0 and FIRST > 0
        if streamed:
            where = dict(
                grid=(ff // tile,),
                in_specs=[smem]
                + [fixed(b.shape) for b in blocks[k]]
                + [pl.BlockSpec((2, feat, tile), lambda j: (0, 0, j)), rest_spec],
                out_specs=[fixed(shape) for shape in shapes],
            )
        else:
            where = dict(
                in_specs=[smem] + whole_specs(INNER + 1) + [rest_spec],
                out_specs=whole_specs(3),
            )
        part, x_hots[c], x_colds[c] = pl.pallas_call(
            functools.partial(hidden_kernel, *sizes, feat, doubled(k), streamed),
            out_shape=[block(shape) for shape in shapes],
            **where,
            compiler_params=params(WIDE if c == 0 and FIRST == 2 else LIMIT),
            cost_estimate=weigh("h"),
            name="hidden",
        )(replica_on, *blocks[k], up_weight, last[0])
        last[0] = x_colds[c]
        if n_tp == 2:
            sums[c] = [part, lax.ppermute(part, "tp", [(0, 1), (1, 0)])]
            grads[c] = sums[c]
        else:
            sums[c] = [lax.psum(part[:, :ff].astype(F32), "tp")]
            grads[c] = [lax.all_gather(part[:, ff:], "tp", axis=1, tiled=True)]

    def step(k):
        f, c = PLAN[k]
        if c is None:
            return select(k)
        sent = (2 if doubled(k) else 1) * rows
        there = [arrived[s] for s in chunks[f]] if f is not None else []
        made = pl.pallas_call(
            functools.partial(
                back_kernel,
                *sizes,
                len(sums[c]),
                len(grads[c]),
                topk,
                share,
                doubled(going[c]),
                len(there),
            ),
            out_shape=[block((sent, width))] * INNER
            + [block((hots, ff)), block((colds, ff))]
            + [block((count, INNER * rows))] * len(there),
            in_specs=[smem]
            + whole_specs(len(sums[c]) + len(grads[c]) + INNER + 1 + len(there))
            + [rest_spec],
            out_specs=whole_specs(INNER + 2 + len(there)),
            compiler_params=params(),
            cost_estimate=weigh("b"),
            name="back",
        )(replica_on, *sums[c], *grads[c], *blocks[going[c]], up_weight, *there, last[0])
        g_hots[c], g_colds[c] = made[INNER : INNER + 2]
        if f is not None:
            picks[f] = made[INNER + 2 :]
        exchange(k, made)
        last[0] = g_colds[c]

    def expand(c):
        more = [along(partials[s - m], m) for s in chunks[c]] if c > 1 else []
        k = coming[c]
        made = pl.pallas_call(
            functools.partial(expand_kernel, m, m * hot_rows, doubled(k), len(more)),
            out_shape=[block((count, width))] * m,
            in_specs=whole_specs(INNER + m + len(more)) + [rest_spec],
            out_specs=whole_specs(m),
            compiler_params=params(),
            cost_estimate=weigh("e"),
            name="expand",
        )(*blocks[k], *picks[c], *more, last[0])
        for s, value in zip(chunks[c], made):
            partials[s] = value
        last[0] = made[0]

    def weight_grad():
        tile = 512 if feat % 512 == 0 else feat
        grad_up, token = pl.pallas_call(
            functools.partial(up_kernel, n),
            out_shape=[block(up_weight.shape), block((8, 128), F32)],
            grid=(up_weight.shape[0], feat // tile),
            in_specs=[smem] + whole_specs(4 * n) + [rest_spec],
            out_specs=[
                pl.BlockSpec((1, tile, ff), lambda e, j: (e, j, 0)),
                pl.BlockSpec((8, 128), lambda e, j: (0, 0)),
            ],
            scratch_shapes=[
                pltpu.VMEM((n * hots, ff), BF16),
                pltpu.VMEM((n * colds, ff), BF16),
            ],
            compiler_params=params(),
            cost_estimate=weigh("u"),
            name="grad_up",
        )(
            replica_on,
            *[x_hots[c] for c in range(n)],
            *[x_colds[c] for c in range(n)],
            *[g_hots[c] for c in range(n)],
            *[g_colds[c] for c in range(n)],
            last[0],
        )
        last[0] = token
        return grad_up

    if own_rows:
        picks[0] = made[INNER + 1 :]
        exchange(0, made[1 : INNER + 1])
    else:
        select(0)
    grad_up = None
    for word in ORDER:
        number = int(word[1:] or 0)
        if word[0] == "u":
            grad_up = weight_grad()
        else:
            {"x": step, "h": hidden, "e": expand}[word[0]](number)

    sums_back = [along(partials[s], m) for s in chunks[n - 1]]
    parts = [sums_back[0], partials[0]]
    for s in chunks[0][1:]:
        parts.append(along(sums_back[s] + partials[s], outer - s))
    mixed, grad_tokens, grad_gates = pl.pallas_call(
        functools.partial(final_kernel, len(parts), topk),
        out_shape=[block((count, share)), block((count, feat)), block((topk, count), F32)],
        in_specs=whole_specs(len(parts)),
        out_specs=whole_specs(3),
        compiler_params=params(),
        cost_estimate=weigh("e"),
        name="final",
    )(*parts)
    return mixed, grad_tokens, grad_gates.T, grad_up


def solution(mesh):
    return jax.shard_map(
        on_device,
        mesh=mesh,
        in_specs=(
            P("ep", "tp"),
            P("ep", None),
            P("ep", None),
            P("ep", "tp", None),
            P(),
            P("ep", "tp"),
        ),
        out_specs=(P("ep", "tp"), P("ep", "tp"), P("ep", None), P("ep", "tp", None)),
        check_vma=False,
    )
```

time: 198 us -> 166 us (0.84)
  Pallas kernels: 76.6 us -> 52.6 us
  local copies, waits for them, and re-layouts: 5.06 us -> 0.02 us
    pallas_call x7 -> x8, Pallas kernels: 39.5 us -> 25.4 us  [the longest x4 11.3 us: hidden(): pl.pallas_call(functools.partial(hidden_kernel, *sizes, feat, doubled(k),...]
    pallas_call x4, Pallas kernels: 31.8 us -> 19.8 us  [step(): pl.pallas_call(functools.partial(back_kernel, *sizes, len(sums[c]), len(g...]
    unnamed x16 -> x10, local copies, waits for them, and re-layouts: 5.06 us -> 0.02 us
    ppermute x21 -> x24, waiting for transfers between devices: 40.8 us -> 37.4 us  [across(): return lax.ppermute(value, 'ep', pairs)]
    ppermute x6, waiting for transfers between devices: 36.5 us -> 38.6 us  [along(): return lax.ppermute(value, 'ep', pairs)]
    pallas_call x1, Pallas kernels: 1.68 us -> 3.77 us  [on_device(): pl.pallas_call(functools.partial(start_kernel, *sizes), out_shape=[block(...]
    ppermute x21 -> x24, starting transfers between devices: 28.1 us -> 26.8 us  [across(): return lax.ppermute(value, 'ep', pairs)]
  transfers between devices with their start and end apart: 31 -> 34, of which waited for: 10 -> 13; matrix products, arithmetic and copies ran while one was open for 0% -> 0% of each run, Pallas kernels for 37% -> 29%
where the time goes in v3:
time: 166 us
  waiting for transfers between devices  76 us (46%)
  Pallas kernels  52.6 us (32%)
  starting transfers between devices  36.6 us (22%)
    ppermute x6, waiting for transfers between devices, along(): return lax.ppermute(value, 'ep', pairs)  38.6 us
    ppermute x24, waiting for transfers between devices, across(): return lax.ppermute(value, 'ep', pairs)  37.4 us
    ppermute x24, starting transfers between devices, across(): return lax.ppermute(value, 'ep', pairs)  26.8 us
    pallas_call x4, Pallas kernels, step(): pl.pallas_call(functools.partial(back_kernel, *sizes, len(sums[c]), len(g...  19.8 us
    pallas_call x4, Pallas kernels, hidden(): pl.pallas_call(functools.partial(hidden_kernel, *sizes, feat, doubled(k),...  11.3 us
    ppermute x6, starting transfers between devices, along(): return lax.ppermute(value, 'ep', pairs)  9.61 us
    pallas_call x1, Pallas kernels, weight_grad(): pl.pallas_call(functools.partial(up_kernel, n), out_shape=[block(up_weigh...  9.39 us
    pallas_call x3, Pallas kernels, select(): pl.pallas_call(functools.partial(select_kernel, *sizes, topk, len(last)),...  4.71 us
  transfers between devices with their start and end apart: 34, of which 13 were waited for; matrix products, arithmetic and copies ran while one was open for 0% of the time, Pallas kernels for 29%

profile of v3, /device:TPU:0, one launch (start us, length us, event | category | flops | bytes accessed | tf_op | source)
XLA Modules:
  0.0 166.1 jit_solution(8437414865628945920)
XLA Ops:
  0.6 3.8 %start.1 = (bf16[128,2688]{1,0:T(8,128)(2,1)}, bf16[72,2688]{1,0:T(8,128)(2,1)}, bf16[72,2688]{1,0:T(8,128)(2,1)}, bf16[72,2688]{1,0:T(8,128)(2,1)}, bf16[72,2688]{1,0:T(8,128)(2,1)}, /*index=5*/bf16[128,288]{1,0:T(8,128)(2,1)}) custom-call(s32[32]{0:T(128)} %plan.25, bf16[128,2048]{1,0:T(8,128)(2,1)} %tokens.1, s32[8,128]{1,0:T(8,128)} %bitcast.5, ...), custom_call_target="tpu_custom_call" | custom-call | flops 5000000000 | bytes 50000000 | tf_op jit(solution)/shard_map/start/pallas_call | solution.py:417
  4.4 3.1 %collective-permute-start = (bf16[128,2688]{1,0:T(8,128)(2,1)}, bf16[128,2688]{1,0:T(8,128)(2,1)S(1)}, u32[]{:S(2)}, u32[]{:S(2)}) collective-permute-start(bf16[128,2688]{1,0:T(8,128)(2,1)} %get-tuple-element.66), channel_id=1, source_target_pairs={{0,8},{2,10},{4,12},{6,14},{8,16},{10,18},{12,20},{14,22},{16,24},... | collective-permute-start | bytes 2064392 | tf_op jit(solution)/shard_map/ppermute | solution.py:381
  11.0 14.2 %collective-permute-done.refs_0_ = bf16[128,2688]{1,0:T(8,128)(2,1)S(1)} collective-permute-done((bf16[128,2688]{1,0:T(8,128)(2,1)}, bf16[128,2688]{1,0:T(8,128)(2,1)S(1)}, u32[]{:S(2)}, u32[]{:S(2)}) %collective-permute-start) | collective-permute-done | bytes 688160 | tf_op jit(solution)/shard_map/ppermute | solution.py:381
  30.3 2.8 %hidden.4 = (bf16[288,1536]{1,0:T(8,128)(2,1)S(1)}, bf16[192,2048]{1,0:T(8,128)(2,1)S(1)}, bf16[96,2048]{1,0:T(8,128)(2,1)S(1)}) custom-call(s32[32]{0:T(128)S(1)} %copy-done.1, bf16[72,2688]{1,0:T(8,128)(2,1)S(1)} %copy-done, bf16[72,2688]{1,0:T(8,128)(2,1)S(1)} %collective-permute-done.6.refs_1_.refs_5_, ...), custom_call_target="tpu_custom_call" | custom-call | flops 5000000000 | bytes 50000000 | tf_op jit(solution)/shard_map/hidden/pallas_call | solution.py:480
  33.2 10.4 %collective-permute-done.1.refs_0_ = bf16[128,2688]{1,0:T(8,128)(2,1)S(1)} collective-permute-done((bf16[128,2688]{1,0:T(8,128)(2,1)S(1)}, bf16[128,2688]{1,0:T(8,128)(2,1)S(1)}, u32[]{:S(2)}, u32[]{:S(2)}) %collective-permute-start.1) | collective-permute-done | bytes 688160 | tf_op jit(solution)/shard_map/ppermute | solution.py:381
  48.7 2.8 %hidden.5 = (bf16[288,1536]{1,0:T(8,128)(2,1)S(1)}, bf16[192,2048]{1,0:T(8,128)(2,1)S(1)}, bf16[96,2048]{1,0:T(8,128)(2,1)S(1)}) custom-call(s32[32]{0:T(128)S(1)} %copy-done.1, bf16[72,2688]{1,0:T(8,128)(2,1)S(1)} %get-tuple-element.67.refs_0_.refs_4_, bf16[72,2688]{1,0:T(8,128)(2,1)S(1)} %collective-permute-done.3.refs_1_.refs_5_, ...), custom_call_target="tpu_custom_call" | custom-call | flops 5000000000 | bytes 50000000 | tf_op jit(solution)/shard_map/hidden/pallas_call | solution.py:480
  51.6 9.4 %collective-permute-done.2.refs_0_ = bf16[128,2688]{1,0:T(8,128)(2,1)S(1)} collective-permute-done((bf16[128,2688]{1,0:T(8,128)(2,1)S(1)}, bf16[128,2688]{1,0:T(8,128)(2,1)S(1)}, u32[]{:S(2)}, u32[]{:S(2)}) %collective-permute-start.2) | collective-permute-done | bytes 688160 | tf_op jit(solution)/shard_map/ppermute | solution.py:381
  66.2 2.8 %hidden.6 = (bf16[288,1536]{1,0:T(8,128)(2,1)S(1)}, bf16[192,2048]{1,0:T(8,128)(2,1)S(1)}, bf16[96,2048]{1,0:T(8,128)(2,1)S(1)}) custom-call(s32[32]{0:T(128)S(1)} %copy-done.1, bf16[72,2688]{1,0:T(8,128)(2,1)S(1)} %get-tuple-element.84.refs_0_.refs_4_, bf16[72,2688]{1,0:T(8,128)(2,1)S(1)} %collective-permute-done.13.refs_1_.refs_5_, ...), custom_call_target="tpu_custom_call" | custom-call | flops 5000000000 | bytes 50000000 | tf_op jit(solution)/shard_map/hidden/pallas_call | solution.py:480
  69.1 4.9 %back.4 = (bf16[72,2688]{1,0:T(8,128)(2,1)S(1)}, bf16[72,2688]{1,0:T(8,128)(2,1)S(1)}, bf16[72,2688]{1,0:T(8,128)(2,1)S(1)}, bf16[72,2688]{1,0:T(8,128)(2,1)S(1)...) custom-call(s32[32]{0:T(128)S(1)} %copy-done.1, bf16[288,1536]{1,0:T(8,128)(2,1)S(1)} %get-tuple-element.83.refs_0_.refs_2_, ...), custom_call_target="tpu_custom_call" | custom-call | flops 100000000 | bytes 1000000 | tf_op jit(solution)/shard_map/back/pallas_call | solution.py:502
  75.2 4.9 %collective-permute-done.10.refs_2_.refs_6_ = bf16[72,2688]{1,0:T(8,128)(2,1)S(1)} collective-permute-done((bf16[72,2688]{1,0:T(8,128)(2,1)S(1)}, bf16[72,2688]{1,0:T(8,128)(2,1)S(1)}, u32[]{:S(2)}, u32[]{:S(2)}) %collective-permute-start.10) | collective-permute-done | bytes 387104 | tf_op jit(solution)/shard_map/ppermute | solution.py:385
  83.8 2.8 %hidden.7 = (bf16[288,1536]{1,0:T(8,128)(2,1)S(1)}, bf16[192,2048]{1,0:T(8,128)(2,1)S(1)}, bf16[96,2048]{1,0:T(8,128)(2,1)S(1)}) custom-call(s32[32]{0:T(128)S(1)} %copy-done.1, bf16[72,2688]{1,0:T(8,128)(2,1)S(1)} %get-tuple-element.79.refs_0_.refs_4_, bf16[72,2688]{1,0:T(8,128)(2,1)S(1)} %collective-permute-done.9.refs_1_.refs_5_, ...), custom_call_target="tpu_custom_call" | custom-call | flops 5000000000 | bytes 50000000 | tf_op jit(solution)/shard_map/hidden/pallas_call | solution.py:480
  86.8 5.4 %collective-permute-done.18.refs_1_ = bf16[72,2688]{1,0:T(8,128)(2,1)S(1)} collective-permute-done((bf16[72,2688]{1,0:T(8,128)(2,1)S(1)}, bf16[72,2688]{1,0:T(8,128)(2,1)S(1)}, u32[]{:S(2)}, u32[]{:S(2)}) %collective-permute-start.18) | collective-permute-done | bytes 387104 | tf_op jit(solution)/shard_map/ppermute | solution.py:385
  92.1 6.4 %collective-permute-done.19.refs_2_ = bf16[72,2688]{1,0:T(8,128)(2,1)S(1)} collective-permute-done((bf16[72,2688]{1,0:T(8,128)(2,1)S(1)}, bf16[72,2688]{1,0:T(8,128)(2,1)S(1)}, u32[]{:S(2)}, u32[]{:S(2)}) %collective-permute-start.19) | collective-permute-done | bytes 387104 | tf_op jit(solution)/shard_map/ppermute | solution.py:385
  99.2 2.5 %collective-permute-start.27 = (bf16[128,2688]{1,0:T(8,128)(2,1)S(1)}, bf16[128,2688]{1,0:T(8,128)(2,1)S(1)}, u32[]{:S(2)}, u32[]{:S(2)}) collective-permute-start(bf16[128,2688]{1,0:T(8,128)(2,1)S(1)} %expand.4.refs_9_), channel_id=1, source_target_pairs={{0,8},{2,10},{4,12},{6,14},{8,16},{10,18},{12,20},{14,22},{16,24},... | collective-permute-start | bytes 2064392 | tf_op jit(solution)/shard_map/ppermute | solution.py:381
  101.7 5.0 %back.5 = (bf16[72,2688]{1,0:T(8,128)(2,1)S(1)}, bf16[72,2688]{1,0:T(8,128)(2,1)S(1)}, bf16[72,2688]{1,0:T(8,128)(2,1)S(1)}, bf16[72,2688]{1,0:T(8,128)(2,1)S(1)...) custom-call(s32[32]{0:T(128)S(1)} %copy-done.1, bf16[288,1536]{1,0:T(8,128)(2,1)S(1)} %get-tuple-element.92.refs_0_.refs_2_, ...), custom_call_target="tpu_custom_call" | custom-call | flops 100000000 | bytes 1000000 | tf_op jit(solution)/shard_map/back/pallas_call | solution.py:502
  110.2 4.9 %back.6 = (bf16[72,2688]{1,0:T(8,128)(2,1)S(1)}, bf16[72,2688]{1,0:T(8,128)(2,1)S(1)}, bf16[72,2688]{1,0:T(8,128)(2,1)S(1)}, bf16[72,2688]{1,0:T(8,128)(2,1)S(1)...) custom-call(s32[32]{0:T(128)S(1)} %copy-done.1, bf16[288,1536]{1,0:T(8,128)(2,1)S(1)} %get-tuple-element.91.refs_0_.refs_2_, ...), custom_call_target="tpu_custom_call" | custom-call | flops 100000000 | bytes 1000000 | tf_op jit(solution)/shard_map/back/pallas_call | solution.py:502
  115.2 4.6 %collective-permute-done.27.refs_5_ = bf16[128,2688]{1,0:T(8,128)(2,1)S(1)} collective-permute-done((bf16[128,2688]{1,0:T(8,128)(2,1)S(1)}, bf16[128,2688]{1,0:T(8,128)(2,1)S(1)}, u32[]{:S(2)}, u32[]{:S(2)}) %collective-permute-start.27) | collective-permute-done | bytes 688160 | tf_op jit(solution)/shard_map/ppermute | solution.py:381
  119.8 6.7 %collective-permute-done.25.refs_2_ = bf16[72,2688]{1,0:T(8,128)(2,1)S(1)} collective-permute-done((bf16[72,2688]{1,0:T(8,128)(2,1)S(1)}, bf16[72,2688]{1,0:T(8,128)(2,1)S(1)}, u32[]{:S(2)}, u32[]{:S(2)}) %collective-permute-start.25) | collective-permute-done | bytes 387104 | tf_op jit(solution)/shard_map/ppermute | solution.py:385
  127.2 3.1 %collective-permute-start.28 = (bf16[128,2688]{1,0:T(8,128)(2,1)S(1)}, bf16[128,2688]{1,0:T(8,128)(2,1)S(1)}, u32[]{:S(2)}, u32[]{:S(2)}) collective-permute-start(bf16[128,2688]{1,0:T(8,128)(2,1)S(1)} %expand.5.refs_9_), channel_id=1, source_target_pairs={{0,8},{2,10},{4,12},{6,14},{8,16},{10,18},{12,20},{14,22},{16,24},... | collective-permute-start | bytes 2064392 | tf_op jit(solution)/shard_map/ppermute | solution.py:381
  133.7 4.9 %back.7 = (bf16[72,2688]{1,0:T(8,128)(2,1)S(1)}, bf16[72,2688]{1,0:T(8,128)(2,1)S(1)}, bf16[72,2688]{1,0:T(8,128)(2,1)S(1)}, bf16[72,2688]{1,0:T(8,128)(2,1)S(1)...) custom-call(s32[32]{0:T(128)S(1)} %copy-done.1, bf16[288,1536]{1,0:T(8,128)(2,1)S(1)} %get-tuple-element.108.refs_0_.refs_2_, ...), custom_call_target="tpu_custom_call" | custom-call | flops 100000000 | bytes 1000000 | tf_op jit(solution)/shard_map/back/pallas_call | solution.py:502
  139.2 2.9 %collective-permute-done.21.refs_1_ = bf16[72,2688]{1,0:T(8,128)(2,1)S(1)} collective-permute-done((bf16[72,2688]{1,0:T(8,128)(2,1)S(1)}, bf16[72,2688]{1,0:T(8,128)(2,1)S(1)}, u32[]{:S(2)}, u32[]{:S(2)}) %collective-permute-start.21) | collective-permute-done | bytes 387104 | tf_op jit(solution)/shard_map/ppermute | solution.py:385
  142.8 6.3 %collective-permute-done.22.refs_2_ = bf16[72,2688]{1,0:T(8,128)(2,1)S(1)} collective-permute-done((bf16[72,2688]{1,0:T(8,128)(2,1)S(1)}, bf16[72,2688]{1,0:T(8,128)(2,1)S(1)}, u32[]{:S(2)}, u32[]{:S(2)}) %collective-permute-start.22) | collective-permute-done | bytes 387104 | tf_op jit(solution)/shard_map/ppermute | solution.py:385
  152.2 9.4 %grad_up.1 = (bf16[2,2048,1024]{2,1,0:T(8,128)(2,1)}, f32[8,128]{1,0:T(8,128)S(1)}) custom-call(s32[32]{0:T(128)S(1)} %copy-done.1, bf16[192,2048]{1,0:T(8,128)(2,1)S(1)} %get-tuple-element.115.refs_0_, bf16[192,2048]{1,0:T(8,128)(2,1)S(1)} %get-tuple-element.116.refs_1_, bf16[192,2048]{1,0:T(8,128)(2,1)S(1)} %get-tuple-element.117.refs_2_, ...), custom_call_target="tpu_custom_call" | custom-call | flops 20000000000 | bytes 200000000 | tf_op jit(solution)/shard_map/grad_up/pallas_call | solution.py:548
  161.6 2.7 %collective-permute-done.32.refs_2_ = bf16[72,2688]{1,0:T(8,128)(2,1)S(1)} collective-permute-done((bf16[72,2688]{1,0:T(8,128)(2,1)S(1)}, bf16[72,2688]{1,0:T(8,128)(2,1)S(1)}, u32[]{:S(2)}, u32[]{:S(2)}) %collective-permute-start.32) | collective-permute-done | bytes 387104 | tf_op jit(solution)/shard_map/ppermute | solution.py:385
  (73 shorter events, 38.4 us)
Async XLA Ops:
  4.4 20.7 %collective-permute-start = (bf16[128,2688]{1,0:T(8,128)(2,1)}, bf16[128,2688]{1,0:T(8,128)(2,1)S(1)}, u32[]{:S(2)}, u32[]{:S(2)}) collective-permute-start(bf16[128,2688]{1,0:T(8,128)(2,1)} %get-tuple-element.66), channel_id=1, source_target_pairs={{0,8},{2,10},{4,12},{6,14},{8,16},{10,18},{12,20},{14,22},{16,24},... | collective-permute-start | bytes 2064392 | tf_op jit(solution)/shard_map/ppermute | solution.py:381
  7.5 20.8 %collective-permute-start.6 = (bf16[72,2688]{1,0:T(8,128)(2,1)}, bf16[72,2688]{1,0:T(8,128)(2,1)S(1)}, u32[]{:S(2)}, u32[]{:S(2)}) collective-permute-start(bf16[72,2688]{1,0:T(8,128)(2,1)} %get-tuple-element.72), channel_id=1, source_target_pairs={{0,2},{2,0},{4,6},{6,4},{8,10},{10,8},{12,14},{14,12},{16,18},{18,... | collective-permute-start | bytes 1161224 | tf_op jit(solution)/shard_map/ppermute | solution.py:385
  9.0 20.8 %collective-permute-start.7 = (bf16[72,2688]{1,0:T(8,128)(2,1)}, bf16[72,2688]{1,0:T(8,128)(2,1)S(1)}, u32[]{:S(2)}, u32[]{:S(2)}) collective-permute-start(bf16[72,2688]{1,0:T(8,128)(2,1)} %get-tuple-element.73), channel_id=1, source_target_pairs={{0,4},{2,6},{4,0},{6,2},{8,12},{10,14},{12,8},{14,10},{16,20},{18,... | collective-permute-start | bytes 1161224 | tf_op jit(solution)/shard_map/ppermute | solution.py:385
  10.5 19.8 %collective-permute-start.8 = (bf16[72,2688]{1,0:T(8,128)(2,1)}, bf16[72,2688]{1,0:T(8,128)(2,1)S(1)}, u32[]{:S(2)}, u32[]{:S(2)}) collective-permute-start(bf16[72,2688]{1,0:T(8,128)(2,1)} %get-tuple-element.74), channel_id=1, source_target_pairs={{0,6},{2,4},{4,2},{6,0},{8,14},{10,12},{12,10},{14,8},{16,22},{18,... | collective-permute-start | bytes 1161224 | tf_op jit(solution)/shard_map/ppermute | solution.py:385
  25.2 18.4 %collective-permute-start.1 = (bf16[128,2688]{1,0:T(8,128)(2,1)S(1)}, bf16[128,2688]{1,0:T(8,128)(2,1)S(1)}, u32[]{:S(2)}, u32[]{:S(2)}) collective-permute-start(bf16[128,2688]{1,0:T(8,128)(2,1)S(1)} %collective-permute-done.refs_0_), channel_id=1, source_target_pairs={{0,8},{2,10},{4,12},{6,14},{8,16},{10,18},{12,20},{14,22},{16,24},... | collective-permute-start | bytes 2064392 | tf_op jit(solution)/shard_map/ppermute | solution.py:381
  26.7 19.7 %collective-permute-start.3 = (bf16[72,2688]{1,0:T(8,128)(2,1)S(1)}, bf16[72,2688]{1,0:T(8,128)(2,1)S(1)}, u32[]{:S(2)}, u32[]{:S(2)}) collective-permute-start(bf16[72,2688]{1,0:T(8,128)(2,1)S(1)} %get-tuple-element.68), channel_id=1, source_target_pairs={{0,2},{2,0},{4,6},{6,4},{8,10},{10,8},{12,14},{14,12},{16,18},{18,... | collective-permute-start | bytes 1161224 | tf_op jit(solution)/shard_map/ppermute | solution.py:385
  28.3 19.7 %collective-permute-start.4 = (bf16[72,2688]{1,0:T(8,128)(2,1)S(1)}, bf16[72,2688]{1,0:T(8,128)(2,1)S(1)}, u32[]{:S(2)}, u32[]{:S(2)}) collective-permute-start(bf16[72,2688]{1,0:T(8,128)(2,1)S(1)} %get-tuple-element.69), channel_id=1, source_target_pairs={{0,4},{2,6},{4,0},{6,2},{8,12},{10,14},{12,8},{14,10},{16,20},{18,... | collective-permute-start | bytes 1161224 | tf_op jit(solution)/shard_map/ppermute | solution.py:385
  29.8 18.9 %collective-permute-start.5 = (bf16[72,2688]{1,0:T(8,128)(2,1)S(1)}, bf16[72,2688]{1,0:T(8,128)(2,1)S(1)}, u32[]{:S(2)}, u32[]{:S(2)}) collective-permute-start(bf16[72,2688]{1,0:T(8,128)(2,1)S(1)} %get-tuple-element.70), channel_id=1, source_target_pairs={{0,6},{2,4},{4,2},{6,0},{8,14},{10,12},{12,10},{14,8},{16,22},{18,... | collective-permute-start | bytes 1161224 | tf_op jit(solution)/shard_map/ppermute | solution.py:385
  45.2 18.6 %collective-permute-start.13 = (bf16[72,2688]{1,0:T(8,128)(2,1)S(1)}, bf16[72,2688]{1,0:T(8,128)(2,1)S(1)}, u32[]{:S(2)}, u32[]{:S(2)}) collective-permute-start(bf16[72,2688]{1,0:T(8,128)(2,1)S(1)} %get-tuple-element.85), channel_id=1, source_target_pairs={{0,2},{2,0},{4,6},{6,4},{8,10},{10,8},{12,14},{14,12},{16,18},{18,... | collective-permute-start | bytes 1161224 | tf_op jit(solution)/shard_map/ppermute | solution.py:385
  46.5 18.7 %collective-permute-start.14 = (bf16[72,2688]{1,0:T(8,128)(2,1)S(1)}, bf16[72,2688]{1,0:T(8,128)(2,1)S(1)}, u32[]{:S(2)}, u32[]{:S(2)}) collective-permute-start(bf16[72,2688]{1,0:T(8,128)(2,1)S(1)} %get-tuple-element.86), channel_id=1, source_target_pairs={{0,4},{2,6},{4,0},{6,2},{8,12},{10,14},{12,8},{14,10},{16,20},{18,... | collective-permute-start | bytes 1161224 | tf_op jit(solution)/shard_map/ppermute | solution.py:385
  48.0 18.2 %collective-permute-start.15 = (bf16[72,2688]{1,0:T(8,128)(2,1)S(1)}, bf16[72,2688]{1,0:T(8,128)(2,1)S(1)}, u32[]{:S(2)}, u32[]{:S(2)}) collective-permute-start(bf16[72,2688]{1,0:T(8,128)(2,1)S(1)} %get-tuple-element.87), channel_id=1, source_target_pairs={{0,6},{2,4},{4,2},{6,0},{8,14},{10,12},{12,10},{14,8},{16,22},{18,... | collective-permute-start | bytes 1161224 | tf_op jit(solution)/shard_map/ppermute | solution.py:385
  65.2 18.6 %collective-permute-start.9 = (bf16[72,2688]{1,0:T(8,128)(2,1)S(1)}, bf16[72,2688]{1,0:T(8,128)(2,1)S(1)}, u32[]{:S(2)}, u32[]{:S(2)}) collective-permute-start(bf16[72,2688]{1,0:T(8,128)(2,1)S(1)} %get-tuple-element.80), channel_id=1, source_target_pairs={{0,2},{2,0},{4,6},{6,4},{8,10},{10,8},{12,14},{14,12},{16,18},{18,... | collective-permute-start | bytes 1161224 | tf_op jit(solution)/shard_map/ppermute | solution.py:385
  69.1 32.6 %collective-permute-start.17 = (bf16[288,1536]{1,0:T(8,128)(2,1)S(1)}, bf16[288,1536]{1,0:T(8,128)(2,1)S(1)}, u32[]{:S(2)}, u32[]{:S(2)}) collective-permute-start(bf16[288,1536]{1,0:T(8,128)(2,1)S(1)} %get-tuple-element.92.refs_0_.refs_2_), channel_id=1, source_target_pairs={{0,1},{1,0},{2,3},{3,2},{4,5},{5,4},{6,7},{7,6},{8,9},{9,8},{10,11... | collective-permute-start | bytes 2654216 | tf_op jit(solution)/shard_map/ppermute | solution.py:490
  74.1 18.0 %collective-permute-start.18 = (bf16[72,2688]{1,0:T(8,128)(2,1)S(1)}, bf16[72,2688]{1,0:T(8,128)(2,1)S(1)}, u32[]{:S(2)}, u32[]{:S(2)}) collective-permute-start(bf16[72,2688]{1,0:T(8,128)(2,1)S(1)} %get-tuple-element.94), channel_id=1, source_target_pairs={{0,2},{2,0},{4,6},{6,4},{8,10},{10,8},{12,14},{14,12},{16,18},{18,... | collective-permute-start | bytes 1161224 | tf_op jit(solution)/shard_map/ppermute | solution.py:385
  80.1 18.5 %collective-permute-start.19 = (bf16[72,2688]{1,0:T(8,128)(2,1)S(1)}, bf16[72,2688]{1,0:T(8,128)(2,1)S(1)}, u32[]{:S(2)}, u32[]{:S(2)}) collective-permute-start(bf16[72,2688]{1,0:T(8,128)(2,1)S(1)} %get-tuple-element.95), channel_id=1, source_target_pairs={{0,4},{2,6},{4,0},{6,2},{8,12},{10,14},{12,8},{14,10},{16,20},{18,... | collective-permute-start | bytes 1161224 | tf_op jit(solution)/shard_map/ppermute | solution.py:385
  86.7 23.5 %collective-permute-start.16 = (bf16[288,1536]{1,0:T(8,128)(2,1)S(1)}, bf16[288,1536]{1,0:T(8,128)(2,1)S(1)}, u32[]{:S(2)}, u32[]{:S(2)}) collective-permute-start(bf16[288,1536]{1,0:T(8,128)(2,1)S(1)} %get-tuple-element.91.refs_0_.refs_2_), channel_id=1, source_target_pairs={{0,1},{1,0},{2,3},{3,2},{4,5},{5,4},{6,7},{7,6},{8,9},{9,8},{10,11... | collective-permute-start | bytes 2654216 | tf_op jit(solution)/shard_map/ppermute | solution.py:490
  99.2 20.6 %collective-permute-start.27 = (bf16[128,2688]{1,0:T(8,128)(2,1)S(1)}, bf16[128,2688]{1,0:T(8,128)(2,1)S(1)}, u32[]{:S(2)}, u32[]{:S(2)}) collective-permute-start(bf16[128,2688]{1,0:T(8,128)(2,1)S(1)} %expand.4.refs_9_), channel_id=1, source_target_pairs={{0,8},{2,10},{4,12},{6,14},{8,16},{10,18},{12,20},{14,22},{16,24},... | collective-permute-start | bytes 2064392 | tf_op jit(solution)/shard_map/ppermute | solution.py:381
  108.2 18.3 %collective-permute-start.25 = (bf16[72,2688]{1,0:T(8,128)(2,1)S(1)}, bf16[72,2688]{1,0:T(8,128)(2,1)S(1)}, u32[]{:S(2)}, u32[]{:S(2)}) collective-permute-start(bf16[72,2688]{1,0:T(8,128)(2,1)S(1)} %get-tuple-element.105), channel_id=1, source_target_pairs={{0,4},{2,6},{4,0},{6,2},{8,12},{10,14},{12,8},{14,10},{16,20},{18,... | collective-permute-start | bytes 1161224 | tf_op jit(solution)/shard_map/ppermute | solution.py:385
  110.2 23.5 %collective-permute-start.29 = (bf16[288,1536]{1,0:T(8,128)(2,1)S(1)}, bf16[288,1536]{1,0:T(8,128)(2,1)S(1)}, u32[]{:S(2)}, u32[]{:S(2)}) collective-permute-start(bf16[288,1536]{1,0:T(8,128)(2,1)S(1)} %get-tuple-element.108.refs_0_.refs_2_), channel_id=1, source_target_pairs={{0,1},{1,0},{2,3},{3,2},{4,5},{5,4},{6,7},{7,6},{8,9},{9,8},{10,11... | collective-permute-start | bytes 2654216 | tf_op jit(solution)/shard_map/ppermute | solution.py:490
  127.2 23.4 %collective-permute-start.28 = (bf16[128,2688]{1,0:T(8,128)(2,1)S(1)}, bf16[128,2688]{1,0:T(8,128)(2,1)S(1)}, u32[]{:S(2)}, u32[]{:S(2)}) collective-permute-start(bf16[128,2688]{1,0:T(8,128)(2,1)S(1)} %expand.5.refs_9_), channel_id=1, source_target_pairs={{0,8},{2,10},{4,12},{6,14},{8,16},{10,18},{12,20},{14,22},{16,24},... | collective-permute-start | bytes 2064392 | tf_op jit(solution)/shard_map/ppermute | solution.py:381
  130.8 18.3 %collective-permute-start.22 = (bf16[72,2688]{1,0:T(8,128)(2,1)S(1)}, bf16[72,2688]{1,0:T(8,128)(2,1)S(1)}, u32[]{:S(2)}, u32[]{:S(2)}) collective-permute-start(bf16[72,2688]{1,0:T(8,128)(2,1)S(1)} %get-tuple-element.101), channel_id=1, source_target_pairs={{0,4},{2,6},{4,0},{6,2},{8,12},{10,14},{12,8},{14,10},{16,20},{18,... | collective-permute-start | bytes 1161224 | tf_op jit(solution)/shard_map/ppermute | solution.py:385
  132.2 18.4 %collective-permute-start.23 = (bf16[72,2688]{1,0:T(8,128)(2,1)S(1)}, bf16[72,2688]{1,0:T(8,128)(2,1)S(1)}, u32[]{:S(2)}, u32[]{:S(2)}) collective-permute-start(bf16[72,2688]{1,0:T(8,128)(2,1)S(1)} %get-tuple-element.102), channel_id=1, source_target_pairs={{0,6},{2,4},{4,2},{6,0},{8,14},{10,12},{12,10},{14,8},{16,22},{18,... | collective-permute-start | bytes 1161224 | tf_op jit(solution)/shard_map/ppermute | solution.py:385
  138.7 22.9 %collective-permute-start.31 = (bf16[72,2688]{1,0:T(8,128)(2,1)S(1)}, bf16[72,2688]{1,0:T(8,128)(2,1)S(1)}, u32[]{:S(2)}, u32[]{:S(2)}) collective-permute-start(bf16[72,2688]{1,0:T(8,128)(2,1)S(1)} %get-tuple-element.111), channel_id=1, source_target_pairs={{0,2},{2,0},{4,6},{6,4},{8,10},{10,8},{12,14},{14,12},{16,18},{18,... | collective-permute-start | bytes 1161224 | tf_op jit(solution)/shard_map/ppermute | solution.py:385
  142.1 22.2 %collective-permute-start.32 = (bf16[72,2688]{1,0:T(8,128)(2,1)S(1)}, bf16[72,2688]{1,0:T(8,128)(2,1)S(1)}, u32[]{:S(2)}, u32[]{:S(2)}) collective-permute-start(bf16[72,2688]{1,0:T(8,128)(2,1)S(1)} %get-tuple-element.112), channel_id=1, source_target_pairs={{0,4},{2,6},{4,0},{6,2},{8,12},{10,14},{12,8},{14,10},{16,20},{18,... | collective-permute-start | bytes 1161224 | tf_op jit(solution)/shard_map/ppermute | solution.py:385
  (15 other events, 255.2 us)

commit v4 on v3

v4 whole, which is shorter than its diff:
```python
import functools

import jax
import jax.numpy as jnp
from jax import lax
from jax.experimental import pallas as pl
from jax.experimental.pallas import tpu as pltpu
from jax.sharding import PartitionSpec as P

INNER = 4
CHUNKS = 4
PLAN = ((0, None), (1, None), (2, None), (3, None), (None, 1), (None, 2), (None, 3), (None, 0))
ORDER = ('x1', 'h0', 'x2', 'h1', 'x3', 'h2', 'r0', 'x4', 'h3', 'x5', 'r3', 'e1', 'x6', 'e2', 'r2', 'x7', 'e3', 'u', 'e0')
PASSED = ()
FIRST = 1
COSTS = {'x': 5000, 'b': 20000, 'h': 5000, 'e': 1, 'u': 20000}
TAIL = 128
LIMIT = 20 * 1024 * 1024
WIDE = 56 * 1024 * 1024
F32, BF16, I32 = jnp.float32, jnp.bfloat16, jnp.int32


def params(limit=LIMIT):
    return pltpu.CompilerParams(vmem_limit_bytes=limit)


def cost(flops, moved):
    return pl.CostEstimate(flops=int(flops), bytes_accessed=int(moved), transcendentals=0)


def whole_specs(n):
    return [pl.BlockSpec(memory_space=pltpu.VMEM)] * n


def hot_of(plan, device):
    return plan[2 * device + 1]


def rows_joined(pieces):
    if all(piece.shape[0] % 16 == 0 for piece in pieces):
        return jnp.concatenate(pieces, 0)
    return jnp.concatenate([piece.astype(F32) for piece in pieces], 0).astype(BF16)


def row_plan(m, hot_rows, cold_rows, plan, shape, axis):
    rows = m * (hot_rows + cold_rows)
    me = lax.axis_index("ep")
    outer, inner = me // INNER, me % INNER
    spot = lax.broadcasted_iota(I32, shape, axis)
    which = jnp.zeros(shape, I32)
    for d in range(1, INNER):
        which += (spot >= d * rows).astype(I32)
    within = spot - which * rows
    is_hot = within < m * hot_rows
    group = jnp.zeros(shape, I32)
    for s in range(1, m):
        edge = jnp.where(is_hot, s * hot_rows, m * hot_rows + s * cold_rows)
        group += (within >= edge).astype(I32)
    slot = jnp.where(is_hot, within - group * hot_rows, within - m * hot_rows - group * cold_rows)
    expert = jnp.zeros(shape, I32)
    for d in range(INNER):
        device = outer * INNER + (inner ^ d)
        hot = hot_of(plan, device)
        ids = jnp.where(is_hot, 2 * device + hot, 2 * device + 1 - hot)
        expert = jnp.where(which == d, ids, expert)
    return expert.astype(F32), slot.astype(F32), group


def pick_rows(m, hot_rows, cold_rows, topk, plan, tails):
    count = tails[0].shape[0]
    cols = INNER * m * (hot_rows + cold_rows)
    expert, slot, group = (
        value[0:1] for value in row_plan(m, hot_rows, cold_rows, plan, (8, cols), 1)
    )
    before = lax.broadcasted_iota(I32, (count, count), 1) < lax.broadcasted_iota(I32, (count, count), 0)
    before = jnp.where(before, 1.0, 0.0).astype(BF16)
    found = []
    for s, ids in enumerate(tails):
        match = ids[:, 0:1] == expert
        for k in range(1, topk):
            match = match | (ids[:, k : k + 1] == expert)
        ones = jnp.where(match, 1.0, 0.0)
        rank = jnp.dot(before, ones.astype(BF16), preferred_element_type=F32)
        found.append(jnp.where((rank == slot) & (group == s), ones, 0.0).astype(BF16))
    return found


def picked(picks, payloads, columns):
    total = None
    for pick, payload in zip(picks, payloads):
        part = lax.dot_general(
            pick[...], payload[:, columns], (((0,), (0,)), ((), ())), preferred_element_type=F32
        )
        total = part if total is None else total + part
    return total


def select_all(m, hot_rows, cold_rows, topk, share, plan, picks, payloads, outs, marks):
    rows, width = outs[0].shape
    feat = width - share
    expert, _, _ = row_plan(m, hot_rows, cold_rows, plan, (INNER * rows, TAIL), 0)
    tail = picked(picks, payloads, slice(width, width + TAIL))
    gate = (tail[:, 2 * topk : 3 * topk] + tail[:, 3 * topk : 4 * topk]) + tail[:, 4 * topk : 5 * topk]
    gate = jnp.sum(jnp.where(tail[:, :topk] == expert[:, :topk], gate, 0.0), 1, keepdims=True)
    lane = lax.broadcasted_iota(I32, tail.shape, 1)
    own = jnp.where((tail == expert) & (lane < 2 * topk), 1.0, 0.0)
    marks[...] = jnp.where(lane == 2 * topk, gate, own)
    step = 512 if feat % 512 == 0 else 128
    for at in [*range(0, feat, step), feat]:
        columns = slice(at, at + step) if at < feat else slice(feat, width)
        total = picked(picks, payloads, columns)
        if at == feat:
            total = gate * total
        for d in range(INNER):
            outs[d][:, columns] = total[d * rows : (d + 1) * rows].astype(BF16)


def start_kernel(m, hot_rows, cold_rows, plan, tokens, routes, gates, grad_out, *refs):
    out, refs = refs[0], refs[1:]
    here_routes, here_gates, sems = refs[-3:]
    outs, marks, picks = refs[:INNER], refs[INNER:-3][:1], refs[INNER:-3][1:]
    count, feat = tokens.shape
    share = grad_out.shape[1]
    topk = routes.shape[0]
    copies = [
        pltpu.make_async_copy(source, target, sems.at[n])
        for n, (source, target) in enumerate(
            (
                (routes, here_routes),
                (gates, here_gates),
                (tokens, out.at[:, :feat]),
                (grad_out, out.at[:, feat : feat + share]),
            )
        )
    ]
    for copy in copies:
        copy.start()
    for copy in copies[:2]:
        copy.wait()
    ids = here_routes[...].astype(F32)
    gate = here_gates[...]
    high = gate.astype(BF16).astype(F32)
    middle = (gate - high).astype(BF16).astype(F32)
    low = (gate - high - middle).astype(BF16).astype(F32)
    rest = jnp.zeros((TAIL - 5 * topk, count), F32)
    tail = jnp.concatenate([ids, ids, high, middle, low, rest], 0).T
    out[:, feat + share :] = tail.astype(BF16)
    if picks:
        picks[0][...] = pick_rows(m, hot_rows, cold_rows, topk, plan, [tail])[0]
    for copy in copies[2:]:
        copy.wait()
    if picks:
        select_all(m, hot_rows, cold_rows, topk, share, plan, picks, [out], outs, marks[0])


def select_kernel(m, hot_rows, cold_rows, topk, share, waits, plan, *refs):
    payloads, refs = refs[:m], refs[m + waits :]
    outs, marks, picks, passed = refs[:INNER], refs[INNER], refs[INNER + 1 : INNER + 1 + m], refs[INNER + 1 + m :]
    width = payloads[0].shape[1]
    for source, target in zip(payloads, passed):
        target[...] = source[...]
    tails = [payload[:, width - TAIL :].astype(F32) for payload in payloads]
    for pick, found in zip(picks, pick_rows(m, hot_rows, cold_rows, topk, plan, tails)):
        pick[...] = found
    select_all(m, hot_rows, cold_rows, topk, share, plan, picks, payloads, outs, marks)


def hidden_kernel(m, hot_rows, cold_rows, feat, streamed, waits, plan, *refs):
    blocks = refs[:INNER]
    weight, part, x_hot, x_cold = refs[INNER], *refs[INNER + 1 + waits :]
    hots = INNER * m * hot_rows
    share = blocks[0].shape[1] - feat
    ff = part.shape[1] - share
    tile = 256 if ff % 256 == 0 else ff
    hot = hot_of(plan, lax.axis_index("ep"))
    split = m * hot_rows

    def gather():
        x_hot[...] = rows_joined([b[:split, :feat] for b in blocks])
        x_cold[...] = rows_joined([b[split:, :feat] for b in blocks])
        part[:hots, ff:] = rows_joined([b[:split, feat:] for b in blocks])
        part[hots:, ff:] = rows_joined([b[split:, feat:] for b in blocks])

    def columns(j, source):
        at = pl.ds(pl.multiple_of(j * tile, tile), tile)
        part[:hots, at] = jnp.dot(
            x_hot[...], weight[hot, :, source], preferred_element_type=F32
        ).astype(BF16)
        part[hots:, at] = jnp.dot(
            x_cold[...], weight[1 - hot, :, source], preferred_element_type=F32
        ).astype(BF16)

    if streamed:
        pl.when(pl.program_id(0) == 0)(gather)
        columns(pl.program_id(0), slice(None))
    else:
        gather()

        @pl.loop(0, ff // tile)
        def _(j):
            columns(j, pl.ds(pl.multiple_of(j * tile, tile), tile))


def back_kernel(m, hot_rows, cold_rows, n_parts, n_grads, share, waits, plan, *refs):
    sums, grads = refs[:n_parts], refs[n_parts : n_parts + n_grads]
    weight, refs = refs[n_parts + n_grads], refs[n_parts + n_grads + 1 + waits :]
    outs, g_hot, g_cold = refs[:INNER], refs[INNER], refs[INNER + 1]
    hots, colds = m * hot_rows, m * cold_rows
    ff = weight.shape[2]
    width = outs[0].shape[1]
    feat = width - share - TAIL
    tile = 512 if feat % 512 == 0 else feat
    tp = lax.axis_index("tp")
    hot = hot_of(plan, lax.axis_index("ep"))

    def put(columns, back_hot, back_cold):
        for d in range(INNER):
            outs[d][:hots, columns] = back_hot[d * hots : (d + 1) * hots].astype(BF16)
            outs[d][hots:, columns] = back_cold[d * colds : (d + 1) * colds].astype(BF16)

    ends = []
    for first, piece, target in ((0, hots, g_hot), (INNER * hots, colds, g_cold)):
        made = []
        per = 1 if piece % 16 == 0 else INNER
        for d in range(0, INNER, per):
            count = piece * per
            now = slice(first + d * piece, first + d * piece + count)
            hidden = sums[0][now, :ff].astype(F32)
            for more in sums[1:]:
                hidden = hidden + more[now, :ff].astype(F32)
            if n_grads == 1:
                row_grad = grads[0][now].astype(F32)
            else:
                mine, other = (g[now, ff:].astype(F32) for g in grads)
                even = tp == 0
                row_grad = jnp.concatenate(
                    [jnp.where(even, mine, other), jnp.where(even, other, mine)], 1
                )
            sig = 1.0 / (1.0 + jnp.exp(-hidden))
            act = (hidden * sig).astype(BF16).astype(F32)
            hidden_grad = row_grad * (sig * (1.0 + hidden * (1.0 - sig)))
            target[d * piece : d * piece + count] = hidden_grad.astype(BF16)
            gate_grad = jnp.sum(act * row_grad, 1, keepdims=True)
            high = gate_grad.astype(BF16).astype(F32)
            low = gate_grad - high
            lane = lax.broadcasted_iota(I32, (count, TAIL), 1)
            end = jnp.where(lane == 0, high, jnp.where(lane == 1, low, 0.0))
            half = None
            for n in range(ff // share):
                piece_act = jnp.where(tp == n, act[:, n * share : (n + 1) * share], 0.0)
                half = piece_act if half is None else half + piece_act
            made.append(jnp.concatenate([half, end], 1))
        ends.append(jnp.concatenate(made, 0))
    put(slice(feat, width), *ends)

    across_rows = (((1,), (1,)), ((), ()))

    def features(j, carry):
        at = pl.ds(pl.multiple_of(j * tile, tile), tile)
        put(
            at,
            lax.dot_general(
                g_hot[...], weight[hot, at, :], across_rows, preferred_element_type=F32
            ),
            lax.dot_general(
                g_cold[...], weight[1 - hot, at, :], across_rows, preferred_element_type=F32
            ),
        )
        return carry

    lax.fori_loop(0, feat // tile, features, 0)


def expand_kernel(m, topk, share, n_more, waits, *refs):
    blocks, picks, marks, refs = refs[:INNER], refs[INNER : INNER + m], refs[INNER + m], refs[INNER + m + 1 :]
    more, outs = refs[:n_more], refs[n_more + waits :]
    width = blocks[0].shape[1]
    feat = width - share - TAIL

    def add(columns, rows):
        for s in range(m):
            total = jnp.dot(picks[s][...], rows, preferred_element_type=F32)
            if more:
                total = total + more[s][:, columns].astype(F32)
            outs[s][:, columns] = total.astype(BF16)

    def joined(columns):
        return rows_joined([b[:, columns] for b in blocks])

    step = 512 if feat % 512 == 0 else 128
    for at in range(0, feat, step):
        add(slice(at, at + step), joined(slice(at, at + step)))
    mark = marks[...]
    gate = mark[:, 2 * topk : 2 * topk + 1]
    columns = slice(feat, feat + share)
    add(columns, (gate * joined(columns).astype(F32)).astype(BF16))
    columns = slice(feat + share, width)
    end = joined(columns).astype(F32)
    gate_grad = (end[:, 0:1] + end[:, 1:2]) / jnp.where(gate > 0.0, gate, 1.0)
    high = gate_grad.astype(BF16).astype(F32)
    lane = lax.broadcasted_iota(I32, end.shape, 1)
    values = jnp.where(lane < topk, high, gate_grad - high)
    add(columns, jnp.where((lane < 2 * topk) & (mark > 0.0), values, 0.0).astype(BF16))


def final_kernel(n, topk, *refs):
    parts = refs[:n]
    mixed, grad_tokens, grad_gates = refs[n:]
    feat, share = grad_tokens.shape[1], mixed.shape[1]

    def total(columns):
        out = parts[0][:, columns].astype(F32)
        for part in parts[1:]:
            out = out + part[:, columns].astype(F32)
        return out

    grad_tokens[...] = total(slice(0, feat)).astype(BF16)
    mixed[...] = total(slice(feat, feat + share)).astype(BF16)
    tail = total(slice(feat + share, feat + share + TAIL))
    tail = tail.T
    grad_gates[...] = tail[:topk] + tail[topk : 2 * topk]


def up_kernel(n, waits, plan, *refs):
    x_hot, x_cold = refs[:n], refs[n : 2 * n]
    g_hot, g_cold = refs[2 * n : 3 * n], refs[3 * n : 4 * n]
    out, token, all_hot, all_cold = refs[4 * n + waits :]
    tile = out.shape[1]
    e, j = pl.program_id(0), pl.program_id(1)
    hot = hot_of(plan, lax.axis_index("ep"))
    at = pl.ds(pl.multiple_of(j * tile, tile), tile)

    @pl.when((e == 0) & (j == 0))
    def _():
        token[...] = jnp.zeros_like(token)
        all_hot[...] = jnp.concatenate([g[...] for g in g_hot], 0)
        all_cold[...] = jnp.concatenate([g[...] for g in g_cold], 0)

    def total(xs, grads):
        rows = jnp.concatenate([x[:, at] for x in xs], 0)
        out[0] = lax.dot_general(
            rows, grads[...], (((0,), (0,)), ((), ())), preferred_element_type=F32
        ).astype(BF16)

    pl.when(e == hot)(lambda: total(x_hot, all_hot))
    pl.when(e != hot)(lambda: total(x_cold, all_cold))


def on_device(tokens, routes, gates, up_weight, replica_on, grad_out):
    count, feat = tokens.shape
    topk = routes.shape[1]
    experts = replica_on.shape[0]
    share = grad_out.shape[1]
    ff = up_weight.shape[2]
    n_ep, n_tp = lax.axis_size("ep"), lax.axis_size("tp")
    outer = n_ep // INNER
    capacity = 3 * count * topk // (4 * experts)
    hot_rows, cold_rows = 2 * capacity, capacity
    width = feat + share + TAIL
    there = feat + share
    smem = pl.BlockSpec(memory_space=pltpu.SMEM)

    def along(value, shift):
        pairs = [
            (o * INNER + i, ((o + shift) % outer) * INNER + i)
            for o in range(outer)
            for i in range(INNER)
        ]
        return lax.ppermute(value, "ep", pairs)

    def across(value, d):
        pairs = [(o * INNER + i, o * INNER + (i ^ d)) for o in range(outer) for i in range(INNER)]
        return lax.ppermute(value, "ep", pairs)

    rest_spec = pl.BlockSpec(memory_space=pl.ANY)
    m = max(1, outer // CHUNKS)
    chunks = [list(range(first, first + m)) for first in range(0, outer, m)]
    n = len(chunks)
    rows = m * (hot_rows + cold_rows)
    hots, colds = INNER * m * hot_rows, INNER * m * cold_rows
    sizes = (m, hot_rows, cold_rows)

    def block(shape, dtype=BF16):
        return jax.ShapeDtypeStruct(shape, dtype)

    def fixed(shape):
        return pl.BlockSpec(shape, lambda j: (0,) * len(shape))

    going = {f: k for k, (f, _) in enumerate(PLAN) if f is not None}
    coming = {r: k for k, (_, r) in enumerate(PLAN) if r is not None}

    def weigh(kind):
        return cost(COSTS[kind] * 10**6, COSTS[kind] * 10**4)

    arrived, picks, marks, blocks, sums, grads, partials = {}, {}, {}, {}, {}, {}, {}
    x_hots, x_colds, g_hots, g_colds = {}, {}, {}, {}

    def exchange(k, made):
        blocks[k] = [made[0]] + [across(made[d], d) for d in range(1, INNER)]

    own_rows = m == 1
    made = pl.pallas_call(
        functools.partial(start_kernel, *sizes),
        out_shape=[block((count, width))]
        + (
            [block((rows, there))] * INNER
            + [block((INNER * rows, TAIL), F32), block((count, INNER * rows))]
            if own_rows
            else []
        ),
        in_specs=[smem] + [rest_spec] * 4,
        out_specs=whole_specs(1 + (INNER + 2 if own_rows else 0)),
        scratch_shapes=[
            pltpu.VMEM((topk, count), I32),
            pltpu.VMEM((topk, count), F32),
            pltpu.SemaphoreType.DMA((4,)),
        ],
        compiler_params=params(WIDE),
        cost_estimate=weigh("x"),
        name="start",
    )(replica_on, tokens, routes.T, gates.T, grad_out)
    payload = made[0]
    last = []
    for c in range(n):
        for s in chunks[c] if c not in PASSED else ():
            if s == 0:
                arrived[s] = payload
            else:
                arrived[s] = along(arrived[s - m], m) if c else along(payload, s)

    def select(k):
        c = PLAN[k][0]
        more = m if c + 1 in PASSED else 0
        made = pl.pallas_call(
            functools.partial(select_kernel, *sizes, topk, share, len(last)),
            out_shape=[block((rows, there))] * INNER
            + [block((INNER * rows, TAIL), F32)]
            + [block((count, INNER * rows))] * m
            + [block((count, width))] * more,
            in_specs=[smem] + whole_specs(m) + [rest_spec] * len(last),
            out_specs=whole_specs(INNER + 1 + m + more),
            compiler_params=params(),
            cost_estimate=weigh("x"),
            name="select",
        )(replica_on, *[arrived[s] for s in chunks[c]], *last)
        marks[c], picks[c] = made[INNER], made[INNER + 1 : INNER + 1 + m]
        exchange(k, made)
        if more:
            for s, value in zip(chunks[c + 1], made[INNER + 1 + m :]):
                arrived[s] = along(value, m)
        last[:] = [picks[c][0]]

    def hidden(c):
        k = going[c]
        tile = 256 if ff % 256 == 0 else ff
        shapes = [(INNER * rows, ff + share), (hots, feat), (colds, feat)]
        streamed = c == 0 and FIRST > 0
        if streamed:
            where = dict(
                grid=(ff // tile,),
                in_specs=[smem]
                + [fixed(b.shape) for b in blocks[k]]
                + [pl.BlockSpec((2, feat, tile), lambda j: (0, 0, j))]
                + [rest_spec] * len(last),
                out_specs=[fixed(shape) for shape in shapes],
            )
        else:
            where = dict(
                in_specs=[smem] + whole_specs(INNER + 1) + [rest_spec] * len(last),
                out_specs=whole_specs(3),
            )
        part, x_hots[c], x_colds[c] = pl.pallas_call(
            functools.partial(hidden_kernel, *sizes, feat, streamed, len(last)),
            out_shape=[block(shape) for shape in shapes],
            **where,
            compiler_params=params(WIDE if c == 0 and FIRST == 2 else LIMIT),
            cost_estimate=weigh("h"),
            name="hidden",
        )(replica_on, *blocks[k], up_weight, *last)
        last[:] = [x_colds[c]]
        if n_tp == 2:
            sums[c] = [part, lax.ppermute(part, "tp", [(0, 1), (1, 0)])]
            grads[c] = sums[c]
        else:
            sums[c] = [lax.psum(part[:, :ff].astype(F32), "tp")]
            grads[c] = [lax.all_gather(part[:, ff:], "tp", axis=1, tiled=True)]

    def step(k):
        f, c = PLAN[k]
        if c is None:
            return select(k)
        made = pl.pallas_call(
            functools.partial(
                back_kernel, *sizes, len(sums[c]), len(grads[c]), share, len(last)
            ),
            out_shape=[block((rows, width))] * INNER + [block((hots, ff)), block((colds, ff))],
            in_specs=[smem]
            + whole_specs(len(sums[c]) + len(grads[c]) + 1)
            + [rest_spec] * len(last),
            out_specs=whole_specs(INNER + 2),
            compiler_params=params(),
            cost_estimate=weigh("b"),
            name="back",
        )(replica_on, *sums[c], *grads[c], up_weight, *last)
        g_hots[c], g_colds[c] = made[INNER : INNER + 2]
        exchange(k, made)
        last[:] = [g_colds[c]]

    def expand(c):
        more = [along(partials[s - m], m) for s in chunks[c]] if c > 1 else []
        k = coming[c]
        made = pl.pallas_call(
            functools.partial(expand_kernel, m, topk, share, len(more), len(last)),
            out_shape=[block((count, width))] * m,
            in_specs=whole_specs(INNER + m + 1 + len(more)) + [rest_spec] * len(last),
            out_specs=whole_specs(m),
            compiler_params=params(),
            cost_estimate=weigh("e"),
            name="expand",
        )(*blocks[k], *picks[c], marks[c], *more, *last)
        for s, value in zip(chunks[c], made):
            partials[s] = value
        last[:] = [made[0]]

    def weight_grad():
        tile = 512 if feat % 512 == 0 else feat
        grad_up, token = pl.pallas_call(
            functools.partial(up_kernel, n, len(last)),
            out_shape=[block(up_weight.shape), block((8, 128), F32)],
            grid=(up_weight.shape[0], feat // tile),
            in_specs=[smem] + whole_specs(4 * n) + [rest_spec] * len(last),
            out_specs=[
                pl.BlockSpec((1, tile, ff), lambda e, j: (e, j, 0)),
                pl.BlockSpec((8, 128), lambda e, j: (0, 0)),
            ],
            scratch_shapes=[
                pltpu.VMEM((n * hots, ff), BF16),
                pltpu.VMEM((n * colds, ff), BF16),
            ],
            compiler_params=params(),
            cost_estimate=weigh("u"),
            name="grad_up",
        )(
            replica_on,
            *[x_hots[c] for c in range(n)],
            *[x_colds[c] for c in range(n)],
            *[g_hots[c] for c in range(n)],
            *[g_colds[c] for c in range(n)],
            *last,
        )
        last[:] = [token]
        return grad_up

    if own_rows:
        marks[0], picks[0] = made[INNER + 1], made[INNER + 2 :]
        exchange(0, made[1 : INNER + 1])
    else:
        select(0)
    grad_up = None
    for word in ORDER:
        number = int(word[1:] or 0)
        if word[0] == "u":
            grad_up = weight_grad()
        elif word[0] == "r":
            last.append(sums[number][-1])
        else:
            {"x": step, "h": hidden, "e": expand}[word[0]](number)

    sums_back = [along(partials[s], m) for s in chunks[n - 1]]
    parts = [sums_back[0], partials[0]]
    for s in chunks[0][1:]:
        parts.append(along(sums_back[s] + partials[s], outer - s))
    mixed, grad_tokens, grad_gates = pl.pallas_call(
        functools.partial(final_kernel, len(parts), topk),
        out_shape=[block((count, share)), block((count, feat)), block((topk, count), F32)],
        in_specs=whole_specs(len(parts)),
        out_specs=whole_specs(3),
        compiler_params=params(),
        cost_estimate=weigh("e"),
        name="final",
    )(*parts)
    return mixed, grad_tokens, grad_gates.T, grad_up


def solution(mesh):
    return jax.shard_map(
        on_device,
        mesh=mesh,
        in_specs=(
            P("ep", "tp"),
            P("ep", None),
            P("ep", None),
            P("ep", "tp", None),
            P(),
            P("ep", "tp"),
        ),
        out_specs=(P("ep", "tp"), P("ep", "tp"), P("ep", None), P("ep", "tp", None)),
        check_vma=False,
    )
```

time: 166 us -> 155 us (0.934)
  waiting for transfers between devices: 76 us -> 67.7 us
  starting transfers between devices: 36.6 us -> 33.2 us
    ppermute x6, starting transfers between devices: 9.61 us -> 3.48 us  [along(): return lax.ppermute(value, 'ep', pairs)]
    ppermute x24, waiting for transfers between devices: 37.4 us -> 31.4 us  [across(): return lax.ppermute(value, 'ep', pairs)]
    ppermute x24, starting transfers between devices: 26.8 us -> 29.5 us  [across(): return lax.ppermute(value, 'ep', pairs)]
    ppermute x6, waiting for transfers between devices: 38.6 us -> 36.3 us  [along(): return lax.ppermute(value, 'ep', pairs)]
  transfers between devices with their start and end apart: 34 -> 34, of which waited for: 13 -> 10; matrix products, arithmetic and copies ran while one was open for 0% -> 0% of each run, Pallas kernels for 29% -> 31%
where the time goes in v4:
time: 155 us; the launch traced here: 154 us
  waiting for transfers between devices  67.7 us (44%)
  Pallas kernels  52.7 us (34%)
  starting transfers between devices  33.2 us (21%)
    ppermute x6, waiting for transfers between devices, along(): return lax.ppermute(value, 'ep', pairs)  36.3 us
    ppermute x24, waiting for transfers between devices, across(): return lax.ppermute(value, 'ep', pairs)  31.4 us
    ppermute x24, starting transfers between devices, across(): return lax.ppermute(value, 'ep', pairs)  29.5 us
    pallas_call x4, Pallas kernels, step(): pl.pallas_call(functools.partial(back_kernel, *sizes, len(sums[c]), len(g...  19.1 us
    pallas_call x4, Pallas kernels, hidden(): pl.pallas_call(functools.partial(hidden_kernel, *sizes, feat, streamed, l...  12.3 us
    pallas_call x1, Pallas kernels, weight_grad(): pl.pallas_call(functools.partial(up_kernel, n, len(last)), out_shape=[blo...  9.47 us
    pallas_call x3, Pallas kernels, select(): pl.pallas_call(functools.partial(select_kernel, *sizes, topk, share, len(...  4.68 us
    pallas_call x1, Pallas kernels, on_device(): pl.pallas_call(functools.partial(start_kernel, *sizes), out_shape=[block(...  3.78 us
  transfers between devices with their start and end apart: 34, of which 10 were waited for; matrix products, arithmetic and copies ran while one was open for 0% of the time, Pallas kernels for 31%

profile of v4, /device:TPU:0, one launch (start us, length us, event | category | flops | bytes accessed | tf_op | source)
XLA Modules:
  0.0 154.5 jit_solution(3172676752821463956)
XLA Ops:
  0.6 3.8 %start.1 = (bf16[128,2688]{1,0:T(8,128)(2,1)}, bf16[72,2560]{1,0:T(8,128)(2,1)}, bf16[72,2560]{1,0:T(8,128)(2,1)}, bf16[72,2560]{1,0:T(8,128)(2,1)}, bf16[72,256...) custom-call(s32[32]{0:T(128)} %plan.25, bf16[128,2048]{1,0:T(8,128)(2,1)} %tokens.1, ...), custom_call_target="tpu_custom_call" | custom-call | flops 5000000000 | bytes 50000000 | tf_op jit(solution)/shard_map/start/pallas_call | solution.py:402
  4.4 3.1 %collective-permute-start = (bf16[128,2688]{1,0:T(8,128)(2,1)}, bf16[128,2688]{1,0:T(8,128)(2,1)S(1)}, u32[]{:S(2)}, u32[]{:S(2)}) collective-permute-start(bf16[128,2688]{1,0:T(8,128)(2,1)} %get-tuple-element.70), channel_id=1, source_target_pairs={{0,8},{2,10},{4,12},{6,14},{8,16},{10,18},{12,20},{14,22},{16,24},... | collective-permute-start | bytes 2064392 | tf_op jit(solution)/shard_map/ppermute | solution.py:369
  11.0 14.2 %collective-permute-done.refs_0_ = bf16[128,2688]{1,0:T(8,128)(2,1)S(1)} collective-permute-done((bf16[128,2688]{1,0:T(8,128)(2,1)}, bf16[128,2688]{1,0:T(8,128)(2,1)S(1)}, u32[]{:S(2)}, u32[]{:S(2)}) %collective-permute-start) | collective-permute-done | bytes 688160 | tf_op jit(solution)/shard_map/ppermute | solution.py:369
  30.3 3.8 %hidden.4 = (bf16[288,1536]{1,0:T(8,128)(2,1)S(1)}, bf16[192,2048]{1,0:T(8,128)(2,1)S(1)}, bf16[96,2048]{1,0:T(8,128)(2,1)S(1)}) custom-call(s32[32]{0:T(128)S(1)} %copy-done.2, bf16[72,2560]{1,0:T(8,128)(2,1)S(1)} %copy-done.3, bf16[72,2560]{1,0:T(8,128)(2,1)S(1)} %collective-permute-done.6.refs_1_, bf16[72,2560]{1,0:T(8,128)(2,1)S(1)} %collective-permute-done.7.refs_2_, ...), custom_call_target="tpu_custom_call" | custom-call | flops 5000000000 | bytes 50000000 | tf_op jit(solution)/shard_map/hidden/pallas_call | solution.py:472
  34.2 9.4 %collective-permute-done.1.refs_0_ = bf16[128,2688]{1,0:T(8,128)(2,1)S(1)} collective-permute-done((bf16[128,2688]{1,0:T(8,128)(2,1)S(1)}, bf16[128,2688]{1,0:T(8,128)(2,1)S(1)}, u32[]{:S(2)}, u32[]{:S(2)}) %collective-permute-start.1) | collective-permute-done | bytes 688160 | tf_op jit(solution)/shard_map/ppermute | solution.py:369
  43.6 1.6 %select.4 = (bf16[72,2560]{1,0:T(8,128)(2,1)S(1)}, bf16[72,2560]{1,0:T(8,128)(2,1)S(1)}, bf16[72,2560]{1,0:T(8,128)(2,1)S(1)}, bf16[72,2560]{1,0:T(8,128)(2,1)S(...) custom-call(s32[32]{0:T(128)S(1)} %copy-done.2, bf16[128,2688]{1,0:T(8,128)(2,1)S(1)} %collective-permute-done.1.refs_0_, ...), custom_call_target="tpu_custom_call" | custom-call | flops 5000000000 | bytes 50000000 | tf_op jit(solution)/shard_map/select/pallas_call | solution.py:434
  48.7 2.8 %hidden.5 = (bf16[288,1536]{1,0:T(8,128)(2,1)S(1)}, bf16[192,2048]{1,0:T(8,128)(2,1)S(1)}, bf16[96,2048]{1,0:T(8,128)(2,1)S(1)}) custom-call(s32[32]{0:T(128)S(1)} %copy-done.2, bf16[72,2560]{1,0:T(8,128)(2,1)S(1)} %get-tuple-element.71.refs_0_, bf16[72,2560]{1,0:T(8,128)(2,1)S(1)} %collective-permute-done.3.refs_1_, ...), custom_call_target="tpu_custom_call" | custom-call | flops 5000000000 | bytes 50000000 | tf_op jit(solution)/shard_map/hidden/pallas_call | solution.py:472
  51.6 9.5 %collective-permute-done.2.refs_0_ = bf16[128,2688]{1,0:T(8,128)(2,1)S(1)} collective-permute-done((bf16[128,2688]{1,0:T(8,128)(2,1)S(1)}, bf16[128,2688]{1,0:T(8,128)(2,1)S(1)}, u32[]{:S(2)}, u32[]{:S(2)}) %collective-permute-start.2) | collective-permute-done | bytes 688160 | tf_op jit(solution)/shard_map/ppermute | solution.py:369
  66.2 2.8 %hidden.6 = (bf16[288,1536]{1,0:T(8,128)(2,1)S(1)}, bf16[192,2048]{1,0:T(8,128)(2,1)S(1)}, bf16[96,2048]{1,0:T(8,128)(2,1)S(1)}) custom-call(s32[32]{0:T(128)S(1)} %copy-done.2, bf16[72,2560]{1,0:T(8,128)(2,1)S(1)} %get-tuple-element.88.refs_0_, bf16[72,2560]{1,0:T(8,128)(2,1)S(1)} %collective-permute-done.13.refs_1_, ...), custom_call_target="tpu_custom_call" | custom-call | flops 5000000000 | bytes 50000000 | tf_op jit(solution)/shard_map/hidden/pallas_call | solution.py:472
  69.2 4.8 %back.4 = (bf16[72,2688]{1,0:T(8,128)(2,1)S(1)}, bf16[72,2688]{1,0:T(8,128)(2,1)S(1)}, bf16[72,2688]{1,0:T(8,128)(2,1)S(1)}, bf16[72,2688]{1,0:T(8,128)(2,1)S(1)...) custom-call(s32[32]{0:T(128)S(1)} %copy-done.2, bf16[288,1536]{1,0:T(8,128)(2,1)S(1)} %get-tuple-element.87.refs_0_.refs_2_, ...), custom_call_target="tpu_custom_call" | custom-call | flops 20000000000 | bytes 200000000 | tf_op jit(solution)/shard_map/back/pallas_call | solution.py:492
  75.0 6.6 %collective-permute-done.10.refs_2_ = bf16[72,2560]{1,0:T(8,128)(2,1)S(1)} collective-permute-done((bf16[72,2560]{1,0:T(8,128)(2,1)S(1)}, bf16[72,2560]{1,0:T(8,128)(2,1)S(1)}, u32[]{:S(2)}, u32[]{:S(2)}) %collective-permute-start.10) | collective-permute-done | bytes 368672 | tf_op jit(solution)/shard_map/ppermute | solution.py:373
  84.1 2.8 %hidden.7 = (bf16[288,1536]{1,0:T(8,128)(2,1)S(1)}, bf16[192,2048]{1,0:T(8,128)(2,1)S(1)}, bf16[96,2048]{1,0:T(8,128)(2,1)S(1)}) custom-call(s32[32]{0:T(128)S(1)} %copy-done.2, bf16[72,2560]{1,0:T(8,128)(2,1)S(1)} %get-tuple-element.83.refs_0_, bf16[72,2560]{1,0:T(8,128)(2,1)S(1)} %collective-permute-done.9.refs_1_, ...), custom_call_target="tpu_custom_call" | custom-call | flops 5000000000 | bytes 50000000 | tf_op jit(solution)/shard_map/hidden/pallas_call | solution.py:472
  87.1 4.8 %back.5 = (bf16[72,2688]{1,0:T(8,128)(2,1)S(1)}, bf16[72,2688]{1,0:T(8,128)(2,1)S(1)}, bf16[72,2688]{1,0:T(8,128)(2,1)S(1)}, bf16[72,2688]{1,0:T(8,128)(2,1)S(1)...) custom-call(s32[32]{0:T(128)S(1)} %copy-done.2, bf16[288,1536]{1,0:T(8,128)(2,1)S(1)} %get-tuple-element.102.refs_0_.refs_2_, ...), custom_call_target="tpu_custom_call" | custom-call | flops 20000000000 | bytes 200000000 | tf_op jit(solution)/shard_map/back/pallas_call | solution.py:492
  94.0 7.0 %collective-permute-done.19.refs_2_ = bf16[72,2688]{1,0:T(8,128)(2,1)S(1)} collective-permute-done((bf16[72,2688]{1,0:T(8,128)(2,1)S(1)}, bf16[72,2688]{1,0:T(8,128)(2,1)S(1)}, u32[]{:S(2)}, u32[]{:S(2)}) %collective-permute-start.19) | collective-permute-done | bytes 387104 | tf_op jit(solution)/shard_map/ppermute | solution.py:373
  101.0 2.5 %collective-permute-start.27 = (bf16[72,2688]{1,0:T(8,128)(2,1)S(1)}, bf16[72,2688]{1,0:T(8,128)(2,1)S(1)}, u32[]{:S(2)}, u32[]{:S(2)}) collective-permute-start(bf16[72,2688]{1,0:T(8,128)(2,1)S(1)} %get-tuple-element.113), channel_id=1, source_target_pairs={{0,6},{2,4},{4,2},{6,0},{8,14},{10,12},{12,10},{14,8},{16,22},{18,... | collective-permute-start | bytes 1161224 | tf_op jit(solution)/shard_map/ppermute | solution.py:373
  104.1 4.8 %back.6 = (bf16[72,2688]{1,0:T(8,128)(2,1)S(1)}, bf16[72,2688]{1,0:T(8,128)(2,1)S(1)}, bf16[72,2688]{1,0:T(8,128)(2,1)S(1)}, bf16[72,2688]{1,0:T(8,128)(2,1)S(1)...) custom-call(s32[32]{0:T(128)S(1)} %copy-done.2, bf16[288,1536]{1,0:T(8,128)(2,1)S(1)} %get-tuple-element.96.refs_0_.refs_2_, ...), custom_call_target="tpu_custom_call" | custom-call | flops 20000000000 | bytes 200000000 | tf_op jit(solution)/shard_map/back/pallas_call | solution.py:492
  109.9 7.6 %collective-permute-done.26.refs_2_ = bf16[72,2688]{1,0:T(8,128)(2,1)S(1)} collective-permute-done((bf16[72,2688]{1,0:T(8,128)(2,1)S(1)}, bf16[72,2688]{1,0:T(8,128)(2,1)S(1)}, u32[]{:S(2)}, u32[]{:S(2)}) %collective-permute-start.26) | collective-permute-done | bytes 387104 | tf_op jit(solution)/shard_map/ppermute | solution.py:373
  117.6 2.5 %collective-permute-start.24 = (bf16[72,2688]{1,0:T(8,128)(2,1)S(1)}, bf16[72,2688]{1,0:T(8,128)(2,1)S(1)}, u32[]{:S(2)}, u32[]{:S(2)}) collective-permute-start(bf16[72,2688]{1,0:T(8,128)(2,1)S(1)} %get-tuple-element.108), channel_id=1, source_target_pairs={{0,6},{2,4},{4,2},{6,0},{8,14},{10,12},{12,10},{14,8},{16,22},{18,... | collective-permute-start | bytes 1161224 | tf_op jit(solution)/shard_map/ppermute | solution.py:373
  120.9 4.8 %back.7 = (bf16[72,2688]{1,0:T(8,128)(2,1)S(1)}, bf16[72,2688]{1,0:T(8,128)(2,1)S(1)}, bf16[72,2688]{1,0:T(8,128)(2,1)S(1)}, bf16[72,2688]{1,0:T(8,128)(2,1)S(1)...) custom-call(s32[32]{0:T(128)S(1)} %copy-done.2, bf16[288,1536]{1,0:T(8,128)(2,1)S(1)} %get-tuple-element.94.refs_0_.refs_2_, ...), custom_call_target="tpu_custom_call" | custom-call | flops 20000000000 | bytes 200000000 | tf_op jit(solution)/shard_map/back/pallas_call | solution.py:492
  126.8 7.2 %collective-permute-done.23.refs_2_ = bf16[72,2688]{1,0:T(8,128)(2,1)S(1)} collective-permute-done((bf16[72,2688]{1,0:T(8,128)(2,1)S(1)}, bf16[72,2688]{1,0:T(8,128)(2,1)S(1)}, u32[]{:S(2)}, u32[]{:S(2)}) %collective-permute-start.23) | collective-permute-done | bytes 387104 | tf_op jit(solution)/shard_map/ppermute | solution.py:373
  134.1 2.5 %collective-permute-start.33 = (bf16[72,2688]{1,0:T(8,128)(2,1)S(1)}, bf16[72,2688]{1,0:T(8,128)(2,1)S(1)}, u32[]{:S(2)}, u32[]{:S(2)}) collective-permute-start(bf16[72,2688]{1,0:T(8,128)(2,1)S(1)} %get-tuple-element.120), channel_id=1, source_target_pairs={{0,6},{2,4},{4,2},{6,0},{8,14},{10,12},{12,10},{14,8},{16,22},{18,... | collective-permute-start | bytes 1161224 | tf_op jit(solution)/shard_map/ppermute | solution.py:373
  138.0 9.5 %grad_up.1 = (bf16[2,2048,1024]{2,1,0:T(8,128)(2,1)}, f32[8,128]{1,0:T(8,128)S(1)}) custom-call(s32[32]{0:T(128)S(1)} %copy-done.2, bf16[192,2048]{1,0:T(8,128)(2,1)S(1)} %get-tuple-element.123.refs_0_, bf16[192,2048]{1,0:T(8,128)(2,1)S(1)} %get-tuple-element.124.refs_1_, bf16[192,2048]{1,0:T(8,128)(2,1)S(1)} %get-tuple-element.125.refs_2_, ...), custom_call_target="tpu_custom_call" | custom-call | flops 20000000000 | bytes 200000000 | tf_op jit(solution)/shard_map/grad_up/pallas_call | solution.py:527
  147.4 2.9 %collective-permute-done.32.refs_2_ = bf16[72,2688]{1,0:T(8,128)(2,1)S(1)} collective-permute-done((bf16[72,2688]{1,0:T(8,128)(2,1)S(1)}, bf16[72,2688]{1,0:T(8,128)(2,1)S(1)}, u32[]{:S(2)}, u32[]{:S(2)}) %collective-permute-start.32) | collective-permute-done | bytes 387104 | tf_op jit(solution)/shard_map/ppermute | solution.py:373
  150.9 2.5 %collective-permute-done.30.refs_0_ = bf16[128,2688]{1,0:T(8,128)(2,1)S(1)} collective-permute-done((bf16[128,2688]{1,0:T(8,128)(2,1)S(1)}, bf16[128,2688]{1,0:T(8,128)(2,1)S(1)}, u32[]{:S(2)}, u32[]{:S(2)}) %collective-permute-start.30) | collective-permute-done | bytes 688160 | tf_op jit(solution)/shard_map/ppermute | solution.py:369
  (75 shorter events, 29.8 us)
Async XLA Ops:
  4.4 20.7 %collective-permute-start = (bf16[128,2688]{1,0:T(8,128)(2,1)}, bf16[128,2688]{1,0:T(8,128)(2,1)S(1)}, u32[]{:S(2)}, u32[]{:S(2)}) collective-permute-start(bf16[128,2688]{1,0:T(8,128)(2,1)} %get-tuple-element.70), channel_id=1, source_target_pairs={{0,8},{2,10},{4,12},{6,14},{8,16},{10,18},{12,20},{14,22},{16,24},... | collective-permute-start | bytes 2064392 | tf_op jit(solution)/shard_map/ppermute | solution.py:369
  7.5 20.8 %collective-permute-start.6 = (bf16[72,2560]{1,0:T(8,128)(2,1)}, bf16[72,2560]{1,0:T(8,128)(2,1)S(1)}, u32[]{:S(2)}, u32[]{:S(2)}) collective-permute-start(bf16[72,2560]{1,0:T(8,128)(2,1)} %get-tuple-element.76), channel_id=1, source_target_pairs={{0,2},{2,0},{4,6},{6,4},{8,10},{10,8},{12,14},{14,12},{16,18},{18,... | collective-permute-start | bytes 1105928 | tf_op jit(solution)/shard_map/ppermute | solution.py:373
  9.0 20.8 %collective-permute-start.7 = (bf16[72,2560]{1,0:T(8,128)(2,1)}, bf16[72,2560]{1,0:T(8,128)(2,1)S(1)}, u32[]{:S(2)}, u32[]{:S(2)}) collective-permute-start(bf16[72,2560]{1,0:T(8,128)(2,1)} %get-tuple-element.77), channel_id=1, source_target_pairs={{0,4},{2,6},{4,0},{6,2},{8,12},{10,14},{12,8},{14,10},{16,20},{18,... | collective-permute-start | bytes 1105928 | tf_op jit(solution)/shard_map/ppermute | solution.py:373
  10.5 19.8 %collective-permute-start.8 = (bf16[72,2560]{1,0:T(8,128)(2,1)}, bf16[72,2560]{1,0:T(8,128)(2,1)S(1)}, u32[]{:S(2)}, u32[]{:S(2)}) collective-permute-start(bf16[72,2560]{1,0:T(8,128)(2,1)} %get-tuple-element.78), channel_id=1, source_target_pairs={{0,6},{2,4},{4,2},{6,0},{8,14},{10,12},{12,10},{14,8},{16,22},{18,... | collective-permute-start | bytes 1105928 | tf_op jit(solution)/shard_map/ppermute | solution.py:373
  25.2 18.4 %collective-permute-start.1 = (bf16[128,2688]{1,0:T(8,128)(2,1)S(1)}, bf16[128,2688]{1,0:T(8,128)(2,1)S(1)}, u32[]{:S(2)}, u32[]{:S(2)}) collective-permute-start(bf16[128,2688]{1,0:T(8,128)(2,1)S(1)} %collective-permute-done.refs_0_), channel_id=1, source_target_pairs={{0,8},{2,10},{4,12},{6,14},{8,16},{10,18},{12,20},{14,22},{16,24},... | collective-permute-start | bytes 2064392 | tf_op jit(solution)/shard_map/ppermute | solution.py:369
  26.7 18.4 %collective-permute-start.3 = (bf16[72,2560]{1,0:T(8,128)(2,1)S(1)}, bf16[72,2560]{1,0:T(8,128)(2,1)S(1)}, u32[]{:S(2)}, u32[]{:S(2)}) collective-permute-start(bf16[72,2560]{1,0:T(8,128)(2,1)S(1)} %get-tuple-element.72), channel_id=1, source_target_pairs={{0,2},{2,0},{4,6},{6,4},{8,10},{10,8},{12,14},{14,12},{16,18},{18,... | collective-permute-start | bytes 1105928 | tf_op jit(solution)/shard_map/ppermute | solution.py:373
  28.3 18.2 %collective-permute-start.4 = (bf16[72,2560]{1,0:T(8,128)(2,1)S(1)}, bf16[72,2560]{1,0:T(8,128)(2,1)S(1)}, u32[]{:S(2)}, u32[]{:S(2)}) collective-permute-start(bf16[72,2560]{1,0:T(8,128)(2,1)S(1)} %get-tuple-element.73), channel_id=1, source_target_pairs={{0,4},{2,6},{4,0},{6,2},{8,12},{10,14},{12,8},{14,10},{16,20},{18,... | collective-permute-start | bytes 1105928 | tf_op jit(solution)/shard_map/ppermute | solution.py:373
  29.8 18.2 %collective-permute-start.5 = (bf16[72,2560]{1,0:T(8,128)(2,1)S(1)}, bf16[72,2560]{1,0:T(8,128)(2,1)S(1)}, u32[]{:S(2)}, u32[]{:S(2)}) collective-permute-start(bf16[72,2560]{1,0:T(8,128)(2,1)S(1)} %get-tuple-element.74), channel_id=1, source_target_pairs={{0,6},{2,4},{4,2},{6,0},{8,14},{10,12},{12,10},{14,8},{16,22},{18,... | collective-permute-start | bytes 1105928 | tf_op jit(solution)/shard_map/ppermute | solution.py:373
  34.1 35.0 %collective-permute-start.16 = (bf16[288,1536]{1,0:T(8,128)(2,1)S(1)}, bf16[288,1536]{1,0:T(8,128)(2,1)S(1)}, u32[]{:S(2)}, u32[]{:S(2)}) collective-permute-start(bf16[288,1536]{1,0:T(8,128)(2,1)S(1)} %get-tuple-element.94.refs_0_.refs_2_), channel_id=1, source_target_pairs={{0,1},{1,0},{2,3},{3,2},{4,5},{5,4},{6,7},{7,6},{8,9},{9,8},{10,11... | collective-permute-start | bytes 2654216 | tf_op jit(solution)/shard_map/ppermute | solution.py:482
  43.6 17.5 %collective-permute-start.2 = (bf16[128,2688]{1,0:T(8,128)(2,1)S(1)}, bf16[128,2688]{1,0:T(8,128)(2,1)S(1)}, u32[]{:S(2)}, u32[]{:S(2)}) collective-permute-start(bf16[128,2688]{1,0:T(8,128)(2,1)S(1)} %collective-permute-done.1.refs_0_), channel_id=1, source_target_pairs={{0,8},{2,10},{4,12},{6,14},{8,16},{10,18},{12,20},{14,22},{16,24},... | collective-permute-start | bytes 2064392 | tf_op jit(solution)/shard_map/ppermute | solution.py:369
  45.2 17.5 %collective-permute-start.13 = (bf16[72,2560]{1,0:T(8,128)(2,1)S(1)}, bf16[72,2560]{1,0:T(8,128)(2,1)S(1)}, u32[]{:S(2)}, u32[]{:S(2)}) collective-permute-start(bf16[72,2560]{1,0:T(8,128)(2,1)S(1)} %get-tuple-element.89), channel_id=1, source_target_pairs={{0,2},{2,0},{4,6},{6,4},{8,10},{10,8},{12,14},{14,12},{16,18},{18,... | collective-permute-start | bytes 1105928 | tf_op jit(solution)/shard_map/ppermute | solution.py:373
  62.7 19.0 %collective-permute-start.10 = (bf16[72,2560]{1,0:T(8,128)(2,1)S(1)}, bf16[72,2560]{1,0:T(8,128)(2,1)S(1)}, u32[]{:S(2)}, u32[]{:S(2)}) collective-permute-start(bf16[72,2560]{1,0:T(8,128)(2,1)S(1)} %get-tuple-element.85), channel_id=1, source_target_pairs={{0,4},{2,6},{4,0},{6,2},{8,12},{10,14},{12,8},{14,10},{16,20},{18,... | collective-permute-start | bytes 1105928 | tf_op jit(solution)/shard_map/ppermute | solution.py:373
  63.8 18.9 %collective-permute-start.11 = (bf16[72,2560]{1,0:T(8,128)(2,1)S(1)}, bf16[72,2560]{1,0:T(8,128)(2,1)S(1)}, u32[]{:S(2)}, u32[]{:S(2)}) collective-permute-start(bf16[72,2560]{1,0:T(8,128)(2,1)S(1)} %get-tuple-element.86), channel_id=1, source_target_pairs={{0,6},{2,4},{4,2},{6,0},{8,14},{10,12},{12,10},{14,8},{16,22},{18,... | collective-permute-start | bytes 1105928 | tf_op jit(solution)/shard_map/ppermute | solution.py:373
  65.2 18.9 %collective-permute-start.9 = (bf16[72,2560]{1,0:T(8,128)(2,1)S(1)}, bf16[72,2560]{1,0:T(8,128)(2,1)S(1)}, u32[]{:S(2)}, u32[]{:S(2)}) collective-permute-start(bf16[72,2560]{1,0:T(8,128)(2,1)S(1)} %get-tuple-element.84), channel_id=1, source_target_pairs={{0,2},{2,0},{4,6},{6,4},{8,10},{10,8},{12,14},{14,12},{16,18},{18,... | collective-permute-start | bytes 1105928 | tf_op jit(solution)/shard_map/ppermute | solution.py:373
  69.1 18.0 %collective-permute-start.21 = (bf16[288,1536]{1,0:T(8,128)(2,1)S(1)}, bf16[288,1536]{1,0:T(8,128)(2,1)S(1)}, u32[]{:S(2)}, u32[]{:S(2)}) collective-permute-start(bf16[288,1536]{1,0:T(8,128)(2,1)S(1)} %get-tuple-element.102.refs_0_.refs_2_), channel_id=1, source_target_pairs={{0,1},{1,0},{2,3},{3,2},{4,5},{5,4},{6,7},{7,6},{8,9},{9,8},{10,11... | collective-permute-start | bytes 2654216 | tf_op jit(solution)/shard_map/ppermute | solution.py:482
  74.0 19.0 %collective-permute-start.18 = (bf16[72,2688]{1,0:T(8,128)(2,1)S(1)}, bf16[72,2688]{1,0:T(8,128)(2,1)S(1)}, u32[]{:S(2)}, u32[]{:S(2)}) collective-permute-start(bf16[72,2688]{1,0:T(8,128)(2,1)S(1)} %get-tuple-element.98), channel_id=1, source_target_pairs={{0,2},{2,0},{4,6},{6,4},{8,10},{10,8},{12,14},{14,12},{16,18},{18,... | collective-permute-start | bytes 1161224 | tf_op jit(solution)/shard_map/ppermute | solution.py:373
  81.6 19.4 %collective-permute-start.19 = (bf16[72,2688]{1,0:T(8,128)(2,1)S(1)}, bf16[72,2688]{1,0:T(8,128)(2,1)S(1)}, u32[]{:S(2)}, u32[]{:S(2)}) collective-permute-start(bf16[72,2688]{1,0:T(8,128)(2,1)S(1)} %get-tuple-element.99), channel_id=1, source_target_pairs={{0,4},{2,6},{4,0},{6,2},{8,12},{10,14},{12,8},{14,10},{16,20},{18,... | collective-permute-start | bytes 1161224 | tf_op jit(solution)/shard_map/ppermute | solution.py:373
  82.7 20.8 %collective-permute-start.20 = (bf16[72,2688]{1,0:T(8,128)(2,1)S(1)}, bf16[72,2688]{1,0:T(8,128)(2,1)S(1)}, u32[]{:S(2)}, u32[]{:S(2)}) collective-permute-start(bf16[72,2688]{1,0:T(8,128)(2,1)S(1)} %get-tuple-element.100), channel_id=1, source_target_pairs={{0,6},{2,4},{4,2},{6,0},{8,14},{10,12},{12,10},{14,8},{16,22},{18,... | collective-permute-start | bytes 1161224 | tf_op jit(solution)/shard_map/ppermute | solution.py:373
  92.9 24.6 %collective-permute-start.26 = (bf16[72,2688]{1,0:T(8,128)(2,1)S(1)}, bf16[72,2688]{1,0:T(8,128)(2,1)S(1)}, u32[]{:S(2)}, u32[]{:S(2)}) collective-permute-start(bf16[72,2688]{1,0:T(8,128)(2,1)S(1)} %get-tuple-element.112), channel_id=1, source_target_pairs={{0,4},{2,6},{4,0},{6,2},{8,12},{10,14},{12,8},{14,10},{16,20},{18,... | collective-permute-start | bytes 1161224 | tf_op jit(solution)/shard_map/ppermute | solution.py:373
  101.0 19.1 %collective-permute-start.27 = (bf16[72,2688]{1,0:T(8,128)(2,1)S(1)}, bf16[72,2688]{1,0:T(8,128)(2,1)S(1)}, u32[]{:S(2)}, u32[]{:S(2)}) collective-permute-start(bf16[72,2688]{1,0:T(8,128)(2,1)S(1)} %get-tuple-element.113), channel_id=1, source_target_pairs={{0,6},{2,4},{4,2},{6,0},{8,14},{10,12},{12,10},{14,8},{16,22},{18,... | collective-permute-start | bytes 1161224 | tf_op jit(solution)/shard_map/ppermute | solution.py:373
  109.0 25.1 %collective-permute-start.23 = (bf16[72,2688]{1,0:T(8,128)(2,1)S(1)}, bf16[72,2688]{1,0:T(8,128)(2,1)S(1)}, u32[]{:S(2)}, u32[]{:S(2)}) collective-permute-start(bf16[72,2688]{1,0:T(8,128)(2,1)S(1)} %get-tuple-element.107), channel_id=1, source_target_pairs={{0,4},{2,6},{4,0},{6,2},{8,12},{10,14},{12,8},{14,10},{16,20},{18,... | collective-permute-start | bytes 1161224 | tf_op jit(solution)/shard_map/ppermute | solution.py:373
  117.6 19.0 %collective-permute-start.24 = (bf16[72,2688]{1,0:T(8,128)(2,1)S(1)}, bf16[72,2688]{1,0:T(8,128)(2,1)S(1)}, u32[]{:S(2)}, u32[]{:S(2)}) collective-permute-start(bf16[72,2688]{1,0:T(8,128)(2,1)S(1)} %get-tuple-element.108), channel_id=1, source_target_pairs={{0,6},{2,4},{4,2},{6,0},{8,14},{10,12},{12,10},{14,8},{16,22},{18,... | collective-permute-start | bytes 1161224 | tf_op jit(solution)/shard_map/ppermute | solution.py:373
  125.7 21.7 %collective-permute-start.31 = (bf16[72,2688]{1,0:T(8,128)(2,1)S(1)}, bf16[72,2688]{1,0:T(8,128)(2,1)S(1)}, u32[]{:S(2)}, u32[]{:S(2)}) collective-permute-start(bf16[72,2688]{1,0:T(8,128)(2,1)S(1)} %get-tuple-element.118), channel_id=1, source_target_pairs={{0,2},{2,0},{4,6},{6,4},{8,10},{10,8},{12,14},{14,12},{16,18},{18,... | collective-permute-start | bytes 1161224 | tf_op jit(solution)/shard_map/ppermute | solution.py:373
  126.3 24.0 %collective-permute-start.32 = (bf16[72,2688]{1,0:T(8,128)(2,1)S(1)}, bf16[72,2688]{1,0:T(8,128)(2,1)S(1)}, u32[]{:S(2)}, u32[]{:S(2)}) collective-permute-start(bf16[72,2688]{1,0:T(8,128)(2,1)S(1)} %get-tuple-element.119), channel_id=1, source_target_pairs={{0,4},{2,6},{4,0},{6,2},{8,12},{10,14},{12,8},{14,10},{16,20},{18,... | collective-permute-start | bytes 1161224 | tf_op jit(solution)/shard_map/ppermute | solution.py:373
  (16 other events, 266.8 us)

commit v5 on v4

--- a/solution.py
+++ b/solution.py
@@ -201,14 +201,13 @@
             columns(j, pl.ds(pl.multiple_of(j * tile, tile), tile))
 
 
-def back_kernel(m, hot_rows, cold_rows, n_parts, n_grads, share, waits, plan, *refs):
+def back_kernel(m, hot_rows, cold_rows, n_parts, n_grads, share, tailed, waits, plan, *refs):
     sums, grads = refs[:n_parts], refs[n_parts : n_parts + n_grads]
     weight, refs = refs[n_parts + n_grads], refs[n_parts + n_grads + 1 + waits :]
     outs, g_hot, g_cold = refs[:INNER], refs[INNER], refs[INNER + 1]
     hots, colds = m * hot_rows, m * cold_rows
-    ff = weight.shape[2]
+    feat, ff = weight.shape[1:]
     width = outs[0].shape[1]
-    feat = width - share - TAIL
     tile = 512 if feat % 512 == 0 else feat
     tp = lax.axis_index("tp")
     hot = hot_of(plan, lax.axis_index("ep"))
@@ -240,16 +239,18 @@
             act = (hidden * sig).astype(BF16).astype(F32)
             hidden_grad = row_grad * (sig * (1.0 + hidden * (1.0 - sig)))
             target[d * piece : d * piece + count] = hidden_grad.astype(BF16)
-            gate_grad = jnp.sum(act * row_grad, 1, keepdims=True)
-            high = gate_grad.astype(BF16).astype(F32)
-            low = gate_grad - high
-            lane = lax.broadcasted_iota(I32, (count, TAIL), 1)
-            end = jnp.where(lane == 0, high, jnp.where(lane == 1, low, 0.0))
             half = None
             for n in range(ff // share):
                 piece_act = jnp.where(tp == n, act[:, n * share : (n + 1) * share], 0.0)
                 half = piece_act if half is None else half + piece_act
-            made.append(jnp.concatenate([half, end], 1))
+            if tailed:
+                gate_grad = jnp.sum(act * row_grad, 1, keepdims=True)
+                high = gate_grad.astype(BF16).astype(F32)
+                low = gate_grad - high
+                lane = lax.broadcasted_iota(I32, (count, TAIL), 1)
+                end = jnp.where(lane == 0, high, jnp.where(lane == 1, low, 0.0))
+                half = jnp.concatenate([half, end], 1)
+            made.append(half)
         ends.append(jnp.concatenate(made, 0))
     put(slice(feat, width), *ends)
 
@@ -271,18 +272,21 @@
     lax.fori_loop(0, feat // tile, features, 0)
 
 
-def expand_kernel(m, topk, share, n_more, waits, *refs):
+def expand_kernel(m, topk, share, tailed, n_more, waits, *refs):
     blocks, picks, marks, refs = refs[:INNER], refs[INNER : INNER + m], refs[INNER + m], refs[INNER + m + 1 :]
-    more, outs = refs[:n_more], refs[n_more + waits :]
-    width = blocks[0].shape[1]
+    payloads, refs = ([], refs) if tailed else (refs[:m], refs[m:])
+    more, outs, apart = refs[:n_more], refs[n_more + waits :][:m], refs[n_more + waits + m :]
+    width = outs[0].shape[1]
     feat = width - share - TAIL
 
-    def add(columns, rows):
+    def add(columns, rows, copies=()):
         for s in range(m):
             total = jnp.dot(picks[s][...], rows, preferred_element_type=F32)
             if more:
                 total = total + more[s][:, columns].astype(F32)
             outs[s][:, columns] = total.astype(BF16)
+            for copy in copies[s : s + 1]:
+                copy[...] = total.astype(BF16)
 
     def joined(columns):
         return rows_joined([b[:, columns] for b in blocks])
@@ -293,19 +297,25 @@
     mark = marks[...]
     gate = mark[:, 2 * topk : 2 * topk + 1]
     columns = slice(feat, feat + share)
-    add(columns, (gate * joined(columns).astype(F32)).astype(BF16))
+    act = joined(columns).astype(F32)
+    add(columns, (gate * act).astype(BF16))
     columns = slice(feat + share, width)
-    end = joined(columns).astype(F32)
-    gate_grad = (end[:, 0:1] + end[:, 1:2]) / jnp.where(gate > 0.0, gate, 1.0)
+    if tailed:
+        end = joined(columns).astype(F32)
+        gate_grad = (end[:, 0:1] + end[:, 1:2]) / jnp.where(gate > 0.0, gate, 1.0)
+    else:
+        grad = picked(picks, payloads, slice(feat, feat + share))
+        gate_grad = jnp.sum(act * grad, 1, keepdims=True)
     high = gate_grad.astype(BF16).astype(F32)
-    lane = lax.broadcasted_iota(I32, end.shape, 1)
+    lane = lax.broadcasted_iota(I32, mark.shape, 1)
     values = jnp.where(lane < topk, high, gate_grad - high)
-    add(columns, jnp.where((lane < 2 * topk) & (mark > 0.0), values, 0.0).astype(BF16))
-
-
-def final_kernel(n, topk, *refs):
-    parts = refs[:n]
-    mixed, grad_tokens, grad_gates = refs[n:]
+    end = jnp.where((lane < 2 * topk) & (mark > 0.0), values, 0.0)
+    add(columns, end.astype(BF16), apart)
+
+
+def final_kernel(n, n_tails, topk, *refs):
+    parts, tails = refs[:n], refs[n : n + n_tails]
+    mixed, grad_tokens, grad_gates = refs[n + n_tails :]
     feat, share = grad_tokens.shape[1], mixed.shape[1]
 
     def total(columns):
@@ -316,9 +326,13 @@
 
     grad_tokens[...] = total(slice(0, feat)).astype(BF16)
     mixed[...] = total(slice(feat, feat + share)).astype(BF16)
-    tail = total(slice(feat + share, feat + share + TAIL))
-    tail = tail.T
-    grad_gates[...] = tail[:topk] + tail[topk : 2 * topk]
+    ends = [tail[...].astype(F32) for tail in tails]
+    ends += [part[:, feat + share :].astype(F32) for part in parts if part.shape[1] > feat + share]
+    end = ends[0]
+    for more in ends[1:]:
+        end = end + more
+    end = end.T
+    grad_gates[...] = end[:topk] + end[topk : 2 * topk]
 
 
 def up_kernel(n, waits, plan, *refs):
@@ -358,6 +372,7 @@
     hot_rows, cold_rows = 2 * capacity, capacity
     width = feat + share + TAIL
     there = feat + share
+    by_hand = n_tp == 2 and outer == CHUNKS
     smem = pl.BlockSpec(memory_space=pltpu.SMEM)
 
     def along(value, shift):
@@ -491,9 +506,10 @@
             return select(k)
         made = pl.pallas_call(
             functools.partial(
-                back_kernel, *sizes, len(sums[c]), len(grads[c]), share, len(last)
+                back_kernel, *sizes, len(sums[c]), len(grads[c]), share, c == 0, len(last)
             ),
-            out_shape=[block((rows, width))] * INNER + [block((hots, ff)), block((colds, ff))],
+            out_shape=[block((rows, there if c else width))] * INNER
+            + [block((hots, ff)), block((colds, ff))],
             in_specs=[smem]
             + whole_specs(len(sums[c]) + len(grads[c]) + 1)
             + [rest_spec] * len(last),
@@ -508,18 +524,23 @@
 
     def expand(c):
         more = [along(partials[s - m], m) for s in chunks[c]] if c > 1 else []
+        payloads = [arrived[s] for s in chunks[c]] if c else []
+        apart = [block((count, TAIL))] if c == n - 1 and by_hand else []
         k = coming[c]
         made = pl.pallas_call(
-            functools.partial(expand_kernel, m, topk, share, len(more), len(last)),
-            out_shape=[block((count, width))] * m,
-            in_specs=whole_specs(INNER + m + 1 + len(more)) + [rest_spec] * len(last),
-            out_specs=whole_specs(m),
+            functools.partial(expand_kernel, m, topk, share, c == 0, len(more), len(last)),
+            out_shape=[block((count, width))] * m + apart,
+            in_specs=whole_specs(INNER + m + 1 + len(payloads) + len(more))
+            + [rest_spec] * len(last),
+            out_specs=whole_specs(m + len(apart)),
             compiler_params=params(),
             cost_estimate=weigh("e"),
             name="expand",
-        )(*blocks[k], *picks[c], marks[c], *more, *last)
+        )(*blocks[k], *picks[c], marks[c], *payloads, *more, *last)
         for s, value in zip(chunks[c], made):
             partials[s] = value
+        if apart:
+            partials["apart"] = made[m]
         last[:] = [made[0]]
 
     def weight_grad():
@@ -567,18 +588,40 @@
             {"x": step, "h": hidden, "e": expand}[word[0]](number)
 
     sums_back = [along(partials[s], m) for s in chunks[n - 1]]
-    parts = [sums_back[0], partials[0]]
-    for s in chunks[0][1:]:
-        parts.append(along(sums_back[s] + partials[s], outer - s))
+    if by_hand:
+        pairs = [
+            (
+                (o * INNER + i) * n_tp + t,
+                (((o + m) % outer) * INNER + i) * n_tp + 1 - t,
+            )
+            for o in range(outer)
+            for i in range(INNER)
+            for t in range(n_tp)
+        ]
+        tails = [lax.ppermute(partials["apart"], ("ep", "tp"), pairs)]
+        parts = [sums_back[0], partials[0]]
+    else:
+        parts, tails, halves = [], [], 0.0
+        for s, value in zip(chunks[0], sums_back):
+            ours = partials[s]
+            if s == 0:
+                parts += [value[:, :there], ours[:, :there]]
+                halves = halves + value[:, there:].astype(F32)
+                tails.append(ours[:, there:])
+            else:
+                parts.append(along(value[:, :there] + ours[:, :there], outer - s))
+                halves = halves + along(value[:, there:], outer - s).astype(F32)
+                tails.append(along(ours[:, there:], outer - s))
+        tails.append(lax.psum(halves, "tp"))
     mixed, grad_tokens, grad_gates = pl.pallas_call(
-        functools.partial(final_kernel, len(parts), topk),
+        functools.partial(final_kernel, len(parts), len(tails), topk),
         out_shape=[block((count, share)), block((count, feat)), block((topk, count), F32)],
-        in_specs=whole_specs(len(parts)),
+        in_specs=whole_specs(len(parts) + len(tails)),
         out_specs=whole_specs(3),
         compiler_params=params(),
         cost_estimate=weigh("e"),
         name="final",
-    )(*parts)
+    )(*parts, *tails)
     return mixed, grad_tokens, grad_gates.T, grad_up
 
 

time: 155 us -> 153 us (0.987)
  waiting for transfers between devices: 67.7 us -> 65.3 us
    ppermute x24, waiting for transfers between devices: 31.4 us -> 26.7 us  [across(): return lax.ppermute(value, 'ep', pairs)]
    ppermute x6, waiting for transfers between devices: 36.3 us -> 38.6 us  [along(): return lax.ppermute(value, 'ep', pairs)]
  transfers between devices with their start and end apart: 34 -> 35, of which waited for: 10 -> 11; matrix products, arithmetic and copies ran while one was open for 0% -> 0% of each run, Pallas kernels for 31% -> 31%
where the time goes in v5:
time: 153 us
  waiting for transfers between devices  65.3 us (43%)
  Pallas kernels  52.7 us (34%)
  starting transfers between devices  34.2 us (22%)
    ppermute x6, waiting for transfers between devices, along(): return lax.ppermute(value, 'ep', pairs)  38.6 us
    ppermute x24, starting transfers between devices, across(): return lax.ppermute(value, 'ep', pairs)  30.5 us
    ppermute x24, waiting for transfers between devices, across(): return lax.ppermute(value, 'ep', pairs)  26.7 us
    pallas_call x4, Pallas kernels, step(): pl.pallas_call(functools.partial(back_kernel, *sizes, len(sums[c]), len(g...  18.4 us
    pallas_call x4, Pallas kernels, hidden(): pl.pallas_call(functools.partial(hidden_kernel, *sizes, feat, streamed, l...  12.2 us
    pallas_call x1, Pallas kernels, weight_grad(): pl.pallas_call(functools.partial(up_kernel, n, len(last)), out_shape=[blo...  9.49 us
    pallas_call x3, Pallas kernels, select(): pl.pallas_call(functools.partial(select_kernel, *sizes, topk, share, len(...  4.68 us
    pallas_call x1, Pallas kernels, on_device(): pl.pallas_call(functools.partial(start_kernel, *sizes), out_shape=[block(...  3.78 us
  transfers between devices with their start and end apart: 35, of which 11 were waited for; matrix products, arithmetic and copies ran while one was open for 0% of the time, Pallas kernels for 31%

profile of v5, /device:TPU:0, one launch (start us, length us, event | category | flops | bytes accessed | tf_op | source)
XLA Modules:
  0.0 153.3 jit_solution(1177562886273544982)
XLA Ops:
  0.6 3.8 %start.1 = (bf16[128,2688]{1,0:T(8,128)(2,1)}, bf16[72,2560]{1,0:T(8,128)(2,1)}, bf16[72,2560]{1,0:T(8,128)(2,1)}, bf16[72,2560]{1,0:T(8,128)(2,1)}, bf16[72,256...) custom-call(s32[32]{0:T(128)} %plan.25, bf16[128,2048]{1,0:T(8,128)(2,1)} %tokens.1, ...), custom_call_target="tpu_custom_call" | custom-call | flops 5000000000 | bytes 50000000 | tf_op jit(solution)/shard_map/start/pallas_call | solution.py:417
  4.4 3.1 %collective-permute-start = (bf16[128,2688]{1,0:T(8,128)(2,1)}, bf16[128,2688]{1,0:T(8,128)(2,1)S(1)}, u32[]{:S(2)}, u32[]{:S(2)}) collective-permute-start(bf16[128,2688]{1,0:T(8,128)(2,1)} %get-tuple-element.72), channel_id=1, source_target_pairs={{0,8},{2,10},{4,12},{6,14},{8,16},{10,18},{12,20},{14,22},{16,24},... | collective-permute-start | bytes 2064392 | tf_op jit(solution)/shard_map/ppermute | solution.py:384
  11.0 14.2 %collective-permute-done.refs_0_.refs_6_ = bf16[128,2688]{1,0:T(8,128)(2,1)S(1)} collective-permute-done((bf16[128,2688]{1,0:T(8,128)(2,1)}, bf16[128,2688]{1,0:T(8,128)(2,1)S(1)}, u32[]{:S(2)}, u32[]{:S(2)}) %collective-permute-start) | collective-permute-done | bytes 688160 | tf_op jit(solution)/shard_map/ppermute | solution.py:384
  30.3 3.8 %hidden.4 = (bf16[288,1536]{1,0:T(8,128)(2,1)S(1)}, bf16[192,2048]{1,0:T(8,128)(2,1)S(1)}, bf16[96,2048]{1,0:T(8,128)(2,1)S(1)}) custom-call(s32[32]{0:T(128)S(1)} %copy-done.2, bf16[72,2560]{1,0:T(8,128)(2,1)S(1)} %copy-done.3, bf16[72,2560]{1,0:T(8,128)(2,1)S(1)} %collective-permute-done.6.refs_1_, bf16[72,2560]{1,0:T(8,128)(2,1)S(1)} %collective-permute-done.7.refs_2_, ...), custom_call_target="tpu_custom_call" | custom-call | flops 5000000000 | bytes 50000000 | tf_op jit(solution)/shard_map/hidden/pallas_call | solution.py:487
  34.2 9.4 %collective-permute-done.1.refs_0_.refs_6_ = bf16[128,2688]{1,0:T(8,128)(2,1)S(1)} collective-permute-done((bf16[128,2688]{1,0:T(8,128)(2,1)S(1)}, bf16[128,2688]{1,0:T(8,128)(2,1)S(1)}, u32[]{:S(2)}, u32[]{:S(2)}) %collective-permute-start.1) | collective-permute-done | bytes 688160 | tf_op jit(solution)/shard_map/ppermute | solution.py:384
  48.7 2.8 %hidden.5 = (bf16[288,1536]{1,0:T(8,128)(2,1)S(1)}, bf16[192,2048]{1,0:T(8,128)(2,1)S(1)}, bf16[96,2048]{1,0:T(8,128)(2,1)S(1)}) custom-call(s32[32]{0:T(128)S(1)} %copy-done.2, bf16[72,2560]{1,0:T(8,128)(2,1)S(1)} %get-tuple-element.73.refs_0_, bf16[72,2560]{1,0:T(8,128)(2,1)S(1)} %collective-permute-done.3.refs_1_, ...), custom_call_target="tpu_custom_call" | custom-call | flops 5000000000 | bytes 50000000 | tf_op jit(solution)/shard_map/hidden/pallas_call | solution.py:487
  51.5 9.5 %collective-permute-done.2.refs_0_.refs_6_ = bf16[128,2688]{1,0:T(8,128)(2,1)S(1)} collective-permute-done((bf16[128,2688]{1,0:T(8,128)(2,1)S(1)}, bf16[128,2688]{1,0:T(8,128)(2,1)S(1)}, u32[]{:S(2)}, u32[]{:S(2)}) %collective-permute-start.2) | collective-permute-done | bytes 688160 | tf_op jit(solution)/shard_map/ppermute | solution.py:384
  66.2 2.8 %hidden.6 = (bf16[288,1536]{1,0:T(8,128)(2,1)S(1)}, bf16[192,2048]{1,0:T(8,128)(2,1)S(1)}, bf16[96,2048]{1,0:T(8,128)(2,1)S(1)}) custom-call(s32[32]{0:T(128)S(1)} %copy-done.2, bf16[72,2560]{1,0:T(8,128)(2,1)S(1)} %get-tuple-element.90.refs_0_, bf16[72,2560]{1,0:T(8,128)(2,1)S(1)} %collective-permute-done.13.refs_1_, ...), custom_call_target="tpu_custom_call" | custom-call | flops 5000000000 | bytes 50000000 | tf_op jit(solution)/shard_map/hidden/pallas_call | solution.py:487
  69.1 4.5 %back.4 = (bf16[72,2560]{1,0:T(8,128)(2,1)S(1)}, bf16[72,2560]{1,0:T(8,128)(2,1)S(1)}, bf16[72,2560]{1,0:T(8,128)(2,1)S(1)}, bf16[72,2560]{1,0:T(8,128)(2,1)S(1)...) custom-call(s32[32]{0:T(128)S(1)} %copy-done.2, bf16[288,1536]{1,0:T(8,128)(2,1)S(1)} %get-tuple-element.89.refs_0_.refs_2_, ...), custom_call_target="tpu_custom_call" | custom-call | flops 20000000000 | bytes 200000000 | tf_op jit(solution)/shard_map/back/pallas_call | solution.py:507
  74.8 6.8 %collective-permute-done.10.refs_2_ = bf16[72,2560]{1,0:T(8,128)(2,1)S(1)} collective-permute-done((bf16[72,2560]{1,0:T(8,128)(2,1)S(1)}, bf16[72,2560]{1,0:T(8,128)(2,1)S(1)}, u32[]{:S(2)}, u32[]{:S(2)}) %collective-permute-start.10) | collective-permute-done | bytes 368672 | tf_op jit(solution)/shard_map/ppermute | solution.py:388
  84.1 2.8 %hidden.7 = (bf16[288,1536]{1,0:T(8,128)(2,1)S(1)}, bf16[192,2048]{1,0:T(8,128)(2,1)S(1)}, bf16[96,2048]{1,0:T(8,128)(2,1)S(1)}) custom-call(s32[32]{0:T(128)S(1)} %copy-done.2, bf16[72,2560]{1,0:T(8,128)(2,1)S(1)} %get-tuple-element.85.refs_0_, bf16[72,2560]{1,0:T(8,128)(2,1)S(1)} %collective-permute-done.9.refs_1_, ...), custom_call_target="tpu_custom_call" | custom-call | flops 5000000000 | bytes 50000000 | tf_op jit(solution)/shard_map/hidden/pallas_call | solution.py:487
  87.0 4.6 %back.5 = (bf16[72,2560]{1,0:T(8,128)(2,1)S(1)}, bf16[72,2560]{1,0:T(8,128)(2,1)S(1)}, bf16[72,2560]{1,0:T(8,128)(2,1)S(1)}, bf16[72,2560]{1,0:T(8,128)(2,1)S(1)...) custom-call(s32[32]{0:T(128)S(1)} %copy-done.2, bf16[288,1536]{1,0:T(8,128)(2,1)S(1)} %get-tuple-element.104.refs_0_.refs_2_, ...), custom_call_target="tpu_custom_call" | custom-call | flops 20000000000 | bytes 200000000 | tf_op jit(solution)/shard_map/back/pallas_call | solution.py:507
  93.7 6.4 %collective-permute-done.19.refs_2_ = bf16[72,2560]{1,0:T(8,128)(2,1)S(1)} collective-permute-done((bf16[72,2560]{1,0:T(8,128)(2,1)S(1)}, bf16[72,2560]{1,0:T(8,128)(2,1)S(1)}, u32[]{:S(2)}, u32[]{:S(2)}) %collective-permute-start.19) | collective-permute-done | bytes 368672 | tf_op jit(solution)/shard_map/ppermute | solution.py:388
  100.2 2.5 %collective-permute-start.27 = (bf16[72,2560]{1,0:T(8,128)(2,1)S(1)}, bf16[72,2560]{1,0:T(8,128)(2,1)S(1)}, u32[]{:S(2)}, u32[]{:S(2)}) collective-permute-start(bf16[72,2560]{1,0:T(8,128)(2,1)S(1)} %get-tuple-element.115), channel_id=1, source_target_pairs={{0,6},{2,4},{4,2},{6,0},{8,14},{10,12},{12,10},{14,8},{16,22},{18,... | collective-permute-start | bytes 1105928 | tf_op jit(solution)/shard_map/ppermute | solution.py:388
  103.8 4.5 %back.6 = (bf16[72,2560]{1,0:T(8,128)(2,1)S(1)}, bf16[72,2560]{1,0:T(8,128)(2,1)S(1)}, bf16[72,2560]{1,0:T(8,128)(2,1)S(1)}, bf16[72,2560]{1,0:T(8,128)(2,1)S(1)...) custom-call(s32[32]{0:T(128)S(1)} %copy-done.2, bf16[288,1536]{1,0:T(8,128)(2,1)S(1)} %get-tuple-element.98.refs_0_.refs_2_, ...), custom_call_target="tpu_custom_call" | custom-call | flops 20000000000 | bytes 200000000 | tf_op jit(solution)/shard_map/back/pallas_call | solution.py:507
  109.4 6.6 %collective-permute-done.26.refs_2_ = bf16[72,2560]{1,0:T(8,128)(2,1)S(1)} collective-permute-done((bf16[72,2560]{1,0:T(8,128)(2,1)S(1)}, bf16[72,2560]{1,0:T(8,128)(2,1)S(1)}, u32[]{:S(2)}, u32[]{:S(2)}) %collective-permute-start.26) | collective-permute-done | bytes 368672 | tf_op jit(solution)/shard_map/ppermute | solution.py:388
  116.0 2.5 %collective-permute-start.24 = (bf16[72,2560]{1,0:T(8,128)(2,1)S(1)}, bf16[72,2560]{1,0:T(8,128)(2,1)S(1)}, u32[]{:S(2)}, u32[]{:S(2)}) collective-permute-start(bf16[72,2560]{1,0:T(8,128)(2,1)S(1)} %get-tuple-element.110), channel_id=1, source_target_pairs={{0,6},{2,4},{4,2},{6,0},{8,14},{10,12},{12,10},{14,8},{16,22},{18,... | collective-permute-start | bytes 1105928 | tf_op jit(solution)/shard_map/ppermute | solution.py:388
  119.7 4.8 %back.7 = (bf16[72,2688]{1,0:T(8,128)(2,1)S(1)}, bf16[72,2688]{1,0:T(8,128)(2,1)S(1)}, bf16[72,2688]{1,0:T(8,128)(2,1)S(1)}, bf16[72,2688]{1,0:T(8,128)(2,1)S(1)...) custom-call(s32[32]{0:T(128)S(1)} %copy-done.2, bf16[288,1536]{1,0:T(8,128)(2,1)S(1)} %get-tuple-element.96.refs_0_.refs_2_, ...), custom_call_target="tpu_custom_call" | custom-call | flops 20000000000 | bytes 200000000 | tf_op jit(solution)/shard_map/back/pallas_call | solution.py:507
  124.5 1.6 %collective-permute-start.31 = (bf16[72,2688]{1,0:T(8,128)(2,1)S(1)}, bf16[72,2688]{1,0:T(8,128)(2,1)S(1)}, u32[]{:S(2)}, u32[]{:S(2)}) collective-permute-start(bf16[72,2688]{1,0:T(8,128)(2,1)S(1)} %get-tuple-element.121), channel_id=1, source_target_pairs={{0,2},{2,0},{4,6},{6,4},{8,10},{10,8},{12,14},{14,12},{16,18},{18,... | collective-permute-start | bytes 1161224 | tf_op jit(solution)/shard_map/ppermute | solution.py:388
  126.6 5.1 %collective-permute-done.23.refs_2_ = bf16[72,2560]{1,0:T(8,128)(2,1)S(1)} collective-permute-done((bf16[72,2560]{1,0:T(8,128)(2,1)S(1)}, bf16[72,2560]{1,0:T(8,128)(2,1)S(1)}, u32[]{:S(2)}, u32[]{:S(2)}) %collective-permute-start.23) | collective-permute-done | bytes 368672 | tf_op jit(solution)/shard_map/ppermute | solution.py:388
  131.7 2.5 %collective-permute-start.33 = (bf16[72,2688]{1,0:T(8,128)(2,1)S(1)}, bf16[72,2688]{1,0:T(8,128)(2,1)S(1)}, u32[]{:S(2)}, u32[]{:S(2)}) collective-permute-start(bf16[72,2688]{1,0:T(8,128)(2,1)S(1)} %get-tuple-element.123), channel_id=1, source_target_pairs={{0,6},{2,4},{4,2},{6,0},{8,14},{10,12},{12,10},{14,8},{16,22},{18,... | collective-permute-start | bytes 1161224 | tf_op jit(solution)/shard_map/ppermute | solution.py:388
  136.8 9.5 %grad_up.1 = (bf16[2,2048,1024]{2,1,0:T(8,128)(2,1)}, f32[8,128]{1,0:T(8,128)S(1)}) custom-call(s32[32]{0:T(128)S(1)} %copy-done.2, bf16[192,2048]{1,0:T(8,128)(2,1)S(1)} %get-tuple-element.126.refs_0_, bf16[192,2048]{1,0:T(8,128)(2,1)S(1)} %get-tuple-element.127.refs_1_, bf16[192,2048]{1,0:T(8,128)(2,1)S(1)} %get-tuple-element.128.refs_2_, ...), custom_call_target="tpu_custom_call" | custom-call | flops 20000000000 | bytes 200000000 | tf_op jit(solution)/shard_map/grad_up/pallas_call | solution.py:548
  146.3 1.7 %collective-permute-done.32.refs_2_ = bf16[72,2688]{1,0:T(8,128)(2,1)S(1)} collective-permute-done((bf16[72,2688]{1,0:T(8,128)(2,1)S(1)}, bf16[72,2688]{1,0:T(8,128)(2,1)S(1)}, u32[]{:S(2)}, u32[]{:S(2)}) %collective-permute-start.32) | collective-permute-done | bytes 387104 | tf_op jit(solution)/shard_map/ppermute | solution.py:388
  148.5 3.6 %collective-permute-done.30.refs_0_ = bf16[128,2688]{1,0:T(8,128)(2,1)S(1)} collective-permute-done((bf16[128,2688]{1,0:T(8,128)(2,1)S(1)}, bf16[128,2688]{1,0:T(8,128)(2,1)S(1)}, u32[]{:S(2)}, u32[]{:S(2)}) %collective-permute-start.30) | collective-permute-done | bytes 688160 | tf_op jit(solution)/shard_map/ppermute | solution.py:384
  (77 shorter events, 32.8 us)
Async XLA Ops:
  4.4 20.7 %collective-permute-start = (bf16[128,2688]{1,0:T(8,128)(2,1)}, bf16[128,2688]{1,0:T(8,128)(2,1)S(1)}, u32[]{:S(2)}, u32[]{:S(2)}) collective-permute-start(bf16[128,2688]{1,0:T(8,128)(2,1)} %get-tuple-element.72), channel_id=1, source_target_pairs={{0,8},{2,10},{4,12},{6,14},{8,16},{10,18},{12,20},{14,22},{16,24},... | collective-permute-start | bytes 2064392 | tf_op jit(solution)/shard_map/ppermute | solution.py:384
  7.5 20.8 %collective-permute-start.6 = (bf16[72,2560]{1,0:T(8,128)(2,1)}, bf16[72,2560]{1,0:T(8,128)(2,1)S(1)}, u32[]{:S(2)}, u32[]{:S(2)}) collective-permute-start(bf16[72,2560]{1,0:T(8,128)(2,1)} %get-tuple-element.78), channel_id=1, source_target_pairs={{0,2},{2,0},{4,6},{6,4},{8,10},{10,8},{12,14},{14,12},{16,18},{18,... | collective-permute-start | bytes 1105928 | tf_op jit(solution)/shard_map/ppermute | solution.py:388
  9.0 20.8 %collective-permute-start.7 = (bf16[72,2560]{1,0:T(8,128)(2,1)}, bf16[72,2560]{1,0:T(8,128)(2,1)S(1)}, u32[]{:S(2)}, u32[]{:S(2)}) collective-permute-start(bf16[72,2560]{1,0:T(8,128)(2,1)} %get-tuple-element.79), channel_id=1, source_target_pairs={{0,4},{2,6},{4,0},{6,2},{8,12},{10,14},{12,8},{14,10},{16,20},{18,... | collective-permute-start | bytes 1105928 | tf_op jit(solution)/shard_map/ppermute | solution.py:388
  10.5 19.8 %collective-permute-start.8 = (bf16[72,2560]{1,0:T(8,128)(2,1)}, bf16[72,2560]{1,0:T(8,128)(2,1)S(1)}, u32[]{:S(2)}, u32[]{:S(2)}) collective-permute-start(bf16[72,2560]{1,0:T(8,128)(2,1)} %get-tuple-element.80), channel_id=1, source_target_pairs={{0,6},{2,4},{4,2},{6,0},{8,14},{10,12},{12,10},{14,8},{16,22},{18,... | collective-permute-start | bytes 1105928 | tf_op jit(solution)/shard_map/ppermute | solution.py:388
  25.2 18.4 %collective-permute-start.1 = (bf16[128,2688]{1,0:T(8,128)(2,1)S(1)}, bf16[128,2688]{1,0:T(8,128)(2,1)S(1)}, u32[]{:S(2)}, u32[]{:S(2)}) collective-permute-start(bf16[128,2688]{1,0:T(8,128)(2,1)S(1)} %collective-permute-done.refs_0_.refs_6_), channel_id=1, source_target_pairs={{0,8},{2,10},{4,12},{6,14},{8,16},{10,18},{12,20},{14,22},{16,24},... | collective-permute-start | bytes 2064392 | tf_op jit(solution)/shard_map/ppermute | solution.py:384
  26.7 18.4 %collective-permute-start.3 = (bf16[72,2560]{1,0:T(8,128)(2,1)S(1)}, bf16[72,2560]{1,0:T(8,128)(2,1)S(1)}, u32[]{:S(2)}, u32[]{:S(2)}) collective-permute-start(bf16[72,2560]{1,0:T(8,128)(2,1)S(1)} %get-tuple-element.74), channel_id=1, source_target_pairs={{0,2},{2,0},{4,6},{6,4},{8,10},{10,8},{12,14},{14,12},{16,18},{18,... | collective-permute-start | bytes 1105928 | tf_op jit(solution)/shard_map/ppermute | solution.py:388
  28.3 18.2 %collective-permute-start.4 = (bf16[72,2560]{1,0:T(8,128)(2,1)S(1)}, bf16[72,2560]{1,0:T(8,128)(2,1)S(1)}, u32[]{:S(2)}, u32[]{:S(2)}) collective-permute-start(bf16[72,2560]{1,0:T(8,128)(2,1)S(1)} %get-tuple-element.75), channel_id=1, source_target_pairs={{0,4},{2,6},{4,0},{6,2},{8,12},{10,14},{12,8},{14,10},{16,20},{18,... | collective-permute-start | bytes 1105928 | tf_op jit(solution)/shard_map/ppermute | solution.py:388
  29.8 18.2 %collective-permute-start.5 = (bf16[72,2560]{1,0:T(8,128)(2,1)S(1)}, bf16[72,2560]{1,0:T(8,128)(2,1)S(1)}, u32[]{:S(2)}, u32[]{:S(2)}) collective-permute-start(bf16[72,2560]{1,0:T(8,128)(2,1)S(1)} %get-tuple-element.76), channel_id=1, source_target_pairs={{0,6},{2,4},{4,2},{6,0},{8,14},{10,12},{12,10},{14,8},{16,22},{18,... | collective-permute-start | bytes 1105928 | tf_op jit(solution)/shard_map/ppermute | solution.py:388
  34.1 34.9 %collective-permute-start.16 = (bf16[288,1536]{1,0:T(8,128)(2,1)S(1)}, bf16[288,1536]{1,0:T(8,128)(2,1)S(1)}, u32[]{:S(2)}, u32[]{:S(2)}) collective-permute-start(bf16[288,1536]{1,0:T(8,128)(2,1)S(1)} %get-tuple-element.96.refs_0_.refs_2_), channel_id=1, source_target_pairs={{0,1},{1,0},{2,3},{3,2},{4,5},{5,4},{6,7},{7,6},{8,9},{9,8},{10,11... | collective-permute-start | bytes 2654216 | tf_op jit(solution)/shard_map/ppermute | solution.py:497
  43.6 17.5 %collective-permute-start.2 = (bf16[128,2688]{1,0:T(8,128)(2,1)S(1)}, bf16[128,2688]{1,0:T(8,128)(2,1)S(1)}, u32[]{:S(2)}, u32[]{:S(2)}) collective-permute-start(bf16[128,2688]{1,0:T(8,128)(2,1)S(1)} %collective-permute-done.1.refs_0_.refs_6_), channel_id=1, source_target_pairs={{0,8},{2,10},{4,12},{6,14},{8,16},{10,18},{12,20},{14,22},{16,24},... | collective-permute-start | bytes 2064392 | tf_op jit(solution)/shard_map/ppermute | solution.py:384
  62.7 19.0 %collective-permute-start.10 = (bf16[72,2560]{1,0:T(8,128)(2,1)S(1)}, bf16[72,2560]{1,0:T(8,128)(2,1)S(1)}, u32[]{:S(2)}, u32[]{:S(2)}) collective-permute-start(bf16[72,2560]{1,0:T(8,128)(2,1)S(1)} %get-tuple-element.87), channel_id=1, source_target_pairs={{0,4},{2,6},{4,0},{6,2},{8,12},{10,14},{12,8},{14,10},{16,20},{18,... | collective-permute-start | bytes 1105928 | tf_op jit(solution)/shard_map/ppermute | solution.py:388
  63.8 18.9 %collective-permute-start.11 = (bf16[72,2560]{1,0:T(8,128)(2,1)S(1)}, bf16[72,2560]{1,0:T(8,128)(2,1)S(1)}, u32[]{:S(2)}, u32[]{:S(2)}) collective-permute-start(bf16[72,2560]{1,0:T(8,128)(2,1)S(1)} %get-tuple-element.88), channel_id=1, source_target_pairs={{0,6},{2,4},{4,2},{6,0},{8,14},{10,12},{12,10},{14,8},{16,22},{18,... | collective-permute-start | bytes 1105928 | tf_op jit(solution)/shard_map/ppermute | solution.py:388
  65.2 18.9 %collective-permute-start.9 = (bf16[72,2560]{1,0:T(8,128)(2,1)S(1)}, bf16[72,2560]{1,0:T(8,128)(2,1)S(1)}, u32[]{:S(2)}, u32[]{:S(2)}) collective-permute-start(bf16[72,2560]{1,0:T(8,128)(2,1)S(1)} %get-tuple-element.86), channel_id=1, source_target_pairs={{0,2},{2,0},{4,6},{6,4},{8,10},{10,8},{12,14},{14,12},{16,18},{18,... | collective-permute-start | bytes 1105928 | tf_op jit(solution)/shard_map/ppermute | solution.py:388
  69.1 18.0 %collective-permute-start.21 = (bf16[288,1536]{1,0:T(8,128)(2,1)S(1)}, bf16[288,1536]{1,0:T(8,128)(2,1)S(1)}, u32[]{:S(2)}, u32[]{:S(2)}) collective-permute-start(bf16[288,1536]{1,0:T(8,128)(2,1)S(1)} %get-tuple-element.104.refs_0_.refs_2_), channel_id=1, source_target_pairs={{0,1},{1,0},{2,3},{3,2},{4,5},{5,4},{6,7},{7,6},{8,9},{9,8},{10,11... | collective-permute-start | bytes 2654216 | tf_op jit(solution)/shard_map/ppermute | solution.py:497
  73.7 19.0 %collective-permute-start.18 = (bf16[72,2560]{1,0:T(8,128)(2,1)S(1)}, bf16[72,2560]{1,0:T(8,128)(2,1)S(1)}, u32[]{:S(2)}, u32[]{:S(2)}) collective-permute-start(bf16[72,2560]{1,0:T(8,128)(2,1)S(1)} %get-tuple-element.100), channel_id=1, source_target_pairs={{0,2},{2,0},{4,6},{6,4},{8,10},{10,8},{12,14},{14,12},{16,18},{18,... | collective-permute-start | bytes 1105928 | tf_op jit(solution)/shard_map/ppermute | solution.py:388
  81.6 18.6 %collective-permute-start.19 = (bf16[72,2560]{1,0:T(8,128)(2,1)S(1)}, bf16[72,2560]{1,0:T(8,128)(2,1)S(1)}, u32[]{:S(2)}, u32[]{:S(2)}) collective-permute-start(bf16[72,2560]{1,0:T(8,128)(2,1)S(1)} %get-tuple-element.101), channel_id=1, source_target_pairs={{0,4},{2,6},{4,0},{6,2},{8,12},{10,14},{12,8},{14,10},{16,20},{18,... | collective-permute-start | bytes 1105928 | tf_op jit(solution)/shard_map/ppermute | solution.py:388
  82.7 20.0 %collective-permute-start.20 = (bf16[72,2560]{1,0:T(8,128)(2,1)S(1)}, bf16[72,2560]{1,0:T(8,128)(2,1)S(1)}, u32[]{:S(2)}, u32[]{:S(2)}) collective-permute-start(bf16[72,2560]{1,0:T(8,128)(2,1)S(1)} %get-tuple-element.102), channel_id=1, source_target_pairs={{0,6},{2,4},{4,2},{6,0},{8,14},{10,12},{12,10},{14,8},{16,22},{18,... | collective-permute-start | bytes 1105928 | tf_op jit(solution)/shard_map/ppermute | solution.py:388
  92.7 23.3 %collective-permute-start.26 = (bf16[72,2560]{1,0:T(8,128)(2,1)S(1)}, bf16[72,2560]{1,0:T(8,128)(2,1)S(1)}, u32[]{:S(2)}, u32[]{:S(2)}) collective-permute-start(bf16[72,2560]{1,0:T(8,128)(2,1)S(1)} %get-tuple-element.114), channel_id=1, source_target_pairs={{0,4},{2,6},{4,0},{6,2},{8,12},{10,14},{12,8},{14,10},{16,20},{18,... | collective-permute-start | bytes 1105928 | tf_op jit(solution)/shard_map/ppermute | solution.py:388
  100.2 18.3 %collective-permute-start.27 = (bf16[72,2560]{1,0:T(8,128)(2,1)S(1)}, bf16[72,2560]{1,0:T(8,128)(2,1)S(1)}, u32[]{:S(2)}, u32[]{:S(2)}) collective-permute-start(bf16[72,2560]{1,0:T(8,128)(2,1)S(1)} %get-tuple-element.115), channel_id=1, source_target_pairs={{0,6},{2,4},{4,2},{6,0},{8,14},{10,12},{12,10},{14,8},{16,22},{18,... | collective-permute-start | bytes 1105928 | tf_op jit(solution)/shard_map/ppermute | solution.py:388
  108.4 17.7 %collective-permute-start.22 = (bf16[72,2560]{1,0:T(8,128)(2,1)S(1)}, bf16[72,2560]{1,0:T(8,128)(2,1)S(1)}, u32[]{:S(2)}, u32[]{:S(2)}) collective-permute-start(bf16[72,2560]{1,0:T(8,128)(2,1)S(1)} %get-tuple-element.108), channel_id=1, source_target_pairs={{0,2},{2,0},{4,6},{6,4},{8,10},{10,8},{12,14},{14,12},{16,18},{18,... | collective-permute-start | bytes 1105928 | tf_op jit(solution)/shard_map/ppermute | solution.py:388
  108.5 23.2 %collective-permute-start.23 = (bf16[72,2560]{1,0:T(8,128)(2,1)S(1)}, bf16[72,2560]{1,0:T(8,128)(2,1)S(1)}, u32[]{:S(2)}, u32[]{:S(2)}) collective-permute-start(bf16[72,2560]{1,0:T(8,128)(2,1)S(1)} %get-tuple-element.109), channel_id=1, source_target_pairs={{0,4},{2,6},{4,0},{6,2},{8,12},{10,14},{12,8},{14,10},{16,20},{18,... | collective-permute-start | bytes 1105928 | tf_op jit(solution)/shard_map/ppermute | solution.py:388
  116.0 18.2 %collective-permute-start.24 = (bf16[72,2560]{1,0:T(8,128)(2,1)S(1)}, bf16[72,2560]{1,0:T(8,128)(2,1)S(1)}, u32[]{:S(2)}, u32[]{:S(2)}) collective-permute-start(bf16[72,2560]{1,0:T(8,128)(2,1)S(1)} %get-tuple-element.110), channel_id=1, source_target_pairs={{0,6},{2,4},{4,2},{6,0},{8,14},{10,12},{12,10},{14,8},{16,22},{18,... | collective-permute-start | bytes 1105928 | tf_op jit(solution)/shard_map/ppermute | solution.py:388
  124.5 21.8 %collective-permute-start.31 = (bf16[72,2688]{1,0:T(8,128)(2,1)S(1)}, bf16[72,2688]{1,0:T(8,128)(2,1)S(1)}, u32[]{:S(2)}, u32[]{:S(2)}) collective-permute-start(bf16[72,2688]{1,0:T(8,128)(2,1)S(1)} %get-tuple-element.121), channel_id=1, source_target_pairs={{0,2},{2,0},{4,6},{6,4},{8,10},{10,8},{12,14},{14,12},{16,18},{18,... | collective-permute-start | bytes 1161224 | tf_op jit(solution)/shard_map/ppermute | solution.py:388
  126.1 21.9 %collective-permute-start.32 = (bf16[72,2688]{1,0:T(8,128)(2,1)S(1)}, bf16[72,2688]{1,0:T(8,128)(2,1)S(1)}, u32[]{:S(2)}, u32[]{:S(2)}) collective-permute-start(bf16[72,2688]{1,0:T(8,128)(2,1)S(1)} %get-tuple-element.122), channel_id=1, source_target_pairs={{0,4},{2,6},{4,0},{6,2},{8,12},{10,14},{12,8},{14,10},{16,20},{18,... | collective-permute-start | bytes 1161224 | tf_op jit(solution)/shard_map/ppermute | solution.py:388
  (17 other events, 273.9 us)

commit v6 on v5

--- a/solution.py
+++ b/solution.py
@@ -11,7 +11,6 @@
 CHUNKS = 4
 PLAN = ((0, None), (1, None), (2, None), (3, None), (None, 1), (None, 2), (None, 3), (None, 0))
 ORDER = ('x1', 'h0', 'x2', 'h1', 'x3', 'h2', 'r0', 'x4', 'h3', 'x5', 'r3', 'e1', 'x6', 'e2', 'r2', 'x7', 'e3', 'u', 'e0')
-PASSED = ()
 FIRST = 1
 COSTS = {'x': 5000, 'b': 20000, 'h': 5000, 'e': 1, 'u': 20000}
 TAIL = 128
@@ -85,21 +84,21 @@
     return found
 
 
-def picked(picks, payloads, columns):
+def picked(picks, sources, columns):
     total = None
-    for pick, payload in zip(picks, payloads):
+    for pick, source in zip(picks, sources):
         part = lax.dot_general(
-            pick[...], payload[:, columns], (((0,), (0,)), ((), ())), preferred_element_type=F32
+            pick[...], source[:, columns], (((0,), (0,)), ((), ())), preferred_element_type=F32
         )
         total = part if total is None else total + part
     return total
 
 
-def select_all(m, hot_rows, cold_rows, topk, share, plan, picks, payloads, outs, marks):
+def select_all(m, hot_rows, cold_rows, topk, share, plan, picks, tokens, rests, outs, marks):
     rows, width = outs[0].shape
     feat = width - share
     expert, _, _ = row_plan(m, hot_rows, cold_rows, plan, (INNER * rows, TAIL), 0)
-    tail = picked(picks, payloads, slice(width, width + TAIL))
+    tail = picked(picks, rests, slice(share, share + TAIL))
     gate = (tail[:, 2 * topk : 3 * topk] + tail[:, 3 * topk : 4 * topk]) + tail[:, 4 * topk : 5 * topk]
     gate = jnp.sum(jnp.where(tail[:, :topk] == expert[:, :topk], gate, 0.0), 1, keepdims=True)
     lane = lax.broadcasted_iota(I32, tail.shape, 1)
@@ -107,18 +106,20 @@
     marks[...] = jnp.where(lane == 2 * topk, gate, own)
     step = 512 if feat % 512 == 0 else 128
     for at in [*range(0, feat, step), feat]:
-        columns = slice(at, at + step) if at < feat else slice(feat, width)
-        total = picked(picks, payloads, columns)
-        if at == feat:
-            total = gate * total
+        if at < feat:
+            columns = slice(at, at + step)
+            total = picked(picks, tokens, columns)
+        else:
+            columns = slice(feat, width)
+            total = gate * picked(picks, rests, slice(0, share))
         for d in range(INNER):
             outs[d][:, columns] = total[d * rows : (d + 1) * rows].astype(BF16)
 
 
 def start_kernel(m, hot_rows, cold_rows, plan, tokens, routes, gates, grad_out, *refs):
     out, refs = refs[0], refs[1:]
-    here_routes, here_gates, sems = refs[-3:]
-    outs, marks, picks = refs[:INNER], refs[INNER:-3][:1], refs[INNER:-3][1:]
+    here, here_routes, here_gates, sems = refs[-4:]
+    outs, marks, picks = refs[:INNER], refs[INNER:-4][:1], refs[INNER:-4][1:]
     count, feat = tokens.shape
     share = grad_out.shape[1]
     topk = routes.shape[0]
@@ -128,8 +129,8 @@
             (
                 (routes, here_routes),
                 (gates, here_gates),
-                (tokens, out.at[:, :feat]),
-                (grad_out, out.at[:, feat : feat + share]),
+                (tokens, here),
+                (grad_out, out.at[:, :share]),
             )
         )
     ]
@@ -144,25 +145,24 @@
     low = (gate - high - middle).astype(BF16).astype(F32)
     rest = jnp.zeros((TAIL - 5 * topk, count), F32)
     tail = jnp.concatenate([ids, ids, high, middle, low, rest], 0).T
-    out[:, feat + share :] = tail.astype(BF16)
+    out[:, share:] = tail.astype(BF16)
     if picks:
         picks[0][...] = pick_rows(m, hot_rows, cold_rows, topk, plan, [tail])[0]
     for copy in copies[2:]:
         copy.wait()
     if picks:
-        select_all(m, hot_rows, cold_rows, topk, share, plan, picks, [out], outs, marks[0])
+        select_all(
+            m, hot_rows, cold_rows, topk, share, plan, picks, [here], [out], outs, marks[0]
+        )
 
 
 def select_kernel(m, hot_rows, cold_rows, topk, share, waits, plan, *refs):
-    payloads, refs = refs[:m], refs[m + waits :]
-    outs, marks, picks, passed = refs[:INNER], refs[INNER], refs[INNER + 1 : INNER + 1 + m], refs[INNER + 1 + m :]
-    width = payloads[0].shape[1]
-    for source, target in zip(payloads, passed):
-        target[...] = source[...]
-    tails = [payload[:, width - TAIL :].astype(F32) for payload in payloads]
+    tokens, rests, refs = refs[:m], refs[m : 2 * m], refs[2 * m + waits :]
+    outs, marks, picks = refs[:INNER], refs[INNER], refs[INNER + 1 :]
+    tails = [rest[:, share:].astype(F32) for rest in rests]
     for pick, found in zip(picks, pick_rows(m, hot_rows, cold_rows, topk, plan, tails)):
         pick[...] = found
-    select_all(m, hot_rows, cold_rows, topk, share, plan, picks, payloads, outs, marks)
+    select_all(m, hot_rows, cold_rows, topk, share, plan, picks, tokens, rests, outs, marks)
 
 
 def hidden_kernel(m, hot_rows, cold_rows, feat, streamed, waits, plan, *refs):
@@ -272,9 +272,10 @@
     lax.fori_loop(0, feat // tile, features, 0)
 
 
-def expand_kernel(m, topk, share, tailed, n_more, waits, *refs):
+def expand_kernel(m, topk, share, c, n_more, waits, *refs):
     blocks, picks, marks, refs = refs[:INNER], refs[INNER : INNER + m], refs[INNER + m], refs[INNER + m + 1 :]
-    payloads, refs = ([], refs) if tailed else (refs[:m], refs[m:])
+    tailed = c == 0
+    rests, refs = ([], refs) if tailed else (refs[:m], refs[m:])
     more, outs, apart = refs[:n_more], refs[n_more + waits :][:m], refs[n_more + waits + m :]
     width = outs[0].shape[1]
     feat = width - share - TAIL
@@ -304,7 +305,7 @@
         end = joined(columns).astype(F32)
         gate_grad = (end[:, 0:1] + end[:, 1:2]) / jnp.where(gate > 0.0, gate, 1.0)
     else:
-        grad = picked(picks, payloads, slice(feat, feat + share))
+        grad = picked(picks, rests, slice(0, share))
         gate_grad = jnp.sum(act * grad, 1, keepdims=True)
     high = gate_grad.astype(BF16).astype(F32)
     lane = lax.broadcasted_iota(I32, mark.shape, 1)
@@ -416,7 +417,7 @@
     own_rows = m == 1
     made = pl.pallas_call(
         functools.partial(start_kernel, *sizes),
-        out_shape=[block((count, width))]
+        out_shape=[block((count, share + TAIL))]
         + (
             [block((rows, there))] * INNER
             + [block((INNER * rows, TAIL), F32), block((count, INNER * rows))]
@@ -426,6 +427,7 @@
         in_specs=[smem] + [rest_spec] * 4,
         out_specs=whole_specs(1 + (INNER + 2 if own_rows else 0)),
         scratch_shapes=[
+            pltpu.VMEM((count, feat), BF16),
             pltpu.VMEM((topk, count), I32),
             pltpu.VMEM((topk, count), F32),
             pltpu.SemaphoreType.DMA((4,)),
@@ -434,35 +436,40 @@
         cost_estimate=weigh("x"),
         name="start",
     )(replica_on, tokens, routes.T, gates.T, grad_out)
-    payload = made[0]
+    groups = [[o * INNER + i for o in range(outer)] for i in range(INNER)]
+    column = lax.all_gather(made[0], "ep", axis_index_groups=groups)
+    here = lax.axis_index("ep") // INNER
+    rests = [
+        lax.dynamic_index_in_dim(column, (here + outer - s) % outer, 0, keepdims=False)
+        for s in range(outer)
+    ]
+
+    def rests_of(c):
+        return [rests[s] for s in chunks[c]]
+
     last = []
     for c in range(n):
-        for s in chunks[c] if c not in PASSED else ():
+        for s in chunks[c]:
             if s == 0:
-                arrived[s] = payload
+                arrived[s] = tokens
             else:
-                arrived[s] = along(arrived[s - m], m) if c else along(payload, s)
+                arrived[s] = along(arrived[s - m], m) if c else along(tokens, s)
 
     def select(k):
         c = PLAN[k][0]
-        more = m if c + 1 in PASSED else 0
         made = pl.pallas_call(
             functools.partial(select_kernel, *sizes, topk, share, len(last)),
             out_shape=[block((rows, there))] * INNER
             + [block((INNER * rows, TAIL), F32)]
-            + [block((count, INNER * rows))] * m
-            + [block((count, width))] * more,
-            in_specs=[smem] + whole_specs(m) + [rest_spec] * len(last),
-            out_specs=whole_specs(INNER + 1 + m + more),
+            + [block((count, INNER * rows))] * m,
+            in_specs=[smem] + whole_specs(2 * m) + [rest_spec] * len(last),
+            out_specs=whole_specs(INNER + 1 + m),
             compiler_params=params(),
             cost_estimate=weigh("x"),
             name="select",
-        )(replica_on, *[arrived[s] for s in chunks[c]], *last)
-        marks[c], picks[c] = made[INNER], made[INNER + 1 : INNER + 1 + m]
+        )(replica_on, *[arrived[s] for s in chunks[c]], *rests_of(c), *last)
+        marks[c], picks[c] = made[INNER], made[INNER + 1 :]
         exchange(k, made)
-        if more:
-            for s, value in zip(chunks[c + 1], made[INNER + 1 + m :]):
-                arrived[s] = along(value, m)
         last[:] = [picks[c][0]]
 
     def hidden(c):
@@ -524,19 +531,19 @@
 
     def expand(c):
         more = [along(partials[s - m], m) for s in chunks[c]] if c > 1 else []
-        payloads = [arrived[s] for s in chunks[c]] if c else []
+        sources = rests_of(c) if c else []
         apart = [block((count, TAIL))] if c == n - 1 and by_hand else []
         k = coming[c]
         made = pl.pallas_call(
-            functools.partial(expand_kernel, m, topk, share, c == 0, len(more), len(last)),
+            functools.partial(expand_kernel, m, topk, share, c, len(more), len(last)),
             out_shape=[block((count, width))] * m + apart,
-            in_specs=whole_specs(INNER + m + 1 + len(payloads) + len(more))
+            in_specs=whole_specs(INNER + m + 1 + len(sources) + len(more))
             + [rest_spec] * len(last),
             out_specs=whole_specs(m + len(apart)),
             compiler_params=params(),
             cost_estimate=weigh("e"),
             name="expand",
-        )(*blocks[k], *picks[c], marks[c], *payloads, *more, *last)
+        )(*blocks[k], *picks[c], marks[c], *sources, *more, *last)
         for s, value in zip(chunks[c], made):
             partials[s] = value
         if apart:

time: 153 us -> 156 us (1.020)
  waiting for transfers between devices: 65.3 us -> 43.8 us
  blocking collectives: 0 us -> 18.6 us
  starting transfers between devices: 34.2 us -> 38.7 us
    ppermute x6, waiting for transfers between devices: 38.6 us -> 14.3 us  [along(): return lax.ppermute(value, 'ep', pairs)]
    all_gather x0 -> x1, blocking collectives: none -> 18.6 us  [on_device(): column = lax.all_gather(made[0], 'ep', axis_index_groups=groups)]
    ppermute x24, starting transfers between devices: 30.5 us -> 33 us  [across(): return lax.ppermute(value, 'ep', pairs)]
    ppermute x6, starting transfers between devices: 3.44 us -> 5.34 us  [along(): return lax.ppermute(value, 'ep', pairs)]
    ppermute x1, waiting for transfers between devices: 0.02 us -> 1.64 us  [on_device(): tails = [lax.ppermute(partials['apart'], ('ep', 'tp'), pairs)]]
  transfers between devices with their start and end apart: 35 -> 35, of which waited for: 11 -> 14; matrix products, arithmetic and copies ran while one was open for 0% -> 0% of each run, Pallas kernels for 31% -> 33%
where the time goes in v6:
time: 156 us; the launch traced here: 155 us
  Pallas kernels  52.8 us (34%)
  waiting for transfers between devices  43.8 us (28%)
  starting transfers between devices  38.7 us (25%)
  blocking collectives  18.6 us (12%)
    ppermute x24, starting transfers between devices, across(): return lax.ppermute(value, 'ep', pairs)  33 us
    ppermute x24, waiting for transfers between devices, across(): return lax.ppermute(value, 'ep', pairs)  27.9 us
    all_gather x1, blocking collectives, on_device(): column = lax.all_gather(made[0], 'ep', axis_index_groups=groups)  18.6 us
    pallas_call x4, Pallas kernels, step(): pl.pallas_call(functools.partial(back_kernel, *sizes, len(sums[c]), len(g...  18.3 us
    ppermute x6, waiting for transfers between devices, along(): return lax.ppermute(value, 'ep', pairs)  14.3 us
    pallas_call x4, Pallas kernels, hidden(): pl.pallas_call(functools.partial(hidden_kernel, *sizes, feat, streamed, l...  12.3 us
    pallas_call x1, Pallas kernels, weight_grad(): pl.pallas_call(functools.partial(up_kernel, n, len(last)), out_shape=[blo...  9.48 us
    ppermute x6, starting transfers between devices, along(): return lax.ppermute(value, 'ep', pairs)  5.34 us
  transfers between devices with their start and end apart: 35, of which 14 were waited for; matrix products, arithmetic and copies ran while one was open for 0% of the time, Pallas kernels for 33%

profile of v6, /device:TPU:0, one launch (start us, length us, event | category | flops | bytes accessed | tf_op | source)
XLA Modules:
  0.0 154.9 jit_solution(1627431167712189060)
XLA Ops:
  0.6 3.1 %collective-permute-start = (bf16[128,2048]{1,0:T(8,128)(2,1)}, bf16[128,2048]{1,0:T(8,128)(2,1)S(1)}, u32[]{:S(2)}, u32[]{:S(2)}) collective-permute-start(bf16[128,2048]{1,0:T(8,128)(2,1)} %tokens.1), channel_id=1, source_target_pairs={{0,8},{2,10},{4,12},{6,14},{8,16},{10,18},{12,20},{14,22},{16,24},... | collective-permute-start | bytes 1572872 | tf_op jit(solution)/shard_map/ppermute | solution.py:385
  3.7 3.8 %start.1 = (bf16[128,640]{1,0:T(8,128)(2,1)}, bf16[72,2560]{1,0:T(8,128)(2,1)}, bf16[72,2560]{1,0:T(8,128)(2,1)}, bf16[72,2560]{1,0:T(8,128)(2,1)}, bf16[72,2560...) custom-call(s32[32]{0:T(128)} %plan.25, bf16[128,2048]{1,0:T(8,128)(2,1)} %tokens.1, ...), custom_call_target="tpu_custom_call" | custom-call | flops 5000000000 | bytes 50000000 | tf_op jit(solution)/shard_map/start/pallas_call | solution.py:418
  11.1 18.6 %all-gather = bf16[512,640]{1,0:T(8,128)(2,1)S(1)} all-gather(bf16[128,640]{1,0:T(8,128)(2,1)} %get-tuple-element.72), channel_id=2, replica_groups={{0,8,16,24},{2,10,18,26},{4,12,20,28},{6,14,22,30},{1,9,17,25},{3,11,19..., dimensions={0}, use_global_device_ids=true | all-gather | bytes 819200 | tf_op jit(solution)/shard_map/all_gather | solution.py:440
  35.8 3.8 %hidden.4 = (bf16[288,1536]{1,0:T(8,128)(2,1)S(1)}, bf16[192,2048]{1,0:T(8,128)(2,1)S(1)}, bf16[96,2048]{1,0:T(8,128)(2,1)S(1)}) custom-call(s32[32]{0:T(128)S(1)} %copy-done.2, bf16[72,2560]{1,0:T(8,128)(2,1)S(1)} %copy-done.3, bf16[72,2560]{1,0:T(8,128)(2,1)S(1)} %collective-permute-done.6.refs_1_, bf16[72,2560]{1,0:T(8,128)(2,1)S(1)} %collective-permute-done.7.refs_2_, ...), custom_call_target="tpu_custom_call" | custom-call | flops 5000000000 | bytes 50000000 | tf_op jit(solution)/shard_map/hidden/pallas_call | solution.py:494
  39.7 3.7 %collective-permute-done.1.refs_0_ = bf16[128,2048]{1,0:T(8,128)(2,1)S(1)} collective-permute-done((bf16[128,2048]{1,0:T(8,128)(2,1)S(1)}, bf16[128,2048]{1,0:T(8,128)(2,1)S(1)}, u32[]{:S(2)}, u32[]{:S(2)}) %collective-permute-start.1) | collective-permute-done | bytes 524320 | tf_op jit(solution)/shard_map/ppermute | solution.py:385
  47.6 3.0 %collective-permute-start.14 = (bf16[72,2560]{1,0:T(8,128)(2,1)S(1)}, bf16[72,2560]{1,0:T(8,128)(2,1)S(1)}, u32[]{:S(2)}, u32[]{:S(2)}) collective-permute-start(bf16[72,2560]{1,0:T(8,128)(2,1)S(1)} %get-tuple-element.92), channel_id=1, source_target_pairs={{0,4},{2,6},{4,0},{6,2},{8,12},{10,14},{12,8},{14,10},{16,20},{18,... | collective-permute-start | bytes 1105928 | tf_op jit(solution)/shard_map/ppermute | solution.py:389
  53.5 2.8 %hidden.5 = (bf16[288,1536]{1,0:T(8,128)(2,1)S(1)}, bf16[192,2048]{1,0:T(8,128)(2,1)S(1)}, bf16[96,2048]{1,0:T(8,128)(2,1)S(1)}) custom-call(s32[32]{0:T(128)S(1)} %copy-done.2, bf16[72,2560]{1,0:T(8,128)(2,1)S(1)} %get-tuple-element.73.refs_0_, bf16[72,2560]{1,0:T(8,128)(2,1)S(1)} %collective-permute-done.3.refs_1_, ...), custom_call_target="tpu_custom_call" | custom-call | flops 5000000000 | bytes 50000000 | tf_op jit(solution)/shard_map/hidden/pallas_call | solution.py:494
  60.6 8.7 %collective-permute-done.14.refs_2_ = bf16[72,2560]{1,0:T(8,128)(2,1)S(1)} collective-permute-done((bf16[72,2560]{1,0:T(8,128)(2,1)S(1)}, bf16[72,2560]{1,0:T(8,128)(2,1)S(1)}, u32[]{:S(2)}, u32[]{:S(2)}) %collective-permute-start.14) | collective-permute-done | bytes 368672 | tf_op jit(solution)/shard_map/ppermute | solution.py:389
  70.6 2.6 %collective-permute-start.9 = (bf16[72,2560]{1,0:T(8,128)(2,1)S(1)}, bf16[72,2560]{1,0:T(8,128)(2,1)S(1)}, u32[]{:S(2)}, u32[]{:S(2)}) collective-permute-start(bf16[72,2560]{1,0:T(8,128)(2,1)S(1)} %get-tuple-element.86), channel_id=1, source_target_pairs={{0,2},{2,0},{4,6},{6,4},{8,10},{10,8},{12,14},{14,12},{16,18},{18,... | collective-permute-start | bytes 1105928 | tf_op jit(solution)/shard_map/ppermute | solution.py:389
  73.3 2.8 %hidden.6 = (bf16[288,1536]{1,0:T(8,128)(2,1)S(1)}, bf16[192,2048]{1,0:T(8,128)(2,1)S(1)}, bf16[96,2048]{1,0:T(8,128)(2,1)S(1)}) custom-call(s32[32]{0:T(128)S(1)} %copy-done.2, bf16[72,2560]{1,0:T(8,128)(2,1)S(1)} %get-tuple-element.90.refs_0_, bf16[72,2560]{1,0:T(8,128)(2,1)S(1)} %collective-permute-done.13.refs_1_, ...), custom_call_target="tpu_custom_call" | custom-call | flops 5000000000 | bytes 50000000 | tf_op jit(solution)/shard_map/hidden/pallas_call | solution.py:494
  76.2 4.5 %back.4 = (bf16[72,2560]{1,0:T(8,128)(2,1)S(1)}, bf16[72,2560]{1,0:T(8,128)(2,1)S(1)}, bf16[72,2560]{1,0:T(8,128)(2,1)S(1)}, bf16[72,2560]{1,0:T(8,128)(2,1)S(1)...) custom-call(s32[32]{0:T(128)S(1)} %copy-done.2, bf16[288,1536]{1,0:T(8,128)(2,1)S(1)} %get-tuple-element.89.refs_0_.refs_2_, ...), custom_call_target="tpu_custom_call" | custom-call | flops 20000000000 | bytes 200000000 | tf_op jit(solution)/shard_map/back/pallas_call | solution.py:514
  82.4 1.9 %collective-permute-start.20 = (bf16[72,2560]{1,0:T(8,128)(2,1)S(1)}, bf16[72,2560]{1,0:T(8,128)(2,1)S(1)}, u32[]{:S(2)}, u32[]{:S(2)}) collective-permute-start(bf16[72,2560]{1,0:T(8,128)(2,1)S(1)} %get-tuple-element.102), channel_id=1, source_target_pairs={{0,6},{2,4},{4,2},{6,0},{8,14},{10,12},{12,10},{14,8},{16,22},{18,... | collective-permute-start | bytes 1105928 | tf_op jit(solution)/shard_map/ppermute | solution.py:389
  84.3 2.8 %hidden.7 = (bf16[288,1536]{1,0:T(8,128)(2,1)S(1)}, bf16[192,2048]{1,0:T(8,128)(2,1)S(1)}, bf16[96,2048]{1,0:T(8,128)(2,1)S(1)}) custom-call(s32[32]{0:T(128)S(1)} %copy-done.2, bf16[72,2560]{1,0:T(8,128)(2,1)S(1)} %get-tuple-element.85.refs_0_, bf16[72,2560]{1,0:T(8,128)(2,1)S(1)} %collective-permute-done.9.refs_1_, ...), custom_call_target="tpu_custom_call" | custom-call | flops 5000000000 | bytes 50000000 | tf_op jit(solution)/shard_map/hidden/pallas_call | solution.py:494
  87.2 4.5 %back.5 = (bf16[72,2560]{1,0:T(8,128)(2,1)S(1)}, bf16[72,2560]{1,0:T(8,128)(2,1)S(1)}, bf16[72,2560]{1,0:T(8,128)(2,1)S(1)}, bf16[72,2560]{1,0:T(8,128)(2,1)S(1)...) custom-call(s32[32]{0:T(128)S(1)} %copy-done.2, bf16[288,1536]{1,0:T(8,128)(2,1)S(1)} %get-tuple-element.104.refs_0_.refs_2_, ...), custom_call_target="tpu_custom_call" | custom-call | flops 20000000000 | bytes 200000000 | tf_op jit(solution)/shard_map/back/pallas_call | solution.py:514
  93.4 6.7 %collective-permute-done.19.refs_2_ = bf16[72,2560]{1,0:T(8,128)(2,1)S(1)} collective-permute-done((bf16[72,2560]{1,0:T(8,128)(2,1)S(1)}, bf16[72,2560]{1,0:T(8,128)(2,1)S(1)}, u32[]{:S(2)}, u32[]{:S(2)}) %collective-permute-start.19) | collective-permute-done | bytes 368672 | tf_op jit(solution)/shard_map/ppermute | solution.py:389
  103.3 4.5 %back.6 = (bf16[72,2560]{1,0:T(8,128)(2,1)S(1)}, bf16[72,2560]{1,0:T(8,128)(2,1)S(1)}, bf16[72,2560]{1,0:T(8,128)(2,1)S(1)}, bf16[72,2560]{1,0:T(8,128)(2,1)S(1)...) custom-call(s32[32]{0:T(128)S(1)} %copy-done.2, bf16[288,1536]{1,0:T(8,128)(2,1)S(1)} %get-tuple-element.98.refs_0_.refs_2_, ...), custom_call_target="tpu_custom_call" | custom-call | flops 20000000000 | bytes 200000000 | tf_op jit(solution)/shard_map/back/pallas_call | solution.py:514
  110.6 5.4 %collective-permute-done.26.refs_2_ = bf16[72,2560]{1,0:T(8,128)(2,1)S(1)} collective-permute-done((bf16[72,2560]{1,0:T(8,128)(2,1)S(1)}, bf16[72,2560]{1,0:T(8,128)(2,1)S(1)}, u32[]{:S(2)}, u32[]{:S(2)}) %collective-permute-start.26) | collective-permute-done | bytes 368672 | tf_op jit(solution)/shard_map/ppermute | solution.py:389
  117.0 2.6 %collective-permute-done.28.refs_7_ = bf16[128,2688]{1,0:T(8,128)(2,1)S(1)} collective-permute-done((bf16[128,2688]{1,0:T(8,128)(2,1)S(1)}, bf16[128,2688]{1,0:T(8,128)(2,1)S(1)}, u32[]{:S(2)}, u32[]{:S(2)}) %collective-permute-start.28) | collective-permute-done | bytes 688160 | tf_op jit(solution)/shard_map/ppermute | solution.py:385
  120.6 4.8 %back.7 = (bf16[72,2688]{1,0:T(8,128)(2,1)S(1)}, bf16[72,2688]{1,0:T(8,128)(2,1)S(1)}, bf16[72,2688]{1,0:T(8,128)(2,1)S(1)}, bf16[72,2688]{1,0:T(8,128)(2,1)S(1)...) custom-call(s32[32]{0:T(128)S(1)} %copy-done.2, bf16[288,1536]{1,0:T(8,128)(2,1)S(1)} %get-tuple-element.96.refs_0_.refs_2_, ...), custom_call_target="tpu_custom_call" | custom-call | flops 20000000000 | bytes 200000000 | tf_op jit(solution)/shard_map/back/pallas_call | solution.py:514
  126.8 1.9 %collective-permute-start.32 = (bf16[72,2688]{1,0:T(8,128)(2,1)S(1)}, bf16[72,2688]{1,0:T(8,128)(2,1)S(1)}, u32[]{:S(2)}, u32[]{:S(2)}) collective-permute-start(bf16[72,2688]{1,0:T(8,128)(2,1)S(1)} %get-tuple-element.122), channel_id=1, source_target_pairs={{0,4},{2,6},{4,0},{6,2},{8,12},{10,14},{12,8},{14,10},{16,20},{18,... | collective-permute-start | bytes 1161224 | tf_op jit(solution)/shard_map/ppermute | solution.py:389
  128.7 3.1 %collective-permute-done.23.refs_2_ = bf16[72,2560]{1,0:T(8,128)(2,1)S(1)} collective-permute-done((bf16[72,2560]{1,0:T(8,128)(2,1)S(1)}, bf16[72,2560]{1,0:T(8,128)(2,1)S(1)}, u32[]{:S(2)}, u32[]{:S(2)}) %collective-permute-start.23) | collective-permute-done | bytes 368672 | tf_op jit(solution)/shard_map/ppermute | solution.py:389
  132.7 4.3 %collective-permute-done.29.refs_7_ = bf16[128,2688]{1,0:T(8,128)(2,1)S(1)} collective-permute-done((bf16[128,2688]{1,0:T(8,128)(2,1)S(1)}, bf16[128,2688]{1,0:T(8,128)(2,1)S(1)}, u32[]{:S(2)}, u32[]{:S(2)}) %collective-permute-start.29) | collective-permute-done | bytes 688160 | tf_op jit(solution)/shard_map/ppermute | solution.py:385
  138.0 9.5 %grad_up.1 = (bf16[2,2048,1024]{2,1,0:T(8,128)(2,1)}, f32[8,128]{1,0:T(8,128)S(1)}) custom-call(s32[32]{0:T(128)S(1)} %copy-done.2, bf16[192,2048]{1,0:T(8,128)(2,1)S(1)} %get-tuple-element.126.refs_0_, bf16[192,2048]{1,0:T(8,128)(2,1)S(1)} %get-tuple-element.127.refs_1_, bf16[192,2048]{1,0:T(8,128)(2,1)S(1)} %get-tuple-element.128.refs_2_, ...), custom_call_target="tpu_custom_call" | custom-call | flops 20000000000 | bytes 200000000 | tf_op jit(solution)/shard_map/grad_up/pallas_call | solution.py:555
  150.1 3.6 %collective-permute-done.30.refs_0_ = bf16[128,2688]{1,0:T(8,128)(2,1)S(1)} collective-permute-done((bf16[128,2688]{1,0:T(8,128)(2,1)S(1)}, bf16[128,2688]{1,0:T(8,128)(2,1)S(1)}, u32[]{:S(2)}, u32[]{:S(2)}) %collective-permute-start.30) | collective-permute-done | bytes 688160 | tf_op jit(solution)/shard_map/ppermute | solution.py:385
  (79 shorter events, 40.8 us)
Async XLA Ops:
  0.6 29.1 %collective-permute-start = (bf16[128,2048]{1,0:T(8,128)(2,1)}, bf16[128,2048]{1,0:T(8,128)(2,1)S(1)}, u32[]{:S(2)}, u32[]{:S(2)}) collective-permute-start(bf16[128,2048]{1,0:T(8,128)(2,1)} %tokens.1), channel_id=1, source_target_pairs={{0,8},{2,10},{4,12},{6,14},{8,16},{10,18},{12,20},{14,22},{16,24},... | collective-permute-start | bytes 1572872 | tf_op jit(solution)/shard_map/ppermute | solution.py:385
  7.5 26.5 %collective-permute-start.6 = (bf16[72,2560]{1,0:T(8,128)(2,1)}, bf16[72,2560]{1,0:T(8,128)(2,1)S(1)}, u32[]{:S(2)}, u32[]{:S(2)}) collective-permute-start(bf16[72,2560]{1,0:T(8,128)(2,1)} %get-tuple-element.78), channel_id=1, source_target_pairs={{0,2},{2,0},{4,6},{6,4},{8,10},{10,8},{12,14},{14,12},{16,18},{18,... | collective-permute-start | bytes 1105928 | tf_op jit(solution)/shard_map/ppermute | solution.py:389
  9.1 26.5 %collective-permute-start.7 = (bf16[72,2560]{1,0:T(8,128)(2,1)}, bf16[72,2560]{1,0:T(8,128)(2,1)S(1)}, u32[]{:S(2)}, u32[]{:S(2)}) collective-permute-start(bf16[72,2560]{1,0:T(8,128)(2,1)} %get-tuple-element.79), channel_id=1, source_target_pairs={{0,4},{2,6},{4,0},{6,2},{8,12},{10,14},{12,8},{14,10},{16,20},{18,... | collective-permute-start | bytes 1105928 | tf_op jit(solution)/shard_map/ppermute | solution.py:389
  10.6 25.2 %collective-permute-start.8 = (bf16[72,2560]{1,0:T(8,128)(2,1)}, bf16[72,2560]{1,0:T(8,128)(2,1)S(1)}, u32[]{:S(2)}, u32[]{:S(2)}) collective-permute-start(bf16[72,2560]{1,0:T(8,128)(2,1)} %get-tuple-element.80), channel_id=1, source_target_pairs={{0,6},{2,4},{4,2},{6,0},{8,14},{10,12},{12,10},{14,8},{16,22},{18,... | collective-permute-start | bytes 1105928 | tf_op jit(solution)/shard_map/ppermute | solution.py:389
  35.5 16.6 %collective-permute-start.5 = (bf16[72,2560]{1,0:T(8,128)(2,1)S(1)}, bf16[72,2560]{1,0:T(8,128)(2,1)S(1)}, u32[]{:S(2)}, u32[]{:S(2)}) collective-permute-start(bf16[72,2560]{1,0:T(8,128)(2,1)S(1)} %get-tuple-element.76), channel_id=1, source_target_pairs={{0,6},{2,4},{4,2},{6,0},{8,14},{10,12},{12,10},{14,8},{16,22},{18,... | collective-permute-start | bytes 1105928 | tf_op jit(solution)/shard_map/ppermute | solution.py:389
  39.6 36.4 %collective-permute-start.16 = (bf16[288,1536]{1,0:T(8,128)(2,1)S(1)}, bf16[288,1536]{1,0:T(8,128)(2,1)S(1)}, u32[]{:S(2)}, u32[]{:S(2)}) collective-permute-start(bf16[288,1536]{1,0:T(8,128)(2,1)S(1)} %get-tuple-element.96.refs_0_.refs_2_), channel_id=1, source_target_pairs={{0,1},{1,0},{2,3},{3,2},{4,5},{5,4},{6,7},{7,6},{8,9},{9,8},{10,11... | collective-permute-start | bytes 2654216 | tf_op jit(solution)/shard_map/ppermute | solution.py:504
  47.6 21.8 %collective-permute-start.14 = (bf16[72,2560]{1,0:T(8,128)(2,1)S(1)}, bf16[72,2560]{1,0:T(8,128)(2,1)S(1)}, u32[]{:S(2)}, u32[]{:S(2)}) collective-permute-start(bf16[72,2560]{1,0:T(8,128)(2,1)S(1)} %get-tuple-element.92), channel_id=1, source_target_pairs={{0,4},{2,6},{4,0},{6,2},{8,12},{10,14},{12,8},{14,10},{16,20},{18,... | collective-permute-start | bytes 1105928 | tf_op jit(solution)/shard_map/ppermute | solution.py:389
  52.1 18.5 %collective-permute-start.15 = (bf16[72,2560]{1,0:T(8,128)(2,1)S(1)}, bf16[72,2560]{1,0:T(8,128)(2,1)S(1)}, u32[]{:S(2)}, u32[]{:S(2)}) collective-permute-start(bf16[72,2560]{1,0:T(8,128)(2,1)S(1)} %get-tuple-element.93), channel_id=1, source_target_pairs={{0,6},{2,4},{4,2},{6,0},{8,14},{10,12},{12,10},{14,8},{16,22},{18,... | collective-permute-start | bytes 1105928 | tf_op jit(solution)/shard_map/ppermute | solution.py:389
  56.4 19.8 %collective-permute-start.12 = (bf16[288,1536]{1,0:T(8,128)(2,1)S(1)}, bf16[288,1536]{1,0:T(8,128)(2,1)S(1)}, u32[]{:S(2)}, u32[]{:S(2)}) collective-permute-start(bf16[288,1536]{1,0:T(8,128)(2,1)S(1)} %get-tuple-element.89.refs_0_.refs_2_), channel_id=1, source_target_pairs={{0,1},{1,0},{2,3},{3,2},{4,5},{5,4},{6,7},{7,6},{8,9},{9,8},{10,11... | collective-permute-start | bytes 2654216 | tf_op jit(solution)/shard_map/ppermute | solution.py:504
  58.8 22.0 %collective-permute-start.10 = (bf16[72,2560]{1,0:T(8,128)(2,1)S(1)}, bf16[72,2560]{1,0:T(8,128)(2,1)S(1)}, u32[]{:S(2)}, u32[]{:S(2)}) collective-permute-start(bf16[72,2560]{1,0:T(8,128)(2,1)S(1)} %get-tuple-element.87), channel_id=1, source_target_pairs={{0,4},{2,6},{4,0},{6,2},{8,12},{10,14},{12,8},{14,10},{16,20},{18,... | collective-permute-start | bytes 1105928 | tf_op jit(solution)/shard_map/ppermute | solution.py:389
  80.8 19.3 %collective-permute-start.19 = (bf16[72,2560]{1,0:T(8,128)(2,1)S(1)}, bf16[72,2560]{1,0:T(8,128)(2,1)S(1)}, u32[]{:S(2)}, u32[]{:S(2)}) collective-permute-start(bf16[72,2560]{1,0:T(8,128)(2,1)S(1)} %get-tuple-element.101), channel_id=1, source_target_pairs={{0,4},{2,6},{4,0},{6,2},{8,12},{10,14},{12,8},{14,10},{16,20},{18,... | collective-permute-start | bytes 1105928 | tf_op jit(solution)/shard_map/ppermute | solution.py:389
  82.4 18.9 %collective-permute-start.20 = (bf16[72,2560]{1,0:T(8,128)(2,1)S(1)}, bf16[72,2560]{1,0:T(8,128)(2,1)S(1)}, u32[]{:S(2)}, u32[]{:S(2)}) collective-permute-start(bf16[72,2560]{1,0:T(8,128)(2,1)S(1)} %get-tuple-element.102), channel_id=1, source_target_pairs={{0,6},{2,4},{4,2},{6,0},{8,14},{10,12},{12,10},{14,8},{16,22},{18,... | collective-permute-start | bytes 1105928 | tf_op jit(solution)/shard_map/ppermute | solution.py:389
  91.8 17.1 %collective-permute-start.25 = (bf16[72,2560]{1,0:T(8,128)(2,1)S(1)}, bf16[72,2560]{1,0:T(8,128)(2,1)S(1)}, u32[]{:S(2)}, u32[]{:S(2)}) collective-permute-start(bf16[72,2560]{1,0:T(8,128)(2,1)S(1)} %get-tuple-element.113), channel_id=1, source_target_pairs={{0,2},{2,0},{4,6},{6,4},{8,10},{10,8},{12,14},{14,12},{16,18},{18,... | collective-permute-start | bytes 1105928 | tf_op jit(solution)/shard_map/ppermute | solution.py:389
  92.2 23.8 %collective-permute-start.26 = (bf16[72,2560]{1,0:T(8,128)(2,1)S(1)}, bf16[72,2560]{1,0:T(8,128)(2,1)S(1)}, u32[]{:S(2)}, u32[]{:S(2)}) collective-permute-start(bf16[72,2560]{1,0:T(8,128)(2,1)S(1)} %get-tuple-element.114), channel_id=1, source_target_pairs={{0,4},{2,6},{4,0},{6,2},{8,12},{10,14},{12,8},{14,10},{16,20},{18,... | collective-permute-start | bytes 1105928 | tf_op jit(solution)/shard_map/ppermute | solution.py:389
  100.2 16.9 %collective-permute-start.27 = (bf16[72,2560]{1,0:T(8,128)(2,1)S(1)}, bf16[72,2560]{1,0:T(8,128)(2,1)S(1)}, u32[]{:S(2)}, u32[]{:S(2)}) collective-permute-start(bf16[72,2560]{1,0:T(8,128)(2,1)S(1)} %get-tuple-element.115), channel_id=1, source_target_pairs={{0,6},{2,4},{4,2},{6,0},{8,14},{10,12},{12,10},{14,8},{16,22},{18,... | collective-permute-start | bytes 1105928 | tf_op jit(solution)/shard_map/ppermute | solution.py:389
  102.1 17.6 %collective-permute-start.28 = (bf16[128,2688]{1,0:T(8,128)(2,1)S(1)}, bf16[128,2688]{1,0:T(8,128)(2,1)S(1)}, u32[]{:S(2)}, u32[]{:S(2)}) collective-permute-start(bf16[128,2688]{1,0:T(8,128)(2,1)S(1)} %expand.4.refs_5_), channel_id=1, source_target_pairs={{0,8},{2,10},{4,12},{6,14},{8,16},{10,18},{12,20},{14,22},{16,24},... | collective-permute-start | bytes 2064392 | tf_op jit(solution)/shard_map/ppermute | solution.py:385
  107.9 18.9 %collective-permute-start.22 = (bf16[72,2560]{1,0:T(8,128)(2,1)S(1)}, bf16[72,2560]{1,0:T(8,128)(2,1)S(1)}, u32[]{:S(2)}, u32[]{:S(2)}) collective-permute-start(bf16[72,2560]{1,0:T(8,128)(2,1)S(1)} %get-tuple-element.108), channel_id=1, source_target_pairs={{0,2},{2,0},{4,6},{6,4},{8,10},{10,8},{12,14},{14,12},{16,18},{18,... | collective-permute-start | bytes 1105928 | tf_op jit(solution)/shard_map/ppermute | solution.py:389
  108.8 22.9 %collective-permute-start.23 = (bf16[72,2560]{1,0:T(8,128)(2,1)S(1)}, bf16[72,2560]{1,0:T(8,128)(2,1)S(1)}, u32[]{:S(2)}, u32[]{:S(2)}) collective-permute-start(bf16[72,2560]{1,0:T(8,128)(2,1)S(1)} %get-tuple-element.109), channel_id=1, source_target_pairs={{0,4},{2,6},{4,0},{6,2},{8,12},{10,14},{12,8},{14,10},{16,20},{18,... | collective-permute-start | bytes 1105928 | tf_op jit(solution)/shard_map/ppermute | solution.py:389
  116.0 16.8 %collective-permute-start.24 = (bf16[72,2560]{1,0:T(8,128)(2,1)S(1)}, bf16[72,2560]{1,0:T(8,128)(2,1)S(1)}, u32[]{:S(2)}, u32[]{:S(2)}) collective-permute-start(bf16[72,2560]{1,0:T(8,128)(2,1)S(1)} %get-tuple-element.110), channel_id=1, source_target_pairs={{0,6},{2,4},{4,2},{6,0},{8,14},{10,12},{12,10},{14,8},{16,22},{18,... | collective-permute-start | bytes 1105928 | tf_op jit(solution)/shard_map/ppermute | solution.py:389
  120.5 16.5 %collective-permute-start.29 = (bf16[128,2688]{1,0:T(8,128)(2,1)S(1)}, bf16[128,2688]{1,0:T(8,128)(2,1)S(1)}, u32[]{:S(2)}, u32[]{:S(2)}) collective-permute-start(bf16[128,2688]{1,0:T(8,128)(2,1)S(1)} %expand.5.refs_5_), channel_id=1, source_target_pairs={{0,8},{2,10},{4,12},{6,14},{8,16},{10,18},{12,20},{14,22},{16,24},... | collective-permute-start | bytes 2064392 | tf_op jit(solution)/shard_map/ppermute | solution.py:385
  125.4 22.1 %collective-permute-start.31 = (bf16[72,2688]{1,0:T(8,128)(2,1)S(1)}, bf16[72,2688]{1,0:T(8,128)(2,1)S(1)}, u32[]{:S(2)}, u32[]{:S(2)}) collective-permute-start(bf16[72,2688]{1,0:T(8,128)(2,1)S(1)} %get-tuple-element.121), channel_id=1, source_target_pairs={{0,2},{2,0},{4,6},{6,4},{8,10},{10,8},{12,14},{14,12},{16,18},{18,... | collective-permute-start | bytes 1161224 | tf_op jit(solution)/shard_map/ppermute | solution.py:389
  126.8 21.1 %collective-permute-start.32 = (bf16[72,2688]{1,0:T(8,128)(2,1)S(1)}, bf16[72,2688]{1,0:T(8,128)(2,1)S(1)}, u32[]{:S(2)}, u32[]{:S(2)}) collective-permute-start(bf16[72,2688]{1,0:T(8,128)(2,1)S(1)} %get-tuple-element.122), channel_id=1, source_target_pairs={{0,4},{2,6},{4,0},{6,2},{8,12},{10,14},{12,8},{14,10},{16,20},{18,... | collective-permute-start | bytes 1161224 | tf_op jit(solution)/shard_map/ppermute | solution.py:389
  131.8 16.2 %collective-permute-start.33 = (bf16[72,2688]{1,0:T(8,128)(2,1)S(1)}, bf16[72,2688]{1,0:T(8,128)(2,1)S(1)}, u32[]{:S(2)}, u32[]{:S(2)}) collective-permute-start(bf16[72,2688]{1,0:T(8,128)(2,1)S(1)} %get-tuple-element.123), channel_id=1, source_target_pairs={{0,6},{2,4},{4,2},{6,0},{8,14},{10,12},{12,10},{14,8},{16,22},{18,... | collective-permute-start | bytes 1161224 | tf_op jit(solution)/shard_map/ppermute | solution.py:389
  137.9 15.9 %collective-permute-start.30 = (bf16[128,2688]{1,0:T(8,128)(2,1)S(1)}, bf16[128,2688]{1,0:T(8,128)(2,1)S(1)}, u32[]{:S(2)}, u32[]{:S(2)}) collective-permute-start(bf16[128,2688]{1,0:T(8,128)(2,1)S(1)} %get-tuple-element.119.refs_16_), channel_id=1, source_target_pairs={{0,8},{2,10},{4,12},{6,14},{8,16},{10,18},{12,20},{14,22},{16,24},... | collective-permute-start | bytes 2064392 | tf_op jit(solution)/shard_map/ppermute | solution.py:385
  (17 other events, 205.6 us)

commit v7 on v6

--- a/solution.py
+++ b/solution.py
@@ -94,11 +94,11 @@
     return total
 
 
-def select_all(m, hot_rows, cold_rows, topk, share, plan, picks, tokens, rests, outs, marks):
+def select_all(m, hot_rows, cold_rows, topk, share, skip, plan, picks, tokens, rests, outs, marks):
     rows, width = outs[0].shape
     feat = width - share
     expert, _, _ = row_plan(m, hot_rows, cold_rows, plan, (INNER * rows, TAIL), 0)
-    tail = picked(picks, rests, slice(share, share + TAIL))
+    tail = picked(picks, rests, slice(skip + share, skip + share + TAIL))
     gate = (tail[:, 2 * topk : 3 * topk] + tail[:, 3 * topk : 4 * topk]) + tail[:, 4 * topk : 5 * topk]
     gate = jnp.sum(jnp.where(tail[:, :topk] == expert[:, :topk], gate, 0.0), 1, keepdims=True)
     lane = lax.broadcasted_iota(I32, tail.shape, 1)
@@ -111,7 +111,7 @@
             total = picked(picks, tokens, columns)
         else:
             columns = slice(feat, width)
-            total = gate * picked(picks, rests, slice(0, share))
+            total = gate * picked(picks, rests, slice(skip, skip + share))
         for d in range(INNER):
             outs[d][:, columns] = total[d * rows : (d + 1) * rows].astype(BF16)
 
@@ -152,17 +152,21 @@
         copy.wait()
     if picks:
         select_all(
-            m, hot_rows, cold_rows, topk, share, plan, picks, [here], [out], outs, marks[0]
+            m, hot_rows, cold_rows, topk, share, 0, plan, picks, [here], [out], outs, marks[0]
         )
 
 
-def select_kernel(m, hot_rows, cold_rows, topk, share, waits, plan, *refs):
+def select_kernel(m, hot_rows, cold_rows, topk, share, skip, waits, plan, *refs):
     tokens, rests, refs = refs[:m], refs[m : 2 * m], refs[2 * m + waits :]
-    outs, marks, picks = refs[:INNER], refs[INNER], refs[INNER + 1 :]
-    tails = [rest[:, share:].astype(F32) for rest in rests]
+    outs, marks, picks, joined = refs[:INNER], refs[INNER], refs[INNER + 1 : INNER + 1 + m], refs[INNER + 1 + m :]
+    tails = [rest[:, skip + share :].astype(F32) for rest in rests]
     for pick, found in zip(picks, pick_rows(m, hot_rows, cold_rows, topk, plan, tails)):
         pick[...] = found
-    select_all(m, hot_rows, cold_rows, topk, share, plan, picks, tokens, rests, outs, marks)
+    select_all(m, hot_rows, cold_rows, topk, share, skip, plan, picks, tokens, rests, outs, marks)
+    for token, rest, target in zip(tokens, rests, joined):
+        feat = token.shape[1]
+        target[:, :feat] = token[...]
+        target[:, feat:] = rest[...]
 
 
 def hidden_kernel(m, hot_rows, cold_rows, feat, streamed, waits, plan, *refs):
@@ -272,9 +276,8 @@
     lax.fori_loop(0, feat // tile, features, 0)
 
 
-def expand_kernel(m, topk, share, c, n_more, waits, *refs):
+def expand_kernel(m, topk, share, tailed, skip, n_more, waits, *refs):
     blocks, picks, marks, refs = refs[:INNER], refs[INNER : INNER + m], refs[INNER + m], refs[INNER + m + 1 :]
-    tailed = c == 0
     rests, refs = ([], refs) if tailed else (refs[:m], refs[m:])
     more, outs, apart = refs[:n_more], refs[n_more + waits :][:m], refs[n_more + waits + m :]
     width = outs[0].shape[1]
@@ -305,7 +308,7 @@
         end = joined(columns).astype(F32)
         gate_grad = (end[:, 0:1] + end[:, 1:2]) / jnp.where(gate > 0.0, gate, 1.0)
     else:
-        grad = picked(picks, rests, slice(0, share))
+        grad = picked(picks, rests, slice(skip, skip + share))
         gate_grad = jnp.sum(act * grad, 1, keepdims=True)
     high = gate_grad.astype(BF16).astype(F32)
     lane = lax.broadcasted_iota(I32, mark.shape, 1)
@@ -436,40 +439,45 @@
         cost_estimate=weigh("x"),
         name="start",
     )(replica_on, tokens, routes.T, gates.T, grad_out)
-    groups = [[o * INNER + i for o in range(outer)] for i in range(INNER)]
-    column = lax.all_gather(made[0], "ep", axis_index_groups=groups)
-    here = lax.axis_index("ep") // INNER
-    rests = [
-        lax.dynamic_index_in_dim(column, (here + outer - s) % outer, 0, keepdims=False)
-        for s in range(outer)
-    ]
-
-    def rests_of(c):
-        return [rests[s] for s in chunks[c]]
-
     last = []
-    for c in range(n):
+    for c in (0, 1):
         for s in chunks[c]:
-            if s == 0:
-                arrived[s] = tokens
+            if c:
+                arrived[s] = [along(piece, m) for piece in arrived[s - m]]
             else:
-                arrived[s] = along(arrived[s - m], m) if c else along(tokens, s)
+                arrived[s] = [along(piece, s) if s else piece for piece in (tokens, made[0])]
+
+    def skip_of(c):
+        return 0 if c < 2 else feat
 
     def select(k):
         c = PLAN[k][0]
-        made = pl.pallas_call(
-            functools.partial(select_kernel, *sizes, topk, share, len(last)),
+        joins = m if c == 1 else 0
+        chosen = pl.pallas_call(
+            functools.partial(select_kernel, *sizes, topk, share, skip_of(c), len(last)),
             out_shape=[block((rows, there))] * INNER
             + [block((INNER * rows, TAIL), F32)]
-            + [block((count, INNER * rows))] * m,
+            + [block((count, INNER * rows))] * m
+            + [block((count, width))] * joins,
             in_specs=[smem] + whole_specs(2 * m) + [rest_spec] * len(last),
-            out_specs=whole_specs(INNER + 1 + m),
+            out_specs=whole_specs(INNER + 1 + m + joins),
             compiler_params=params(),
             cost_estimate=weigh("x"),
             name="select",
-        )(replica_on, *[arrived[s] for s in chunks[c]], *rests_of(c), *last)
-        marks[c], picks[c] = made[INNER], made[INNER + 1 :]
-        exchange(k, made)
+        )(
+            replica_on,
+            *[arrived[s][0] for s in chunks[c]],
+            *[arrived[s][-1] for s in chunks[c]],
+            *last,
+        )
+        marks[c], picks[c] = chosen[INNER], chosen[INNER + 1 : INNER + 1 + m]
+        if joins:
+            now = chosen[INNER + 1 + m :]
+            for after in (2, 3):
+                now = [along(value, m) for value in now]
+                for s, value in zip(chunks[after], now):
+                    arrived[s] = [value]
+        exchange(k, chosen)
         last[:] = [picks[c][0]]
 
     def hidden(c):
@@ -531,11 +539,13 @@
 
     def expand(c):
         more = [along(partials[s - m], m) for s in chunks[c]] if c > 1 else []
-        sources = rests_of(c) if c else []
+        sources = [arrived[s][-1] for s in chunks[c]] if c else []
         apart = [block((count, TAIL))] if c == n - 1 and by_hand else []
         k = coming[c]
         made = pl.pallas_call(
-            functools.partial(expand_kernel, m, topk, share, c, len(more), len(last)),
+            functools.partial(
+                expand_kernel, m, topk, share, c == 0, skip_of(c), len(more), len(last)
+            ),
             out_shape=[block((count, width))] * m + apart,
             in_specs=whole_specs(INNER + m + 1 + len(sources) + len(more))
             + [rest_spec] * len(last),

time: 156 us -> 155 us (level)
  waiting for transfers between devices: 43.8 us -> 65.6 us
  blocking collectives: 18.6 us -> 0 us
  starting transfers between devices: 38.7 us -> 35.1 us
    ppermute x6 -> x7, waiting for transfers between devices: 14.3 us -> 39.7 us  [along(): return lax.ppermute(value, 'ep', pairs)]
    all_gather x1 -> x0, blocking collectives: 18.6 us -> none  [on_device(): column = lax.all_gather(made[0], 'ep', axis_index_groups=groups)]
    ppermute x24, waiting for transfers between devices: 27.9 us -> 22.4 us  [across(): return lax.ppermute(value, 'ep', pairs)]
    ppermute x24, starting transfers between devices: 33 us -> 29.7 us  [across(): return lax.ppermute(value, 'ep', pairs)]
    ppermute x1, waiting for transfers between devices: 1.64 us -> 3.46 us  [on_device(): tails = [lax.ppermute(partials['apart'], ('ep', 'tp'), pairs)]]
    ppermute x6 -> x7, starting transfers between devices: 5.34 us -> 5.12 us  [along(): return lax.ppermute(value, 'ep', pairs)]
  transfers between devices with their start and end apart: 35 -> 36, of which waited for: 14 -> 13; matrix products, arithmetic and copies ran while one was open for 0% -> 0% of each run, Pallas kernels for 33% -> 33%
where the time goes in v7:
time: 155 us; the launch traced here: 154 us
  waiting for transfers between devices  65.6 us (42%)
  Pallas kernels  52.8 us (34%)
  starting transfers between devices  35.1 us (23%)
    ppermute x7, waiting for transfers between devices, along(): return lax.ppermute(value, 'ep', pairs)  39.7 us
    ppermute x24, starting transfers between devices, across(): return lax.ppermute(value, 'ep', pairs)  29.7 us
    ppermute x24, waiting for transfers between devices, across(): return lax.ppermute(value, 'ep', pairs)  22.4 us
    pallas_call x4, Pallas kernels, step(): pl.pallas_call(functools.partial(back_kernel, *sizes, len(sums[c]), len(g...  18.4 us
    pallas_call x4, Pallas kernels, hidden(): pl.pallas_call(functools.partial(hidden_kernel, *sizes, feat, streamed, l...  12.3 us
    pallas_call x1, Pallas kernels, weight_grad(): pl.pallas_call(functools.partial(up_kernel, n, len(last)), out_shape=[blo...  9.48 us
    ppermute x7, starting transfers between devices, along(): return lax.ppermute(value, 'ep', pairs)  5.12 us
    pallas_call x3, Pallas kernels, select(): pl.pallas_call(functools.partial(select_kernel, *sizes, topk, share, skip...  4.68 us
  transfers between devices with their start and end apart: 36, of which 13 were waited for; matrix products, arithmetic and copies ran while one was open for 0% of the time, Pallas kernels for 33%

profile of v7, /device:TPU:0, one launch (start us, length us, event | category | flops | bytes accessed | tf_op | source)
XLA Modules:
  0.0 154.4 jit_solution(10199373833634505902)
XLA Ops:
  0.6 3.1 %collective-permute-start = (bf16[128,2048]{1,0:T(8,128)(2,1)}, bf16[128,2048]{1,0:T(8,128)(2,1)S(1)}, u32[]{:S(2)}, u32[]{:S(2)}) collective-permute-start(bf16[128,2048]{1,0:T(8,128)(2,1)} %tokens.1), channel_id=1, source_target_pairs={{0,8},{2,10},{4,12},{6,14},{8,16},{10,18},{12,20},{14,22},{16,24},... | collective-permute-start | bytes 1572872 | tf_op jit(solution)/shard_map/ppermute | solution.py:388
  3.7 3.8 %start.1 = (bf16[128,640]{1,0:T(8,128)(2,1)}, bf16[72,2560]{1,0:T(8,128)(2,1)}, bf16[72,2560]{1,0:T(8,128)(2,1)}, bf16[72,2560]{1,0:T(8,128)(2,1)}, bf16[72,2560...) custom-call(s32[32]{0:T(128)} %plan.25, bf16[128,2048]{1,0:T(8,128)(2,1)} %tokens.1, s32[8,128]{1,0:T(8,128)} %bitcast.5, ...), custom_call_target="tpu_custom_call" | custom-call | flops 5000000000 | bytes 50000000 | tf_op jit(solution)/shard_map/start/pallas_call | solution.py:421
  12.6 8.8 %collective-permute-done.1.refs_1_.refs_6_ = bf16[128,640]{1,0:T(8,128)(2,1)S(1)} collective-permute-done((bf16[128,640]{1,0:T(8,128)(2,1)}, bf16[128,640]{1,0:T(8,128)(2,1)S(1)}, u32[]{:S(2)}, u32[]{:S(2)}) %collective-permute-start.1) | collective-permute-done | bytes 163872 | tf_op jit(solution)/shard_map/ppermute | solution.py:388
  29.8 3.8 %hidden.4 = (bf16[288,1536]{1,0:T(8,128)(2,1)S(1)}, bf16[192,2048]{1,0:T(8,128)(2,1)S(1)}, bf16[96,2048]{1,0:T(8,128)(2,1)S(1)}) custom-call(s32[32]{0:T(128)S(1)} %copy-done.2, bf16[72,2560]{1,0:T(8,128)(2,1)S(1)} %copy-done.3, bf16[72,2560]{1,0:T(8,128)(2,1)S(1)} %collective-permute-done.7.refs_1_, bf16[72,2560]{1,0:T(8,128)(2,1)S(1)} %collective-permute-done.8.refs_2_, ...), custom_call_target="tpu_custom_call" | custom-call | flops 5000000000 | bytes 50000000 | tf_op jit(solution)/shard_map/hidden/pallas_call | solution.py:502
  33.7 7.8 %collective-permute-done.2.refs_0_.refs_1_.refs_6_ = bf16[128,2688]{1,0:T(8,128)(2,1)S(1)} collective-permute-done((bf16[128,2688]{1,0:T(8,128)(2,1)S(1)}, bf16[128,2688]{1,0:T(8,128)(2,1)S(1)}, u32[]{:S(2)}, u32[]{:S(2)}) %collective-permute-start.2) | collective-permute-done | bytes 688160 | tf_op jit(solution)/shard_map/ppermute | solution.py:388
  46.6 2.8 %hidden.5 = (bf16[288,1536]{1,0:T(8,128)(2,1)S(1)}, bf16[192,2048]{1,0:T(8,128)(2,1)S(1)}, bf16[96,2048]{1,0:T(8,128)(2,1)S(1)}) custom-call(s32[32]{0:T(128)S(1)} %copy-done.2, bf16[72,2560]{1,0:T(8,128)(2,1)S(1)} %get-tuple-element.75.refs_0_, bf16[72,2560]{1,0:T(8,128)(2,1)S(1)} %collective-permute-done.4.refs_1_, ...), custom_call_target="tpu_custom_call" | custom-call | flops 5000000000 | bytes 50000000 | tf_op jit(solution)/shard_map/hidden/pallas_call | solution.py:502
  49.4 9.5 %collective-permute-done.3.refs_0_.refs_1_.refs_6_ = bf16[128,2688]{1,0:T(8,128)(2,1)S(1)} collective-permute-done((bf16[128,2688]{1,0:T(8,128)(2,1)S(1)}, bf16[128,2688]{1,0:T(8,128)(2,1)S(1)}, u32[]{:S(2)}, u32[]{:S(2)}) %collective-permute-start.3) | collective-permute-done | bytes 688160 | tf_op jit(solution)/shard_map/ppermute | solution.py:388
  64.1 2.8 %hidden.6 = (bf16[288,1536]{1,0:T(8,128)(2,1)S(1)}, bf16[192,2048]{1,0:T(8,128)(2,1)S(1)}, bf16[96,2048]{1,0:T(8,128)(2,1)S(1)}) custom-call(s32[32]{0:T(128)S(1)} %copy-done.2, bf16[72,2560]{1,0:T(8,128)(2,1)S(1)} %get-tuple-element.92.refs_0_, bf16[72,2560]{1,0:T(8,128)(2,1)S(1)} %collective-permute-done.14.refs_1_, ...), custom_call_target="tpu_custom_call" | custom-call | flops 5000000000 | bytes 50000000 | tf_op jit(solution)/shard_map/hidden/pallas_call | solution.py:502
  67.0 4.5 %back.4 = (bf16[72,2560]{1,0:T(8,128)(2,1)S(1)}, bf16[72,2560]{1,0:T(8,128)(2,1)S(1)}, bf16[72,2560]{1,0:T(8,128)(2,1)S(1)}, bf16[72,2560]{1,0:T(8,128)(2,1)S(1)...) custom-call(s32[32]{0:T(128)S(1)} %copy-done.2, bf16[288,1536]{1,0:T(8,128)(2,1)S(1)} %get-tuple-element.91.refs_0_.refs_2_, ...), custom_call_target="tpu_custom_call" | custom-call | flops 20000000000 | bytes 200000000 | tf_op jit(solution)/shard_map/back/pallas_call | solution.py:522
  74.3 5.9 %collective-permute-done.11.refs_2_ = bf16[72,2560]{1,0:T(8,128)(2,1)S(1)} collective-permute-done((bf16[72,2560]{1,0:T(8,128)(2,1)S(1)}, bf16[72,2560]{1,0:T(8,128)(2,1)S(1)}, u32[]{:S(2)}, u32[]{:S(2)}) %collective-permute-start.11) | collective-permute-done | bytes 368672 | tf_op jit(solution)/shard_map/ppermute | solution.py:392
  81.8 2.8 %hidden.7 = (bf16[288,1536]{1,0:T(8,128)(2,1)S(1)}, bf16[192,2048]{1,0:T(8,128)(2,1)S(1)}, bf16[96,2048]{1,0:T(8,128)(2,1)S(1)}) custom-call(s32[32]{0:T(128)S(1)} %copy-done.2, bf16[72,2560]{1,0:T(8,128)(2,1)S(1)} %get-tuple-element.87.refs_0_, bf16[72,2560]{1,0:T(8,128)(2,1)S(1)} %collective-permute-done.10.refs_1_, ...), custom_call_target="tpu_custom_call" | custom-call | flops 5000000000 | bytes 50000000 | tf_op jit(solution)/shard_map/hidden/pallas_call | solution.py:502
  84.7 4.5 %back.5 = (bf16[72,2560]{1,0:T(8,128)(2,1)S(1)}, bf16[72,2560]{1,0:T(8,128)(2,1)S(1)}, bf16[72,2560]{1,0:T(8,128)(2,1)S(1)}, bf16[72,2560]{1,0:T(8,128)(2,1)S(1)...) custom-call(s32[32]{0:T(128)S(1)} %copy-done.2, bf16[288,1536]{1,0:T(8,128)(2,1)S(1)} %get-tuple-element.106.refs_0_.refs_2_, ...), custom_call_target="tpu_custom_call" | custom-call | flops 20000000000 | bytes 200000000 | tf_op jit(solution)/shard_map/back/pallas_call | solution.py:522
  89.3 2.1 %collective-permute-start.26 = (bf16[72,2560]{1,0:T(8,128)(2,1)S(1)}, bf16[72,2560]{1,0:T(8,128)(2,1)S(1)}, u32[]{:S(2)}, u32[]{:S(2)}) collective-permute-start(bf16[72,2560]{1,0:T(8,128)(2,1)S(1)} %get-tuple-element.115), channel_id=1, source_target_pairs={{0,2},{2,0},{4,6},{6,4},{8,10},{10,8},{12,14},{14,12},{16,18},{18,... | collective-permute-start | bytes 1105928 | tf_op jit(solution)/shard_map/ppermute | solution.py:392
  91.3 4.6 %collective-permute-done.20.refs_2_ = bf16[72,2560]{1,0:T(8,128)(2,1)S(1)} collective-permute-done((bf16[72,2560]{1,0:T(8,128)(2,1)S(1)}, bf16[72,2560]{1,0:T(8,128)(2,1)S(1)}, u32[]{:S(2)}, u32[]{:S(2)}) %collective-permute-start.20) | collective-permute-done | bytes 368672 | tf_op jit(solution)/shard_map/ppermute | solution.py:392
  98.7 4.5 %back.6 = (bf16[72,2560]{1,0:T(8,128)(2,1)S(1)}, bf16[72,2560]{1,0:T(8,128)(2,1)S(1)}, bf16[72,2560]{1,0:T(8,128)(2,1)S(1)}, bf16[72,2560]{1,0:T(8,128)(2,1)S(1)...) custom-call(s32[32]{0:T(128)S(1)} %copy-done.2, bf16[288,1536]{1,0:T(8,128)(2,1)S(1)} %get-tuple-element.100.refs_0_.refs_2_, ...), custom_call_target="tpu_custom_call" | custom-call | flops 20000000000 | bytes 200000000 | tf_op jit(solution)/shard_map/back/pallas_call | solution.py:522
  103.2 2.1 %collective-permute-start.23 = (bf16[72,2560]{1,0:T(8,128)(2,1)S(1)}, bf16[72,2560]{1,0:T(8,128)(2,1)S(1)}, u32[]{:S(2)}, u32[]{:S(2)}) collective-permute-start(bf16[72,2560]{1,0:T(8,128)(2,1)S(1)} %get-tuple-element.110), channel_id=1, source_target_pairs={{0,2},{2,0},{4,6},{6,4},{8,10},{10,8},{12,14},{14,12},{16,18},{18,... | collective-permute-start | bytes 1105928 | tf_op jit(solution)/shard_map/ppermute | solution.py:392
  105.3 6.2 %collective-permute-done.27.refs_2_ = bf16[72,2560]{1,0:T(8,128)(2,1)S(1)} collective-permute-done((bf16[72,2560]{1,0:T(8,128)(2,1)S(1)}, bf16[72,2560]{1,0:T(8,128)(2,1)S(1)}, u32[]{:S(2)}, u32[]{:S(2)}) %collective-permute-start.27) | collective-permute-done | bytes 368672 | tf_op jit(solution)/shard_map/ppermute | solution.py:392
  113.2 3.9 %collective-permute-done.29.refs_7_ = bf16[128,2688]{1,0:T(8,128)(2,1)S(1)} collective-permute-done((bf16[128,2688]{1,0:T(8,128)(2,1)S(1)}, bf16[128,2688]{1,0:T(8,128)(2,1)S(1)}, u32[]{:S(2)}, u32[]{:S(2)}) %collective-permute-start.29) | collective-permute-done | bytes 688160 | tf_op jit(solution)/shard_map/ppermute | solution.py:388
  118.0 4.8 %back.7 = (bf16[72,2688]{1,0:T(8,128)(2,1)S(1)}, bf16[72,2688]{1,0:T(8,128)(2,1)S(1)}, bf16[72,2688]{1,0:T(8,128)(2,1)S(1)}, bf16[72,2688]{1,0:T(8,128)(2,1)S(1)...) custom-call(s32[32]{0:T(128)S(1)} %copy-done.2, bf16[288,1536]{1,0:T(8,128)(2,1)S(1)} %get-tuple-element.98.refs_0_.refs_2_, ...), custom_call_target="tpu_custom_call" | custom-call | flops 20000000000 | bytes 200000000 | tf_op jit(solution)/shard_map/back/pallas_call | solution.py:522
  124.9 2.4 %collective-permute-done.24.refs_2_ = bf16[72,2560]{1,0:T(8,128)(2,1)S(1)} collective-permute-done((bf16[72,2560]{1,0:T(8,128)(2,1)S(1)}, bf16[72,2560]{1,0:T(8,128)(2,1)S(1)}, u32[]{:S(2)}, u32[]{:S(2)}) %collective-permute-start.24) | collective-permute-done | bytes 368672 | tf_op jit(solution)/shard_map/ppermute | solution.py:392
  128.9 6.5 %collective-permute-done.30.refs_7_ = bf16[128,2688]{1,0:T(8,128)(2,1)S(1)} collective-permute-done((bf16[128,2688]{1,0:T(8,128)(2,1)S(1)}, bf16[128,2688]{1,0:T(8,128)(2,1)S(1)}, u32[]{:S(2)}, u32[]{:S(2)}) %collective-permute-start.30) | collective-permute-done | bytes 688160 | tf_op jit(solution)/shard_map/ppermute | solution.py:388
  136.5 9.5 %grad_up.1 = (bf16[2,2048,1024]{2,1,0:T(8,128)(2,1)}, f32[8,128]{1,0:T(8,128)S(1)}) custom-call(s32[32]{0:T(128)S(1)} %copy-done.2, bf16[192,2048]{1,0:T(8,128)(2,1)S(1)} %get-tuple-element.128.refs_0_, bf16[192,2048]{1,0:T(8,128)(2,1)S(1)} %get-tuple-element.129.refs_1_, bf16[192,2048]{1,0:T(8,128)(2,1)S(1)} %get-tuple-element.130.refs_2_, ...), custom_call_target="tpu_custom_call" | custom-call | flops 20000000000 | bytes 200000000 | tf_op jit(solution)/shard_map/grad_up/pallas_call | solution.py:565
  146.5 3.5 %collective-permute-done.35.refs_2_ = bf16[128,128]{1,0:T(8,128)(2,1)S(1)} collective-permute-done((bf16[128,128]{1,0:T(8,128)(2,1)S(1)}, bf16[128,128]{1,0:T(8,128)(2,1)S(1)}, u32[]{:S(2)}, u32[]{:S(2)}) %collective-permute-start.35) | collective-permute-done | bytes 32800 | tf_op jit(solution)/shard_map/ppermute | solution.py:618
  150.0 3.3 %collective-permute-done.31.refs_0_ = bf16[128,2688]{1,0:T(8,128)(2,1)S(1)} collective-permute-done((bf16[128,2688]{1,0:T(8,128)(2,1)S(1)}, bf16[128,2688]{1,0:T(8,128)(2,1)S(1)}, u32[]{:S(2)}, u32[]{:S(2)}) %collective-permute-start.31) | collective-permute-done | bytes 688160 | tf_op jit(solution)/shard_map/ppermute | solution.py:388
  (79 shorter events, 39.9 us)
Async XLA Ops:
  0.6 20.7 %collective-permute-start = (bf16[128,2048]{1,0:T(8,128)(2,1)}, bf16[128,2048]{1,0:T(8,128)(2,1)S(1)}, u32[]{:S(2)}, u32[]{:S(2)}) collective-permute-start(bf16[128,2048]{1,0:T(8,128)(2,1)} %tokens.1), channel_id=1, source_target_pairs={{0,8},{2,10},{4,12},{6,14},{8,16},{10,18},{12,20},{14,22},{16,24},... | collective-permute-start | bytes 1572872 | tf_op jit(solution)/shard_map/ppermute | solution.py:388
  12.2 17.6 %collective-permute-start.9 = (bf16[72,2560]{1,0:T(8,128)(2,1)}, bf16[72,2560]{1,0:T(8,128)(2,1)S(1)}, u32[]{:S(2)}, u32[]{:S(2)}) collective-permute-start(bf16[72,2560]{1,0:T(8,128)(2,1)} %get-tuple-element.82), channel_id=1, source_target_pairs={{0,6},{2,4},{4,2},{6,0},{8,14},{10,12},{12,10},{14,8},{16,22},{18,... | collective-permute-start | bytes 1105928 | tf_op jit(solution)/shard_map/ppermute | solution.py:392
  22.9 18.5 %collective-permute-start.2 = (bf16[128,2688]{1,0:T(8,128)(2,1)S(1)}, bf16[128,2688]{1,0:T(8,128)(2,1)S(1)}, u32[]{:S(2)}, u32[]{:S(2)}) collective-permute-start(bf16[128,2688]{1,0:T(8,128)(2,1)S(1)} %get-tuple-element.74), channel_id=1, source_target_pairs={{0,8},{2,10},{4,12},{6,14},{8,16},{10,18},{12,20},{14,22},{16,24},... | collective-permute-start | bytes 2064392 | tf_op jit(solution)/shard_map/ppermute | solution.py:388
  23.0 20.0 %collective-permute-start.4 = (bf16[72,2560]{1,0:T(8,128)(2,1)S(1)}, bf16[72,2560]{1,0:T(8,128)(2,1)S(1)}, u32[]{:S(2)}, u32[]{:S(2)}) collective-permute-start(bf16[72,2560]{1,0:T(8,128)(2,1)S(1)} %get-tuple-element.76), channel_id=1, source_target_pairs={{0,2},{2,0},{4,6},{6,4},{8,10},{10,8},{12,14},{14,12},{16,18},{18,... | collective-permute-start | bytes 1105928 | tf_op jit(solution)/shard_map/ppermute | solution.py:392
  24.6 19.7 %collective-permute-start.5 = (bf16[72,2560]{1,0:T(8,128)(2,1)S(1)}, bf16[72,2560]{1,0:T(8,128)(2,1)S(1)}, u32[]{:S(2)}, u32[]{:S(2)}) collective-permute-start(bf16[72,2560]{1,0:T(8,128)(2,1)S(1)} %get-tuple-element.77), channel_id=1, source_target_pairs={{0,4},{2,6},{4,0},{6,2},{8,12},{10,14},{12,8},{14,10},{16,20},{18,... | collective-permute-start | bytes 1105928 | tf_op jit(solution)/shard_map/ppermute | solution.py:392
  28.0 17.9 %collective-permute-start.6 = (bf16[72,2560]{1,0:T(8,128)(2,1)S(1)}, bf16[72,2560]{1,0:T(8,128)(2,1)S(1)}, u32[]{:S(2)}, u32[]{:S(2)}) collective-permute-start(bf16[72,2560]{1,0:T(8,128)(2,1)S(1)} %get-tuple-element.78), channel_id=1, source_target_pairs={{0,6},{2,4},{4,2},{6,0},{8,14},{10,12},{12,10},{14,8},{16,22},{18,... | collective-permute-start | bytes 1105928 | tf_op jit(solution)/shard_map/ppermute | solution.py:392
  33.6 33.3 %collective-permute-start.17 = (bf16[288,1536]{1,0:T(8,128)(2,1)S(1)}, bf16[288,1536]{1,0:T(8,128)(2,1)S(1)}, u32[]{:S(2)}, u32[]{:S(2)}) collective-permute-start(bf16[288,1536]{1,0:T(8,128)(2,1)S(1)} %get-tuple-element.98.refs_0_.refs_2_), channel_id=1, source_target_pairs={{0,1},{1,0},{2,3},{3,2},{4,5},{5,4},{6,7},{7,6},{8,9},{9,8},{10,11... | collective-permute-start | bytes 2654216 | tf_op jit(solution)/shard_map/ppermute | solution.py:512
  41.4 17.5 %collective-permute-start.3 = (bf16[128,2688]{1,0:T(8,128)(2,1)S(1)}, bf16[128,2688]{1,0:T(8,128)(2,1)S(1)}, u32[]{:S(2)}, u32[]{:S(2)}) collective-permute-start(bf16[128,2688]{1,0:T(8,128)(2,1)S(1)} %collective-permute-done.2.refs_0_.refs_1_.refs_6_), channel_id=1, source_target_pairs={{0,8},{2,10},{4,12},{6,14},{8,16},{10,18},{12,20},{14,22},{16,24},... | collective-permute-start | bytes 2064392 | tf_op jit(solution)/shard_map/ppermute | solution.py:388
  43.0 17.5 %collective-permute-start.14 = (bf16[72,2560]{1,0:T(8,128)(2,1)S(1)}, bf16[72,2560]{1,0:T(8,128)(2,1)S(1)}, u32[]{:S(2)}, u32[]{:S(2)}) collective-permute-start(bf16[72,2560]{1,0:T(8,128)(2,1)S(1)} %get-tuple-element.93), channel_id=1, source_target_pairs={{0,2},{2,0},{4,6},{6,4},{8,10},{10,8},{12,14},{14,12},{16,18},{18,... | collective-permute-start | bytes 1105928 | tf_op jit(solution)/shard_map/ppermute | solution.py:392
  45.8 17.4 %collective-permute-start.16 = (bf16[72,2560]{1,0:T(8,128)(2,1)S(1)}, bf16[72,2560]{1,0:T(8,128)(2,1)S(1)}, u32[]{:S(2)}, u32[]{:S(2)}) collective-permute-start(bf16[72,2560]{1,0:T(8,128)(2,1)S(1)} %get-tuple-element.95), channel_id=1, source_target_pairs={{0,6},{2,4},{4,2},{6,0},{8,14},{10,12},{12,10},{14,8},{16,22},{18,... | collective-permute-start | bytes 1105928 | tf_op jit(solution)/shard_map/ppermute | solution.py:392
  61.6 18.6 %collective-permute-start.11 = (bf16[72,2560]{1,0:T(8,128)(2,1)S(1)}, bf16[72,2560]{1,0:T(8,128)(2,1)S(1)}, u32[]{:S(2)}, u32[]{:S(2)}) collective-permute-start(bf16[72,2560]{1,0:T(8,128)(2,1)S(1)} %get-tuple-element.89), channel_id=1, source_target_pairs={{0,4},{2,6},{4,0},{6,2},{8,12},{10,14},{12,8},{14,10},{16,20},{18,... | collective-permute-start | bytes 1105928 | tf_op jit(solution)/shard_map/ppermute | solution.py:392
  63.2 18.6 %collective-permute-start.12 = (bf16[72,2560]{1,0:T(8,128)(2,1)S(1)}, bf16[72,2560]{1,0:T(8,128)(2,1)S(1)}, u32[]{:S(2)}, u32[]{:S(2)}) collective-permute-start(bf16[72,2560]{1,0:T(8,128)(2,1)S(1)} %get-tuple-element.90), channel_id=1, source_target_pairs={{0,6},{2,4},{4,2},{6,0},{8,14},{10,12},{12,10},{14,8},{16,22},{18,... | collective-permute-start | bytes 1105928 | tf_op jit(solution)/shard_map/ppermute | solution.py:392
  66.9 17.8 %collective-permute-start.22 = (bf16[288,1536]{1,0:T(8,128)(2,1)S(1)}, bf16[288,1536]{1,0:T(8,128)(2,1)S(1)}, u32[]{:S(2)}, u32[]{:S(2)}) collective-permute-start(bf16[288,1536]{1,0:T(8,128)(2,1)S(1)} %get-tuple-element.106.refs_0_.refs_2_), channel_id=1, source_target_pairs={{0,1},{1,0},{2,3},{3,2},{4,5},{5,4},{6,7},{7,6},{8,9},{9,8},{10,11... | collective-permute-start | bytes 2654216 | tf_op jit(solution)/shard_map/ppermute | solution.py:512
  71.5 19.8 %collective-permute-start.19 = (bf16[72,2560]{1,0:T(8,128)(2,1)S(1)}, bf16[72,2560]{1,0:T(8,128)(2,1)S(1)}, u32[]{:S(2)}, u32[]{:S(2)}) collective-permute-start(bf16[72,2560]{1,0:T(8,128)(2,1)S(1)} %get-tuple-element.102), channel_id=1, source_target_pairs={{0,2},{2,0},{4,6},{6,4},{8,10},{10,8},{12,14},{14,12},{16,18},{18,... | collective-permute-start | bytes 1105928 | tf_op jit(solution)/shard_map/ppermute | solution.py:392
  72.6 23.4 %collective-permute-start.20 = (bf16[72,2560]{1,0:T(8,128)(2,1)S(1)}, bf16[72,2560]{1,0:T(8,128)(2,1)S(1)}, u32[]{:S(2)}, u32[]{:S(2)}) collective-permute-start(bf16[72,2560]{1,0:T(8,128)(2,1)S(1)} %get-tuple-element.103), channel_id=1, source_target_pairs={{0,4},{2,6},{4,0},{6,2},{8,12},{10,14},{12,8},{14,10},{16,20},{18,... | collective-permute-start | bytes 1105928 | tf_op jit(solution)/shard_map/ppermute | solution.py:392
  80.2 17.4 %collective-permute-start.21 = (bf16[72,2560]{1,0:T(8,128)(2,1)S(1)}, bf16[72,2560]{1,0:T(8,128)(2,1)S(1)}, u32[]{:S(2)}, u32[]{:S(2)}) collective-permute-start(bf16[72,2560]{1,0:T(8,128)(2,1)S(1)} %get-tuple-element.104), channel_id=1, source_target_pairs={{0,6},{2,4},{4,2},{6,0},{8,14},{10,12},{12,10},{14,8},{16,22},{18,... | collective-permute-start | bytes 1105928 | tf_op jit(solution)/shard_map/ppermute | solution.py:392
  91.3 20.2 %collective-permute-start.27 = (bf16[72,2560]{1,0:T(8,128)(2,1)S(1)}, bf16[72,2560]{1,0:T(8,128)(2,1)S(1)}, u32[]{:S(2)}, u32[]{:S(2)}) collective-permute-start(bf16[72,2560]{1,0:T(8,128)(2,1)S(1)} %get-tuple-element.116), channel_id=1, source_target_pairs={{0,4},{2,6},{4,0},{6,2},{8,12},{10,14},{12,8},{14,10},{16,20},{18,... | collective-permute-start | bytes 1105928 | tf_op jit(solution)/shard_map/ppermute | solution.py:392
  98.5 18.6 %collective-permute-start.29 = (bf16[128,2688]{1,0:T(8,128)(2,1)S(1)}, bf16[128,2688]{1,0:T(8,128)(2,1)S(1)}, u32[]{:S(2)}, u32[]{:S(2)}) collective-permute-start(bf16[128,2688]{1,0:T(8,128)(2,1)S(1)} %expand.4.refs_5_), channel_id=1, source_target_pairs={{0,8},{2,10},{4,12},{6,14},{8,16},{10,18},{12,20},{14,22},{16,24},... | collective-permute-start | bytes 2064392 | tf_op jit(solution)/shard_map/ppermute | solution.py:388
  103.2 20.6 %collective-permute-start.23 = (bf16[72,2560]{1,0:T(8,128)(2,1)S(1)}, bf16[72,2560]{1,0:T(8,128)(2,1)S(1)}, u32[]{:S(2)}, u32[]{:S(2)}) collective-permute-start(bf16[72,2560]{1,0:T(8,128)(2,1)S(1)} %get-tuple-element.110), channel_id=1, source_target_pairs={{0,2},{2,0},{4,6},{6,4},{8,10},{10,8},{12,14},{14,12},{16,18},{18,... | collective-permute-start | bytes 1105928 | tf_op jit(solution)/shard_map/ppermute | solution.py:392
  105.3 22.0 %collective-permute-start.24 = (bf16[72,2560]{1,0:T(8,128)(2,1)S(1)}, bf16[72,2560]{1,0:T(8,128)(2,1)S(1)}, u32[]{:S(2)}, u32[]{:S(2)}) collective-permute-start(bf16[72,2560]{1,0:T(8,128)(2,1)S(1)} %get-tuple-element.111), channel_id=1, source_target_pairs={{0,4},{2,6},{4,0},{6,2},{8,12},{10,14},{12,8},{14,10},{16,20},{18,... | collective-permute-start | bytes 1105928 | tf_op jit(solution)/shard_map/ppermute | solution.py:392
  117.9 17.5 %collective-permute-start.30 = (bf16[128,2688]{1,0:T(8,128)(2,1)S(1)}, bf16[128,2688]{1,0:T(8,128)(2,1)S(1)}, u32[]{:S(2)}, u32[]{:S(2)}) collective-permute-start(bf16[128,2688]{1,0:T(8,128)(2,1)S(1)} %expand.5.refs_5_), channel_id=1, source_target_pairs={{0,8},{2,10},{4,12},{6,14},{8,16},{10,18},{12,20},{14,22},{16,24},... | collective-permute-start | bytes 2064392 | tf_op jit(solution)/shard_map/ppermute | solution.py:388
  122.8 23.2 %collective-permute-start.32 = (bf16[72,2688]{1,0:T(8,128)(2,1)S(1)}, bf16[72,2688]{1,0:T(8,128)(2,1)S(1)}, u32[]{:S(2)}, u32[]{:S(2)}) collective-permute-start(bf16[72,2688]{1,0:T(8,128)(2,1)S(1)} %get-tuple-element.123), channel_id=1, source_target_pairs={{0,2},{2,0},{4,6},{6,4},{8,10},{10,8},{12,14},{14,12},{16,18},{18,... | collective-permute-start | bytes 1161224 | tf_op jit(solution)/shard_map/ppermute | solution.py:392
  123.9 22.1 %collective-permute-start.33 = (bf16[72,2688]{1,0:T(8,128)(2,1)S(1)}, bf16[72,2688]{1,0:T(8,128)(2,1)S(1)}, u32[]{:S(2)}, u32[]{:S(2)}) collective-permute-start(bf16[72,2688]{1,0:T(8,128)(2,1)S(1)} %get-tuple-element.124), channel_id=1, source_target_pairs={{0,4},{2,6},{4,0},{6,2},{8,12},{10,14},{12,8},{14,10},{16,20},{18,... | collective-permute-start | bytes 1161224 | tf_op jit(solution)/shard_map/ppermute | solution.py:392
  127.3 18.7 %collective-permute-start.34 = (bf16[72,2688]{1,0:T(8,128)(2,1)S(1)}, bf16[72,2688]{1,0:T(8,128)(2,1)S(1)}, u32[]{:S(2)}, u32[]{:S(2)}) collective-permute-start(bf16[72,2688]{1,0:T(8,128)(2,1)S(1)} %get-tuple-element.125), channel_id=1, source_target_pairs={{0,6},{2,4},{4,2},{6,0},{8,14},{10,12},{12,10},{14,8},{16,22},{18,... | collective-permute-start | bytes 1161224 | tf_op jit(solution)/shard_map/ppermute | solution.py:392
  (18 other events, 267.8 us)

commit v8 on v7

--- a/solution.py
+++ b/solution.py
@@ -10,7 +10,7 @@
 INNER = 4
 CHUNKS = 4
 PLAN = ((0, None), (1, None), (2, None), (3, None), (None, 1), (None, 2), (None, 3), (None, 0))
-ORDER = ('x1', 'h0', 'x2', 'h1', 'x3', 'h2', 'r0', 'x4', 'h3', 'x5', 'r3', 'e1', 'x6', 'e2', 'r2', 'x7', 'e3', 'u', 'e0')
+ORDER = ('x1', 'h0', 'x2', 'h1', 'x3', 'h2', 'r0', 'x4', 'h3', 'x5', 'r3', 'e1', 'x6', 'e2', 'r2', 'x7', 'z', 'e3', 'u', 'e0')
 FIRST = 1
 COSTS = {'x': 5000, 'b': 20000, 'h': 5000, 'e': 1, 'u': 20000}
 TAIL = 128
@@ -521,9 +521,9 @@
             return select(k)
         made = pl.pallas_call(
             functools.partial(
-                back_kernel, *sizes, len(sums[c]), len(grads[c]), share, c == 0, len(last)
+                back_kernel, *sizes, len(sums[c]), len(grads[c]), share, c < 2, len(last)
             ),
-            out_shape=[block((rows, there if c else width))] * INNER
+            out_shape=[block((rows, width if c < 2 else there))] * INNER
             + [block((hots, ff)), block((colds, ff))],
             in_specs=[smem]
             + whole_specs(len(sums[c]) + len(grads[c]) + 1)
@@ -537,14 +537,16 @@
         exchange(k, made)
         last[:] = [g_colds[c]]
 
+    homes = {}
+
     def expand(c):
-        more = [along(partials[s - m], m) for s in chunks[c]] if c > 1 else []
-        sources = [arrived[s][-1] for s in chunks[c]] if c else []
+        more = [along(partials[s - m], m) for s in chunks[c]] if c > 2 else []
+        sources = [arrived[s][-1] for s in chunks[c]] if c > 1 else []
         apart = [block((count, TAIL))] if c == n - 1 and by_hand else []
         k = coming[c]
         made = pl.pallas_call(
             functools.partial(
-                expand_kernel, m, topk, share, c == 0, skip_of(c), len(more), len(last)
+                expand_kernel, m, topk, share, c < 2, skip_of(c), len(more), len(last)
             ),
             out_shape=[block((count, width))] * m + apart,
             in_specs=whole_specs(INNER + m + 1 + len(sources) + len(more))
@@ -556,6 +558,8 @@
         )(*blocks[k], *picks[c], marks[c], *sources, *more, *last)
         for s, value in zip(chunks[c], made):
             partials[s] = value
+            if c == 1:
+                homes[s - m] = along(value, outer - m)
         if apart:
             partials["apart"] = made[m]
         last[:] = [made[0]]
@@ -601,6 +605,8 @@
             grad_up = weight_grad()
         elif word[0] == "r":
             last.append(sums[number][-1])
+        elif word[0] == "z":
+            last.append(homes[0])
         else:
             {"x": step, "h": hidden, "e": expand}[word[0]](number)
 
@@ -616,16 +622,16 @@
             for t in range(n_tp)
         ]
         tails = [lax.ppermute(partials["apart"], ("ep", "tp"), pairs)]
-        parts = [sums_back[0], partials[0]]
+        parts = [sums_back[0], partials[0], homes[0]]
     else:
         parts, tails, halves = [], [], 0.0
         for s, value in zip(chunks[0], sums_back):
-            ours = partials[s]
             if s == 0:
-                parts += [value[:, :there], ours[:, :there]]
+                parts += [array[:, :there] for array in (value, partials[0], homes[0])]
                 halves = halves + value[:, there:].astype(F32)
-                tails.append(ours[:, there:])
+                tails += [partials[0][:, there:], homes[0][:, there:]]
             else:
+                ours = partials[s] + homes[s]
                 parts.append(along(value[:, :there] + ours[:, :there], outer - s))
                 halves = halves + along(value[:, there:], outer - s).astype(F32)
                 tails.append(along(ours[:, there:], outer - s))

time: 155 us -> 154 us (level)
    ppermute x24, waiting for transfers between devices: 22.4 us -> 37.5 us  [across(): return lax.ppermute(value, 'ep', pairs)]
    ppermute x7, waiting for transfers between devices: 39.7 us -> 29.1 us  [along(): return lax.ppermute(value, 'ep', pairs)]
    ppermute x1, waiting for transfers between devices: 3.46 us -> 0.01 us  [on_device(): tails = [lax.ppermute(partials['apart'], ('ep', 'tp'), pairs)]]
  transfers between devices with their start and end apart: 36 -> 36, of which waited for: 13 -> 14; matrix products, arithmetic and copies ran while one was open for 0% -> 0% of each run, Pallas kernels for 33% -> 33%
where the time goes in v8:
time: 154 us
  waiting for transfers between devices  66.6 us (43%)
  Pallas kernels  52.8 us (34%)
  starting transfers between devices  33.7 us (22%)
    ppermute x24, waiting for transfers between devices, across(): return lax.ppermute(value, 'ep', pairs)  37.5 us
    ppermute x7, waiting for transfers between devices, along(): return lax.ppermute(value, 'ep', pairs)  29.1 us
    ppermute x24, starting transfers between devices, across(): return lax.ppermute(value, 'ep', pairs)  28.3 us
    pallas_call x4, Pallas kernels, step(): pl.pallas_call(functools.partial(back_kernel, *sizes, len(sums[c]), len(g...  18.6 us
    pallas_call x4, Pallas kernels, hidden(): pl.pallas_call(functools.partial(hidden_kernel, *sizes, feat, streamed, l...  12.2 us
    pallas_call x1, Pallas kernels, weight_grad(): pl.pallas_call(functools.partial(up_kernel, n, len(last)), out_shape=[blo...  9.5 us
    ppermute x7, starting transfers between devices, along(): return lax.ppermute(value, 'ep', pairs)  5.12 us
    pallas_call x3, Pallas kernels, select(): pl.pallas_call(functools.partial(select_kernel, *sizes, topk, share, skip...  4.68 us
  transfers between devices with their start and end apart: 36, of which 14 were waited for; matrix products, arithmetic and copies ran while one was open for 0% of the time, Pallas kernels for 33%

profile of v8, /device:TPU:0, one launch (start us, length us, event | category | flops | bytes accessed | tf_op | source)
XLA Modules:
  0.0 154.1 jit_solution(12784713653820396775)
XLA Ops:
  0.6 3.1 %collective-permute-start = (bf16[128,2048]{1,0:T(8,128)(2,1)}, bf16[128,2048]{1,0:T(8,128)(2,1)S(1)}, u32[]{:S(2)}, u32[]{:S(2)}) collective-permute-start(bf16[128,2048]{1,0:T(8,128)(2,1)} %tokens.1), channel_id=1, source_target_pairs={{0,8},{2,10},{4,12},{6,14},{8,16},{10,18},{12,20},{14,22},{16,24},... | collective-permute-start | bytes 1572872 | tf_op jit(solution)/shard_map/ppermute | solution.py:388
  3.7 3.8 %start.1 = (bf16[128,640]{1,0:T(8,128)(2,1)}, bf16[72,2560]{1,0:T(8,128)(2,1)}, bf16[72,2560]{1,0:T(8,128)(2,1)}, bf16[72,2560]{1,0:T(8,128)(2,1)}, bf16[72,2560...) custom-call(s32[32]{0:T(128)} %plan.25, bf16[128,2048]{1,0:T(8,128)(2,1)} %tokens.1, s32[8,128]{1,0:T(8,128)} %bitcast.5, ...), custom_call_target="tpu_custom_call" | custom-call | flops 5000000000 | bytes 50000000 | tf_op jit(solution)/shard_map/start/pallas_call | solution.py:421
  12.6 8.8 %collective-permute-done.1.refs_1_ = bf16[128,640]{1,0:T(8,128)(2,1)S(1)} collective-permute-done((bf16[128,640]{1,0:T(8,128)(2,1)}, bf16[128,640]{1,0:T(8,128)(2,1)S(1)}, u32[]{:S(2)}, u32[]{:S(2)}) %collective-permute-start.1) | collective-permute-done | bytes 163872 | tf_op jit(solution)/shard_map/ppermute | solution.py:388
  26.1 1.9 %collective-permute-done.8.refs_2_ = bf16[72,2560]{1,0:T(8,128)(2,1)S(1)} collective-permute-done((bf16[72,2560]{1,0:T(8,128)(2,1)}, bf16[72,2560]{1,0:T(8,128)(2,1)S(1)}, u32[]{:S(2)}, u32[]{:S(2)}) %collective-permute-start.8) | collective-permute-done | bytes 368672 | tf_op jit(solution)/shard_map/ppermute | solution.py:392
  29.8 3.7 %hidden.4 = (bf16[288,1536]{1,0:T(8,128)(2,1)S(1)}, bf16[192,2048]{1,0:T(8,128)(2,1)S(1)}, bf16[96,2048]{1,0:T(8,128)(2,1)S(1)}) custom-call(s32[32]{0:T(128)S(1)} %copy-done.2, bf16[72,2560]{1,0:T(8,128)(2,1)S(1)} %copy-done.3, bf16[72,2560]{1,0:T(8,128)(2,1)S(1)} %collective-permute-done.7.refs_1_, bf16[72,2560]{1,0:T(8,128)(2,1)S(1)} %collective-permute-done.8.refs_2_, ...), custom_call_target="tpu_custom_call" | custom-call | flops 5000000000 | bytes 50000000 | tf_op jit(solution)/shard_map/hidden/pallas_call | solution.py:502
  33.6 7.8 %collective-permute-done.2.refs_0_.refs_1_.refs_6_ = bf16[128,2688]{1,0:T(8,128)(2,1)S(1)} collective-permute-done((bf16[128,2688]{1,0:T(8,128)(2,1)S(1)}, bf16[128,2688]{1,0:T(8,128)(2,1)S(1)}, u32[]{:S(2)}, u32[]{:S(2)}) %collective-permute-start.2) | collective-permute-done | bytes 688160 | tf_op jit(solution)/shard_map/ppermute | solution.py:388
  46.6 2.8 %hidden.5 = (bf16[288,1536]{1,0:T(8,128)(2,1)S(1)}, bf16[192,2048]{1,0:T(8,128)(2,1)S(1)}, bf16[96,2048]{1,0:T(8,128)(2,1)S(1)}) custom-call(s32[32]{0:T(128)S(1)} %copy-done.2, bf16[72,2560]{1,0:T(8,128)(2,1)S(1)} %get-tuple-element.75.refs_0_, bf16[72,2560]{1,0:T(8,128)(2,1)S(1)} %collective-permute-done.4.refs_1_, ...), custom_call_target="tpu_custom_call" | custom-call | flops 5000000000 | bytes 50000000 | tf_op jit(solution)/shard_map/hidden/pallas_call | solution.py:502
  49.4 9.5 %collective-permute-done.3.refs_0_.refs_1_.refs_6_ = bf16[128,2688]{1,0:T(8,128)(2,1)S(1)} collective-permute-done((bf16[128,2688]{1,0:T(8,128)(2,1)S(1)}, bf16[128,2688]{1,0:T(8,128)(2,1)S(1)}, u32[]{:S(2)}, u32[]{:S(2)}) %collective-permute-start.3) | collective-permute-done | bytes 688160 | tf_op jit(solution)/shard_map/ppermute | solution.py:388
  61.6 1.7 %collective-permute-start.11 = (bf16[72,2560]{1,0:T(8,128)(2,1)S(1)}, bf16[72,2560]{1,0:T(8,128)(2,1)S(1)}, u32[]{:S(2)}, u32[]{:S(2)}) collective-permute-start(bf16[72,2560]{1,0:T(8,128)(2,1)S(1)} %get-tuple-element.89), channel_id=1, source_target_pairs={{0,4},{2,6},{4,0},{6,2},{8,12},{10,14},{12,8},{14,10},{16,20},{18,... | collective-permute-start | bytes 1105928 | tf_op jit(solution)/shard_map/ppermute | solution.py:392
  64.1 2.8 %hidden.6 = (bf16[288,1536]{1,0:T(8,128)(2,1)S(1)}, bf16[192,2048]{1,0:T(8,128)(2,1)S(1)}, bf16[96,2048]{1,0:T(8,128)(2,1)S(1)}) custom-call(s32[32]{0:T(128)S(1)} %copy-done.2, bf16[72,2560]{1,0:T(8,128)(2,1)S(1)} %get-tuple-element.92.refs_0_, bf16[72,2560]{1,0:T(8,128)(2,1)S(1)} %collective-permute-done.14.refs_1_, ...), custom_call_target="tpu_custom_call" | custom-call | flops 5000000000 | bytes 50000000 | tf_op jit(solution)/shard_map/hidden/pallas_call | solution.py:502
  67.0 4.8 %back.4 = (bf16[72,2688]{1,0:T(8,128)(2,1)S(1)}, bf16[72,2688]{1,0:T(8,128)(2,1)S(1)}, bf16[72,2688]{1,0:T(8,128)(2,1)S(1)}, bf16[72,2688]{1,0:T(8,128)(2,1)S(1)...) custom-call(s32[32]{0:T(128)S(1)} %copy-done.2, bf16[288,1536]{1,0:T(8,128)(2,1)S(1)} %get-tuple-element.91.refs_0_.refs_2_, ...), custom_call_target="tpu_custom_call" | custom-call | flops 20000000000 | bytes 200000000 | tf_op jit(solution)/shard_map/back/pallas_call | solution.py:522
  74.5 5.7 %collective-permute-done.11.refs_2_ = bf16[72,2560]{1,0:T(8,128)(2,1)S(1)} collective-permute-done((bf16[72,2560]{1,0:T(8,128)(2,1)S(1)}, bf16[72,2560]{1,0:T(8,128)(2,1)S(1)}, u32[]{:S(2)}, u32[]{:S(2)}) %collective-permute-start.11) | collective-permute-done | bytes 368672 | tf_op jit(solution)/shard_map/ppermute | solution.py:392
  81.8 2.8 %hidden.7 = (bf16[288,1536]{1,0:T(8,128)(2,1)S(1)}, bf16[192,2048]{1,0:T(8,128)(2,1)S(1)}, bf16[96,2048]{1,0:T(8,128)(2,1)S(1)}) custom-call(s32[32]{0:T(128)S(1)} %copy-done.2, bf16[72,2560]{1,0:T(8,128)(2,1)S(1)} %get-tuple-element.87.refs_0_, bf16[72,2560]{1,0:T(8,128)(2,1)S(1)} %collective-permute-done.10.refs_1_, ...), custom_call_target="tpu_custom_call" | custom-call | flops 5000000000 | bytes 50000000 | tf_op jit(solution)/shard_map/hidden/pallas_call | solution.py:502
  84.7 4.6 %back.5 = (bf16[72,2560]{1,0:T(8,128)(2,1)S(1)}, bf16[72,2560]{1,0:T(8,128)(2,1)S(1)}, bf16[72,2560]{1,0:T(8,128)(2,1)S(1)}, bf16[72,2560]{1,0:T(8,128)(2,1)S(1)...) custom-call(s32[32]{0:T(128)S(1)} %copy-done.2, bf16[288,1536]{1,0:T(8,128)(2,1)S(1)} %get-tuple-element.106.refs_0_.refs_2_, ...), custom_call_target="tpu_custom_call" | custom-call | flops 20000000000 | bytes 200000000 | tf_op jit(solution)/shard_map/back/pallas_call | solution.py:522
  89.3 2.1 %collective-permute-start.26 = (bf16[72,2560]{1,0:T(8,128)(2,1)S(1)}, bf16[72,2560]{1,0:T(8,128)(2,1)S(1)}, u32[]{:S(2)}, u32[]{:S(2)}) collective-permute-start(bf16[72,2560]{1,0:T(8,128)(2,1)S(1)} %get-tuple-element.115), channel_id=1, source_target_pairs={{0,2},{2,0},{4,6},{6,4},{8,10},{10,8},{12,14},{14,12},{16,18},{18,... | collective-permute-start | bytes 1105928 | tf_op jit(solution)/shard_map/ppermute | solution.py:392
  91.4 5.4 %collective-permute-done.20.refs_2_ = bf16[72,2688]{1,0:T(8,128)(2,1)S(1)} collective-permute-done((bf16[72,2688]{1,0:T(8,128)(2,1)S(1)}, bf16[72,2688]{1,0:T(8,128)(2,1)S(1)}, u32[]{:S(2)}, u32[]{:S(2)}) %collective-permute-start.20) | collective-permute-done | bytes 387104 | tf_op jit(solution)/shard_map/ppermute | solution.py:392
  99.2 4.5 %back.6 = (bf16[72,2560]{1,0:T(8,128)(2,1)S(1)}, bf16[72,2560]{1,0:T(8,128)(2,1)S(1)}, bf16[72,2560]{1,0:T(8,128)(2,1)S(1)}, bf16[72,2560]{1,0:T(8,128)(2,1)S(1)...) custom-call(s32[32]{0:T(128)S(1)} %copy-done.2, bf16[288,1536]{1,0:T(8,128)(2,1)S(1)} %get-tuple-element.100.refs_0_.refs_2_, ...), custom_call_target="tpu_custom_call" | custom-call | flops 20000000000 | bytes 200000000 | tf_op jit(solution)/shard_map/back/pallas_call | solution.py:522
  104.4 8.1 %collective-permute-done.27.refs_2_ = bf16[72,2560]{1,0:T(8,128)(2,1)S(1)} collective-permute-done((bf16[72,2560]{1,0:T(8,128)(2,1)S(1)}, bf16[72,2560]{1,0:T(8,128)(2,1)S(1)}, u32[]{:S(2)}, u32[]{:S(2)}) %collective-permute-start.27) | collective-permute-done | bytes 368672 | tf_op jit(solution)/shard_map/ppermute | solution.py:392
  117.1 4.8 %back.7 = (bf16[72,2688]{1,0:T(8,128)(2,1)S(1)}, bf16[72,2688]{1,0:T(8,128)(2,1)S(1)}, bf16[72,2688]{1,0:T(8,128)(2,1)S(1)}, bf16[72,2688]{1,0:T(8,128)(2,1)S(1)...) custom-call(s32[32]{0:T(128)S(1)} %copy-done.2, bf16[288,1536]{1,0:T(8,128)(2,1)S(1)} %get-tuple-element.98.refs_0_.refs_2_, ...), custom_call_target="tpu_custom_call" | custom-call | flops 20000000000 | bytes 200000000 | tf_op jit(solution)/shard_map/back/pallas_call | solution.py:522
  121.8 3.3 %collective-permute-done.23.refs_1_ = bf16[72,2560]{1,0:T(8,128)(2,1)S(1)} collective-permute-done((bf16[72,2560]{1,0:T(8,128)(2,1)S(1)}, bf16[72,2560]{1,0:T(8,128)(2,1)S(1)}, u32[]{:S(2)}, u32[]{:S(2)}) %collective-permute-start.23) | collective-permute-done | bytes 368672 | tf_op jit(solution)/shard_map/ppermute | solution.py:392
  126.4 6.2 %collective-permute-done.24.refs_2_ = bf16[72,2560]{1,0:T(8,128)(2,1)S(1)} collective-permute-done((bf16[72,2560]{1,0:T(8,128)(2,1)S(1)}, bf16[72,2560]{1,0:T(8,128)(2,1)S(1)}, u32[]{:S(2)}, u32[]{:S(2)}) %collective-permute-start.24) | collective-permute-done | bytes 368672 | tf_op jit(solution)/shard_map/ppermute | solution.py:392
  136.2 9.5 %grad_up.1 = (bf16[2,2048,1024]{2,1,0:T(8,128)(2,1)}, f32[8,128]{1,0:T(8,128)S(1)}) custom-call(s32[32]{0:T(128)S(1)} %copy-done.2, bf16[192,2048]{1,0:T(8,128)(2,1)S(1)} %get-tuple-element.128.refs_0_, bf16[192,2048]{1,0:T(8,128)(2,1)S(1)} %get-tuple-element.129.refs_1_, bf16[192,2048]{1,0:T(8,128)(2,1)S(1)} %get-tuple-element.130.refs_2_, ...), custom_call_target="tpu_custom_call" | custom-call | flops 20000000000 | bytes 200000000 | tf_op jit(solution)/shard_map/grad_up/pallas_call | solution.py:569
  145.7 3.6 %collective-permute-done.33.refs_2_ = bf16[72,2688]{1,0:T(8,128)(2,1)S(1)} collective-permute-done((bf16[72,2688]{1,0:T(8,128)(2,1)S(1)}, bf16[72,2688]{1,0:T(8,128)(2,1)S(1)}, u32[]{:S(2)}, u32[]{:S(2)}) %collective-permute-start.33) | collective-permute-done | bytes 387104 | tf_op jit(solution)/shard_map/ppermute | solution.py:392
  149.9 3.0 %collective-permute-done.31.refs_0_ = bf16[128,2688]{1,0:T(8,128)(2,1)S(1)} collective-permute-done((bf16[128,2688]{1,0:T(8,128)(2,1)S(1)}, bf16[128,2688]{1,0:T(8,128)(2,1)S(1)}, u32[]{:S(2)}, u32[]{:S(2)}) %collective-permute-start.31) | collective-permute-done | bytes 688160 | tf_op jit(solution)/shard_map/ppermute | solution.py:388
  (79 shorter events, 39.0 us)
Async XLA Ops:
  0.6 20.7 %collective-permute-start = (bf16[128,2048]{1,0:T(8,128)(2,1)}, bf16[128,2048]{1,0:T(8,128)(2,1)S(1)}, u32[]{:S(2)}, u32[]{:S(2)}) collective-permute-start(bf16[128,2048]{1,0:T(8,128)(2,1)} %tokens.1), channel_id=1, source_target_pairs={{0,8},{2,10},{4,12},{6,14},{8,16},{10,18},{12,20},{14,22},{16,24},... | collective-permute-start | bytes 1572872 | tf_op jit(solution)/shard_map/ppermute | solution.py:388
  10.6 17.3 %collective-permute-start.8 = (bf16[72,2560]{1,0:T(8,128)(2,1)}, bf16[72,2560]{1,0:T(8,128)(2,1)S(1)}, u32[]{:S(2)}, u32[]{:S(2)}) collective-permute-start(bf16[72,2560]{1,0:T(8,128)(2,1)} %get-tuple-element.81), channel_id=1, source_target_pairs={{0,4},{2,6},{4,0},{6,2},{8,12},{10,14},{12,8},{14,10},{16,20},{18,... | collective-permute-start | bytes 1105928 | tf_op jit(solution)/shard_map/ppermute | solution.py:392
  12.2 17.6 %collective-permute-start.9 = (bf16[72,2560]{1,0:T(8,128)(2,1)}, bf16[72,2560]{1,0:T(8,128)(2,1)S(1)}, u32[]{:S(2)}, u32[]{:S(2)}) collective-permute-start(bf16[72,2560]{1,0:T(8,128)(2,1)} %get-tuple-element.82), channel_id=1, source_target_pairs={{0,6},{2,4},{4,2},{6,0},{8,14},{10,12},{12,10},{14,8},{16,22},{18,... | collective-permute-start | bytes 1105928 | tf_op jit(solution)/shard_map/ppermute | solution.py:392
  22.9 18.5 %collective-permute-start.2 = (bf16[128,2688]{1,0:T(8,128)(2,1)S(1)}, bf16[128,2688]{1,0:T(8,128)(2,1)S(1)}, u32[]{:S(2)}, u32[]{:S(2)}) collective-permute-start(bf16[128,2688]{1,0:T(8,128)(2,1)S(1)} %get-tuple-element.74), channel_id=1, source_target_pairs={{0,8},{2,10},{4,12},{6,14},{8,16},{10,18},{12,20},{14,22},{16,24},... | collective-permute-start | bytes 2064392 | tf_op jit(solution)/shard_map/ppermute | solution.py:388
  23.0 20.0 %collective-permute-start.4 = (bf16[72,2560]{1,0:T(8,128)(2,1)S(1)}, bf16[72,2560]{1,0:T(8,128)(2,1)S(1)}, u32[]{:S(2)}, u32[]{:S(2)}) collective-permute-start(bf16[72,2560]{1,0:T(8,128)(2,1)S(1)} %get-tuple-element.76), channel_id=1, source_target_pairs={{0,2},{2,0},{4,6},{6,4},{8,10},{10,8},{12,14},{14,12},{16,18},{18,... | collective-permute-start | bytes 1105928 | tf_op jit(solution)/shard_map/ppermute | solution.py:392
  24.6 19.7 %collective-permute-start.5 = (bf16[72,2560]{1,0:T(8,128)(2,1)S(1)}, bf16[72,2560]{1,0:T(8,128)(2,1)S(1)}, u32[]{:S(2)}, u32[]{:S(2)}) collective-permute-start(bf16[72,2560]{1,0:T(8,128)(2,1)S(1)} %get-tuple-element.77), channel_id=1, source_target_pairs={{0,4},{2,6},{4,0},{6,2},{8,12},{10,14},{12,8},{14,10},{16,20},{18,... | collective-permute-start | bytes 1105928 | tf_op jit(solution)/shard_map/ppermute | solution.py:392
  28.0 17.9 %collective-permute-start.6 = (bf16[72,2560]{1,0:T(8,128)(2,1)S(1)}, bf16[72,2560]{1,0:T(8,128)(2,1)S(1)}, u32[]{:S(2)}, u32[]{:S(2)}) collective-permute-start(bf16[72,2560]{1,0:T(8,128)(2,1)S(1)} %get-tuple-element.78), channel_id=1, source_target_pairs={{0,6},{2,4},{4,2},{6,0},{8,14},{10,12},{12,10},{14,8},{16,22},{18,... | collective-permute-start | bytes 1105928 | tf_op jit(solution)/shard_map/ppermute | solution.py:392
  33.5 33.4 %collective-permute-start.17 = (bf16[288,1536]{1,0:T(8,128)(2,1)S(1)}, bf16[288,1536]{1,0:T(8,128)(2,1)S(1)}, u32[]{:S(2)}, u32[]{:S(2)}) collective-permute-start(bf16[288,1536]{1,0:T(8,128)(2,1)S(1)} %get-tuple-element.98.refs_0_.refs_2_), channel_id=1, source_target_pairs={{0,1},{1,0},{2,3},{3,2},{4,5},{5,4},{6,7},{7,6},{8,9},{9,8},{10,11... | collective-permute-start | bytes 2654216 | tf_op jit(solution)/shard_map/ppermute | solution.py:512
  41.4 17.5 %collective-permute-start.3 = (bf16[128,2688]{1,0:T(8,128)(2,1)S(1)}, bf16[128,2688]{1,0:T(8,128)(2,1)S(1)}, u32[]{:S(2)}, u32[]{:S(2)}) collective-permute-start(bf16[128,2688]{1,0:T(8,128)(2,1)S(1)} %collective-permute-done.2.refs_0_.refs_1_.refs_6_), channel_id=1, source_target_pairs={{0,8},{2,10},{4,12},{6,14},{8,16},{10,18},{12,20},{14,22},{16,24},... | collective-permute-start | bytes 2064392 | tf_op jit(solution)/shard_map/ppermute | solution.py:388
  43.0 17.5 %collective-permute-start.14 = (bf16[72,2560]{1,0:T(8,128)(2,1)S(1)}, bf16[72,2560]{1,0:T(8,128)(2,1)S(1)}, u32[]{:S(2)}, u32[]{:S(2)}) collective-permute-start(bf16[72,2560]{1,0:T(8,128)(2,1)S(1)} %get-tuple-element.93), channel_id=1, source_target_pairs={{0,2},{2,0},{4,6},{6,4},{8,10},{10,8},{12,14},{14,12},{16,18},{18,... | collective-permute-start | bytes 1105928 | tf_op jit(solution)/shard_map/ppermute | solution.py:392
  44.3 17.2 %collective-permute-start.15 = (bf16[72,2560]{1,0:T(8,128)(2,1)S(1)}, bf16[72,2560]{1,0:T(8,128)(2,1)S(1)}, u32[]{:S(2)}, u32[]{:S(2)}) collective-permute-start(bf16[72,2560]{1,0:T(8,128)(2,1)S(1)} %get-tuple-element.94), channel_id=1, source_target_pairs={{0,4},{2,6},{4,0},{6,2},{8,12},{10,14},{12,8},{14,10},{16,20},{18,... | collective-permute-start | bytes 1105928 | tf_op jit(solution)/shard_map/ppermute | solution.py:392
  45.8 17.4 %collective-permute-start.16 = (bf16[72,2560]{1,0:T(8,128)(2,1)S(1)}, bf16[72,2560]{1,0:T(8,128)(2,1)S(1)}, u32[]{:S(2)}, u32[]{:S(2)}) collective-permute-start(bf16[72,2560]{1,0:T(8,128)(2,1)S(1)} %get-tuple-element.95), channel_id=1, source_target_pairs={{0,6},{2,4},{4,2},{6,0},{8,14},{10,12},{12,10},{14,8},{16,22},{18,... | collective-permute-start | bytes 1105928 | tf_op jit(solution)/shard_map/ppermute | solution.py:392
  61.6 18.6 %collective-permute-start.11 = (bf16[72,2560]{1,0:T(8,128)(2,1)S(1)}, bf16[72,2560]{1,0:T(8,128)(2,1)S(1)}, u32[]{:S(2)}, u32[]{:S(2)}) collective-permute-start(bf16[72,2560]{1,0:T(8,128)(2,1)S(1)} %get-tuple-element.89), channel_id=1, source_target_pairs={{0,4},{2,6},{4,0},{6,2},{8,12},{10,14},{12,8},{14,10},{16,20},{18,... | collective-permute-start | bytes 1105928 | tf_op jit(solution)/shard_map/ppermute | solution.py:392
  63.2 18.6 %collective-permute-start.12 = (bf16[72,2560]{1,0:T(8,128)(2,1)S(1)}, bf16[72,2560]{1,0:T(8,128)(2,1)S(1)}, u32[]{:S(2)}, u32[]{:S(2)}) collective-permute-start(bf16[72,2560]{1,0:T(8,128)(2,1)S(1)} %get-tuple-element.90), channel_id=1, source_target_pairs={{0,6},{2,4},{4,2},{6,0},{8,14},{10,12},{12,10},{14,8},{16,22},{18,... | collective-permute-start | bytes 1105928 | tf_op jit(solution)/shard_map/ppermute | solution.py:392
  66.9 17.8 %collective-permute-start.22 = (bf16[288,1536]{1,0:T(8,128)(2,1)S(1)}, bf16[288,1536]{1,0:T(8,128)(2,1)S(1)}, u32[]{:S(2)}, u32[]{:S(2)}) collective-permute-start(bf16[288,1536]{1,0:T(8,128)(2,1)S(1)} %get-tuple-element.106.refs_0_.refs_2_), channel_id=1, source_target_pairs={{0,1},{1,0},{2,3},{3,2},{4,5},{5,4},{6,7},{7,6},{8,9},{9,8},{10,11... | collective-permute-start | bytes 2654216 | tf_op jit(solution)/shard_map/ppermute | solution.py:512
  71.8 19.6 %collective-permute-start.19 = (bf16[72,2688]{1,0:T(8,128)(2,1)S(1)}, bf16[72,2688]{1,0:T(8,128)(2,1)S(1)}, u32[]{:S(2)}, u32[]{:S(2)}) collective-permute-start(bf16[72,2688]{1,0:T(8,128)(2,1)S(1)} %get-tuple-element.102), channel_id=1, source_target_pairs={{0,2},{2,0},{4,6},{6,4},{8,10},{10,8},{12,14},{14,12},{16,18},{18,... | collective-permute-start | bytes 1161224 | tf_op jit(solution)/shard_map/ppermute | solution.py:392
  72.8 23.9 %collective-permute-start.20 = (bf16[72,2688]{1,0:T(8,128)(2,1)S(1)}, bf16[72,2688]{1,0:T(8,128)(2,1)S(1)}, u32[]{:S(2)}, u32[]{:S(2)}) collective-permute-start(bf16[72,2688]{1,0:T(8,128)(2,1)S(1)} %get-tuple-element.103), channel_id=1, source_target_pairs={{0,4},{2,6},{4,0},{6,2},{8,12},{10,14},{12,8},{14,10},{16,20},{18,... | collective-permute-start | bytes 1161224 | tf_op jit(solution)/shard_map/ppermute | solution.py:392
  80.2 18.2 %collective-permute-start.21 = (bf16[72,2688]{1,0:T(8,128)(2,1)S(1)}, bf16[72,2688]{1,0:T(8,128)(2,1)S(1)}, u32[]{:S(2)}, u32[]{:S(2)}) collective-permute-start(bf16[72,2688]{1,0:T(8,128)(2,1)S(1)} %get-tuple-element.104), channel_id=1, source_target_pairs={{0,6},{2,4},{4,2},{6,0},{8,14},{10,12},{12,10},{14,8},{16,22},{18,... | collective-permute-start | bytes 1161224 | tf_op jit(solution)/shard_map/ppermute | solution.py:392
  91.4 21.2 %collective-permute-start.27 = (bf16[72,2560]{1,0:T(8,128)(2,1)S(1)}, bf16[72,2560]{1,0:T(8,128)(2,1)S(1)}, u32[]{:S(2)}, u32[]{:S(2)}) collective-permute-start(bf16[72,2560]{1,0:T(8,128)(2,1)S(1)} %get-tuple-element.116), channel_id=1, source_target_pairs={{0,4},{2,6},{4,0},{6,2},{8,12},{10,14},{12,8},{14,10},{16,20},{18,... | collective-permute-start | bytes 1105928 | tf_op jit(solution)/shard_map/ppermute | solution.py:392
  98.9 36.3 %collective-permute-start.30 = (bf16[128,2688]{1,0:T(8,128)(2,1)S(1)}, bf16[128,2688]{1,0:T(8,128)(2,1)S(1)}, u32[]{:S(2)}, u32[]{:S(2)}) collective-permute-start(bf16[128,2688]{1,0:T(8,128)(2,1)S(1)} %expand.4.refs_5_), channel_id=1, source_target_pairs={{0,24},{2,26},{4,28},{6,30},{8,0},{10,2},{12,4},{14,6},{16,8},{18,... | collective-permute-start | bytes 2064392 | tf_op jit(solution)/shard_map/ppermute | solution.py:388
  113.4 21.8 %collective-permute-start.29 = (bf16[128,2688]{1,0:T(8,128)(2,1)S(1)}, bf16[128,2688]{1,0:T(8,128)(2,1)S(1)}, u32[]{:S(2)}, u32[]{:S(2)}) collective-permute-start(bf16[128,2688]{1,0:T(8,128)(2,1)S(1)} %expand.5.refs_5_), channel_id=1, source_target_pairs={{0,8},{2,10},{4,12},{6,14},{8,16},{10,18},{12,20},{14,22},{16,24},... | collective-permute-start | bytes 2064392 | tf_op jit(solution)/shard_map/ppermute | solution.py:388
  114.9 17.7 %collective-permute-start.24 = (bf16[72,2560]{1,0:T(8,128)(2,1)S(1)}, bf16[72,2560]{1,0:T(8,128)(2,1)S(1)}, u32[]{:S(2)}, u32[]{:S(2)}) collective-permute-start(bf16[72,2560]{1,0:T(8,128)(2,1)S(1)} %get-tuple-element.111), channel_id=1, source_target_pairs={{0,4},{2,6},{4,0},{6,2},{8,12},{10,14},{12,8},{14,10},{16,20},{18,... | collective-permute-start | bytes 1105928 | tf_op jit(solution)/shard_map/ppermute | solution.py:392
  115.6 18.4 %collective-permute-start.25 = (bf16[72,2560]{1,0:T(8,128)(2,1)S(1)}, bf16[72,2560]{1,0:T(8,128)(2,1)S(1)}, u32[]{:S(2)}, u32[]{:S(2)}) collective-permute-start(bf16[72,2560]{1,0:T(8,128)(2,1)S(1)} %get-tuple-element.112), channel_id=1, source_target_pairs={{0,6},{2,4},{4,2},{6,0},{8,14},{10,12},{12,10},{14,8},{16,22},{18,... | collective-permute-start | bytes 1105928 | tf_op jit(solution)/shard_map/ppermute | solution.py:392
  125.1 20.7 %collective-permute-start.32 = (bf16[72,2688]{1,0:T(8,128)(2,1)S(1)}, bf16[72,2688]{1,0:T(8,128)(2,1)S(1)}, u32[]{:S(2)}, u32[]{:S(2)}) collective-permute-start(bf16[72,2688]{1,0:T(8,128)(2,1)S(1)} %get-tuple-element.123), channel_id=1, source_target_pairs={{0,2},{2,0},{4,6},{6,4},{8,10},{10,8},{12,14},{14,12},{16,18},{18,... | collective-permute-start | bytes 1161224 | tf_op jit(solution)/shard_map/ppermute | solution.py:392
  (18 other events, 265.4 us)

commit v9 on v8

--- a/solution.py
+++ b/solution.py
@@ -10,7 +10,7 @@
 INNER = 4
 CHUNKS = 4
 PLAN = ((0, None), (1, None), (2, None), (3, None), (None, 1), (None, 2), (None, 3), (None, 0))
-ORDER = ('x1', 'h0', 'x2', 'h1', 'x3', 'h2', 'r0', 'x4', 'h3', 'x5', 'r3', 'e1', 'x6', 'e2', 'r2', 'x7', 'z', 'e3', 'u', 'e0')
+ORDER = ('x1', 'h0', 'x2', 'h1', 'x3', 'h2', 'r0', 'x4', 'h3', 'x5', 'r3', 'e1', 'x6', 'z', 'e2', 'r2', 'x7', 'e3', 'u', 'e0')
 FIRST = 1
 COSTS = {'x': 5000, 'b': 20000, 'h': 5000, 'e': 1, 'u': 20000}
 TAIL = 128

time: 154 us -> 153 us (level)
  waiting for transfers between devices: 66.6 us -> 64.3 us
    ppermute x24, waiting for transfers between devices: 37.5 us -> 25.6 us  [across(): return lax.ppermute(value, 'ep', pairs)]
    ppermute x7, waiting for transfers between devices: 29.1 us -> 35.5 us  [along(): return lax.ppermute(value, 'ep', pairs)]
    ppermute x1, waiting for transfers between devices: 0.01 us -> 3.14 us  [on_device(): tails = [lax.ppermute(partials['apart'], ('ep', 'tp'), pairs)]]
  transfers between devices with their start and end apart: 36 -> 36, of which waited for: 14 -> 14; matrix products, arithmetic and copies ran while one was open for 0% -> 0% of each run, Pallas kernels for 33% -> 34%
where the time goes in v9:
time: 153 us
  waiting for transfers between devices  64.3 us (42%)
  Pallas kernels  52.8 us (35%)
  starting transfers between devices  35.1 us (23%)
    ppermute x7, waiting for transfers between devices, along(): return lax.ppermute(value, 'ep', pairs)  35.5 us
    ppermute x24, starting transfers between devices, across(): return lax.ppermute(value, 'ep', pairs)  29.7 us
    ppermute x24, waiting for transfers between devices, across(): return lax.ppermute(value, 'ep', pairs)  25.6 us
    pallas_call x4, Pallas kernels, step(): pl.pallas_call(functools.partial(back_kernel, *sizes, len(sums[c]), len(g...  18.6 us
    pallas_call x4, Pallas kernels, hidden(): pl.pallas_call(functools.partial(hidden_kernel, *sizes, feat, streamed, l...  12.3 us
    pallas_call x1, Pallas kernels, weight_grad(): pl.pallas_call(functools.partial(up_kernel, n, len(last)), out_shape=[blo...  9.49 us
    ppermute x7, starting transfers between devices, along(): return lax.ppermute(value, 'ep', pairs)  5.12 us
    pallas_call x3, Pallas kernels, select(): pl.pallas_call(functools.partial(select_kernel, *sizes, topk, share, skip...  4.68 us
  transfers between devices with their start and end apart: 36, of which 14 were waited for; matrix products, arithmetic and copies ran while one was open for 0% of the time, Pallas kernels for 34%

profile of v9, /device:TPU:0, one launch (start us, length us, event | category | flops | bytes accessed | tf_op | source)
XLA Modules:
  0.0 153.1 jit_solution(14660527800139864538)
XLA Ops:
  0.6 3.1 %collective-permute-start = (bf16[128,2048]{1,0:T(8,128)(2,1)}, bf16[128,2048]{1,0:T(8,128)(2,1)S(1)}, u32[]{:S(2)}, u32[]{:S(2)}) collective-permute-start(bf16[128,2048]{1,0:T(8,128)(2,1)} %tokens.1), channel_id=1, source_target_pairs={{0,8},{2,10},{4,12},{6,14},{8,16},{10,18},{12,20},{14,22},{16,24},... | collective-permute-start | bytes 1572872 | tf_op jit(solution)/shard_map/ppermute | solution.py:388
  3.7 3.8 %start.1 = (bf16[128,640]{1,0:T(8,128)(2,1)}, bf16[72,2560]{1,0:T(8,128)(2,1)}, bf16[72,2560]{1,0:T(8,128)(2,1)}, bf16[72,2560]{1,0:T(8,128)(2,1)}, bf16[72,2560...) custom-call(s32[32]{0:T(128)} %plan.25, bf16[128,2048]{1,0:T(8,128)(2,1)} %tokens.1, s32[8,128]{1,0:T(8,128)} %bitcast.5, ...), custom_call_target="tpu_custom_call" | custom-call | flops 5000000000 | bytes 50000000 | tf_op jit(solution)/shard_map/start/pallas_call | solution.py:421
  12.6 8.8 %collective-permute-done.1.refs_1_ = bf16[128,640]{1,0:T(8,128)(2,1)S(1)} collective-permute-done((bf16[128,640]{1,0:T(8,128)(2,1)}, bf16[128,640]{1,0:T(8,128)(2,1)S(1)}, u32[]{:S(2)}, u32[]{:S(2)}) %collective-permute-start.1) | collective-permute-done | bytes 163872 | tf_op jit(solution)/shard_map/ppermute | solution.py:388
  26.1 1.9 %collective-permute-done.8.refs_2_ = bf16[72,2560]{1,0:T(8,128)(2,1)S(1)} collective-permute-done((bf16[72,2560]{1,0:T(8,128)(2,1)}, bf16[72,2560]{1,0:T(8,128)(2,1)S(1)}, u32[]{:S(2)}, u32[]{:S(2)}) %collective-permute-start.8) | collective-permute-done | bytes 368672 | tf_op jit(solution)/shard_map/ppermute | solution.py:392
  29.8 3.8 %hidden.4 = (bf16[288,1536]{1,0:T(8,128)(2,1)S(1)}, bf16[192,2048]{1,0:T(8,128)(2,1)S(1)}, bf16[96,2048]{1,0:T(8,128)(2,1)S(1)}) custom-call(s32[32]{0:T(128)S(1)} %copy-done.2, bf16[72,2560]{1,0:T(8,128)(2,1)S(1)} %copy-done.3, bf16[72,2560]{1,0:T(8,128)(2,1)S(1)} %collective-permute-done.7.refs_1_, bf16[72,2560]{1,0:T(8,128)(2,1)S(1)} %collective-permute-done.8.refs_2_, ...), custom_call_target="tpu_custom_call" | custom-call | flops 5000000000 | bytes 50000000 | tf_op jit(solution)/shard_map/hidden/pallas_call | solution.py:502
  33.7 7.7 %collective-permute-done.2.refs_0_.refs_1_.refs_6_ = bf16[128,2688]{1,0:T(8,128)(2,1)S(1)} collective-permute-done((bf16[128,2688]{1,0:T(8,128)(2,1)S(1)}, bf16[128,2688]{1,0:T(8,128)(2,1)S(1)}, u32[]{:S(2)}, u32[]{:S(2)}) %collective-permute-start.2) | collective-permute-done | bytes 688160 | tf_op jit(solution)/shard_map/ppermute | solution.py:388
  46.6 2.8 %hidden.5 = (bf16[288,1536]{1,0:T(8,128)(2,1)S(1)}, bf16[192,2048]{1,0:T(8,128)(2,1)S(1)}, bf16[96,2048]{1,0:T(8,128)(2,1)S(1)}) custom-call(s32[32]{0:T(128)S(1)} %copy-done.2, bf16[72,2560]{1,0:T(8,128)(2,1)S(1)} %get-tuple-element.75.refs_0_, bf16[72,2560]{1,0:T(8,128)(2,1)S(1)} %collective-permute-done.4.refs_1_, ...), custom_call_target="tpu_custom_call" | custom-call | flops 5000000000 | bytes 50000000 | tf_op jit(solution)/shard_map/hidden/pallas_call | solution.py:502
  49.4 9.5 %collective-permute-done.3.refs_0_.refs_1_.refs_6_ = bf16[128,2688]{1,0:T(8,128)(2,1)S(1)} collective-permute-done((bf16[128,2688]{1,0:T(8,128)(2,1)S(1)}, bf16[128,2688]{1,0:T(8,128)(2,1)S(1)}, u32[]{:S(2)}, u32[]{:S(2)}) %collective-permute-start.3) | collective-permute-done | bytes 688160 | tf_op jit(solution)/shard_map/ppermute | solution.py:388
  64.1 2.9 %hidden.6 = (bf16[288,1536]{1,0:T(8,128)(2,1)S(1)}, bf16[192,2048]{1,0:T(8,128)(2,1)S(1)}, bf16[96,2048]{1,0:T(8,128)(2,1)S(1)}) custom-call(s32[32]{0:T(128)S(1)} %copy-done.2, bf16[72,2560]{1,0:T(8,128)(2,1)S(1)} %get-tuple-element.92.refs_0_, bf16[72,2560]{1,0:T(8,128)(2,1)S(1)} %collective-permute-done.14.refs_1_, ...), custom_call_target="tpu_custom_call" | custom-call | flops 5000000000 | bytes 50000000 | tf_op jit(solution)/shard_map/hidden/pallas_call | solution.py:502
  67.0 4.8 %back.4 = (bf16[72,2688]{1,0:T(8,128)(2,1)S(1)}, bf16[72,2688]{1,0:T(8,128)(2,1)S(1)}, bf16[72,2688]{1,0:T(8,128)(2,1)S(1)}, bf16[72,2688]{1,0:T(8,128)(2,1)S(1)...) custom-call(s32[32]{0:T(128)S(1)} %copy-done.2, bf16[288,1536]{1,0:T(8,128)(2,1)S(1)} %get-tuple-element.91.refs_0_.refs_2_, ...), custom_call_target="tpu_custom_call" | custom-call | flops 20000000000 | bytes 200000000 | tf_op jit(solution)/shard_map/back/pallas_call | solution.py:522
  74.5 5.7 %collective-permute-done.11.refs_2_ = bf16[72,2560]{1,0:T(8,128)(2,1)S(1)} collective-permute-done((bf16[72,2560]{1,0:T(8,128)(2,1)S(1)}, bf16[72,2560]{1,0:T(8,128)(2,1)S(1)}, u32[]{:S(2)}, u32[]{:S(2)}) %collective-permute-start.11) | collective-permute-done | bytes 368672 | tf_op jit(solution)/shard_map/ppermute | solution.py:392
  81.8 2.8 %hidden.7 = (bf16[288,1536]{1,0:T(8,128)(2,1)S(1)}, bf16[192,2048]{1,0:T(8,128)(2,1)S(1)}, bf16[96,2048]{1,0:T(8,128)(2,1)S(1)}) custom-call(s32[32]{0:T(128)S(1)} %copy-done.2, bf16[72,2560]{1,0:T(8,128)(2,1)S(1)} %get-tuple-element.87.refs_0_, bf16[72,2560]{1,0:T(8,128)(2,1)S(1)} %collective-permute-done.10.refs_1_, ...), custom_call_target="tpu_custom_call" | custom-call | flops 5000000000 | bytes 50000000 | tf_op jit(solution)/shard_map/hidden/pallas_call | solution.py:502
  84.7 4.5 %back.5 = (bf16[72,2560]{1,0:T(8,128)(2,1)S(1)}, bf16[72,2560]{1,0:T(8,128)(2,1)S(1)}, bf16[72,2560]{1,0:T(8,128)(2,1)S(1)}, bf16[72,2560]{1,0:T(8,128)(2,1)S(1)...) custom-call(s32[32]{0:T(128)S(1)} %copy-done.2, bf16[288,1536]{1,0:T(8,128)(2,1)S(1)} %get-tuple-element.106.refs_0_.refs_2_, ...), custom_call_target="tpu_custom_call" | custom-call | flops 20000000000 | bytes 200000000 | tf_op jit(solution)/shard_map/back/pallas_call | solution.py:522
  89.3 2.0 %collective-permute-start.26 = (bf16[72,2560]{1,0:T(8,128)(2,1)S(1)}, bf16[72,2560]{1,0:T(8,128)(2,1)S(1)}, u32[]{:S(2)}, u32[]{:S(2)}) collective-permute-start(bf16[72,2560]{1,0:T(8,128)(2,1)S(1)} %get-tuple-element.115), channel_id=1, source_target_pairs={{0,2},{2,0},{4,6},{6,4},{8,10},{10,8},{12,14},{14,12},{16,18},{18,... | collective-permute-start | bytes 1105928 | tf_op jit(solution)/shard_map/ppermute | solution.py:392
  91.3 5.4 %collective-permute-done.20.refs_2_ = bf16[72,2688]{1,0:T(8,128)(2,1)S(1)} collective-permute-done((bf16[72,2688]{1,0:T(8,128)(2,1)S(1)}, bf16[72,2688]{1,0:T(8,128)(2,1)S(1)}, u32[]{:S(2)}, u32[]{:S(2)}) %collective-permute-start.20) | collective-permute-done | bytes 387104 | tf_op jit(solution)/shard_map/ppermute | solution.py:392
  99.2 4.5 %back.6 = (bf16[72,2560]{1,0:T(8,128)(2,1)S(1)}, bf16[72,2560]{1,0:T(8,128)(2,1)S(1)}, bf16[72,2560]{1,0:T(8,128)(2,1)S(1)}, bf16[72,2560]{1,0:T(8,128)(2,1)S(1)...) custom-call(s32[32]{0:T(128)S(1)} %copy-done.2, bf16[288,1536]{1,0:T(8,128)(2,1)S(1)} %get-tuple-element.100.refs_0_.refs_2_, ...), custom_call_target="tpu_custom_call" | custom-call | flops 20000000000 | bytes 200000000 | tf_op jit(solution)/shard_map/back/pallas_call | solution.py:522
  103.7 2.1 %collective-permute-start.23 = (bf16[72,2560]{1,0:T(8,128)(2,1)S(1)}, bf16[72,2560]{1,0:T(8,128)(2,1)S(1)}, u32[]{:S(2)}, u32[]{:S(2)}) collective-permute-start(bf16[72,2560]{1,0:T(8,128)(2,1)S(1)} %get-tuple-element.110), channel_id=1, source_target_pairs={{0,2},{2,0},{4,6},{6,4},{8,10},{10,8},{12,14},{14,12},{16,18},{18,... | collective-permute-start | bytes 1105928 | tf_op jit(solution)/shard_map/ppermute | solution.py:392
  105.8 6.5 %collective-permute-done.27.refs_2_ = bf16[72,2560]{1,0:T(8,128)(2,1)S(1)} collective-permute-done((bf16[72,2560]{1,0:T(8,128)(2,1)S(1)}, bf16[72,2560]{1,0:T(8,128)(2,1)S(1)}, u32[]{:S(2)}, u32[]{:S(2)}) %collective-permute-start.27) | collective-permute-done | bytes 368672 | tf_op jit(solution)/shard_map/ppermute | solution.py:392
  116.7 4.8 %back.7 = (bf16[72,2688]{1,0:T(8,128)(2,1)S(1)}, bf16[72,2688]{1,0:T(8,128)(2,1)S(1)}, bf16[72,2688]{1,0:T(8,128)(2,1)S(1)}, bf16[72,2688]{1,0:T(8,128)(2,1)S(1)...) custom-call(s32[32]{0:T(128)S(1)} %copy-done.2, bf16[288,1536]{1,0:T(8,128)(2,1)S(1)} %get-tuple-element.98.refs_0_.refs_2_, ...), custom_call_target="tpu_custom_call" | custom-call | flops 20000000000 | bytes 200000000 | tf_op jit(solution)/shard_map/back/pallas_call | solution.py:522
  123.6 4.5 %collective-permute-done.24.refs_2_ = bf16[72,2560]{1,0:T(8,128)(2,1)S(1)} collective-permute-done((bf16[72,2560]{1,0:T(8,128)(2,1)S(1)}, bf16[72,2560]{1,0:T(8,128)(2,1)S(1)}, u32[]{:S(2)}, u32[]{:S(2)}) %collective-permute-start.24) | collective-permute-done | bytes 368672 | tf_op jit(solution)/shard_map/ppermute | solution.py:392
  129.7 4.4 %collective-permute-done.30.refs_7_ = bf16[128,2688]{1,0:T(8,128)(2,1)S(1)} collective-permute-done((bf16[128,2688]{1,0:T(8,128)(2,1)S(1)}, bf16[128,2688]{1,0:T(8,128)(2,1)S(1)}, u32[]{:S(2)}, u32[]{:S(2)}) %collective-permute-start.30) | collective-permute-done | bytes 688160 | tf_op jit(solution)/shard_map/ppermute | solution.py:388
  135.1 9.5 %grad_up.1 = (bf16[2,2048,1024]{2,1,0:T(8,128)(2,1)}, f32[8,128]{1,0:T(8,128)S(1)}) custom-call(s32[32]{0:T(128)S(1)} %copy-done.2, bf16[192,2048]{1,0:T(8,128)(2,1)S(1)} %get-tuple-element.128.refs_0_, bf16[192,2048]{1,0:T(8,128)(2,1)S(1)} %get-tuple-element.129.refs_1_, bf16[192,2048]{1,0:T(8,128)(2,1)S(1)} %get-tuple-element.130.refs_2_, ...), custom_call_target="tpu_custom_call" | custom-call | flops 20000000000 | bytes 200000000 | tf_op jit(solution)/shard_map/grad_up/pallas_call | solution.py:569
  145.5 3.1 %collective-permute-done.35.refs_3_ = bf16[128,128]{1,0:T(8,128)(2,1)S(1)} collective-permute-done((bf16[128,128]{1,0:T(8,128)(2,1)S(1)}, bf16[128,128]{1,0:T(8,128)(2,1)S(1)}, u32[]{:S(2)}, u32[]{:S(2)}) %collective-permute-start.35) | collective-permute-done | bytes 32800 | tf_op jit(solution)/shard_map/ppermute | solution.py:624
  148.6 3.3 %collective-permute-done.31.refs_0_ = bf16[128,2688]{1,0:T(8,128)(2,1)S(1)} collective-permute-done((bf16[128,2688]{1,0:T(8,128)(2,1)S(1)}, bf16[128,2688]{1,0:T(8,128)(2,1)S(1)}, u32[]{:S(2)}, u32[]{:S(2)}) %collective-permute-start.31) | collective-permute-done | bytes 688160 | tf_op jit(solution)/shard_map/ppermute | solution.py:388
  (79 shorter events, 40.0 us)
Async XLA Ops:
  0.6 20.7 %collective-permute-start = (bf16[128,2048]{1,0:T(8,128)(2,1)}, bf16[128,2048]{1,0:T(8,128)(2,1)S(1)}, u32[]{:S(2)}, u32[]{:S(2)}) collective-permute-start(bf16[128,2048]{1,0:T(8,128)(2,1)} %tokens.1), channel_id=1, source_target_pairs={{0,8},{2,10},{4,12},{6,14},{8,16},{10,18},{12,20},{14,22},{16,24},... | collective-permute-start | bytes 1572872 | tf_op jit(solution)/shard_map/ppermute | solution.py:388
  10.6 17.3 %collective-permute-start.8 = (bf16[72,2560]{1,0:T(8,128)(2,1)}, bf16[72,2560]{1,0:T(8,128)(2,1)S(1)}, u32[]{:S(2)}, u32[]{:S(2)}) collective-permute-start(bf16[72,2560]{1,0:T(8,128)(2,1)} %get-tuple-element.81), channel_id=1, source_target_pairs={{0,4},{2,6},{4,0},{6,2},{8,12},{10,14},{12,8},{14,10},{16,20},{18,... | collective-permute-start | bytes 1105928 | tf_op jit(solution)/shard_map/ppermute | solution.py:392
  12.2 17.6 %collective-permute-start.9 = (bf16[72,2560]{1,0:T(8,128)(2,1)}, bf16[72,2560]{1,0:T(8,128)(2,1)S(1)}, u32[]{:S(2)}, u32[]{:S(2)}) collective-permute-start(bf16[72,2560]{1,0:T(8,128)(2,1)} %get-tuple-element.82), channel_id=1, source_target_pairs={{0,6},{2,4},{4,2},{6,0},{8,14},{10,12},{12,10},{14,8},{16,22},{18,... | collective-permute-start | bytes 1105928 | tf_op jit(solution)/shard_map/ppermute | solution.py:392
  22.9 18.5 %collective-permute-start.2 = (bf16[128,2688]{1,0:T(8,128)(2,1)S(1)}, bf16[128,2688]{1,0:T(8,128)(2,1)S(1)}, u32[]{:S(2)}, u32[]{:S(2)}) collective-permute-start(bf16[128,2688]{1,0:T(8,128)(2,1)S(1)} %get-tuple-element.74), channel_id=1, source_target_pairs={{0,8},{2,10},{4,12},{6,14},{8,16},{10,18},{12,20},{14,22},{16,24},... | collective-permute-start | bytes 2064392 | tf_op jit(solution)/shard_map/ppermute | solution.py:388
  23.0 20.0 %collective-permute-start.4 = (bf16[72,2560]{1,0:T(8,128)(2,1)S(1)}, bf16[72,2560]{1,0:T(8,128)(2,1)S(1)}, u32[]{:S(2)}, u32[]{:S(2)}) collective-permute-start(bf16[72,2560]{1,0:T(8,128)(2,1)S(1)} %get-tuple-element.76), channel_id=1, source_target_pairs={{0,2},{2,0},{4,6},{6,4},{8,10},{10,8},{12,14},{14,12},{16,18},{18,... | collective-permute-start | bytes 1105928 | tf_op jit(solution)/shard_map/ppermute | solution.py:392
  24.6 19.7 %collective-permute-start.5 = (bf16[72,2560]{1,0:T(8,128)(2,1)S(1)}, bf16[72,2560]{1,0:T(8,128)(2,1)S(1)}, u32[]{:S(2)}, u32[]{:S(2)}) collective-permute-start(bf16[72,2560]{1,0:T(8,128)(2,1)S(1)} %get-tuple-element.77), channel_id=1, source_target_pairs={{0,4},{2,6},{4,0},{6,2},{8,12},{10,14},{12,8},{14,10},{16,20},{18,... | collective-permute-start | bytes 1105928 | tf_op jit(solution)/shard_map/ppermute | solution.py:392
  28.0 17.9 %collective-permute-start.6 = (bf16[72,2560]{1,0:T(8,128)(2,1)S(1)}, bf16[72,2560]{1,0:T(8,128)(2,1)S(1)}, u32[]{:S(2)}, u32[]{:S(2)}) collective-permute-start(bf16[72,2560]{1,0:T(8,128)(2,1)S(1)} %get-tuple-element.78), channel_id=1, source_target_pairs={{0,6},{2,4},{4,2},{6,0},{8,14},{10,12},{12,10},{14,8},{16,22},{18,... | collective-permute-start | bytes 1105928 | tf_op jit(solution)/shard_map/ppermute | solution.py:392
  33.6 33.3 %collective-permute-start.17 = (bf16[288,1536]{1,0:T(8,128)(2,1)S(1)}, bf16[288,1536]{1,0:T(8,128)(2,1)S(1)}, u32[]{:S(2)}, u32[]{:S(2)}) collective-permute-start(bf16[288,1536]{1,0:T(8,128)(2,1)S(1)} %get-tuple-element.98.refs_0_.refs_2_), channel_id=1, source_target_pairs={{0,1},{1,0},{2,3},{3,2},{4,5},{5,4},{6,7},{7,6},{8,9},{9,8},{10,11... | collective-permute-start | bytes 2654216 | tf_op jit(solution)/shard_map/ppermute | solution.py:512
  41.4 17.5 %collective-permute-start.3 = (bf16[128,2688]{1,0:T(8,128)(2,1)S(1)}, bf16[128,2688]{1,0:T(8,128)(2,1)S(1)}, u32[]{:S(2)}, u32[]{:S(2)}) collective-permute-start(bf16[128,2688]{1,0:T(8,128)(2,1)S(1)} %collective-permute-done.2.refs_0_.refs_1_.refs_6_), channel_id=1, source_target_pairs={{0,8},{2,10},{4,12},{6,14},{8,16},{10,18},{12,20},{14,22},{16,24},... | collective-permute-start | bytes 2064392 | tf_op jit(solution)/shard_map/ppermute | solution.py:388
  43.0 17.5 %collective-permute-start.14 = (bf16[72,2560]{1,0:T(8,128)(2,1)S(1)}, bf16[72,2560]{1,0:T(8,128)(2,1)S(1)}, u32[]{:S(2)}, u32[]{:S(2)}) collective-permute-start(bf16[72,2560]{1,0:T(8,128)(2,1)S(1)} %get-tuple-element.93), channel_id=1, source_target_pairs={{0,2},{2,0},{4,6},{6,4},{8,10},{10,8},{12,14},{14,12},{16,18},{18,... | collective-permute-start | bytes 1105928 | tf_op jit(solution)/shard_map/ppermute | solution.py:392
  45.8 17.4 %collective-permute-start.16 = (bf16[72,2560]{1,0:T(8,128)(2,1)S(1)}, bf16[72,2560]{1,0:T(8,128)(2,1)S(1)}, u32[]{:S(2)}, u32[]{:S(2)}) collective-permute-start(bf16[72,2560]{1,0:T(8,128)(2,1)S(1)} %get-tuple-element.95), channel_id=1, source_target_pairs={{0,6},{2,4},{4,2},{6,0},{8,14},{10,12},{12,10},{14,8},{16,22},{18,... | collective-permute-start | bytes 1105928 | tf_op jit(solution)/shard_map/ppermute | solution.py:392
  61.6 18.6 %collective-permute-start.11 = (bf16[72,2560]{1,0:T(8,128)(2,1)S(1)}, bf16[72,2560]{1,0:T(8,128)(2,1)S(1)}, u32[]{:S(2)}, u32[]{:S(2)}) collective-permute-start(bf16[72,2560]{1,0:T(8,128)(2,1)S(1)} %get-tuple-element.89), channel_id=1, source_target_pairs={{0,4},{2,6},{4,0},{6,2},{8,12},{10,14},{12,8},{14,10},{16,20},{18,... | collective-permute-start | bytes 1105928 | tf_op jit(solution)/shard_map/ppermute | solution.py:392
  63.2 18.6 %collective-permute-start.12 = (bf16[72,2560]{1,0:T(8,128)(2,1)S(1)}, bf16[72,2560]{1,0:T(8,128)(2,1)S(1)}, u32[]{:S(2)}, u32[]{:S(2)}) collective-permute-start(bf16[72,2560]{1,0:T(8,128)(2,1)S(1)} %get-tuple-element.90), channel_id=1, source_target_pairs={{0,6},{2,4},{4,2},{6,0},{8,14},{10,12},{12,10},{14,8},{16,22},{18,... | collective-permute-start | bytes 1105928 | tf_op jit(solution)/shard_map/ppermute | solution.py:392
  66.9 17.8 %collective-permute-start.22 = (bf16[288,1536]{1,0:T(8,128)(2,1)S(1)}, bf16[288,1536]{1,0:T(8,128)(2,1)S(1)}, u32[]{:S(2)}, u32[]{:S(2)}) collective-permute-start(bf16[288,1536]{1,0:T(8,128)(2,1)S(1)} %get-tuple-element.106.refs_0_.refs_2_), channel_id=1, source_target_pairs={{0,1},{1,0},{2,3},{3,2},{4,5},{5,4},{6,7},{7,6},{8,9},{9,8},{10,11... | collective-permute-start | bytes 2654216 | tf_op jit(solution)/shard_map/ppermute | solution.py:512
  71.8 19.5 %collective-permute-start.19 = (bf16[72,2688]{1,0:T(8,128)(2,1)S(1)}, bf16[72,2688]{1,0:T(8,128)(2,1)S(1)}, u32[]{:S(2)}, u32[]{:S(2)}) collective-permute-start(bf16[72,2688]{1,0:T(8,128)(2,1)S(1)} %get-tuple-element.102), channel_id=1, source_target_pairs={{0,2},{2,0},{4,6},{6,4},{8,10},{10,8},{12,14},{14,12},{16,18},{18,... | collective-permute-start | bytes 1161224 | tf_op jit(solution)/shard_map/ppermute | solution.py:392
  72.9 23.9 %collective-permute-start.20 = (bf16[72,2688]{1,0:T(8,128)(2,1)S(1)}, bf16[72,2688]{1,0:T(8,128)(2,1)S(1)}, u32[]{:S(2)}, u32[]{:S(2)}) collective-permute-start(bf16[72,2688]{1,0:T(8,128)(2,1)S(1)} %get-tuple-element.103), channel_id=1, source_target_pairs={{0,4},{2,6},{4,0},{6,2},{8,12},{10,14},{12,8},{14,10},{16,20},{18,... | collective-permute-start | bytes 1161224 | tf_op jit(solution)/shard_map/ppermute | solution.py:392
  80.2 18.2 %collective-permute-start.21 = (bf16[72,2688]{1,0:T(8,128)(2,1)S(1)}, bf16[72,2688]{1,0:T(8,128)(2,1)S(1)}, u32[]{:S(2)}, u32[]{:S(2)}) collective-permute-start(bf16[72,2688]{1,0:T(8,128)(2,1)S(1)} %get-tuple-element.104), channel_id=1, source_target_pairs={{0,6},{2,4},{4,2},{6,0},{8,14},{10,12},{12,10},{14,8},{16,22},{18,... | collective-permute-start | bytes 1161224 | tf_op jit(solution)/shard_map/ppermute | solution.py:392
  91.3 21.0 %collective-permute-start.27 = (bf16[72,2560]{1,0:T(8,128)(2,1)S(1)}, bf16[72,2560]{1,0:T(8,128)(2,1)S(1)}, u32[]{:S(2)}, u32[]{:S(2)}) collective-permute-start(bf16[72,2560]{1,0:T(8,128)(2,1)S(1)} %get-tuple-element.116), channel_id=1, source_target_pairs={{0,4},{2,6},{4,0},{6,2},{8,12},{10,14},{12,8},{14,10},{16,20},{18,... | collective-permute-start | bytes 1105928 | tf_op jit(solution)/shard_map/ppermute | solution.py:392
  103.7 18.8 %collective-permute-start.23 = (bf16[72,2560]{1,0:T(8,128)(2,1)S(1)}, bf16[72,2560]{1,0:T(8,128)(2,1)S(1)}, u32[]{:S(2)}, u32[]{:S(2)}) collective-permute-start(bf16[72,2560]{1,0:T(8,128)(2,1)S(1)} %get-tuple-element.110), channel_id=1, source_target_pairs={{0,2},{2,0},{4,6},{6,4},{8,10},{10,8},{12,14},{14,12},{16,18},{18,... | collective-permute-start | bytes 1105928 | tf_op jit(solution)/shard_map/ppermute | solution.py:392
  105.8 22.3 %collective-permute-start.24 = (bf16[72,2560]{1,0:T(8,128)(2,1)S(1)}, bf16[72,2560]{1,0:T(8,128)(2,1)S(1)}, u32[]{:S(2)}, u32[]{:S(2)}) collective-permute-start(bf16[72,2560]{1,0:T(8,128)(2,1)S(1)} %get-tuple-element.111), channel_id=1, source_target_pairs={{0,4},{2,6},{4,0},{6,2},{8,12},{10,14},{12,8},{14,10},{16,20},{18,... | collective-permute-start | bytes 1105928 | tf_op jit(solution)/shard_map/ppermute | solution.py:392
  112.3 17.4 %collective-permute-start.25 = (bf16[72,2560]{1,0:T(8,128)(2,1)S(1)}, bf16[72,2560]{1,0:T(8,128)(2,1)S(1)}, u32[]{:S(2)}, u32[]{:S(2)}) collective-permute-start(bf16[72,2560]{1,0:T(8,128)(2,1)S(1)} %get-tuple-element.112), channel_id=1, source_target_pairs={{0,6},{2,4},{4,2},{6,0},{8,14},{10,12},{12,10},{14,8},{16,22},{18,... | collective-permute-start | bytes 1105928 | tf_op jit(solution)/shard_map/ppermute | solution.py:392
  116.6 17.5 %collective-permute-start.30 = (bf16[128,2688]{1,0:T(8,128)(2,1)S(1)}, bf16[128,2688]{1,0:T(8,128)(2,1)S(1)}, u32[]{:S(2)}, u32[]{:S(2)}) collective-permute-start(bf16[128,2688]{1,0:T(8,128)(2,1)S(1)} %expand.5.refs_5_), channel_id=1, source_target_pairs={{0,8},{2,10},{4,12},{6,14},{8,16},{10,18},{12,20},{14,22},{16,24},... | collective-permute-start | bytes 2064392 | tf_op jit(solution)/shard_map/ppermute | solution.py:388
  121.4 23.2 %collective-permute-start.32 = (bf16[72,2688]{1,0:T(8,128)(2,1)S(1)}, bf16[72,2688]{1,0:T(8,128)(2,1)S(1)}, u32[]{:S(2)}, u32[]{:S(2)}) collective-permute-start(bf16[72,2688]{1,0:T(8,128)(2,1)S(1)} %get-tuple-element.123), channel_id=1, source_target_pairs={{0,2},{2,0},{4,6},{6,4},{8,10},{10,8},{12,14},{14,12},{16,18},{18,... | collective-permute-start | bytes 1161224 | tf_op jit(solution)/shard_map/ppermute | solution.py:392
  122.6 22.1 %collective-permute-start.33 = (bf16[72,2688]{1,0:T(8,128)(2,1)S(1)}, bf16[72,2688]{1,0:T(8,128)(2,1)S(1)}, u32[]{:S(2)}, u32[]{:S(2)}) collective-permute-start(bf16[72,2688]{1,0:T(8,128)(2,1)S(1)} %get-tuple-element.124), channel_id=1, source_target_pairs={{0,4},{2,6},{4,0},{6,2},{8,12},{10,14},{12,8},{14,10},{16,20},{18,... | collective-permute-start | bytes 1161224 | tf_op jit(solution)/shard_map/ppermute | solution.py:392
  (18 other events, 269.0 us)
